TPU v7x, 32 devices: a whole 2x2x4 slice. The times are simulated.
32 devices in a mesh: dp: 4 (over y, x), fsdp: 8 (over z, core).
Axes of the slice: x: 2, y: 2, z: 4, core: 2. Of those that a mesh axis runs over, the one named last changes fastest.
Arguments:
- latents: bfloat16 [64, 256, 384], P(('dp', 'fsdp')), may hold values from -6 to 6
- cond: bfloat16 [64, 384], P(('dp', 'fsdp')), may hold values from -6 to 6
- counts: int32 [32], P(('dp', 'fsdp')), may hold values from 1 to 2, as said below
- cotangent: bfloat16 [64, 256, 384], P(('dp', 'fsdp')), may hold values from -6 to 6
- modulation_weight: bfloat16 [384, 2304], P('fsdp'), may hold values from -0.3125 to 0.3125
- modulation_bias: bfloat16 [2304], P('fsdp'), may hold values from -1.796875 to 1.796875
- projection_weight: bfloat16 [384, 1152], P('fsdp'), may hold values from -0.3125 to 0.3125
- query_value_bias: bfloat16 [768], P('fsdp'), may hold values from -1.796875 to 1.796875
- output_weight: bfloat16 [384, 384], P('fsdp'), may hold values from -1.25 to 1.25
- output_bias: bfloat16 [384], P('fsdp'), may hold values from -1.796875 to 1.796875
- up_weight: bfloat16 [384, 1536], P('fsdp'), may hold values from -0.3125 to 0.3125
- up_bias: bfloat16 [1536], P('fsdp'), may hold values from -1.796875 to 1.796875
- down_weight: bfloat16 [1536, 384], P('fsdp'), may hold values from -0.3125 to 0.3125
- down_bias: bfloat16 [384], P('fsdp'), may hold values from -1.796875 to 1.796875
Outputs:
- result: bfloat16 [64, 256, 384], P(('dp', 'fsdp'))
- latent_grad: bfloat16 [64, 256, 384], P(('dp', 'fsdp'))
- cond_grad: bfloat16 [64, 384], P(('dp', 'fsdp'))
- grad_modulation_weight: float32 [384, 2304], P('fsdp')
- grad_modulation_bias: float32 [2304], P('fsdp')
- grad_projection_weight: float32 [384, 1152], P('fsdp')
- grad_query_value_bias: float32 [768], P('fsdp')
- grad_output_weight: float32 [384, 384], P('fsdp')
- grad_output_bias: float32 [384], P('fsdp')
- grad_up_weight: float32 [384, 1536], P('fsdp')
- grad_up_bias: float32 [1536], P('fsdp')
- grad_down_weight: float32 [1536, 384], P('fsdp')
- grad_down_bias: float32 [384], P('fsdp')
Inputs may be any that keep to these rules, and one draw needn't show every extreme that they name: `counts`: slots i of a device with i < its count hold live latents, the others padding; some device holds 2 live latents and some holds 1.
All inputs are finite; a program needn't handle non-finite values.
Results may differ from a plain program's by a relative error of at most 0.015.
The roundings to bfloat16 on the way count: a program that leaves them out, or rounds other values in their place, can miss the bound.
Values may be sent and summed in bfloat16 or wider, within the bound.
No kernel may reach another device: no remote copies, remote signals or barrier semaphores. Data moves between devices by JAX's collectives and lax.ppermute only.
A program may use at most 128 MiB of HBM per device.

v0:
```python
import jax
import jax.numpy as jnp
from jax import lax
from jax.sharding import PartitionSpec as P

HEADS = 6
HEAD_DIM = 64
MICRO = 2


def layer_norm(vector):
    row_mean = jnp.mean(vector, axis=-1, keepdims=True)
    centered = vector - row_mean
    variance = jnp.mean(centered * centered, axis=-1, keepdims=True)
    return centered * lax.rsqrt(variance + 1e-06)


def modulate(vector, offset, stretch):
    return layer_norm(vector) * (1.0 + stretch[:, None, :]) + offset[:, None, :]


def forward_pass(gathered, inputs, conditions):
    (
        modulation_weight,
        modulation_bias,
        projection_weight,
        query_value_bias,
        output_weight,
        output_bias,
        up_weight,
        up_bias,
        down_weight,
        down_bias,
    ) = gathered
    members, length, features = inputs.shape
    flat_rows = members * length
    cond_low = jax.nn.silu(conditions).astype(jnp.bfloat16)
    modulation = jnp.dot(cond_low, modulation_weight, preferred_element_type=jnp.float32)
    modulation = modulation + modulation_bias.astype(jnp.float32)
    pieces = jnp.split(modulation, 6, axis=-1)
    normed_one = (
        modulate(inputs, pieces[0], pieces[1]).astype(jnp.bfloat16).reshape(flat_rows, features)
    )
    bias_full = query_value_bias.astype(jnp.float32)
    joined_bias = jnp.concatenate(
        [bias_full[:features], jnp.zeros((features,), jnp.float32), bias_full[features:]]
    )
    projected = (
        jnp.dot(normed_one, projection_weight, preferred_element_type=jnp.float32) + joined_bias
    )
    projected = projected.astype(jnp.bfloat16).reshape(members, length, 3, HEADS, HEAD_DIM)
    queries = projected[:, :, 0]
    key_rows = projected[:, :, 1]
    values = projected[:, :, 2]
    scores = jnp.einsum(
        "bqhd,bkhd->bhqk", queries, key_rows, preferred_element_type=jnp.float32
    ) * HEAD_DIM ** (-0.5)
    row_max = jnp.max(scores, axis=-1, keepdims=True)
    exponent = jnp.exp(scores - row_max)
    row_total = jnp.sum(exponent, axis=-1, keepdims=True)
    probability = exponent / row_total
    log_total = row_max + jnp.log(row_total)
    attended = jnp.einsum(
        "bhqk,bkhd->bqhd",
        probability.astype(jnp.bfloat16),
        values,
        preferred_element_type=jnp.float32,
    )
    attended = attended.astype(jnp.bfloat16).reshape(flat_rows, features)
    branch = jnp.dot(
        attended, output_weight, preferred_element_type=jnp.float32
    ) + output_bias.astype(jnp.float32)
    branch = branch.reshape(members, length, features)
    middle = inputs + pieces[2][:, None, :] * branch
    normed_two = (
        modulate(middle, pieces[3], pieces[4]).astype(jnp.bfloat16).reshape(flat_rows, features)
    )
    pre_act = jnp.dot(normed_two, up_weight, preferred_element_type=jnp.float32) + up_bias.astype(
        jnp.float32
    )
    activated = jax.nn.gelu(pre_act, approximate=True).astype(jnp.bfloat16)
    mlp_out = jnp.dot(
        activated, down_weight, preferred_element_type=jnp.float32
    ) + down_bias.astype(jnp.float32)
    mlp_out = mlp_out.reshape(members, length, features)
    output = middle + pieces[5][:, None, :] * mlp_out
    return (
        output,
        cond_low,
        pieces,
        normed_one,
        queries,
        key_rows,
        values,
        log_total,
        attended,
        branch,
        middle,
        normed_two,
        pre_act,
        activated,
        mlp_out,
    )


def backward_pass(gathered, saved, inputs, conditions, upstream):
    (
        modulation_weight,
        modulation_bias,
        projection_weight,
        query_value_bias,
        output_weight,
        output_bias,
        up_weight,
        up_bias,
        down_weight,
        down_bias,
    ) = gathered
    (
        output,
        cond_low,
        pieces,
        normed_one,
        queries,
        key_rows,
        values,
        log_total,
        attended,
        branch,
        middle,
        normed_two,
        pre_act,
        activated,
        mlp_out,
    ) = saved
    members, length, features = inputs.shape
    flat_rows = members * length
    grad_gate_two = jnp.sum(upstream * mlp_out, axis=1)
    grad_mlp = (pieces[5][:, None, :] * upstream).astype(jnp.bfloat16).reshape(flat_rows, features)
    grad_down = jnp.einsum("nf,nd->fd", activated, grad_mlp, preferred_element_type=jnp.float32)
    grad_down_b = jnp.sum(grad_mlp.astype(jnp.float32), axis=0)
    grad_activated = jnp.einsum(
        "nd,fd->nf", grad_mlp, down_weight, preferred_element_type=jnp.float32
    )
    gelu_out, gelu_pull = jax.vjp(lambda vector: jax.nn.gelu(vector, approximate=True), pre_act)
    grad_pre = gelu_pull(grad_activated)[0].astype(jnp.bfloat16)
    grad_up = jnp.einsum("nd,nf->df", normed_two, grad_pre, preferred_element_type=jnp.float32)
    grad_up_b = jnp.sum(grad_pre.astype(jnp.float32), axis=0)
    grad_normed_two = jnp.einsum(
        "nf,df->nd", grad_pre, up_weight, preferred_element_type=jnp.float32
    )
    second_out, second_pull = jax.vjp(modulate, middle, pieces[3], pieces[4])
    grad_middle, grad_shift_two, grad_scale_two = second_pull(
        grad_normed_two.reshape(members, length, features)
    )
    grad_middle = grad_middle + upstream
    grad_gate_one = jnp.sum(grad_middle * branch, axis=1)
    grad_branch = (
        (pieces[2][:, None, :] * grad_middle).astype(jnp.bfloat16).reshape(flat_rows, features)
    )
    grad_output = jnp.einsum("nd,ne->de", attended, grad_branch, preferred_element_type=jnp.float32)
    grad_output_b = jnp.sum(grad_branch.astype(jnp.float32), axis=0)
    grad_attended = jnp.einsum(
        "ne,de->nd", grad_branch, output_weight, preferred_element_type=jnp.float32
    )
    grad_attended = grad_attended.astype(jnp.bfloat16).reshape(members, length, HEADS, HEAD_DIM)
    scale_factor = HEAD_DIM ** (-0.5)
    scores = (
        jnp.einsum("bqhd,bkhd->bhqk", queries, key_rows, preferred_element_type=jnp.float32)
        * scale_factor
    )
    probability = jnp.exp(scores - log_total)
    grad_values = jnp.einsum(
        "bhqk,bqhd->bkhd",
        probability.astype(jnp.bfloat16),
        grad_attended,
        preferred_element_type=jnp.float32,
    )
    grad_prob = jnp.einsum(
        "bqhd,bkhd->bhqk", grad_attended, values, preferred_element_type=jnp.float32
    )
    row_delta = jnp.sum(grad_prob * probability, axis=-1, keepdims=True)
    grad_scores = (probability * (grad_prob - row_delta)).astype(jnp.bfloat16)
    grad_queries = (
        jnp.einsum("bhqk,bkhd->bqhd", grad_scores, key_rows, preferred_element_type=jnp.float32)
        * scale_factor
    )
    grad_keys = (
        jnp.einsum("bhqk,bqhd->bkhd", grad_scores, queries, preferred_element_type=jnp.float32)
        * scale_factor
    )
    grad_projected = jnp.stack([grad_queries, grad_keys, grad_values], axis=2)
    grad_projected = grad_projected.astype(jnp.bfloat16).reshape(flat_rows, 3 * features)
    grad_projection = jnp.einsum(
        "nd,ne->de", normed_one, grad_projected, preferred_element_type=jnp.float32
    )
    column_sums = jnp.sum(grad_projected.astype(jnp.float32), axis=0)
    grad_query_value = jnp.concatenate([column_sums[:features], column_sums[2 * features :]])
    grad_normed_one = jnp.einsum(
        "ne,de->nd", grad_projected, projection_weight, preferred_element_type=jnp.float32
    )
    first_out, first_pull = jax.vjp(modulate, inputs, pieces[0], pieces[1])
    grad_input, grad_shift_one, grad_scale_one = first_pull(
        grad_normed_one.reshape(members, length, features)
    )
    grad_input = grad_input + grad_middle
    grad_modulation = jnp.concatenate(
        [
            grad_shift_one,
            grad_scale_one,
            grad_gate_one,
            grad_shift_two,
            grad_scale_two,
            grad_gate_two,
        ],
        axis=-1,
    ).astype(jnp.bfloat16)
    grad_mod_weight = jnp.einsum(
        "bc,be->ce", cond_low, grad_modulation, preferred_element_type=jnp.float32
    )
    grad_mod_bias = jnp.sum(grad_modulation.astype(jnp.float32), axis=0)
    grad_silu = jnp.einsum(
        "be,ce->bc", grad_modulation, modulation_weight, preferred_element_type=jnp.float32
    )
    silu_out, silu_pull = jax.vjp(jax.nn.silu, conditions)
    grad_conditions = silu_pull(grad_silu)[0]
    weight_grads = (
        grad_mod_weight,
        grad_mod_bias,
        grad_projection,
        grad_query_value,
        grad_output,
        grad_output_b,
        grad_up,
        grad_up_b,
        grad_down,
        grad_down_b,
    )
    return (weight_grads, grad_input, grad_conditions)


def on_device(
    latents,
    cond,
    counts,
    cotangent,
    modulation_weight,
    modulation_bias,
    projection_weight,
    query_value_bias,
    output_weight,
    output_bias,
    up_weight,
    up_bias,
    down_weight,
    down_bias,
):
    lat_slots = latents.shape[0]
    per_micro = lat_slots // MICRO
    alive_all = (jnp.arange(lat_slots) < counts[0]).astype(jnp.float32)
    kept = (
        lax.all_gather(modulation_weight, "fsdp", axis=0, tiled=True),
        lax.all_gather(modulation_bias, "fsdp", axis=0, tiled=True),
        lax.all_gather(projection_weight, "fsdp", axis=0, tiled=True),
        lax.all_gather(query_value_bias, "fsdp", axis=0, tiled=True),
        lax.all_gather(output_weight, "fsdp", axis=0, tiled=True),
        lax.all_gather(output_bias, "fsdp", axis=0, tiled=True),
        lax.all_gather(up_weight, "fsdp", axis=0, tiled=True),
        lax.all_gather(up_bias, "fsdp", axis=0, tiled=True),
        lax.all_gather(down_weight, "fsdp", axis=0, tiled=True),
        lax.all_gather(down_bias, "fsdp", axis=0, tiled=True),
    )
    outputs = []
    input_grads = []
    cond_grads = []
    totals = None
    for micro_index in range(MICRO):
        start = micro_index * per_micro
        inputs = latents[start : start + per_micro].astype(jnp.float32)
        conditions = cond[start : start + per_micro].astype(jnp.float32)
        alive_mask = alive_all[start : start + per_micro]
        saved = forward_pass(kept, inputs, conditions)
        outputs.append((saved[0] * alive_mask[:, None, None]).astype(jnp.bfloat16))
        upstream = (
            cotangent[start : start + per_micro].astype(jnp.float32) * alive_mask[:, None, None]
        )
        weight_grads, grad_input, grad_conditions = backward_pass(
            kept, saved, inputs, conditions, upstream
        )
        input_grads.append(grad_input.astype(jnp.bfloat16))
        cond_grads.append(grad_conditions.astype(jnp.bfloat16))
        totals = (
            weight_grads
            if totals is None
            else tuple((left + right for left, right in zip(totals, weight_grads)))
        )
    totals = (
        lax.psum_scatter(totals[0], "fsdp", scatter_dimension=0, tiled=True),
        lax.psum_scatter(totals[1], "fsdp", scatter_dimension=0, tiled=True),
        lax.psum_scatter(totals[2], "fsdp", scatter_dimension=0, tiled=True),
        lax.psum_scatter(totals[3], "fsdp", scatter_dimension=0, tiled=True),
        lax.psum_scatter(totals[4], "fsdp", scatter_dimension=0, tiled=True),
        lax.psum_scatter(totals[5], "fsdp", scatter_dimension=0, tiled=True),
        lax.psum_scatter(totals[6], "fsdp", scatter_dimension=0, tiled=True),
        lax.psum_scatter(totals[7], "fsdp", scatter_dimension=0, tiled=True),
        lax.psum_scatter(totals[8], "fsdp", scatter_dimension=0, tiled=True),
        lax.psum_scatter(totals[9], "fsdp", scatter_dimension=0, tiled=True),
    )
    totals = (
        lax.psum(totals[0].astype(jnp.bfloat16), "dp").astype(jnp.float32),
        lax.psum(totals[1].astype(jnp.bfloat16), "dp").astype(jnp.float32),
        lax.psum(totals[2].astype(jnp.bfloat16), "dp").astype(jnp.float32),
        lax.psum(totals[3].astype(jnp.bfloat16), "dp").astype(jnp.float32),
        lax.psum(totals[4].astype(jnp.bfloat16), "dp").astype(jnp.float32),
        lax.psum(totals[5].astype(jnp.bfloat16), "dp").astype(jnp.float32),
        lax.psum(totals[6].astype(jnp.bfloat16), "dp").astype(jnp.float32),
        lax.psum(totals[7].astype(jnp.bfloat16), "dp").astype(jnp.float32),
        lax.psum(totals[8].astype(jnp.bfloat16), "dp").astype(jnp.float32),
        lax.psum(totals[9].astype(jnp.bfloat16), "dp").astype(jnp.float32),
    )
    return (
        jnp.concatenate(outputs, axis=0),
        jnp.concatenate(input_grads, axis=0),
        jnp.concatenate(cond_grads, axis=0),
        totals[0],
        totals[1],
        totals[2],
        totals[3],
        totals[4],
        totals[5],
        totals[6],
        totals[7],
        totals[8],
        totals[9],
    )


def solution(mesh):
    placed = (
        P(("dp", "fsdp"), None, None),
        P(("dp", "fsdp"), None),
        P(("dp", "fsdp")),
        P(("dp", "fsdp"), None, None),
        P("fsdp", None),
        P("fsdp"),
        P("fsdp", None),
        P("fsdp"),
        P("fsdp", None),
        P("fsdp"),
        P("fsdp", None),
        P("fsdp"),
        P("fsdp", None),
        P("fsdp"),
    )
    return jax.shard_map(
        on_device,
        mesh=mesh,
        in_specs=placed,
        out_specs=(
            P(("dp", "fsdp"), None, None),
            P(("dp", "fsdp"), None, None),
            P(("dp", "fsdp"), None),
            P("fsdp", None),
            P("fsdp"),
            P("fsdp", None),
            P("fsdp"),
            P("fsdp", None),
            P("fsdp"),
            P("fsdp", None),
            P("fsdp"),
            P("fsdp", None),
            P("fsdp"),
        ),
        check_vma=False,
    )
```

profile of v0, /device:TPU:0, one launch (start us, length us, event | category | flops | bytes accessed | tf_op | source)
XLA Modules:
  0.0 394.5 jit_solution(872267637937504119)
XLA Ops:
  20.3 31.2 %all-reduce.11 = (bf16[768]{0:T(1024)(128)(2,1)S(1)}, bf16[2304]{0:T(1024)(128)(2,1)S(1)}, bf16[1536]{0:T(1024)(128)(2,1)S(1)}, bf16[384]{0:T(512)(128)(2,1)S(1)}, bf16[384]{0:T(512)(128)(2,1)}) all-reduce(bf16[768]{0:T(1024)(128)(2,1)S(1)} %dynamic-update-slice.1, ...), channel_id=1, replica_groups=mesh['dp'=4,'fsdp'=8] {'fsdp'}, use_global_device_ids=true, to_apply=%add.1 | all-reduce | flops 5376 | bytes 21504
  51.4 19.0 %all_gather.32 = bf16[384,1152]{1,0:T(8,128)(2,1)S(1)} all-gather(bf16[48,1152]{1,0:T(8,128)(2,1)} %param.20), channel_id=1, replica_groups=mesh['dp'=4,'fsdp'=8] {'fsdp'}, dimensions={0}, use_global_device_ids=true | all-gather | bytes 995328 | tf_op jit(solution)/shard_map/all_gather | solution.py:264
  70.8 16.2 %all_gather.34 = bf16[384,384]{1,0:T(8,128)(2,1)} all-gather(bf16[48,384]{1,0:T(8,128)(2,1)S(1)} %copy-done.55), channel_id=1, replica_groups=mesh['dp'=4,'fsdp'=8] {'fsdp'}, dimensions={0}, use_global_device_ids=true | all-gather | bytes 331776 | tf_op jit(solution)/shard_map/all_gather | solution.py:266
  87.1 2.0 convolution_reduce_fusion.1
  90.2 1.4 fusion
  91.6 2.1 copy.57
  93.7 1.4 fusion.124
  95.4 1.4 convolution_convert_fusion.3
  98.9 3.2 convolution_add_fusion.6
  102.1 4.6 %convert_reduce_fusion.1 = (f32[1536]{0:T(1024)}, bf16[256,1536]{1,0:T(8,128)(2,1)S(1)}) fusion(f32[256,1536]{1,0:T(8,128)} %convolution_add_fusion.6, bf16[1536,384]{1,0:T(8,128)(2,1)} %all-gather.8.cloned.1.call-done, f32[384]{0:T(512)S(1)} %get-tuple-element.125, f32[]{:T(128)} %bitcast.16, bf16[2,256,384]{2,1,0:T(8,128)(2,1)} %param.17), kind=kOutput, calls=%fused_computation.29 | convolution fusion | flops 311032320 | bytes 3743744 | tf_op jit(solution)/shard_map/nd,fd->nf/dot_general | solution.py:142
  108.2 2.1 convert_reduce_fusion.6
  120.5 1.4 fusion.125
  122.3 1.4 convolution_convert_fusion.2
  123.9 2.0 fusion.116
  127.4 2.9 convert_reduce_fusion
  131.8 1.4 convert_reduce_fusion.8
  134.2 1.7 copy.65
  135.9 1.4 convolution_bitcast_fusion
  141.7 1.9 convolution_add_fusion
  144.7 1.8 fusion.110
  146.6 2.1 convolution_add_fusion.2
  149.6 3.0 fusion.77
  152.6 3.0 convolution_add_fusion.1
  159.6 1.6 reduce_sum.400
  161.2 1.6 reduce_sum.385
  162.8 1.6 reduce_sum.391
  164.4 3.2 fusion.49
  167.7 1.6 reduce_sum.394
  170.8 1.9 fusion.42
  173.6 2.6 convolution_add_fusion.8
  176.7 3.5 fusion.53
  188.6 2.9 multiply_add_fusion
  197.9 2.0 convolution_add_fusion.7
  201.6 1.7 pad_maximum_fusion
  205.4 1.6 convert_element_type.383
  207.0 8.7 %reduce-scatter.12.cloned.1.call-done = f32[48,1536]{1,0:T(8,128)} async-done(((f32[384,1536]{1,0:T(8,128)}), f32[48,1536]{1,0:T(8,128)}) %reduce-scatter.12.cloned.1.call-update) | async-done | bytes 294928 | tf_op jit(solution)/shard_map/reduce_scatter | solution.py:304
  215.7 1.6 convert_element_type.395
  217.3 35.9 %reduce-scatter.14.cloned.1.call-done = f32[192,384]{1,0:T(8,128)} async-done(((f32[1536,384]{1,0:T(8,128)}), f32[192,384]{1,0:T(8,128)}) %reduce-scatter.14.cloned.1.call-update) | async-done | bytes 294928 | tf_op jit(solution)/shard_map/reduce_scatter | solution.py:306
  253.3 1.6 convert_element_type.401
  254.9 43.8 %reduce-scatter.6.cloned.1.call-done = f32[48,2304]{1,0:T(8,128)} async-done(((f32[384,2304]{1,0:T(8,128)}), f32[48,2304]{1,0:T(8,128)}) %reduce-scatter.6.cloned.1.call-update) | async-done | bytes 442384 | tf_op jit(solution)/shard_map/reduce_scatter | solution.py:298
  298.7 1.7 convert_element_type.379
  301.1 26.8 %all-reduce.10 = (bf16[2304]{0:T(1024)(128)(2,1)S(1)}, bf16[768]{0:T(1024)(128)(2,1)S(1)}, bf16[384]{0:T(512)(128)(2,1)S(1)}, bf16[1536]{0:T(1024)(128)(2,1)S(1)}, bf16[384]{0:T(512)(128)(2,1)S(1)}) all-reduce(f32[2304]{0:T(1024)S(1)} %convert_add_fusion.4, ...), channel_id=3, replica_groups=mesh['dp'=4,'fsdp'=8] {'fsdp'}, use_global_device_ids=true, to_apply=%region_36.37.clone | all-reduce | flops 5376 | bytes 32256
  331.7 16.7 %all-reduce.12 = (bf16[288]{0:T(512)(128)(2,1)S(1)}, bf16[96]{0:T(256)(128)(2,1)S(1)}, bf16[48,384]{1,0:T(8,128)(2,1)S(1)}, bf16[48]{0:T(256)(128)(2,1)S(1)}, bf...) all-reduce(bf16[288]{0:T(512)(128)(2,1)S(1)} %dynamic-slice.20, ...), channel_id=1, replica_groups=mesh['dp'=4,'fsdp'=8] {'dp'}, use_global_device_ids=true, to_apply=%region_37.38 | all-reduce | flops 19104 | bytes 76416 | tf_op jit(solution)/shard_map/psum | solution.py:311
  351.7 29.6 %all-reduce.16.cloned.1.call-done = (bf16[48,2304]{1,0:T(8,128)(2,1)}, bf16[48,1152]{1,0:T(8,128)(2,1)}, bf16[48,1536]{1,0:T(8,128)(2,1)}, bf16[192,384]{1,0:T(8,128)(2,1)}) async-done(((bf16[48,2304]{1,0:T(8,128)(2,1)}, bf16[48,1152]{1,0:T(8,128)(2,1)}, bf16[48,1536]{1,0:T(8,128)(2,1)}, bf16[192,384]{1,0:T(8,128)(2,1)}), (bf16[48,2304]{1,0:T(8,128)(2,1)}, bf16[48,1152]{1,0:T(8,128)(2,1)}, ...) | async-done | bytes 626704 | tf_op jit(solution)/shard_map/psum | solution.py:310
  381.3 1.7 convert_element_type.380
  383.0 1.6 convert_element_type.384
  384.6 1.6 convert_element_type.396
  386.3 1.6 convert_element_type.402
  (410 shorter events, 65.5 us)
Async XLA Ops:
  7.2 79.9 %copy-start.52 = (bf16[2,384]{1,0:T(2,128)(2,1)S(1)}, bf16[2,384]{1,0:T(2,128)(2,1)}, u32[]{:S(2)}) copy-start(bf16[2,384]{1,0:T(2,128)(2,1)} %param.15) | copy-start | bytes 4612
  7.2 63.2 %copy-start.1 = (bf16[2,256,384]{2,1,0:T(8,128)(2,1)S(1)}, bf16[2,256,384]{2,1,0:T(8,128)(2,1)}, u32[]{:S(2)}) copy-start(bf16[2,256,384]{2,1,0:T(8,128)(2,1)} %param.14) | copy-start | bytes 1179652
  7.2 63.6 %copy-start.55 = (bf16[48,384]{1,0:T(8,128)(2,1)S(1)}, bf16[48,384]{1,0:T(8,128)(2,1)}, u32[]{:S(2)}) copy-start(bf16[48,384]{1,0:T(8,128)(2,1)} %param.22) | copy-start | bytes 110596
  7.2 79.8 %all-gather.4.cloned.1.call-start = ((), (), s32[]{:S(2)}) async-start(), calls=%async_computation.5 | async-start | bytes 1990656 | tf_op jit(solution)/shard_map/all_gather | solution.py:262
  7.9 90.9 %all-gather.6.cloned.1.call-start = ((), (), s32[]{:S(2)}) async-start(), calls=%async_computation.6 | async-start | bytes 1327104 | tf_op jit(solution)/shard_map/all_gather | solution.py:268
  8.7 93.4 %all-gather.8.cloned.1.call-start = ((), (), s32[]{:S(2)}) async-start(), calls=%async_computation.7 | async-start | bytes 1327104 | tf_op jit(solution)/shard_map/all_gather | solution.py:270
  9.4 195.9 %reduce-scatter.8.cloned.1.call-start = ((), (), s32[]{:S(2)}) async-start(), calls=%async_computation.9 | async-start | bytes 1990656 | tf_op jit(solution)/shard_map/reduce_scatter | solution.py:300
  12.1 77.0 %copy-start.98 = (f32[1,384]{1,0:T(1,128)}, f32[1,384]{1,0:T(1,128)S(1)}, u32[]{:S(2)}) copy-start(f32[1,384]{1,0:T(1,128)S(1)} %get-tuple-element.72) | copy-start | bytes 4612
  12.1 77.0 %copy-start.100 = (f32[1,384]{1,0:T(1,128)}, f32[1,384]{1,0:T(1,128)S(1)}, u32[]{:S(2)}) copy-start(f32[1,384]{1,0:T(1,128)S(1)} %get-tuple-element.73) | copy-start | bytes 4612
  51.4 45.4 %copy-start.87 = (f32[384]{0:T(512)}, f32[384]{0:T(512)S(1)}, u32[]{:S(2)}) copy-start(f32[384]{0:T(512)S(1)} %convert_element_type.338) | copy-start | bytes 4612
  70.4 19.7 %copy-start.41 = (bf16[384,1152]{1,0:T(8,128)(2,1)}, bf16[384,1152]{1,0:T(8,128)(2,1)S(1)}, u32[]{:S(2)}) copy-start(bf16[384,1152]{1,0:T(8,128)(2,1)S(1)} %all_gather.32) | copy-start | bytes 2654212
  70.6 19.6 %copy-start.67 = (f32[256]{0:T(256)}, f32[256]{0:T(256)S(1)}, u32[]{:S(2)}) copy-start(f32[256]{0:T(256)S(1)} %broadcast_multiply_fusion.3) | copy-start | bytes 3076
  70.8 16.3 %copy-start.103 = (f32[256]{0:T(256)}, f32[256]{0:T(256)S(1)}, u32[]{:S(2)}) copy-start(f32[256]{0:T(256)S(1)} %fusion.46) | copy-start | bytes 3076
  70.8 19.4 %copy-start.70 = (f32[256]{0:T(256)}, f32[256]{0:T(256)S(1)}, u32[]{:S(2)}) copy-start(f32[256]{0:T(256)S(1)} %fusion.97) | copy-start | bytes 3076
  90.1 8.8 %copy-start.91 = (f32[384]{0:T(512)}, f32[384]{0:T(512)S(1)}, u32[]{:S(2)}) copy-start(f32[384]{0:T(512)S(1)} %get-tuple-element.124) | copy-start | bytes 4612
  90.1 17.7 %copy-start.62 = (f32[384]{0:T(512)}, f32[384]{0:T(512)S(1)}, u32[]{:S(2)}) copy-start(f32[384]{0:T(512)S(1)} %get-tuple-element.123) | copy-start | bytes 4612
  90.1 18.0 %copy-start.83 = (f32[384]{0:T(512)}, f32[384]{0:T(512)S(1)}, u32[]{:S(2)}) copy-start(f32[384]{0:T(512)S(1)} %get-tuple-element.36) | copy-start | bytes 4612
  90.1 18.0 %copy-start.117 = (f32[384]{0:T(512)}, f32[384]{0:T(512)S(1)}, u32[]{:S(2)}) copy-start(f32[384]{0:T(512)S(1)} %get-tuple-element.125) | copy-start | bytes 4612
  97.9 9.9 %copy-start.81 = (f32[256]{0:T(256)}, f32[256]{0:T(256)S(1)}, u32[]{:S(2)}) copy-start(f32[256]{0:T(256)S(1)} %broadcast_multiply_fusion.2) | copy-start | bytes 3076
  98.8 9.0 %copy-start.96 = (f32[256]{0:T(256)}, f32[256]{0:T(256)S(1)}, u32[]{:S(2)}) copy-start(f32[256]{0:T(256)S(1)} %fusion.98) | copy-start | bytes 3076
  125.9 5.6 %copy-start.9 = (f32[1,256,384]{2,1,0:T(8,128)}, f32[1,256,384]{2,1,0:T(8,128)S(1)}, u32[]{:S(2)}) copy-start(f32[1,256,384]{2,1,0:T(8,128)S(1)} %get-tuple-element.77) | copy-start | bytes 1179652
  125.9 5.6 %copy-start.73 = (f32[256]{0:T(256)}, f32[256]{0:T(256)S(1)}, u32[]{:S(2)}) copy-start(f32[256]{0:T(256)S(1)} %broadcast_multiply_fusion) | copy-start | bytes 3076
  126.1 5.4 %copy-start.94 = (f32[256]{0:T(256)}, f32[256]{0:T(256)S(1)}, u32[]{:S(2)}) copy-start(f32[256]{0:T(256)S(1)} %fusion.100) | copy-start | bytes 3076
  143.7 71.9 %reduce-scatter.12.cloned.1.call-start = ((), (), s32[]{:S(2)}) async-start(), calls=%async_computation.11 | async-start | bytes 2654208 | tf_op jit(solution)/shard_map/reduce_scatter | solution.py:304
  148.6 104.6 %reduce-scatter.14.cloned.1.call-start = ((), (), s32[]{:S(2)}) async-start(), calls=%async_computation.12 | async-start | bytes 2654208 | tf_op jit(solution)/shard_map/reduce_scatter | solution.py:306
  155.6 143.1 %reduce-scatter.6.cloned.1.call-start = ((), (), s32[]{:S(2)}) async-start(), calls=%async_computation.8 | async-start | bytes 3981312 | tf_op jit(solution)/shard_map/reduce_scatter | solution.py:298
  191.5 5.2 %copy-start.36 = (bf16[256,384]{1,0:T(8,128)(2,1)S(1)}, bf16[256,384]{1,0:T(8,128)(2,1)}, u32[]{:S(2)}) copy-start(bf16[256,384]{1,0:T(8,128)(2,1)} %copy-done.35) | copy-start | bytes 589828
  191.5 139.3 %reduce-scatter.10.cloned.1.call-start = ((), (), s32[]{:S(2)}) async-start(), calls=%async_computation.10 | async-start | bytes 663552 | tf_op jit(solution)/shard_map/reduce_scatter | solution.py:302
  199.9 4.6 %copy-start.53 = (bf16[2,384]{1,0:T(2,128)(2,1)S(1)}, bf16[2,384]{1,0:T(2,128)(2,1)}, u32[]{:S(2)}) copy-start(bf16[2,384]{1,0:T(2,128)(2,1)} %param.15) | copy-start | bytes 4612
  199.9 4.6 %copy-start.54 = (bf16[2304,1]{0,1:T(2,128)(2,1)S(1)}, bf16[2304,1]{0,1:T(2,128)(2,1)}, u32[]{:S(2)}) copy-start(bf16[2304,1]{0,1:T(2,128)(2,1)} %reshape.989) | copy-start | bytes 13828
  200.0 4.7 %copy-start.99 = (f32[1,384]{1,0:T(1,128)S(1)}, f32[1,384]{1,0:T(1,128)}, u32[]{:S(2)}) copy-start(f32[1,384]{1,0:T(1,128)} %copy-done.98) | copy-start | bytes 4612
  200.0 4.7 %copy-start.101 = (f32[1,384]{1,0:T(1,128)S(1)}, f32[1,384]{1,0:T(1,128)}, u32[]{:S(2)}) copy-start(f32[1,384]{1,0:T(1,128)} %copy-done.100) | copy-start | bytes 4612
  200.0 181.3 %all-reduce.16.cloned.1.call-start = ((), (), s32[]{:S(2)}) async-start(), calls=%async_computation.13 | async-start | bytes 1253376 | tf_op jit(solution)/shard_map/psum | solution.py:310
  205.2 95.8 %copy-start.115 = (f32[384]{0:T(512)S(1)}, f32[384]{0:T(512)}, u32[]{:S(2)}) copy-start(f32[384]{0:T(512)} %get-tuple-element.82) | copy-start | bytes 4612
  205.2 95.8 %copy-start.116 = (f32[384]{0:T(512)S(1)}, f32[384]{0:T(512)}, u32[]{:S(2)}) copy-start(f32[384]{0:T(512)} %get-tuple-element.64) | copy-start | bytes 4612
  205.2 95.8 %copy-start.122 = (f32[1536]{0:T(1024)S(1)}, f32[1536]{0:T(1024)}, u32[]{:S(2)}) copy-start(f32[1536]{0:T(1024)} %get-tuple-element.116) | copy-start | bytes 18436
  205.2 95.8 %copy-start.123 = (f32[1536]{0:T(1024)S(1)}, f32[1536]{0:T(1024)}, u32[]{:S(2)}) copy-start(f32[1536]{0:T(1024)} %get-tuple-element.118) | copy-start | bytes 18436
  205.2 95.8 %copy-start.113 = (f32[384]{0:T(512)S(1)}, f32[384]{0:T(512)}, u32[]{:S(2)}) copy-start(f32[384]{0:T(512)} %get-tuple-element.21) | copy-start | bytes 4612
  205.3 95.8 %copy-start.114 = (f32[384]{0:T(512)S(1)}, f32[384]{0:T(512)}, u32[]{:S(2)}) copy-start(f32[384]{0:T(512)} %get-tuple-element.22) | copy-start | bytes 4612
  205.3 123.0 %copy-start.128 = (f32[256]{0:T(256)S(1)}, f32[256]{0:T(256)}, u32[]{:S(2)}) copy-start(f32[256]{0:T(256)} %get-tuple-element.16) | copy-start | bytes 3076
  205.3 123.0 %copy-start.23 = (f32[256,384]{1,0:T(8,128)S(1)}, f32[256,384]{1,0:T(8,128)}, u32[]{:S(2)}) copy-start(f32[256,384]{1,0:T(8,128)} %get-tuple-element.115) | copy-start | bytes 1179652
  205.3 123.0 %copy-start.26 = (f32[1,256,384]{2,1,0:T(8,128)S(1)}, f32[1,256,384]{2,1,0:T(8,128)}, u32[]{:S(2)}) copy-start(f32[1,256,384]{2,1,0:T(8,128)} %copy-done.24) | copy-start | bytes 1179652
  205.3 123.0 %copy-start.59 = (f32[384]{0:T(512)S(1)}, f32[384]{0:T(512)}, u32[]{:S(2)}) copy-start(f32[384]{0:T(512)} %get-tuple-element.40) | copy-start | bytes 4612
  205.3 123.0 %copy-start.77 = (f32[256]{0:T(256)S(1)}, f32[256]{0:T(256)}, u32[]{:S(2)}) copy-start(f32[256]{0:T(256)} %copy-done.75) | copy-start | bytes 3076
  205.3 123.0 %copy-start.80 = (f32[256]{0:T(256)S(1)}, f32[256]{0:T(256)}, u32[]{:S(2)}) copy-start(f32[256]{0:T(256)} %copy-done.78) | copy-start | bytes 3076
  205.3 123.0 %copy-start.106 = (f32[256]{0:T(256)S(1)}, f32[256]{0:T(256)}, u32[]{:S(2)}) copy-start(f32[256]{0:T(256)} %copy-done.105) | copy-start | bytes 3076
  205.3 123.0 %copy-start.109 = (f32[256]{0:T(256)S(1)}, f32[256]{0:T(256)}, u32[]{:S(2)}) copy-start(f32[256]{0:T(256)} %copy-done.107) | copy-start | bytes 3076
  217.3 111.9 %copy-start.46 = (bf16[1,256,384]{2,1,0:T(8,128)(2,1)S(1)}, bf16[1,256,384]{2,1,0:T(8,128)(2,1)}, u32[]{:S(2)}) copy-start(bf16[1,256,384]{2,1,0:T(8,128)(2,1)} %get-tuple-element.86) | copy-start | bytes 589828
  (93 other events, 190.5 us)
Sparse Core Ops, SparseCore 0:
  9.7 29.4 all-gather.3
  40.8 27.6 all-gather.5
  70.1 22.8 all-gather.7
  143.8 35.1 reduce-scatter.7
  181.2 34.4 reduce-scatter.11
  217.8 35.3 reduce-scatter.13
  255.6 43.0 reduce-scatter.5
  301.1 29.6 reduce-scatter.9
  335.6 45.6 all-reduce.15
where the time goes:
time: 396 us; the launch traced here: 394 us
  waiting for transfers between devices  121 us (31%)
  blocking collectives  110 us (28%)
  matrix products  59.8 us (15%)
  other arithmetic  48.4 us (12%)
  local copies, waits for them, and re-layouts  33.4 us (8%)
  between operations  21.4 us (5%)
    unnamed x2, blocking collectives  58 us
    reduce_scatter x1, waiting for transfers between devices, on_device(): lax.psum_scatter(totals[0], 'fsdp', scatter_dimension=0, tiled=True)  43.8 us
    reduce_scatter x1, waiting for transfers between devices, on_device(): lax.psum_scatter(totals[8], 'fsdp', scatter_dimension=0, tiled=True)  35.9 us
    psum x1, waiting for transfers between devices, on_device(): lax.psum(totals[0].astype(jnp.bfloat16), 'dp').astype(jnp.float32)  29.6 us
    unnamed x290, local copies, waits for them, and re-layouts  21.7 us
    all_gather x1, blocking collectives, on_device(): lax.all_gather(projection_weight, 'fsdp', axis=0, tiled=True)  19 us
    psum x1, blocking collectives, on_device(): lax.psum(totals[1].astype(jnp.bfloat16), 'dp').astype(jnp.float32)  16.7 us
    all_gather x1, blocking collectives, on_device(): lax.all_gather(output_weight, 'fsdp', axis=0, tiled=True)  16.2 us
  transfers between devices with their start and end apart: 9, of which 5 were waited for; matrix products, arithmetic and copies ran while one was open for 23% of the time, Pallas kernels for 0%

commit v1 on v0

--- a/solution.py
+++ b/solution.py
@@ -1,11 +1,600 @@
+import functools
+
 import jax
 import jax.numpy as jnp
 from jax import lax
+from jax.experimental import pallas as pl
+from jax.experimental.pallas import tpu as pltpu
 from jax.sharding import PartitionSpec as P
 
 HEADS = 6
 HEAD_DIM = 64
 MICRO = 2
+F32 = jnp.float32
+BF16 = jnp.bfloat16
+BOTH = ("dp", "fsdp")
+NN = (((1,), (0,)), ((), ()))
+NT = (((1,), (1,)), ((), ()))
+TN = (((0,), (0,)), ((), ()))
+
+
+def dot(left, right, dims=NN):
+    return lax.dot_general(left, right, dims, preferred_element_type=F32)
+
+
+def smem():
+    return pl.BlockSpec(memory_space=pltpu.SMEM)
+
+
+def vmem():
+    return pl.BlockSpec(memory_space=pltpu.VMEM)
+
+
+def call(body, name, ids, ins, outs, scratch=(), flops=0, limit=48):
+    moved = sum(a.size * a.dtype.itemsize for a in ins) + sum(
+        jnp.dtype(t).itemsize * functools.reduce(lambda a, b: a * b, s, 1) for s, t in outs
+    )
+    return pl.pallas_call(
+        body,
+        out_shape=[jax.ShapeDtypeStruct(s, t) for s, t in outs],
+        in_specs=[smem()] + [vmem()] * len(ins),
+        out_specs=[vmem()] * len(outs),
+        scratch_shapes=list(scratch),
+        compiler_params=pltpu.CompilerParams(vmem_limit_bytes=limit * 1024 * 1024),
+        cost_estimate=pl.CostEstimate(flops=flops, bytes_accessed=moved, transcendentals=0),
+        name=name,
+    )(ids, *ins)
+
+
+def offsets(ids):
+    d, f = ids[0], ids[1]
+    core = lax.rem(f, 2)
+    first = 1 + core
+    second = 2 - core
+    return d, f, (0, first, second, 3), (0, second, first, 3)
+
+
+def flip(a, b):
+    return lax.bitwise_xor(a, b)
+
+
+def pick_body(ids, proj, outw, up, down, cond, q_po, q_ud, c_low):
+    d = ids[0]
+    width = outw.shape[1]
+    rows = outw.shape[0]
+
+    @pl.when(d < 3)
+    def _():
+        q_po[...] = proj[:, pl.ds(pl.multiple_of(lax.min(d, 2) * width, 128), width)]
+
+    @pl.when(d == 3)
+    def _():
+        q_po[...] = outw[...]
+
+    q_ud[0] = up[:, pl.ds(pl.multiple_of(d * width, 128), width)]
+    q_ud[1] = down[pl.ds(pl.multiple_of(d * rows, 16), rows), :]
+    c = cond[...].astype(F32)
+    c_low[...] = (c / (1.0 + jnp.exp(-c))).astype(BF16)
+
+
+def one_hot(shape, shift):
+    r = lax.broadcasted_iota(jnp.int32, shape, 0)
+    c = lax.broadcasted_iota(jnp.int32, shape, 1)
+    return jnp.where(c == r + shift, 1.0, 0.0).astype(BF16)
+
+
+def mod_body(ids, c0, c1, c2, c3, wmod, bmod, bqv, bout, bup, bdown, k0, k1, k2, k3, send):
+    f = ids[1]
+    wide = wmod.shape[1]
+    rows = wmod.shape[0]
+    feat = c0.shape[1]
+    r = lax.broadcasted_iota(jnp.int32, (feat, rows), 0)
+    c = lax.broadcasted_iota(jnp.int32, (feat, rows), 1)
+    select = jnp.where(r == c + f * rows, 1.0, 0.0).astype(BF16)
+
+    def place(ref, total):
+        n = ref.shape[1]
+        return dot(ref[...], one_hot((n, total), f * n))
+
+    bias = place(bmod, wide)
+    row_two = jnp.concatenate([place(bup, 4 * feat), place(bqv, 2 * feat)], axis=1)
+    row_three = jnp.concatenate(
+        [place(bout, feat), place(bdown, feat), jnp.zeros((1, 4 * feat), F32)], axis=1
+    )
+    for zm, (ref, keep) in enumerate(zip((c0, c1, c2, c3), (k0, k1, k2, k3))):
+        own = dot(ref[...], select).astype(BF16)
+        part = dot(own, wmod[...]) + bias
+        keep[0:2, :] = part[0:2]
+        keep[2:3, :] = row_two
+        keep[3:4, :] = row_three
+        send[zm, 0:2, :] = part[2:4]
+        send[zm, 2:3, :] = row_two
+        send[zm, 3:4, :] = row_three
+
+
+def norm_parts(x):
+    mean = jnp.mean(x, axis=-1, keepdims=True)
+    centered = x - mean
+    rstd = lax.rsqrt(jnp.mean(centered * centered, axis=-1, keepdims=True) + 1e-06)
+    return centered * rstd, rstd
+
+
+def lane_masks(rows):
+    lane = lax.broadcasted_iota(jnp.int32, (rows, 2 * HEAD_DIM), 1)
+    return lane < HEAD_DIM
+
+
+def attend_body(
+    ids, w0, w1, w2, w3, o0, o1, o2, o3, p0, p1, p2, p3, lat, wpo, mod, n1, proj, att
+):
+    d, f, mine, theirs = offsets(ids)
+    rows = w0.shape[1]
+    feat = w0.shape[2]
+    for refs, flips, base in (((w0, w1, w2, w3), mine, f), ((o0, o1, o2, o3), theirs, flip(f, 1))):
+        for ref, how in zip(refs, flips):
+            block = flip(d, how)
+            for zm in range(4):
+                at = pl.multiple_of(flip(base, 2 * zm) * rows, 16)
+                wpo[block, pl.ds(at, rows), :] = ref[zm]
+    mod[...] = (p0[...] + p1[...]) + (p2[...] + p3[...])
+    length = lat.shape[1]
+    low_half = lane_masks(length)
+    qv = mod[2:3, 4 * feat :]
+
+    def one(i, carry):
+        at = pl.multiple_of(i * length, 256)
+        x = lat[i].astype(F32)
+        xhat, rstd = norm_parts(x)
+        row = mod[pl.ds(i, 1), :]
+        n = (xhat * (1.0 + row[:, feat : 2 * feat]) + row[:, :feat]).astype(BF16)
+        n1[pl.ds(at, length), :] = n
+        proj[pl.ds(at, length), 0:feat] = (dot(n, wpo[0]) + qv[:, :feat]).astype(BF16)
+        proj[pl.ds(at, length), feat : 2 * feat] = dot(n, wpo[1]).astype(BF16)
+        proj[pl.ds(at, length), 2 * feat :] = (dot(n, wpo[2]) + qv[:, feat:]).astype(BF16)
+        for pair in range(HEADS // 2):
+            lo = pair * 2 * HEAD_DIM
+            hi = lo + 2 * HEAD_DIM
+            q = proj[pl.ds(at, length), lo:hi]
+            k = proj[pl.ds(at, length), feat + lo : feat + hi]
+            v = proj[pl.ds(at, length), 2 * feat + lo : 2 * feat + hi]
+            zero = jnp.zeros_like(q)
+            outs = []
+            for side in range(2):
+                q_one = jnp.where(low_half, q, zero) if side == 0 else jnp.where(low_half, zero, q)
+                s = dot(q_one, k, NT) * HEAD_DIM ** (-0.5)
+                e = jnp.exp(s - jnp.max(s, axis=-1, keepdims=True))
+                inv = 1.0 / jnp.sum(e, axis=-1, keepdims=True)
+                outs.append(dot((e * inv).astype(BF16), v))
+            att[pl.ds(at, length), lo:hi] = jnp.where(low_half, outs[0], outs[1]).astype(BF16)
+        return carry
+
+    lax.fori_loop(0, lat.shape[0], one, 0)
+
+
+def spread(tmp, at_row, dm, keeps, sends, rows, f, slot=None):
+    swapped = (0, 2, 1, 3)[dm]
+    for zm in range(4):
+        for ref, owner in ((keeps[dm], flip(f, 2 * zm)), (sends[swapped], flip(f, 2 * zm + 1))):
+            piece = tmp[pl.ds(pl.multiple_of(at_row(owner), 16), rows), :]
+            if slot is None:
+                ref[zm] = piece
+            else:
+                ref[zm, slot] = piece
+
+
+def mlp_body(
+    ids, w0, w1, w2, w3, o0, o1, o2, o3, wout, mod, lat, cot, att,
+    res, gmid, gbr, gatt, gsum, gmod, k0, k1, k2, k3, s0, s1, s2, s3,
+    wu, wd, n2s, acts, dgs, gmlps, gpres, n2t, tmp, tmpd,
+):
+    d, f, mine, theirs = offsets(ids)
+    count = ids[2]
+    rows = w0.shape[2]
+    feat = w0.shape[3]
+    hidden = wd.shape[0]
+    blocks = hidden // feat
+    for refs, flips, base in (((w0, w1, w2, w3), mine, f), ((o0, o1, o2, o3), theirs, flip(f, 1))):
+        for ref, how in zip(refs, flips):
+            block = flip(d, how)
+            for zm in range(4):
+                owner = flip(base, 2 * zm)
+                wu[block, pl.ds(pl.multiple_of(owner * rows, 16), rows), :] = ref[zm, 0]
+                wd[pl.ds(pl.multiple_of(owner * 4 * rows + block * rows, 16), rows), :] = ref[zm, 1]
+    length = lat.shape[1]
+    bup = mod[2:3, : 4 * feat]
+    bout = mod[3:4, :feat]
+    bdown = mod[3:4, feat : 2 * feat]
+    gsum[...] = jnp.zeros_like(gsum)
+
+    def one(i, carry):
+        at = pl.multiple_of(i * length, 256)
+        part = pl.ds(at, length)
+        row = mod[pl.ds(i, 1), :]
+        gate_one, shift, scale, gate_two = (row[:, j * feat : (j + 1) * feat] for j in (2, 3, 4, 5))
+        alive = jnp.where(i < count, 1.0, 0.0).astype(F32)
+        branch = dot(att[part, :], wout[0]) + bout
+        middle = lat[i].astype(F32) + gate_one * branch
+        xhat, rstd = norm_parts(middle)
+        n2 = (xhat * (1.0 + scale) + shift).astype(BF16)
+        n2s[part, :] = n2
+        mlp = jnp.zeros((length, feat), F32) + bdown
+        for j in range(blocks):
+            cols = slice(j * feat, (j + 1) * feat)
+            v = dot(n2, wu[j]) + bup[:, cols]
+            t = jnp.tanh(0.7978845608028654 * (v + 0.044715 * v * v * v))
+            half = 0.5 * (1.0 + t)
+            act = (v * half).astype(BF16)
+            dgs[:, cols] = half + 0.5 * v * (1.0 - t * t) * (
+                0.7978845608028654 * (1.0 + 0.134145 * v * v)
+            )
+            acts[part, cols] = act
+            mlp = mlp + dot(act, wd[cols, :])
+        res[i] = (alive * (middle + gate_two * mlp)).astype(BF16)
+        upstream = alive * cot[i].astype(F32)
+        g_gate_two = jnp.sum(upstream * mlp, axis=0, keepdims=True)
+        gmlp = (gate_two * upstream).astype(BF16)
+        gmlps[part, :] = gmlp
+        gn = jnp.zeros((length, feat), F32)
+        for j in range(blocks):
+            cols = slice(j * feat, (j + 1) * feat)
+            gpre = (dot(gmlp, wd[cols, :], NT) * dgs[:, cols]).astype(BF16)
+            gpres[part, cols] = gpre
+            gn = gn + dot(gpre, wu[j], NT)
+            gsum[:, feat + j * feat : 2 * feat + j * feat] += jnp.sum(
+                gpre.astype(F32), axis=0, keepdims=True
+            )
+        g_shift = jnp.sum(gn, axis=0, keepdims=True)
+        g_scale = jnp.sum(gn * xhat, axis=0, keepdims=True)
+        gx = gn * (1.0 + scale)
+        gmiddle = upstream + rstd * (
+            gx
+            - jnp.mean(gx, axis=-1, keepdims=True)
+            - xhat * jnp.mean(gx * xhat, axis=-1, keepdims=True)
+        )
+        gmid[i] = gmiddle
+        g_gate_one = jnp.sum(gmiddle * branch, axis=0, keepdims=True)
+        gbranch = (gate_one * gmiddle).astype(BF16)
+        gbr[part, :] = gbranch
+        gatt[part, :] = dot(gbranch, wout[0], NT).astype(BF16)
+        gsum[:, 0:feat] += jnp.sum(gbranch.astype(F32), axis=0, keepdims=True)
+        gsum[:, 5 * feat : 6 * feat] += jnp.sum(gmlp.astype(F32), axis=0, keepdims=True)
+        gmod[pl.ds(i, 1), :] = jnp.concatenate([g_gate_one, g_shift, g_scale, g_gate_two], axis=1)
+        return carry
+
+    lax.fori_loop(0, lat.shape[0], one, 0)
+    keeps, sends = (k0, k1, k2, k3), (s0, s1, s2, s3)
+    for j in range(blocks):
+        cols = slice(j * feat, (j + 1) * feat)
+        tmpd[cols, :] = dot(acts[:, cols], gmlps[...], TN).astype(BF16)
+    n2t[...] = n2s[...].T
+    for dm in (1, 3, 0, 2):
+        block = flip(d, mine[dm])
+        spread(tmpd, lambda o: (o * 4 + block) * rows, dm, keeps, sends, rows, f, 1)
+        tmp[...] = dot(
+            n2t[...], gpres[:, pl.ds(pl.multiple_of(block * feat, 128), feat)]
+        ).astype(BF16)
+        spread(tmp, lambda o: o * rows, dm, keeps, sends, rows, f, 0)
+
+
+def attend_back_body(
+    ids, proj, gatt, att, gbr, n1, gsum, gproj, bias, k0, k1, k2, k3, s0, s1, s2, s3,
+    gall, xts, tmp, *, length,
+):
+    d, f, mine, _ = offsets(ids)
+    feat = att.shape[1]
+    rows = k0.shape[1]
+    low_half = lane_masks(length)
+
+    def one(i, carry):
+        part = pl.ds(pl.multiple_of(i * length, 256), length)
+        for pair in range(HEADS // 2):
+            lo = pair * 2 * HEAD_DIM
+            hi = lo + 2 * HEAD_DIM
+            q = proj[part, lo:hi]
+            k = proj[part, feat + lo : feat + hi]
+            v = proj[part, 2 * feat + lo : 2 * feat + hi]
+            ga = gatt[part, lo:hi]
+            zero = jnp.zeros_like(q)
+            gq = jnp.zeros(q.shape, F32)
+            gk = jnp.zeros(q.shape, F32)
+            gv = jnp.zeros(q.shape, F32)
+            for side in range(2):
+                own = lambda a: (
+                    jnp.where(low_half, a, zero) if side == 0 else jnp.where(low_half, zero, a)
+                )
+                q_one, ga_one = own(q), own(ga)
+                s = dot(k, q_one, NT) * HEAD_DIM ** (-0.5)
+                e = jnp.exp(s - jnp.max(s, axis=0, keepdims=True))
+                prob = e * (1.0 / jnp.sum(e, axis=0, keepdims=True))
+                gv = gv + dot(prob.astype(BF16), ga_one)
+                gp = dot(v, ga_one, NT)
+                delta = jnp.sum(gp * prob, axis=0, keepdims=True)
+                gs = (prob * (gp - delta)).astype(BF16)
+                gk = gk + dot(gs, q_one)
+                gq = gq + dot(gs, own(k), TN)
+            gall[part, lo:hi] = (gq * HEAD_DIM ** (-0.5)).astype(BF16)
+            gall[part, feat + lo : feat + hi] = (gk * HEAD_DIM ** (-0.5)).astype(BF16)
+            gall[part, 2 * feat + lo : 2 * feat + hi] = gv.astype(BF16)
+        return carry
+
+    lax.fori_loop(0, proj.shape[0] // length, one, 0)
+    gproj[...] = gall[:, : 3 * feat]
+    gall[:, 3 * feat :] = gbr[...]
+    xts[0] = n1[...].T
+    xts[1] = att[...].T
+    keeps, sends = (k0, k1, k2, k3), (s0, s1, s2, s3)
+    for dm in (1, 3, 0, 2):
+        block = flip(d, mine[dm])
+        tmp[...] = dot(
+            xts[jnp.where(block == 3, 1, 0)],
+            gall[:, pl.ds(pl.multiple_of(block * feat, 128), feat)],
+        ).astype(BF16)
+        spread(tmp, lambda o: o * rows, dm, keeps, sends, rows, f)
+    bias[:, 0:feat] = jnp.sum(gall[:, 0:feat].astype(F32), axis=0, keepdims=True)
+    bias[:, feat : 2 * feat] = jnp.sum(
+        gall[:, 2 * feat : 3 * feat].astype(F32), axis=0, keepdims=True
+    )
+    bias[:, 2 * feat :] = gsum[...]
+
+
+def input_back_body(ids, gproj, wpo, lat, gmid, mod, gmod, lgrad, gm):
+    length = lat.shape[1]
+    feat = lat.shape[2]
+
+    def one(i, carry):
+        part = pl.ds(pl.multiple_of(i * length, 256), length)
+        row = mod[pl.ds(i, 1), :]
+        xhat, rstd = norm_parts(lat[i].astype(F32))
+        gn = dot(gproj[part, 0:feat], wpo[0], NT)
+        gn = gn + dot(gproj[part, feat : 2 * feat], wpo[1], NT)
+        gn = gn + dot(gproj[part, 2 * feat :], wpo[2], NT)
+        g_shift = jnp.sum(gn, axis=0, keepdims=True)
+        g_scale = jnp.sum(gn * xhat, axis=0, keepdims=True)
+        gx = gn * (1.0 + row[:, feat : 2 * feat])
+        lgrad[i] = (
+            gmid[i]
+            + rstd
+            * (
+                gx
+                - jnp.mean(gx, axis=-1, keepdims=True)
+                - xhat * jnp.mean(gx * xhat, axis=-1, keepdims=True)
+            )
+        ).astype(BF16)
+        gm[pl.ds(i, 1), :] = jnp.concatenate(
+            [g_shift, g_scale, gmod[pl.ds(i, 1), :]], axis=1
+        )
+        return carry
+
+    lax.fori_loop(0, lat.shape[0], one, 0)
+
+
+def cond_back_body(ids, g0, g1, g2, g3, wmod, x0, x1, x2, x3):
+    f = ids[1]
+    rows = wmod.shape[0]
+    place = one_hot((rows, x0.shape[1]), f * rows).astype(F32)
+    for ref, out in zip((g0, g1, g2, g3), (x0, x1, x2, x3)):
+        part = dot(ref[...], wmod[...], NT)
+        out[...] = lax.dot_general(
+            part, place, NN, preferred_element_type=F32, precision=lax.Precision.HIGHEST
+        )
+
+
+def mod_weight_body(ids, *refs):
+    conds, grads, (wgrad, bgrad) = refs[:4], refs[4:8], refs[8:]
+    f = ids[1]
+    rows = wgrad.shape[0]
+    feat = conds[0].shape[1]
+    select = one_hot((rows, feat), f * rows)
+    total = None
+    sums = None
+    for c, g in zip(conds, grads):
+        grad = g[...]
+        own = dot(select, c[...], NT).astype(BF16)
+        term = dot(own, grad)
+        total = term if total is None else total + term
+        s = jnp.sum(grad.astype(F32), axis=0, keepdims=True)
+        sums = s if sums is None else sums + s
+    wgrad[...] = total
+    bgrad[...] = sums
+
+
+def final_po_body(ids, g0, g1, g2, g3, gp, go):
+    d, _, mine, _ = offsets(ids)
+    feat = go.shape[1]
+    for ref, how in zip((g0, g1, g2, g3), mine):
+        block = flip(d, how)
+
+        @pl.when(block < 3)
+        def _():
+            at = pl.multiple_of(lax.min(block, 2) * feat, 128)
+            gp[:, pl.ds(at, feat)] = ref[...].astype(F32)
+
+        @pl.when(block == 3)
+        def _():
+            go[...] = ref[...].astype(F32)
+
+
+def final_ud_body(ids, g0, g1, g2, g3, gu, gd):
+    d, _, mine, _ = offsets(ids)
+    rows, feat = g0.shape[1:]
+    for ref, how in zip((g0, g1, g2, g3), mine):
+        block = flip(d, how)
+        gu[:, pl.ds(pl.multiple_of(block * feat, 128), feat)] = ref[0].astype(F32)
+        gd[pl.ds(pl.multiple_of(block * rows, 16), rows), :] = ref[1].astype(F32)
+
+
+def routes():
+    core, first, second = [], [], []
+    levels = {1: [], 2: [], 3: []}
+    for d in range(4):
+        for f in range(8):
+            i = d * 8 + f
+            core.append((i, i ^ 1))
+            a = 1 if f % 2 == 0 else 2
+            first.append((i, (d ^ a) * 8 + f))
+            second.append((i, (d ^ (3 - a)) * 8 + f))
+            for m in levels:
+                levels[m].append((i, d * 8 + (f ^ (2 * m))))
+    return core, first, second, levels
+
+
+def add_low(*parts):
+    total = parts[0].astype(F32)
+    for part in parts[1:]:
+        total = total + part.astype(F32)
+    return total.astype(BF16)
+
+
+def on_device_blocks(
+    latents, cond, counts, cotangent, modulation_weight, modulation_bias, projection_weight,
+    query_value_bias, output_weight, output_bias, up_weight, up_bias, down_weight, down_bias,
+):
+    core, first, second, levels = routes()
+
+    def move(x, route):
+        return lax.ppermute(x, BOTH, route)
+
+    slots, length, feat = latents.shape
+    rows = projection_weight.shape[0]
+    hidden = up_weight.shape[1]
+    wide = modulation_weight.shape[1]
+    tokens = slots * length
+    d = lax.axis_index("dp")
+    f = lax.axis_index("fsdp")
+    ids = jnp.stack([d, f, counts[0]]).astype(jnp.int32)
+
+    q_po, q_ud, c_low = call(
+        pick_body, "pick", ids,
+        [projection_weight, output_weight, up_weight, down_weight, cond],
+        [((rows, feat), BF16), ((2, rows, feat), BF16), ((slots, feat), BF16)],
+    )
+
+    def gather(q):
+        own = jnp.stack([q] + [move(q, levels[m]) for m in (1, 2, 3)])
+        a = move(own, first)
+        b = move(own, second)
+        ab = move(a, second)
+        mine = [own, a, b, ab]
+        return mine + [move(x, core) for x in mine]
+
+    c_pair = jnp.concatenate([c_low, move(c_low, core)], axis=0)
+    c_all = [c_pair] + [move(c_pair, levels[m]) for m in (1, 2, 3)]
+    w_po = gather(q_po)
+    *kept, sent = call(
+        mod_body, "modulation", ids,
+        c_all + [
+            modulation_weight, modulation_bias[None], query_value_bias[None],
+            output_bias[None], up_bias[None], down_bias[None],
+        ],
+        [((4, wide), F32)] * 4 + [((4, 4, wide), F32)],
+    )
+    arrived = move(sent, core)
+    paid = [kept[m] + arrived[m] for m in range(4)]
+    paid = [paid[0]] + [move(paid[m], levels[m]) for m in (1, 2, 3)]
+    w_ud = gather(q_ud)
+
+    wpo, mod, n1, proj, att = call(
+        attend_body, "attention", ids, w_po + paid + [latents],
+        [((4, feat, feat), BF16), ((4, wide), F32), ((tokens, feat), BF16),
+         ((tokens, 3 * feat), BF16), ((tokens, feat), BF16)],
+        flops=2 * tokens * feat * (3 * feat + 4 * length),
+    )
+    wout = wpo[3:4]
+    ud_shape = ((4, 2, rows, feat), BF16)
+    po_shape = ((4, rows, feat), BF16)
+    res, gmid, gbr, gatt, gsum, gmod, *ud = call(
+        mlp_body, "mlp", ids, w_ud + [wout, mod, latents, cotangent, att],
+        [((slots, length, feat), BF16), ((slots, length, feat), F32), ((tokens, feat), BF16),
+         ((tokens, feat), BF16), ((1, 6 * feat), F32), ((slots, 4 * feat), F32)] + [ud_shape] * 8,
+        [
+            pltpu.VMEM((4, feat, feat), BF16), pltpu.VMEM((hidden, feat), BF16),
+            pltpu.VMEM((tokens, feat), BF16), pltpu.VMEM((tokens, hidden), BF16),
+            pltpu.VMEM((length, hidden), F32), pltpu.VMEM((tokens, feat), BF16),
+            pltpu.VMEM((tokens, hidden), BF16), pltpu.VMEM((feat, tokens), BF16),
+            pltpu.VMEM((feat, feat), BF16), pltpu.VMEM((hidden, feat), BF16),
+        ],
+        flops=2 * tokens * feat * (6 * hidden + 2 * feat),
+    )
+
+    def scatter(pieces):
+        keeps, sends = pieces[:4], pieces[4:]
+        from_core = {m: move(sends[m], core) for m in (1, 3, 0, 2)}
+        summed = {m: add_low(keeps[m], from_core[m]) for m in (1, 3, 0, 2)}
+        to_zero = move(summed[1], first)
+        to_two = move(summed[3], first)
+        summed_two = add_low(summed[2], to_two)
+        last = move(summed_two, second)
+        base = add_low(summed[0], to_zero)
+        total = [add_low(base[m], last[m]) for m in range(4)]
+        own = add_low(total[0], *[move(total[m], levels[m]) for m in (1, 2, 3)])
+        a = move(own, first)
+        b = move(own, second)
+        return [own, a, b, move(a, second)]
+
+    g_ud = scatter(ud)
+    gproj, bias, *po = call(
+        functools.partial(attend_back_body, length=length), "attention_back", ids,
+        [proj, gatt, att, gbr, n1, gsum],
+        [((tokens, 3 * feat), BF16), ((1, 8 * feat), F32)] + [po_shape] * 8,
+        [pltpu.VMEM((tokens, 4 * feat), BF16), pltpu.VMEM((2, feat, tokens), BF16),
+         pltpu.VMEM((feat, feat), BF16)],
+        flops=2 * tokens * feat * (4 * feat + 10 * length),
+    )
+    g_po = scatter(po)
+    lgrad, gm = call(
+        input_back_body, "input_back", ids, [gproj, wpo, latents, gmid, mod, gmod],
+        [((slots, length, feat), BF16), ((slots, wide), F32)],
+        flops=2 * tokens * feat * 3 * feat,
+    )
+    gm = gm.astype(BF16)
+
+    gm_pair = jnp.concatenate([gm, move(gm, core)], axis=0)
+    gm_all = [gm_pair] + [move(gm_pair, levels[m]) for m in (1, 2, 3)]
+    back = call(
+        cond_back_body, "cond_back", ids, gm_all + [modulation_weight],
+        [((2 * slots, feat), F32)] * 4,
+    )
+    silu_pair = back[0]
+    for m in (1, 2, 3):
+        silu_pair = silu_pair + move(back[m], levels[m])
+    grad_silu = silu_pair[:slots] + move(silu_pair[slots:], core)
+    cond_full = cond.astype(F32)
+    sig = 1.0 / (1.0 + jnp.exp(-cond_full))
+    cond_grad = (grad_silu * (sig * (1.0 + cond_full * (1.0 - sig)))).astype(BF16)
+
+    def over_dp(own):
+        a = move(own, first)
+        b = move(own, second)
+        return [own, a, b, move(a, second)]
+
+    c_every = over_dp(jnp.concatenate(c_all, axis=0))
+    gm_every = over_dp(jnp.concatenate(gm_all, axis=0))
+    g_mod_weight, g_mod_bias = call(
+        mod_weight_body, "mod_weight", ids, c_every + gm_every,
+        [((rows, wide), F32), ((1, wide), F32)],
+    )
+
+    bias = bias + move(bias, core)
+    bias = bias + move(bias, levels[1])
+    bias = bias + move(bias, levels[2])
+    bias = bias + move(bias, first)
+    bias = (bias + move(bias, second))[0]
+
+    def share(vector):
+        size = vector.shape[0] // 8
+        return lax.dynamic_slice_in_dim(vector, f * size, size)
+
+    g_proj, g_out = call(
+        final_po_body, "final_po", ids, g_po, [((rows, 3 * feat), F32), ((rows, feat), F32)]
+    )
+    g_up, g_down = call(
+        final_ud_body, "final_ud", ids, g_ud, [((rows, hidden), F32), ((4 * rows, feat), F32)]
+    )
+    return (
+        res, lgrad, cond_grad, g_mod_weight, share(g_mod_bias[0]), g_proj, share(bias[: 2 * feat]),
+        g_out, share(bias[2 * feat : 3 * feat]), g_up, share(bias[3 * feat : 7 * feat]),
+        g_down, share(bias[7 * feat :]),
+    )
 
 
 def layer_norm(vector):
@@ -336,6 +925,8 @@
 
 
 def solution(mesh):
+    small = mesh.shape["dp"] == 4 and mesh.shape["fsdp"] == 8
+    program = on_device_blocks if small else on_device
     placed = (
         P(("dp", "fsdp"), None, None),
         P(("dp", "fsdp"), None),
@@ -353,7 +944,7 @@
         P("fsdp"),
     )
     return jax.shard_map(
-        on_device,
+        program,
         mesh=mesh,
         in_specs=placed,
         out_specs=(

time: 396 us -> 169 us (0.43)
  blocking collectives: 110 us -> 0 us
  waiting for transfers between devices: 121 us -> 48.9 us
  starting transfers between devices: 0.62 us -> 68.9 us
  matrix products: 59.8 us -> 0 us
  other arithmetic: 48.4 us -> 2.62 us
  Pallas kernels: 0 us -> 35.2 us
  local copies, waits for them, and re-layouts: 33.4 us -> 11.6 us
  between operations: 21.4 us -> 1.8 us
    reduce_scatter x5 -> x0, waiting for transfers between devices: 89.1 us -> none  [the longest x1 43.8 us: on_device(): lax.psum_scatter(totals[0], 'fsdp', scatter_dimension=0, tiled=True)]
    ppermute x0 -> x73, starting transfers between devices: none -> 68.9 us  [move(): return lax.ppermute(x, BOTH, route)]
    dot_general x40 -> x0, matrix products: 59.8 us -> none  [the longest x2 7.43 us: backward_pass(): jnp.einsum('nd,fd->nf', grad_mlp, down_weight, preferred_element_type=jnp...]
    unnamed x2 -> x0, blocking collectives: 58 us -> none
    ppermute x0 -> x73, waiting for transfers between devices: none -> 48.9 us  [move(): return lax.ppermute(x, BOTH, route)]
    pallas_call x0 -> x10, Pallas kernels: none -> 35.2 us  [call(): pl.pallas_call(body, out_shape=[jax.ShapeDtypeStruct(s, t) for s, t in ou...]
    all_gather x2 -> x0, blocking collectives: 35.1 us -> none  [the longest x1 19 us: on_device(): lax.all_gather(projection_weight, 'fsdp', axis=0, tiled=True)]
    psum x1 -> x0, waiting for transfers between devices: 29.6 us -> none  [on_device(): lax.psum(totals[0].astype(jnp.bfloat16), 'dp').astype(jnp.float32)]
  transfers between devices with their start and end apart: 9 -> 73, of which waited for: 5 -> 22; matrix products, arithmetic and copies ran while one was open for 23% -> 4% of each run, Pallas kernels for 0% -> 7%
where the time goes in v1:
time: 169 us
  starting transfers between devices  68.9 us (41%)
  waiting for transfers between devices  48.9 us (29%)
  Pallas kernels  35.2 us (21%)
  local copies, waits for them, and re-layouts  11.6 us (7%)
  other arithmetic  2.62 us (2%)
  between operations  1.8 us (1%)
    ppermute x73, starting transfers between devices, move(): return lax.ppermute(x, BOTH, route)  68.9 us
    ppermute x73, waiting for transfers between devices, move(): return lax.ppermute(x, BOTH, route)  48.9 us
    pallas_call x10, Pallas kernels, call(): pl.pallas_call(body, out_shape=[jax.ShapeDtypeStruct(s, t) for s, t in ou...  35.2 us
    unnamed x36, local copies, waits for them, and re-layouts  7.57 us
  transfers between devices with their start and end apart: 73, of which 22 were waited for; matrix products, arithmetic and copies ran while one was open for 4% of the time, Pallas kernels for 7%

profile of v1, /device:TPU:0, one launch (start us, length us, event | category | flops | bytes accessed | tf_op | source)
XLA Modules:
  0.0 169.0 jit_solution(5128068732021181727)
XLA Ops:
  6.2 3.1 %collective-permute-start = (bf16[2,48,384]{2,1,0:T(8,128)(2,1)S(1)}, bf16[2,48,384]{2,1,0:T(8,128)(2,1)S(1)}, u32[]{:S(2)}, u32[]{:S(2)}) collective-permute-start(bf16[2,48,384]{2,1,0:T(8,128)(2,1)S(1)} %get-tuple-element.62), channel_id=1, source_target_pairs={{0,2},{1,3},{2,0},{3,1},{4,6},{5,7},{6,4},{7,5},{8,10},{9,11},{10,... | collective-permute-start | bytes 221192 | tf_op jit(solution)/shard_map/ppermute | solution.py:455
  9.3 2.6 %collective-permute-start.1 = (bf16[2,48,384]{2,1,0:T(8,128)(2,1)S(1)}, bf16[2,48,384]{2,1,0:T(8,128)(2,1)S(1)}, u32[]{:S(2)}, u32[]{:S(2)}) collective-permute-start(bf16[2,48,384]{2,1,0:T(8,128)(2,1)S(1)} %get-tuple-element.62), channel_id=1, source_target_pairs={{0,4},{1,5},{2,6},{3,7},{4,0},{5,1},{6,2},{7,3},{8,12},{9,13},{10,... | collective-permute-start | bytes 221192 | tf_op jit(solution)/shard_map/ppermute | solution.py:455
  11.9 5.2 %collective-permute-done.1 = bf16[2,48,384]{2,1,0:T(8,128)(2,1)S(1)} collective-permute-done((bf16[2,48,384]{2,1,0:T(8,128)(2,1)S(1)}, bf16[2,48,384]{2,1,0:T(8,128)(2,1)S(1)}, u32[]{:S(2)}, u32[]{:S(2)}) %collective-permute-start.1) | collective-permute-done | bytes 73760 | tf_op jit(solution)/shard_map/ppermute | solution.py:455
  18.2 1.6 collective-permute-start.3
  22.1 1.7 collective-permute-start.22
  23.8 1.3 collective-permute-start.10
  25.9 2.2 %collective-permute-start.12 = (bf16[48,384]{1,0:T(8,128)(2,1)S(1)}, bf16[48,384]{1,0:T(8,128)(2,1)S(1)}, u32[]{:S(2)}, u32[]{:S(2)}) collective-permute-start(bf16[48,384]{1,0:T(8,128)(2,1)S(1)} %get-tuple-element.63), channel_id=1, source_target_pairs={{0,6},{1,7},{2,4},{3,5},{4,2},{5,3},{6,0},{7,1},{8,14},{9,15},{10,... | collective-permute-start | bytes 110600 | tf_op jit(solution)/shard_map/ppermute | solution.py:455
  28.2 1.6 collective-permute-start.23
  31.1 2.5 %collective-permute-done.23.c3 = bf16[4,384]{1,0:T(4,128)(2,1)S(1)} collective-permute-done((bf16[4,384]{1,0:T(4,128)(2,1)S(1)}, bf16[4,384]{1,0:T(4,128)(2,1)S(1)}, u32[]{:S(2)}, u32[]{:S(2)}) %collective-permute-start.23) | collective-permute-done | bytes 3104 | tf_op jit(solution)/shard_map/ppermute | solution.py:455
  35.5 1.7 modulation.1
  38.0 1.5 collective-permute-start.14
  40.2 1.3 collective-permute-start.5
  41.6 1.9 %collective-permute-done.13.w1 = bf16[4,48,384]{2,1,0:T(8,128)(2,1)S(1)} collective-permute-done((bf16[4,48,384]{2,1,0:T(8,128)(2,1)S(1)}, bf16[4,48,384]{2,1,0:T(8,128)(2,1)S(1)}, u32[]{:S(2)}, u32[]{:S(2)}) %collective-permute-start.13) | collective-permute-done | bytes 147488 | tf_op jit(solution)/shard_map/ppermute | solution.py:455
  43.7 1.9 %collective-permute-start.26 = (f32[4,2304]{1,0:T(4,128)S(1)}, f32[4,2304]{1,0:T(4,128)S(1)}, u32[]{:S(2)}, u32[]{:S(2)}) collective-permute-start(f32[4,2304]{1,0:T(4,128)S(1)} %get-tuple-element.118), channel_id=1, source_target_pairs={{0,4},{1,5},{2,6},{3,7},{4,0},{5,1},{6,2},{7,3},{8,12},{9,13},{10,... | collective-permute-start | bytes 110600 | tf_op jit(solution)/shard_map/ppermute | solution.py:455
  45.6 2.2 %collective-permute-start.15 = (bf16[4,48,384]{2,1,0:T(8,128)(2,1)S(1)}, bf16[4,48,384]{2,1,0:T(8,128)(2,1)S(1)}, u32[]{:S(2)}, u32[]{:S(2)}) collective-permute-start(bf16[4,48,384]{2,1,0:T(8,128)(2,1)S(1)} %collective-permute-done.13.w1), channel_id=1, source_target_pairs={{0,16},{1,9},{2,18},{3,11},{4,20},{5,13},{6,22},{7,15},{8,24},{9,1... | collective-permute-start | bytes 442376 | tf_op jit(solution)/shard_map/ppermute | solution.py:455
  48.6 1.8 %collective-permute-start.27 = (f32[4,2304]{1,0:T(4,128)S(1)}, f32[4,2304]{1,0:T(4,128)S(1)}, u32[]{:S(2)}, u32[]{:S(2)}) collective-permute-start(f32[4,2304]{1,0:T(4,128)S(1)} %get-tuple-element.117), channel_id=1, source_target_pairs={{0,6},{1,7},{2,4},{3,5},{4,2},{5,3},{6,0},{7,1},{8,14},{9,15},{10,... | collective-permute-start | bytes 110600 | tf_op jit(solution)/shard_map/ppermute | solution.py:455
  50.4 4.0 %collective-permute-done.27.p3 = f32[4,2304]{1,0:T(4,128)S(1)} collective-permute-done((f32[4,2304]{1,0:T(4,128)S(1)}, f32[4,2304]{1,0:T(4,128)S(1)}, u32[]{:S(2)}, u32[]{:S(2)}) %collective-permute-start.27) | collective-permute-done | bytes 36896 | tf_op jit(solution)/shard_map/ppermute | solution.py:455
  55.9 1.7 %collective-permute-done.19.o3 = bf16[4,48,384]{2,1,0:T(8,128)(2,1)S(1)} collective-permute-done((bf16[4,48,384]{2,1,0:T(8,128)(2,1)S(1)}, bf16[4,48,384]{2,1,0:T(8,128)(2,1)S(1)}, u32[]{:S(2)}, u32[]{:S(2)}) %collective-permute-start.19) | collective-permute-done | bytes 147488 | tf_op jit(solution)/shard_map/ppermute | solution.py:455
  57.6 4.2 %attention.1 = (bf16[4,384,384]{2,1,0:T(8,128)(2,1)S(1)}, f32[4,2304]{1,0:T(4,128)S(1)}, bf16[512,384]{1,0:T(8,128)(2,1)S(1)}, bf16[512,1152]{1,0:T(8,128)(2,1)S(1)}, bf16[512,384]{1,0:T(8,128)(2,1)S(1)}) custom-call(s32[3]{0:T(128)S(1)} %pad_add_fusion.ids, bf16[4,48,384]{2,1,0:T(8,128)(2,1)S(1)} %pad_maximum_fusion.1.w0, ...), custom_call_target="tpu_custom_call" | custom-call | flops 855638016 | bytes 4902912 | tf_op jit(solution)/shard_map/attention/pallas_call | solution.py:37
  62.7 12.0 %mlp.1 = (bf16[2,256,384]{2,1,0:T(8,128)(2,1)}, f32[2,256,384]{2,1,0:T(8,128)}, bf16[512,384]{1,0:T(8,128)(2,1)S(1)}, bf16[512,384]{1,0:T(8,128)(2,1)S(1)}, f32[...) custom-call(s32[3]{0:T(128)S(1)} %pad_add_fusion.ids, ...), custom_call_target="tpu_custom_call" | custom-call | flops 3925868544 | bytes 8217600 | tf_op jit(solution)/shard_map/mlp/pallas_call | solution.py:37
  74.7 7.2 %attention_back.1 = (bf16[512,1152]{1,0:T(8,128)(2,1)S(1)}, f32[1,3072]{1,0:T(1,128)S(1)}, bf16[4,48,384]{2,1,0:T(8,128)(2,1)S(1)}, bf16[4,48,384]{2,1,0:T(8,128...) custom-call(s32[3]{0:T(128)S(1)} %pad_add_fusion.ids, ...), custom_call_target="tpu_custom_call" | custom-call | flops 1610612736 | bytes 5133312 | tf_op jit(solution)/shard_map/attention_back/pallas_call | solution.py:37
  82.5 3.0 %input_back.1 = (bf16[2,256,384]{2,1,0:T(8,128)(2,1)}, f32[2,2304]{1,0:T(2,128)S(1)}) custom-call(s32[3]{0:T(128)S(1)} %pad_add_fusion.ids, bf16[512,1152]{1,0:T(8,128)(2,1)S(1)} %get-tuple-element.79.gproj, bf16[4,384,384]{2,1,0:T(8,128)(2,1)S(1)} %get-tuple-element.70.wpo, bf16[2,256,384]{2,1,0:T(8,128)(2,1)S(1)} %copy-done.3, ...), custom_call_target="tpu_custom_call" | custom-call | flops 452984832 | bytes 3999744 | tf_op jit(solution)/shard_map/input_back/pallas_call | solution.py:37
  86.8 2.3 %collective-permute-start.30 = (bf16[4,2304]{1,0:T(4,128)(2,1)S(1)}, bf16[4,2304]{1,0:T(4,128)(2,1)S(1)}, u32[]{:S(2)}, u32[]{:S(2)}) collective-permute-start(bf16[4,2304]{1,0:T(4,128)(2,1)S(1)} %pad_maximum_fusion.2.g0), channel_id=1, source_target_pairs={{0,4},{1,5},{2,6},{3,7},{4,0},{5,1},{6,2},{7,3},{8,12},{9,13},{10,... | collective-permute-start | bytes 55304 | tf_op jit(solution)/shard_map/ppermute | solution.py:455
  89.2 2.1 %collective-permute-start.31 = (bf16[4,2304]{1,0:T(4,128)(2,1)S(1)}, bf16[4,2304]{1,0:T(4,128)(2,1)S(1)}, u32[]{:S(2)}, u32[]{:S(2)}) collective-permute-start(bf16[4,2304]{1,0:T(4,128)(2,1)S(1)} %pad_maximum_fusion.2.g0), channel_id=1, source_target_pairs={{0,6},{1,7},{2,4},{3,5},{4,2},{5,3},{6,0},{7,1},{8,14},{9,15},{10,... | collective-permute-start | bytes 55304 | tf_op jit(solution)/shard_map/ppermute | solution.py:455
  91.3 3.7 %collective-permute-done.56 = f32[1,3072]{1,0:T(1,128)S(1)} collective-permute-done((f32[1,3072]{1,0:T(1,128)S(1)}, f32[1,3072]{1,0:T(1,128)S(1)}, u32[]{:S(2)}, u32[]{:S(2)}) %collective-permute-start.56) | collective-permute-done | bytes 12320 | tf_op jit(solution)/shard_map/ppermute | solution.py:455
  95.5 1.9 %cond_back.1 = (f32[4,384]{1,0:T(4,128)S(1)}, f32[4,384]{1,0:T(4,128)S(1)}, f32[4,384]{1,0:T(4,128)S(1)}, f32[4,384]{1,0:T(4,128)S(1)}) custom-call(s32[3]{0:T(128)S(1)} %pad_add_fusion.ids, bf16[4,2304]{1,0:T(4,128)(2,1)S(1)} %pad_maximum_fusion.2.g0, bf16[4,2304]{1,0:T(4,128)(2,1)S(1)} %collective-permute-done.29.g1, ...), custom_call_target="tpu_custom_call" | custom-call | bytes 319488 | tf_op jit(solution)/shard_map/cond_back/pallas_call | solution.py:37
  97.4 2.1 %collective-permute-start.32 = (f32[4,384]{1,0:T(4,128)S(1)}, f32[4,384]{1,0:T(4,128)S(1)}, u32[]{:S(2)}, u32[]{:S(2)}) collective-permute-start(f32[4,384]{1,0:T(4,128)S(1)} %get-tuple-element.85), channel_id=1, source_target_pairs={{0,2},{1,3},{2,0},{3,1},{4,6},{5,7},{6,4},{7,5},{8,10},{9,11},{10,... | collective-permute-start | bytes 18440 | tf_op jit(solution)/shard_map/ppermute | solution.py:455
  100.0 1.8 %collective-permute-start.34 = (f32[4,384]{1,0:T(4,128)S(1)}, f32[4,384]{1,0:T(4,128)S(1)}, u32[]{:S(2)}, u32[]{:S(2)}) collective-permute-start(f32[4,384]{1,0:T(4,128)S(1)} %get-tuple-element.87), channel_id=1, source_target_pairs={{0,6},{1,7},{2,4},{3,5},{4,2},{5,3},{6,0},{7,1},{8,14},{9,15},{10,... | collective-permute-start | bytes 18440 | tf_op jit(solution)/shard_map/ppermute | solution.py:455
  102.6 1.5 collective-permute-start.58
  104.1 1.4 collective-permute-done.34
  105.6 2.1 %collective-permute-start.37 = (bf16[16,384]{1,0:T(8,128)(2,1)S(1)}, bf16[16,384]{1,0:T(8,128)(2,1)S(1)}, u32[]{:S(2)}, u32[]{:S(2)}) collective-permute-start(bf16[16,384]{1,0:T(8,128)(2,1)S(1)} %concatenate.16.refs_0_), channel_id=1, source_target_pairs={{0,16},{1,9},{2,18},{3,11},{4,20},{5,13},{6,22},{7,15},{8,24},{9,1... | collective-permute-start | bytes 36872 | tf_op jit(solution)/shard_map/ppermute | solution.py:455
  108.4 2.0 %collective-permute-start.59 = (f32[1,3072]{1,0:T(1,128)S(1)}, f32[1,3072]{1,0:T(1,128)S(1)}, u32[]{:S(2)}, u32[]{:S(2)}) collective-permute-start(f32[1,3072]{1,0:T(1,128)S(1)} %add.171), channel_id=1, source_target_pairs={{0,16},{1,9},{2,18},{3,11},{4,20},{5,13},{6,22},{7,15},{8,24},{9,1... | collective-permute-start | bytes 36872 | tf_op jit(solution)/shard_map/ppermute | solution.py:455
  115.5 1.3 collective-permute-start.61
  116.7 3.0 %collective-permute-done.44 = bf16[4,48,384]{2,1,0:T(8,128)(2,1)S(1)} collective-permute-done((bf16[4,48,384]{2,1,0:T(8,128)(2,1)S(1)}, bf16[4,48,384]{2,1,0:T(8,128)(2,1)S(1)}, u32[]{:S(2)}, u32[]{:S(2)}) %collective-permute-start.44) | collective-permute-done | bytes 147488 | tf_op jit(solution)/shard_map/ppermute | solution.py:455
  121.7 1.4 collective-permute-start.63
  123.2 1.8 %collective-permute-done.47 = bf16[4,48,384]{2,1,0:T(8,128)(2,1)S(1)} collective-permute-done((bf16[4,48,384]{2,1,0:T(8,128)(2,1)S(1)}, bf16[4,48,384]{2,1,0:T(8,128)(2,1)S(1)}, u32[]{:S(2)}, u32[]{:S(2)}) %collective-permute-start.47) | collective-permute-done | bytes 147488 | tf_op jit(solution)/shard_map/ppermute | solution.py:455
  126.6 1.2 collective-permute-start.48
  127.8 5.5 %collective-permute-done.65 = bf16[4,2,48,384]{3,2,1,0:T(8,128)(2,1)S(1)} collective-permute-done((bf16[4,2,48,384]{3,2,1,0:T(8,128)(2,1)S(1)}, bf16[4,2,48,384]{3,2,1,0:T(8,128)(2,1)S(1)}, u32[]{:S(2)}, u32[]{:S(2)}) %collective-permute-start.65) | collective-permute-done | bytes 294944 | tf_op jit(solution)/shard_map/ppermute | solution.py:455
  134.3 1.7 %collective-permute-start.66 = (bf16[4,2,48,384]{3,2,1,0:T(8,128)(2,1)S(1)}, bf16[4,2,48,384]{3,2,1,0:T(8,128)(2,1)S(1)}, u32[]{:S(2)}, u32[]{:S(2)}) collective-permute-start(bf16[4,2,48,384]{3,2,1,0:T(8,128)(2,1)S(1)} %add_convert_fusion), channel_id=1, source_target_pairs={{0,16},{1,9},{2,18},{3,11},{4,20},{5,13},{6,22},{7,15},{8,24},{9,1... | collective-permute-start | bytes 884744 | tf_op jit(solution)/shard_map/ppermute | solution.py:455
  136.2 6.0 %collective-permute-done.62 = bf16[4,2,48,384]{3,2,1,0:T(8,128)(2,1)S(1)} collective-permute-done((bf16[4,2,48,384]{3,2,1,0:T(8,128)(2,1)S(1)}, bf16[4,2,48,384]{3,2,1,0:T(8,128)(2,1)S(1)}, u32[]{:S(2)}, u32[]{:S(2)}) %collective-permute-start.62) | collective-permute-done | bytes 294944 | tf_op jit(solution)/shard_map/ppermute | solution.py:455
  142.7 2.2 %collective-permute-start.51 = (bf16[48,384]{1,0:T(8,128)(2,1)S(1)}, bf16[48,384]{1,0:T(8,128)(2,1)S(1)}, u32[]{:S(2)}, u32[]{:S(2)}) collective-permute-start(bf16[48,384]{1,0:T(8,128)(2,1)S(1)} %get-tuple-element.115), channel_id=1, source_target_pairs={{0,6},{1,7},{2,4},{3,5},{4,2},{5,3},{6,0},{7,1},{8,14},{9,15},{10,... | collective-permute-start | bytes 110600 | tf_op jit(solution)/shard_map/ppermute | solution.py:455
  146.0 2.8 %collective-permute-done.50 = bf16[48,384]{1,0:T(8,128)(2,1)S(1)} collective-permute-done((bf16[48,384]{1,0:T(8,128)(2,1)S(1)}, bf16[48,384]{1,0:T(8,128)(2,1)S(1)}, u32[]{:S(2)}, u32[]{:S(2)}) %collective-permute-start.50) | collective-permute-done | bytes 36896 | tf_op jit(solution)/shard_map/ppermute | solution.py:455
  148.8 2.2 %collective-permute-start.69 = (bf16[2,48,384]{2,1,0:T(8,128)(2,1)S(1)}, bf16[2,48,384]{2,1,0:T(8,128)(2,1)S(1)}, u32[]{:S(2)}, u32[]{:S(2)}) collective-permute-start(bf16[2,48,384]{2,1,0:T(8,128)(2,1)S(1)} %get-tuple-element.112), channel_id=1, source_target_pairs={{0,6},{1,7},{2,4},{3,5},{4,2},{5,3},{6,0},{7,1},{8,14},{9,15},{10,... | collective-permute-start | bytes 221192 | tf_op jit(solution)/shard_map/ppermute | solution.py:455
  151.9 2.1 %collective-permute-done.68 = bf16[2,48,384]{2,1,0:T(8,128)(2,1)S(1)} collective-permute-done((bf16[2,48,384]{2,1,0:T(8,128)(2,1)S(1)}, bf16[2,48,384]{2,1,0:T(8,128)(2,1)S(1)}, u32[]{:S(2)}, u32[]{:S(2)}) %collective-permute-start.68) | collective-permute-done | bytes 73760 | tf_op jit(solution)/shard_map/ppermute | solution.py:455
  155.1 1.4 collective-permute-start.52
  163.5 2.1 %mod_weight.1 = (f32[48,2304]{1,0:T(8,128)}, f32[1,2304]{1,0:T(1,128)S(1)}) custom-call(s32[3]{0:T(128)S(1)} %pad_add_fusion.ids, bf16[16,384]{1,0:T(8,128)(2,1)S(1)} %concatenate.16.refs_0_, bf16[16,384]{1,0:T(8,128)(2,1)S(1)} %collective-permute-done.36.refs_1_, bf16[16,384]{1,0:T(8,128)(2,1)S(1)} %collective-permute-done.37.refs_2_, ...), custom_call_target="tpu_custom_call" | custom-call | bytes 795648 | tf_op jit(solution)/shard_map/mod_weight/pallas_call | solution.py:37
  166.3 1.3 final_po.1
  167.6 1.4 final_ud.1
  (183 shorter events, 42.8 us)
Async XLA Ops:
  6.2 5.7 %collective-permute-start = (bf16[2,48,384]{2,1,0:T(8,128)(2,1)S(1)}, bf16[2,48,384]{2,1,0:T(8,128)(2,1)S(1)}, u32[]{:S(2)}, u32[]{:S(2)}) collective-permute-start(bf16[2,48,384]{2,1,0:T(8,128)(2,1)S(1)} %get-tuple-element.62), channel_id=1, source_target_pairs={{0,2},{1,3},{2,0},{3,1},{4,6},{5,7},{6,4},{7,5},{8,10},{9,11},{10,... | collective-permute-start | bytes 221192 | tf_op jit(solution)/shard_map/ppermute | solution.py:455
  9.3 7.8 %collective-permute-start.1 = (bf16[2,48,384]{2,1,0:T(8,128)(2,1)S(1)}, bf16[2,48,384]{2,1,0:T(8,128)(2,1)S(1)}, u32[]{:S(2)}, u32[]{:S(2)}) collective-permute-start(bf16[2,48,384]{2,1,0:T(8,128)(2,1)S(1)} %get-tuple-element.62), channel_id=1, source_target_pairs={{0,4},{1,5},{2,6},{3,7},{4,0},{5,1},{6,2},{7,3},{8,12},{9,13},{10,... | collective-permute-start | bytes 221192 | tf_op jit(solution)/shard_map/ppermute | solution.py:455
  11.9 6.3 %collective-permute-start.2 = (bf16[2,48,384]{2,1,0:T(8,128)(2,1)S(1)}, bf16[2,48,384]{2,1,0:T(8,128)(2,1)S(1)}, u32[]{:S(2)}, u32[]{:S(2)}) collective-permute-start(bf16[2,48,384]{2,1,0:T(8,128)(2,1)S(1)} %get-tuple-element.62), channel_id=1, source_target_pairs={{0,6},{1,7},{2,4},{3,5},{4,2},{5,3},{6,0},{7,1},{8,14},{9,15},{10,... | collective-permute-start | bytes 221192 | tf_op jit(solution)/shard_map/ppermute | solution.py:455
  18.2 22.0 %collective-permute-start.3 = (bf16[4,2,48,384]{3,2,1,0:T(8,128)(2,1)S(1)}, bf16[4,2,48,384]{3,2,1,0:T(8,128)(2,1)S(1)}, u32[]{:S(2)}, u32[]{:S(2)}) collective-permute-start(bf16[4,2,48,384]{3,2,1,0:T(8,128)(2,1)S(1)} %pad_maximum_fusion.w0), channel_id=1, source_target_pairs={{0,8},{1,17},{2,10},{3,19},{4,12},{5,21},{6,14},{7,23},{8,0},{9,25... | collective-permute-start | bytes 884744 | tf_op jit(solution)/shard_map/ppermute | solution.py:455
  22.1 6.1 %collective-permute-start.22 = (bf16[4,384]{1,0:T(4,128)(2,1)S(1)}, bf16[4,384]{1,0:T(4,128)(2,1)S(1)}, u32[]{:S(2)}, u32[]{:S(2)}) collective-permute-start(bf16[4,384]{1,0:T(4,128)(2,1)S(1)} %pad_maximum_fusion.3.c0), channel_id=1, source_target_pairs={{0,4},{1,5},{2,6},{3,7},{4,0},{5,1},{6,2},{7,3},{8,12},{9,13},{10,... | collective-permute-start | bytes 9224 | tf_op jit(solution)/shard_map/ppermute | solution.py:455
  23.8 13.5 %collective-permute-start.10 = (bf16[48,384]{1,0:T(8,128)(2,1)S(1)}, bf16[48,384]{1,0:T(8,128)(2,1)S(1)}, u32[]{:S(2)}, u32[]{:S(2)}) collective-permute-start(bf16[48,384]{1,0:T(8,128)(2,1)S(1)} %get-tuple-element.63), channel_id=1, source_target_pairs={{0,2},{1,3},{2,0},{3,1},{4,6},{5,7},{6,4},{7,5},{8,10},{9,11},{10,... | collective-permute-start | bytes 110600 | tf_op jit(solution)/shard_map/ppermute | solution.py:455
  25.1 12.2 %collective-permute-start.11 = (bf16[48,384]{1,0:T(8,128)(2,1)S(1)}, bf16[48,384]{1,0:T(8,128)(2,1)S(1)}, u32[]{:S(2)}, u32[]{:S(2)}) collective-permute-start(bf16[48,384]{1,0:T(8,128)(2,1)S(1)} %get-tuple-element.63), channel_id=1, source_target_pairs={{0,4},{1,5},{2,6},{3,7},{4,0},{5,1},{6,2},{7,3},{8,12},{9,13},{10,... | collective-permute-start | bytes 110600 | tf_op jit(solution)/shard_map/ppermute | solution.py:455
  25.9 11.4 %collective-permute-start.12 = (bf16[48,384]{1,0:T(8,128)(2,1)S(1)}, bf16[48,384]{1,0:T(8,128)(2,1)S(1)}, u32[]{:S(2)}, u32[]{:S(2)}) collective-permute-start(bf16[48,384]{1,0:T(8,128)(2,1)S(1)} %get-tuple-element.63), channel_id=1, source_target_pairs={{0,6},{1,7},{2,4},{3,5},{4,2},{5,3},{6,0},{7,1},{8,14},{9,15},{10,... | collective-permute-start | bytes 110600 | tf_op jit(solution)/shard_map/ppermute | solution.py:455
  37.4 6.1 %collective-permute-start.13 = (bf16[4,48,384]{2,1,0:T(8,128)(2,1)S(1)}, bf16[4,48,384]{2,1,0:T(8,128)(2,1)S(1)}, u32[]{:S(2)}, u32[]{:S(2)}) collective-permute-start(bf16[4,48,384]{2,1,0:T(8,128)(2,1)S(1)} %pad_maximum_fusion.1.w0), channel_id=1, source_target_pairs={{0,8},{1,17},{2,10},{3,19},{4,12},{5,21},{6,14},{7,23},{8,0},{9,25... | collective-permute-start | bytes 442376 | tf_op jit(solution)/shard_map/ppermute | solution.py:455
  38.0 5.7 %collective-permute-start.14 = (bf16[4,48,384]{2,1,0:T(8,128)(2,1)S(1)}, bf16[4,48,384]{2,1,0:T(8,128)(2,1)S(1)}, u32[]{:S(2)}, u32[]{:S(2)}) collective-permute-start(bf16[4,48,384]{2,1,0:T(8,128)(2,1)S(1)} %pad_maximum_fusion.1.w0), channel_id=1, source_target_pairs={{0,16},{1,9},{2,18},{3,11},{4,20},{5,13},{6,22},{7,15},{8,24},{9,1... | collective-permute-start | bytes 442376 | tf_op jit(solution)/shard_map/ppermute | solution.py:455
  39.5 6.1 %collective-permute-start.16 = (bf16[4,48,384]{2,1,0:T(8,128)(2,1)S(1)}, bf16[4,48,384]{2,1,0:T(8,128)(2,1)S(1)}, u32[]{:S(2)}, u32[]{:S(2)}) collective-permute-start(bf16[4,48,384]{2,1,0:T(8,128)(2,1)S(1)} %pad_maximum_fusion.1.w0), channel_id=1, source_target_pairs={{0,1},{1,0},{2,3},{3,2},{4,5},{5,4},{6,7},{7,6},{8,9},{9,8},{10,11... | collective-permute-start | bytes 442376 | tf_op jit(solution)/shard_map/ppermute | solution.py:455
  39.5 15.5 %collective-permute-start.4 = (bf16[4,2,48,384]{3,2,1,0:T(8,128)(2,1)S(1)}, bf16[4,2,48,384]{3,2,1,0:T(8,128)(2,1)S(1)}, u32[]{:S(2)}, u32[]{:S(2)}) collective-permute-start(bf16[4,2,48,384]{3,2,1,0:T(8,128)(2,1)S(1)} %pad_maximum_fusion.w0), channel_id=1, source_target_pairs={{0,16},{1,9},{2,18},{3,11},{4,20},{5,13},{6,22},{7,15},{8,24},{9,1... | collective-permute-start | bytes 884744 | tf_op jit(solution)/shard_map/ppermute | solution.py:455
  40.2 15.2 %collective-permute-start.5 = (bf16[4,2,48,384]{3,2,1,0:T(8,128)(2,1)S(1)}, bf16[4,2,48,384]{3,2,1,0:T(8,128)(2,1)S(1)}, u32[]{:S(2)}, u32[]{:S(2)}) collective-permute-start(bf16[4,2,48,384]{3,2,1,0:T(8,128)(2,1)S(1)} %collective-permute-done.3.w1), channel_id=1, source_target_pairs={{0,16},{1,9},{2,18},{3,11},{4,20},{5,13},{6,22},{7,15},{8,24},{9,1... | collective-permute-start | bytes 884744 | tf_op jit(solution)/shard_map/ppermute | solution.py:455
  45.6 8.8 %collective-permute-start.15 = (bf16[4,48,384]{2,1,0:T(8,128)(2,1)S(1)}, bf16[4,48,384]{2,1,0:T(8,128)(2,1)S(1)}, u32[]{:S(2)}, u32[]{:S(2)}) collective-permute-start(bf16[4,48,384]{2,1,0:T(8,128)(2,1)S(1)} %collective-permute-done.13.w1), channel_id=1, source_target_pairs={{0,16},{1,9},{2,18},{3,11},{4,20},{5,13},{6,22},{7,15},{8,24},{9,1... | collective-permute-start | bytes 442376 | tf_op jit(solution)/shard_map/ppermute | solution.py:455
  47.8 7.1 %collective-permute-start.17 = (bf16[4,48,384]{2,1,0:T(8,128)(2,1)S(1)}, bf16[4,48,384]{2,1,0:T(8,128)(2,1)S(1)}, u32[]{:S(2)}, u32[]{:S(2)}) collective-permute-start(bf16[4,48,384]{2,1,0:T(8,128)(2,1)S(1)} %collective-permute-done.13.w1), channel_id=1, source_target_pairs={{0,1},{1,0},{2,3},{3,2},{4,5},{5,4},{6,7},{7,6},{8,9},{9,8},{10,11... | collective-permute-start | bytes 442376 | tf_op jit(solution)/shard_map/ppermute | solution.py:455
  48.6 5.8 %collective-permute-start.27 = (f32[4,2304]{1,0:T(4,128)S(1)}, f32[4,2304]{1,0:T(4,128)S(1)}, u32[]{:S(2)}, u32[]{:S(2)}) collective-permute-start(f32[4,2304]{1,0:T(4,128)S(1)} %get-tuple-element.117), channel_id=1, source_target_pairs={{0,6},{1,7},{2,4},{3,5},{4,2},{5,3},{6,0},{7,1},{8,14},{9,15},{10,... | collective-permute-start | bytes 110600 | tf_op jit(solution)/shard_map/ppermute | solution.py:455
  54.4 8.3 %collective-permute-start.6 = (bf16[4,2,48,384]{3,2,1,0:T(8,128)(2,1)S(1)}, bf16[4,2,48,384]{3,2,1,0:T(8,128)(2,1)S(1)}, u32[]{:S(2)}, u32[]{:S(2)}) collective-permute-start(bf16[4,2,48,384]{3,2,1,0:T(8,128)(2,1)S(1)} %pad_maximum_fusion.w0), channel_id=1, source_target_pairs={{0,1},{1,0},{2,3},{3,2},{4,5},{5,4},{6,7},{7,6},{8,9},{9,8},{10,11... | collective-permute-start | bytes 884744 | tf_op jit(solution)/shard_map/ppermute | solution.py:455
  54.9 7.8 %collective-permute-start.7 = (bf16[4,2,48,384]{3,2,1,0:T(8,128)(2,1)S(1)}, bf16[4,2,48,384]{3,2,1,0:T(8,128)(2,1)S(1)}, u32[]{:S(2)}, u32[]{:S(2)}) collective-permute-start(bf16[4,2,48,384]{3,2,1,0:T(8,128)(2,1)S(1)} %collective-permute-done.3.w1), channel_id=1, source_target_pairs={{0,1},{1,0},{2,3},{3,2},{4,5},{5,4},{6,7},{7,6},{8,9},{9,8},{10,11... | collective-permute-start | bytes 884744 | tf_op jit(solution)/shard_map/ppermute | solution.py:455
  55.0 7.7 %collective-permute-start.8 = (bf16[4,2,48,384]{3,2,1,0:T(8,128)(2,1)S(1)}, bf16[4,2,48,384]{3,2,1,0:T(8,128)(2,1)S(1)}, u32[]{:S(2)}, u32[]{:S(2)}) collective-permute-start(bf16[4,2,48,384]{3,2,1,0:T(8,128)(2,1)S(1)} %collective-permute-done.4.w2), channel_id=1, source_target_pairs={{0,1},{1,0},{2,3},{3,2},{4,5},{5,4},{6,7},{7,6},{8,9},{9,8},{10,11... | collective-permute-start | bytes 884744 | tf_op jit(solution)/shard_map/ppermute | solution.py:455
  55.4 7.3 %collective-permute-start.9 = (bf16[4,2,48,384]{3,2,1,0:T(8,128)(2,1)S(1)}, bf16[4,2,48,384]{3,2,1,0:T(8,128)(2,1)S(1)}, u32[]{:S(2)}, u32[]{:S(2)}) collective-permute-start(bf16[4,2,48,384]{3,2,1,0:T(8,128)(2,1)S(1)} %collective-permute-done.5.w3), channel_id=1, source_target_pairs={{0,1},{1,0},{2,3},{3,2},{4,5},{5,4},{6,7},{7,6},{8,9},{9,8},{10,11... | collective-permute-start | bytes 884744 | tf_op jit(solution)/shard_map/ppermute | solution.py:455
  86.8 8.7 %collective-permute-start.29 = (bf16[4,2304]{1,0:T(4,128)(2,1)S(1)}, bf16[4,2304]{1,0:T(4,128)(2,1)S(1)}, u32[]{:S(2)}, u32[]{:S(2)}) collective-permute-start(bf16[4,2304]{1,0:T(4,128)(2,1)S(1)} %pad_maximum_fusion.2.g0), channel_id=1, source_target_pairs={{0,2},{1,3},{2,0},{3,1},{4,6},{5,7},{6,4},{7,5},{8,10},{9,11},{10,... | collective-permute-start | bytes 55304 | tf_op jit(solution)/shard_map/ppermute | solution.py:455
  86.8 8.7 %collective-permute-start.30 = (bf16[4,2304]{1,0:T(4,128)(2,1)S(1)}, bf16[4,2304]{1,0:T(4,128)(2,1)S(1)}, u32[]{:S(2)}, u32[]{:S(2)}) collective-permute-start(bf16[4,2304]{1,0:T(4,128)(2,1)S(1)} %pad_maximum_fusion.2.g0), channel_id=1, source_target_pairs={{0,4},{1,5},{2,6},{3,7},{4,0},{5,1},{6,2},{7,3},{8,12},{9,13},{10,... | collective-permute-start | bytes 55304 | tf_op jit(solution)/shard_map/ppermute | solution.py:455
  89.2 6.3 %collective-permute-start.31 = (bf16[4,2304]{1,0:T(4,128)(2,1)S(1)}, bf16[4,2304]{1,0:T(4,128)(2,1)S(1)}, u32[]{:S(2)}, u32[]{:S(2)}) collective-permute-start(bf16[4,2304]{1,0:T(4,128)(2,1)S(1)} %pad_maximum_fusion.2.g0), channel_id=1, source_target_pairs={{0,6},{1,7},{2,4},{3,5},{4,2},{5,3},{6,0},{7,1},{8,14},{9,15},{10,... | collective-permute-start | bytes 55304 | tf_op jit(solution)/shard_map/ppermute | solution.py:455
  95.0 7.6 %collective-permute-start.57 = (f32[1,3072]{1,0:T(1,128)S(1)}, f32[1,3072]{1,0:T(1,128)S(1)}, u32[]{:S(2)}, u32[]{:S(2)}) collective-permute-start(f32[1,3072]{1,0:T(1,128)S(1)} %add.169), channel_id=1, source_target_pairs={{0,4},{1,5},{2,6},{3,7},{4,0},{5,1},{6,2},{7,3},{8,12},{9,13},{10,... | collective-permute-start | bytes 36872 | tf_op jit(solution)/shard_map/ppermute | solution.py:455
  97.4 6.7 %collective-permute-start.32 = (f32[4,384]{1,0:T(4,128)S(1)}, f32[4,384]{1,0:T(4,128)S(1)}, u32[]{:S(2)}, u32[]{:S(2)}) collective-permute-start(f32[4,384]{1,0:T(4,128)S(1)} %get-tuple-element.85), channel_id=1, source_target_pairs={{0,2},{1,3},{2,0},{3,1},{4,6},{5,7},{6,4},{7,5},{8,10},{9,11},{10,... | collective-permute-start | bytes 18440 | tf_op jit(solution)/shard_map/ppermute | solution.py:455
  100.0 5.4 %collective-permute-start.34 = (f32[4,384]{1,0:T(4,128)S(1)}, f32[4,384]{1,0:T(4,128)S(1)}, u32[]{:S(2)}, u32[]{:S(2)}) collective-permute-start(f32[4,384]{1,0:T(4,128)S(1)} %get-tuple-element.87), channel_id=1, source_target_pairs={{0,6},{1,7},{2,4},{3,5},{4,2},{5,3},{6,0},{7,1},{8,14},{9,15},{10,... | collective-permute-start | bytes 18440 | tf_op jit(solution)/shard_map/ppermute | solution.py:455
  101.9 5.7 %collective-permute-start.36 = (bf16[16,384]{1,0:T(8,128)(2,1)S(1)}, bf16[16,384]{1,0:T(8,128)(2,1)S(1)}, u32[]{:S(2)}, u32[]{:S(2)}) collective-permute-start(bf16[16,384]{1,0:T(8,128)(2,1)S(1)} %concatenate.16.refs_0_), channel_id=1, source_target_pairs={{0,8},{1,17},{2,10},{3,19},{4,12},{5,21},{6,14},{7,23},{8,0},{9,25... | collective-permute-start | bytes 36872 | tf_op jit(solution)/shard_map/ppermute | solution.py:455
  105.6 51.0 %collective-permute-start.37 = (bf16[16,384]{1,0:T(8,128)(2,1)S(1)}, bf16[16,384]{1,0:T(8,128)(2,1)S(1)}, u32[]{:S(2)}, u32[]{:S(2)}) collective-permute-start(bf16[16,384]{1,0:T(8,128)(2,1)S(1)} %concatenate.16.refs_0_), channel_id=1, source_target_pairs={{0,16},{1,9},{2,18},{3,11},{4,20},{5,13},{6,22},{7,15},{8,24},{9,1... | collective-permute-start | bytes 36872 | tf_op jit(solution)/shard_map/ppermute | solution.py:455
  107.6 51.3 %collective-permute-start.38 = (bf16[16,384]{1,0:T(8,128)(2,1)S(1)}, bf16[16,384]{1,0:T(8,128)(2,1)S(1)}, u32[]{:S(2)}, u32[]{:S(2)}) collective-permute-start(bf16[16,384]{1,0:T(8,128)(2,1)S(1)} %collective-permute-done.36.refs_1_), channel_id=1, source_target_pairs={{0,16},{1,9},{2,18},{3,11},{4,20},{5,13},{6,22},{7,15},{8,24},{9,1... | collective-permute-start | bytes 36872 | tf_op jit(solution)/shard_map/ppermute | solution.py:455
  107.7 12.1 %collective-permute-start.64 = (bf16[4,2,48,384]{3,2,1,0:T(8,128)(2,1)S(1)}, bf16[4,2,48,384]{3,2,1,0:T(8,128)(2,1)}, u32[]{:S(2)}, u32[]{:S(2)}) collective-permute-start(bf16[4,2,48,384]{3,2,1,0:T(8,128)(2,1)S(1)} %get-tuple-element.108), channel_id=1, source_target_pairs={{0,1},{1,0},{2,3},{3,2},{4,5},{5,4},{6,7},{7,6},{8,9},{9,8},{10,11... | collective-permute-start | bytes 884744 | tf_op jit(solution)/shard_map/ppermute | solution.py:455
  115.5 10.4 %collective-permute-start.61 = (bf16[4,2,48,384]{3,2,1,0:T(8,128)(2,1)S(1)}, bf16[4,2,48,384]{3,2,1,0:T(8,128)(2,1)S(1)}, u32[]{:S(2)}, u32[]{:S(2)}) collective-permute-start(bf16[4,2,48,384]{3,2,1,0:T(8,128)(2,1)S(1)} %get-tuple-element.104), channel_id=1, source_target_pairs={{0,1},{1,0},{2,3},{3,2},{4,5},{5,4},{6,7},{7,6},{8,9},{9,8},{10,11... | collective-permute-start | bytes 884744 | tf_op jit(solution)/shard_map/ppermute | solution.py:455
  125.0 8.3 %collective-permute-start.65 = (bf16[4,2,48,384]{3,2,1,0:T(8,128)(2,1)S(1)}, bf16[4,2,48,384]{3,2,1,0:T(8,128)(2,1)S(1)}, u32[]{:S(2)}, u32[]{:S(2)}) collective-permute-start(bf16[4,2,48,384]{3,2,1,0:T(8,128)(2,1)S(1)} %add_convert_fusion.1), channel_id=1, source_target_pairs={{0,8},{1,17},{2,10},{3,19},{4,12},{5,21},{6,14},{7,23},{8,0},{9,25... | collective-permute-start | bytes 884744 | tf_op jit(solution)/shard_map/ppermute | solution.py:455
  125.9 10.1 %collective-permute-start.60 = (bf16[4,2,48,384]{3,2,1,0:T(8,128)(2,1)S(1)}, bf16[4,2,48,384]{3,2,1,0:T(8,128)(2,1)S(1)}, u32[]{:S(2)}, u32[]{:S(2)}) collective-permute-start(bf16[4,2,48,384]{3,2,1,0:T(8,128)(2,1)S(1)} %get-tuple-element.102), channel_id=1, source_target_pairs={{0,1},{1,0},{2,3},{3,2},{4,5},{5,4},{6,7},{7,6},{8,9},{9,8},{10,11... | collective-permute-start | bytes 884744 | tf_op jit(solution)/shard_map/ppermute | solution.py:455
  126.6 7.7 %collective-permute-start.48 = (bf16[4,48,384]{2,1,0:T(8,128)(2,1)S(1)}, bf16[4,48,384]{2,1,0:T(8,128)(2,1)S(1)}, u32[]{:S(2)}, u32[]{:S(2)}) collective-permute-start(bf16[4,48,384]{2,1,0:T(8,128)(2,1)S(1)} %add_convert_fusion.6), channel_id=1, source_target_pairs={{0,16},{1,9},{2,18},{3,11},{4,20},{5,13},{6,22},{7,15},{8,24},{9,1... | collective-permute-start | bytes 442376 | tf_op jit(solution)/shard_map/ppermute | solution.py:455
  133.3 8.9 %collective-permute-start.62 = (bf16[4,2,48,384]{3,2,1,0:T(8,128)(2,1)S(1)}, bf16[4,2,48,384]{3,2,1,0:T(8,128)(2,1)S(1)}, u32[]{:S(2)}, u32[]{:S(2)}) collective-permute-start(bf16[4,2,48,384]{3,2,1,0:T(8,128)(2,1)S(1)} %add_convert_fusion.4), channel_id=1, source_target_pairs={{0,8},{1,17},{2,10},{3,19},{4,12},{5,21},{6,14},{7,23},{8,0},{9,25... | collective-permute-start | bytes 884744 | tf_op jit(solution)/shard_map/ppermute | solution.py:455
  134.3 8.4 %collective-permute-start.66 = (bf16[4,2,48,384]{3,2,1,0:T(8,128)(2,1)S(1)}, bf16[4,2,48,384]{3,2,1,0:T(8,128)(2,1)S(1)}, u32[]{:S(2)}, u32[]{:S(2)}) collective-permute-start(bf16[4,2,48,384]{3,2,1,0:T(8,128)(2,1)S(1)} %add_convert_fusion), channel_id=1, source_target_pairs={{0,16},{1,9},{2,18},{3,11},{4,20},{5,13},{6,22},{7,15},{8,24},{9,1... | collective-permute-start | bytes 884744 | tf_op jit(solution)/shard_map/ppermute | solution.py:455
  136.0 8.9 %collective-permute-start.49 = (bf16[48,384]{1,0:T(8,128)(2,1)S(1)}, bf16[48,384]{1,0:T(8,128)(2,1)S(1)}, u32[]{:S(2)}, u32[]{:S(2)}) collective-permute-start(bf16[48,384]{1,0:T(8,128)(2,1)S(1)} %get-tuple-element.114), channel_id=1, source_target_pairs={{0,2},{1,3},{2,0},{3,1},{4,6},{5,7},{6,4},{7,5},{8,10},{9,11},{10,... | collective-permute-start | bytes 110600 | tf_op jit(solution)/shard_map/ppermute | solution.py:455
  142.2 6.6 %collective-permute-start.50 = (bf16[48,384]{1,0:T(8,128)(2,1)S(1)}, bf16[48,384]{1,0:T(8,128)(2,1)S(1)}, u32[]{:S(2)}, u32[]{:S(2)}) collective-permute-start(bf16[48,384]{1,0:T(8,128)(2,1)S(1)} %get-tuple-element.116), channel_id=1, source_target_pairs={{0,4},{1,5},{2,6},{3,7},{4,0},{5,1},{6,2},{7,3},{8,12},{9,13},{10,... | collective-permute-start | bytes 110600 | tf_op jit(solution)/shard_map/ppermute | solution.py:455
  142.7 6.1 %collective-permute-start.51 = (bf16[48,384]{1,0:T(8,128)(2,1)S(1)}, bf16[48,384]{1,0:T(8,128)(2,1)S(1)}, u32[]{:S(2)}, u32[]{:S(2)}) collective-permute-start(bf16[48,384]{1,0:T(8,128)(2,1)S(1)} %get-tuple-element.115), channel_id=1, source_target_pairs={{0,6},{1,7},{2,4},{3,5},{4,2},{5,3},{6,0},{7,1},{8,14},{9,15},{10,... | collective-permute-start | bytes 110600 | tf_op jit(solution)/shard_map/ppermute | solution.py:455
  145.0 6.1 %collective-permute-start.67 = (bf16[2,48,384]{2,1,0:T(8,128)(2,1)S(1)}, bf16[2,48,384]{2,1,0:T(8,128)(2,1)S(1)}, u32[]{:S(2)}, u32[]{:S(2)}) collective-permute-start(bf16[2,48,384]{2,1,0:T(8,128)(2,1)S(1)} %get-tuple-element.111), channel_id=1, source_target_pairs={{0,2},{1,3},{2,0},{3,1},{4,6},{5,7},{6,4},{7,5},{8,10},{9,11},{10,... | collective-permute-start | bytes 221192 | tf_op jit(solution)/shard_map/ppermute | solution.py:455
  148.8 6.3 %collective-permute-start.69 = (bf16[2,48,384]{2,1,0:T(8,128)(2,1)S(1)}, bf16[2,48,384]{2,1,0:T(8,128)(2,1)S(1)}, u32[]{:S(2)}, u32[]{:S(2)}) collective-permute-start(bf16[2,48,384]{2,1,0:T(8,128)(2,1)S(1)} %get-tuple-element.112), channel_id=1, source_target_pairs={{0,6},{1,7},{2,4},{3,5},{4,2},{5,3},{6,0},{7,1},{8,14},{9,15},{10,... | collective-permute-start | bytes 221192 | tf_op jit(solution)/shard_map/ppermute | solution.py:455
  151.1 6.8 %collective-permute-start.39 = (bf16[16,2304]{1,0:T(8,128)(2,1)S(1)}, bf16[16,2304]{1,0:T(8,128)(2,1)S(1)}, u32[]{:S(2)}, u32[]{:S(2)}) collective-permute-start(bf16[16,2304]{1,0:T(8,128)(2,1)S(1)} %concatenate.17.refs_4_), channel_id=1, source_target_pairs={{0,8},{1,17},{2,10},{3,19},{4,12},{5,21},{6,14},{7,23},{8,0},{9,25... | collective-permute-start | bytes 221192 | tf_op jit(solution)/shard_map/ppermute | solution.py:455
  154.1 6.9 %collective-permute-start.40 = (bf16[16,2304]{1,0:T(8,128)(2,1)S(1)}, bf16[16,2304]{1,0:T(8,128)(2,1)S(1)}, u32[]{:S(2)}, u32[]{:S(2)}) collective-permute-start(bf16[16,2304]{1,0:T(8,128)(2,1)S(1)} %concatenate.17.refs_4_), channel_id=1, source_target_pairs={{0,16},{1,9},{2,18},{3,11},{4,20},{5,13},{6,22},{7,15},{8,24},{9,1... | collective-permute-start | bytes 221192 | tf_op jit(solution)/shard_map/ppermute | solution.py:455
  157.8 5.7 %collective-permute-start.41 = (bf16[16,2304]{1,0:T(8,128)(2,1)S(1)}, bf16[16,2304]{1,0:T(8,128)(2,1)S(1)}, u32[]{:S(2)}, u32[]{:S(2)}) collective-permute-start(bf16[16,2304]{1,0:T(8,128)(2,1)S(1)} %collective-permute-done.39.refs_5_), channel_id=1, source_target_pairs={{0,16},{1,9},{2,18},{3,11},{4,20},{5,13},{6,22},{7,15},{8,24},{9,1... | collective-permute-start | bytes 221192 | tf_op jit(solution)/shard_map/ppermute | solution.py:455
  158.9 7.4 %collective-permute-start.53 = (bf16[48,384]{1,0:T(8,128)(2,1)S(1)}, bf16[48,384]{1,0:T(8,128)(2,1)S(1)}, u32[]{:S(2)}, u32[]{:S(2)}) collective-permute-start(bf16[48,384]{1,0:T(8,128)(2,1)S(1)} %fusion.9.g0), channel_id=1, source_target_pairs={{0,16},{1,9},{2,18},{3,11},{4,20},{5,13},{6,22},{7,15},{8,24},{9,1... | collective-permute-start | bytes 110600 | tf_op jit(solution)/shard_map/ppermute | solution.py:455
  159.9 6.4 %collective-permute-start.54 = (bf16[48,384]{1,0:T(8,128)(2,1)S(1)}, bf16[48,384]{1,0:T(8,128)(2,1)S(1)}, u32[]{:S(2)}, u32[]{:S(2)}) collective-permute-start(bf16[48,384]{1,0:T(8,128)(2,1)S(1)} %collective-permute-done.52.g1), channel_id=1, source_target_pairs={{0,16},{1,9},{2,18},{3,11},{4,20},{5,13},{6,22},{7,15},{8,24},{9,1... | collective-permute-start | bytes 110600 | tf_op jit(solution)/shard_map/ppermute | solution.py:455
  160.9 6.7 %collective-permute-start.71 = (bf16[2,48,384]{2,1,0:T(8,128)(2,1)S(1)}, bf16[2,48,384]{2,1,0:T(8,128)(2,1)S(1)}, u32[]{:S(2)}, u32[]{:S(2)}) collective-permute-start(bf16[2,48,384]{2,1,0:T(8,128)(2,1)S(1)} %fusion.2.g0), channel_id=1, source_target_pairs={{0,16},{1,9},{2,18},{3,11},{4,20},{5,13},{6,22},{7,15},{8,24},{9,1... | collective-permute-start | bytes 221192 | tf_op jit(solution)/shard_map/ppermute | solution.py:455
  161.9 5.7 %collective-permute-start.72 = (bf16[2,48,384]{2,1,0:T(8,128)(2,1)S(1)}, bf16[2,48,384]{2,1,0:T(8,128)(2,1)S(1)}, u32[]{:S(2)}, u32[]{:S(2)}) collective-permute-start(bf16[2,48,384]{2,1,0:T(8,128)(2,1)S(1)} %collective-permute-done.70.g1), channel_id=1, source_target_pairs={{0,16},{1,9},{2,18},{3,11},{4,20},{5,13},{6,22},{7,15},{8,24},{9,1... | collective-permute-start | bytes 221192 | tf_op jit(solution)/shard_map/ppermute | solution.py:455
  (43 other events, 254.9 us)

commit v2 on v1

--- a/solution.py
+++ b/solution.py
@@ -16,6 +16,7 @@
 NN = (((1,), (0,)), ((), ()))
 NT = (((1,), (1,)), ((), ()))
 TN = (((0,), (0,)), ((), ()))
+LEVELS = (0, 2, 1, 3)
 
 
 def dot(left, right, dims=NN):
@@ -30,20 +31,25 @@
     return pl.BlockSpec(memory_space=pltpu.VMEM)
 
 
-def call(body, name, ids, ins, outs, scratch=(), flops=0, limit=48):
+def hbm():
+    return pl.BlockSpec(memory_space=pltpu.HBM)
+
+
+def call(body, name, ids, ins, outs, scratch=(), flops=0, limit=48, far=()):
+    fixed = [] if ids is None else [ids]
     moved = sum(a.size * a.dtype.itemsize for a in ins) + sum(
         jnp.dtype(t).itemsize * functools.reduce(lambda a, b: a * b, s, 1) for s, t in outs
     )
     return pl.pallas_call(
         body,
         out_shape=[jax.ShapeDtypeStruct(s, t) for s, t in outs],
-        in_specs=[smem()] + [vmem()] * len(ins),
+        in_specs=[smem()] * len(fixed) + [hbm() if i in far else vmem() for i in range(len(ins))],
         out_specs=[vmem()] * len(outs),
         scratch_shapes=list(scratch),
         compiler_params=pltpu.CompilerParams(vmem_limit_bytes=limit * 1024 * 1024),
         cost_estimate=pl.CostEstimate(flops=flops, bytes_accessed=moved, transcendentals=0),
         name=name,
-    )(ids, *ins)
+    )(*fixed, *ins)
 
 
 def offsets(ids):
@@ -58,23 +64,42 @@
     return lax.bitwise_xor(a, b)
 
 
-def pick_body(ids, proj, outw, up, down, cond, q_po, q_ud, c_low):
-    d = ids[0]
-    width = outw.shape[1]
-    rows = outw.shape[0]
+def pick_body(proj, outw, up, down, cond, q_all, c_in, sems):
+    d = lax.axis_index("dp")
+    rows, width = outw.shape
+    at = pl.ds(pl.multiple_of(d * width, 128), width)
+    at_proj = pl.ds(pl.multiple_of(lax.min(d, 2) * width, 128), width)
+    q_po = q_all.at[pl.ds(0, rows), :]
+    copies = [
+        pltpu.make_async_copy(cond, c_in, sems.at[0]),
+        pltpu.make_async_copy(up.at[:, at], q_all.at[pl.ds(rows, rows), :], sems.at[1]),
+        pltpu.make_async_copy(
+            down.at[pl.ds(pl.multiple_of(d * rows, 16), rows), :],
+            q_all.at[pl.ds(2 * rows, rows), :],
+            sems.at[2],
+        ),
+    ]
+    for copy in copies:
+        copy.start()
 
     @pl.when(d < 3)
     def _():
-        q_po[...] = proj[:, pl.ds(pl.multiple_of(lax.min(d, 2) * width, 128), width)]
+        copy = pltpu.make_async_copy(proj.at[:, at_proj], q_po, sems.at[3])
+        copy.start()
+        copy.wait()
 
     @pl.when(d == 3)
     def _():
-        q_po[...] = outw[...]
-
-    q_ud[0] = up[:, pl.ds(pl.multiple_of(d * width, 128), width)]
-    q_ud[1] = down[pl.ds(pl.multiple_of(d * rows, 16), rows), :]
-    c = cond[...].astype(F32)
-    c_low[...] = (c / (1.0 + jnp.exp(-c))).astype(BF16)
+        copy = pltpu.make_async_copy(outw, q_po, sems.at[3])
+        copy.start()
+        copy.wait()
+
+    for copy in copies:
+        copy.wait()
+    c = c_in[...].astype(F32)
+    c = c / (1.0 + jnp.exp(-c))
+    blank = jnp.zeros((16 - c.shape[0], width), F32)
+    q_all[3 * rows :, :] = jnp.concatenate([c, blank], axis=0).astype(BF16)
 
 
 def one_hot(shape, shift):
@@ -83,33 +108,37 @@
     return jnp.where(c == r + shift, 1.0, 0.0).astype(BF16)
 
 
-def mod_body(ids, c0, c1, c2, c3, wmod, bmod, bqv, bout, bup, bdown, k0, k1, k2, k3, send):
+def prepare_body(wmod_in, f0, f1, f2, f3, f4, wmod, placed):
+    f = lax.axis_index("fsdp")
+    wmod[...] = wmod_in[...]
+    rows = []
+    for ref in (f0, f1, f2, f3, f4):
+        size = ref.shape[0]
+        rows.append(dot(ref[...].reshape(1, size), one_hot((size, 8 * size), f * size)))
+    bias, b_qv, b_out, b_up, b_down = rows
+    feat = b_out.shape[1]
+    placed[0:1, :] = bias
+    placed[1:2, :] = jnp.concatenate([b_up, b_qv], axis=1)
+    placed[2:3, :] = jnp.concatenate([b_out, b_down, jnp.zeros((1, 4 * feat), F32)], axis=1)
+
+
+def mod_body(ids, c_own, c_other, wmod, placed, keep_lo, keep_hi, send):
     f = ids[1]
-    wide = wmod.shape[1]
-    rows = wmod.shape[0]
-    feat = c0.shape[1]
+    rows, wide = wmod.shape
+    feat = c_own.shape[1]
+    slots = c_own.shape[0] // 4
     r = lax.broadcasted_iota(jnp.int32, (feat, rows), 0)
     c = lax.broadcasted_iota(jnp.int32, (feat, rows), 1)
     select = jnp.where(r == c + f * rows, 1.0, 0.0).astype(BF16)
-
-    def place(ref, total):
-        n = ref.shape[1]
-        return dot(ref[...], one_hot((n, total), f * n))
-
-    bias = place(bmod, wide)
-    row_two = jnp.concatenate([place(bup, 4 * feat), place(bqv, 2 * feat)], axis=1)
-    row_three = jnp.concatenate(
-        [place(bout, feat), place(bdown, feat), jnp.zeros((1, 4 * feat), F32)], axis=1
-    )
-    for zm, (ref, keep) in enumerate(zip((c0, c1, c2, c3), (k0, k1, k2, k3))):
-        own = dot(ref[...], select).astype(BF16)
-        part = dot(own, wmod[...]) + bias
-        keep[0:2, :] = part[0:2]
-        keep[2:3, :] = row_two
-        keep[3:4, :] = row_three
-        send[zm, 0:2, :] = part[2:4]
-        send[zm, 2:3, :] = row_two
-        send[zm, 3:4, :] = row_three
+    stacked = jnp.concatenate([c_own[...].astype(F32), c_other[...].astype(F32)], axis=0)
+    own = dot(stacked.astype(BF16), select).astype(BF16)
+    part = dot(own, wmod[...]) + placed[0:1, :]
+    for n in range(4):
+        keep = (keep_lo, keep_lo, keep_hi, keep_hi)[n]
+        keep[n % 2, 0:slots, :] = part[slots * n : slots * (n + 1)]
+        send[n, 0:slots, :] = part[slots * (n + 4) : slots * (n + 5)]
+        keep[n % 2, 2:4, :] = placed[1:3, :]
+        send[n, 2:4, :] = placed[1:3, :]
 
 
 def norm_parts(x):
@@ -125,18 +154,24 @@
 
 
 def attend_body(
-    ids, w0, w1, w2, w3, o0, o1, o2, o3, p0, p1, p2, p3, lat, wpo, mod, n1, proj, att
+    ids, *refs,
 ):
     d, f, mine, theirs = offsets(ids)
-    rows = w0.shape[1]
-    feat = w0.shape[2]
-    for refs, flips, base in (((w0, w1, w2, w3), mine, f), ((o0, o1, o2, o3), theirs, flip(f, 1))):
-        for ref, how in zip(refs, flips):
+    pieces, (m_proj, m_out, o_proj, o_out, p0, p1, lat, wpo, mod, n1, proj, att) = refs[:16], refs[16:]
+    rows, feat = m_out.shape
+    whole = ((m_proj, m_out), (o_proj, o_out))
+    split = (pieces[:8], mine, f), (pieces[8:], theirs, flip(f, 1))
+    for (p_ref, o_ref), (found, flips, base) in zip(whole, split):
+        at = pl.multiple_of(base * rows, 16)
+        for block in range(3):
+            wpo[block, pl.ds(at, rows), :] = p_ref[:, block * feat : (block + 1) * feat]
+        wpo[3, pl.ds(at, rows), :] = o_ref[...]
+        for n, how in enumerate(flips):
             block = flip(d, how)
-            for zm in range(4):
+            for zm, get in ((2, found[n]), (1, found[4 + n].at[0]), (3, found[4 + n].at[1])):
                 at = pl.multiple_of(flip(base, 2 * zm) * rows, 16)
-                wpo[block, pl.ds(at, rows), :] = ref[zm]
-    mod[...] = (p0[...] + p1[...]) + (p2[...] + p3[...])
+                wpo[block, pl.ds(at, rows), :] = get[0:rows, :]
+    mod[...] = p0[0] + p1[...]
     length = lat.shape[1]
     low_half = lane_masks(length)
     qv = mod[2:3, 4 * feat :]
@@ -171,35 +206,55 @@
     lax.fori_loop(0, lat.shape[0], one, 0)
 
 
-def spread(tmp, at_row, dm, keeps, sends, rows, f, slot=None):
+def spread(tmp, at_row, dm, pieces, rows, f, slot=None):
+    keep_odd, keep_even, send_odd, send_even = pieces
+    keep = (keep_even, keep_odd)[dm % 2]
     swapped = (0, 2, 1, 3)[dm]
-    for zm in range(4):
-        for ref, owner in ((keeps[dm], flip(f, 2 * zm)), (sends[swapped], flip(f, 2 * zm + 1))):
+    send = (send_even, send_odd)[swapped % 2]
+    for place, zm in enumerate(LEVELS):
+        for ref, at, owner in (
+            (keep, dm // 2, flip(f, 2 * zm)),
+            (send, swapped // 2, flip(f, 2 * zm + 1)),
+        ):
             piece = tmp[pl.ds(pl.multiple_of(at_row(owner), 16), rows), :]
             if slot is None:
-                ref[zm] = piece
+                ref[at, place] = piece
             else:
-                ref[zm, slot] = piece
+                ref[at, place, slot] = piece
 
 
 def mlp_body(
-    ids, w0, w1, w2, w3, o0, o1, o2, o3, wout, mod, lat, cot, att,
-    res, gmid, gbr, gatt, gsum, gmod, k0, k1, k2, k3, s0, s1, s2, s3,
+    ids, *refs,
+):
+    mlp_steps(ids, refs[:16], *refs[16:])
+
+
+def mlp_steps(
+    ids, pieces, m_up, m_down, o_up, o_down, wout, mod, lat, cot, att,
+    res, gmid, gbr, gatt, gsum, gmod, k_odd, k_even, s_odd, s_even,
     wu, wd, n2s, acts, dgs, gmlps, gpres, n2t, tmp, tmpd,
 ):
     d, f, mine, theirs = offsets(ids)
     count = ids[2]
-    rows = w0.shape[2]
-    feat = w0.shape[3]
+    rows, feat = m_up.shape[0], m_down.shape[1]
     hidden = wd.shape[0]
     blocks = hidden // feat
-    for refs, flips, base in (((w0, w1, w2, w3), mine, f), ((o0, o1, o2, o3), theirs, flip(f, 1))):
-        for ref, how in zip(refs, flips):
+    whole = ((m_up, m_down), (o_up, o_down))
+    split = (pieces[:8], mine, f), (pieces[8:], theirs, flip(f, 1))
+    for (u_ref, d_ref), (found, flips, base) in zip(whole, split):
+        at = pl.multiple_of(base * rows, 16)
+        for block in range(blocks):
+            wu[block, pl.ds(at, rows), :] = u_ref[:, block * feat : (block + 1) * feat]
+        wd[pl.ds(pl.multiple_of(base * 4 * rows, 16), 4 * rows), :] = d_ref[...]
+        for n, how in enumerate(flips):
             block = flip(d, how)
-            for zm in range(4):
+            for zm, get in ((2, found[n]), (1, found[4 + n].at[0]), (3, found[4 + n].at[1])):
                 owner = flip(base, 2 * zm)
-                wu[block, pl.ds(pl.multiple_of(owner * rows, 16), rows), :] = ref[zm, 0]
-                wd[pl.ds(pl.multiple_of(owner * 4 * rows + block * rows, 16), rows), :] = ref[zm, 1]
+                wu[block, pl.ds(pl.multiple_of(owner * rows, 16), rows), :] = get[
+                    rows : 2 * rows, :
+                ]
+                at = pl.multiple_of((owner * 4 + block) * rows, 16)
+                wd[pl.ds(at, rows), :] = get[2 * rows : 3 * rows, :]
     length = lat.shape[1]
     bup = mod[2:3, : 4 * feat]
     bout = mod[3:4, :feat]
@@ -262,27 +317,27 @@
         return carry
 
     lax.fori_loop(0, lat.shape[0], one, 0)
-    keeps, sends = (k0, k1, k2, k3), (s0, s1, s2, s3)
+    pieces = (k_odd, k_even, s_odd, s_even)
     for j in range(blocks):
         cols = slice(j * feat, (j + 1) * feat)
         tmpd[cols, :] = dot(acts[:, cols], gmlps[...], TN).astype(BF16)
     n2t[...] = n2s[...].T
     for dm in (1, 3, 0, 2):
         block = flip(d, mine[dm])
-        spread(tmpd, lambda o: (o * 4 + block) * rows, dm, keeps, sends, rows, f, 1)
+        spread(tmpd, lambda o: (o * 4 + block) * rows, dm, pieces, rows, f, 1)
         tmp[...] = dot(
             n2t[...], gpres[:, pl.ds(pl.multiple_of(block * feat, 128), feat)]
         ).astype(BF16)
-        spread(tmp, lambda o: o * rows, dm, keeps, sends, rows, f, 0)
+        spread(tmp, lambda o: o * rows, dm, pieces, rows, f, 0)
 
 
 def attend_back_body(
-    ids, proj, gatt, att, gbr, n1, gsum, gproj, bias, k0, k1, k2, k3, s0, s1, s2, s3,
+    ids, proj, gatt, att, gbr, n1, gsum, gproj, bias, k_odd, k_even, s_odd, s_even,
     gall, xts, tmp, *, length,
 ):
     d, f, mine, _ = offsets(ids)
     feat = att.shape[1]
-    rows = k0.shape[1]
+    rows = k_odd.shape[2]
     low_half = lane_masks(length)
 
     def one(i, carry):
@@ -322,14 +377,14 @@
     gall[:, 3 * feat :] = gbr[...]
     xts[0] = n1[...].T
     xts[1] = att[...].T
-    keeps, sends = (k0, k1, k2, k3), (s0, s1, s2, s3)
+    pieces = (k_odd, k_even, s_odd, s_even)
     for dm in (1, 3, 0, 2):
         block = flip(d, mine[dm])
         tmp[...] = dot(
             xts[jnp.where(block == 3, 1, 0)],
             gall[:, pl.ds(pl.multiple_of(block * feat, 128), feat)],
         ).astype(BF16)
-        spread(tmp, lambda o: o * rows, dm, keeps, sends, rows, f)
+        spread(tmp, lambda o: o * rows, dm, pieces, rows, f)
     bias[:, 0:feat] = jnp.sum(gall[:, 0:feat].astype(F32), axis=0, keepdims=True)
     bias[:, feat : 2 * feat] = jnp.sum(
         gall[:, 2 * feat : 3 * feat].astype(F32), axis=0, keepdims=True
@@ -337,7 +392,7 @@
     bias[:, 2 * feat :] = gsum[...]
 
 
-def input_back_body(ids, gproj, wpo, lat, gmid, mod, gmod, lgrad, gm):
+def input_back_body(ids, gproj, wpo, lat, gmid, mod, gmod, bias, lgrad, gm, full):
     length = lat.shape[1]
     feat = lat.shape[2]
 
@@ -360,72 +415,97 @@
                 - xhat * jnp.mean(gx * xhat, axis=-1, keepdims=True)
             )
         ).astype(BF16)
-        gm[pl.ds(i, 1), :] = jnp.concatenate(
+        full[pl.ds(i, 1), : 6 * feat] = jnp.concatenate(
             [g_shift, g_scale, gmod[pl.ds(i, 1), :]], axis=1
         )
         return carry
 
     lax.fori_loop(0, lat.shape[0], one, 0)
-
-
-def cond_back_body(ids, g0, g1, g2, g3, wmod, x0, x1, x2, x3):
+    full[0:1, 6 * feat :] = bias[:, : 4 * feat]
+    full[1:2, 6 * feat :] = bias[:, 4 * feat :]
+    gm[...] = full[...].astype(BF16)
+
+
+def cond_back_body(ids, g0, g2, g1, g3, wmod, lo, hi):
     f = ids[1]
-    rows = wmod.shape[0]
-    place = one_hot((rows, x0.shape[1]), f * rows).astype(F32)
-    for ref, out in zip((g0, g1, g2, g3), (x0, x1, x2, x3)):
-        part = dot(ref[...], wmod[...], NT)
-        out[...] = lax.dot_general(
-            part, place, NN, preferred_element_type=F32, precision=lax.Precision.HIGHEST
-        )
-
-
-def mod_weight_body(ids, *refs):
-    conds, grads, (wgrad, bgrad) = refs[:4], refs[4:8], refs[8:]
+    rows, wide = wmod.shape
+    place = one_hot((rows, lo.shape[2]), f * rows)
+    lo[...] = jnp.zeros_like(lo)
+    hi[...] = jnp.zeros_like(hi)
+    for ref, out, at in ((g0, lo, 0), (g2, lo, 1), (g1, hi, 0), (g3, hi, 1)):
+        part = dot(ref[:, :wide], wmod[...], NT).astype(BF16)
+        out[at, 0 : part.shape[0], :] = dot(part, place).astype(BF16)
+
+
+def mod_weight_body(ids, e0, e1, e2, e3, wgrad, bgrad):
     f = ids[1]
-    rows = wgrad.shape[0]
-    feat = conds[0].shape[1]
+    rows, wide = wgrad.shape
+    feat = wide // 6
+    grad_wide = e0.shape[1] - feat
     select = one_hot((rows, feat), f * rows)
     total = None
     sums = None
-    for c, g in zip(conds, grads):
-        grad = g[...]
-        own = dot(select, c[...], NT).astype(BF16)
-        term = dot(own, grad)
+    for ref in (e0, e1, e2, e3):
+        own = dot(select, ref[:, grad_wide:], NT).astype(BF16)
+        term = dot(own, ref[:, :wide])
         total = term if total is None else total + term
-        s = jnp.sum(grad.astype(F32), axis=0, keepdims=True)
-        sums = s if sums is None else sums + s
+        low = ref[:, :grad_wide].astype(F32)
+        sums = low if sums is None else sums + low
     wgrad[...] = total
-    bgrad[...] = sums
-
-
-def final_po_body(ids, g0, g1, g2, g3, gp, go):
+    low = sums[:, wide:]
+    odd = lax.broadcasted_iota(jnp.int32, low.shape, 0) % 2 == 1
+    bgrad[:, :wide] = jnp.sum(sums[:, :wide], axis=0, keepdims=True)
+    bgrad[:, wide : wide + 4 * feat] = jnp.sum(jnp.where(odd, 0.0, low), axis=0, keepdims=True)
+    bgrad[:, wide + 4 * feat :] = jnp.sum(jnp.where(odd, low, 0.0), axis=0, keepdims=True)
+
+
+def merge_body(ids, keep_ud, got_ud, keep_po, got_po, out):
+    rows = keep_po.shape[2]
+    for at in range(out.shape[0]):
+        for place in range(out.shape[1]):
+            out[at, place, 0:rows] = add_low(keep_po[at, place], got_po[at, place])
+            for slot in range(2):
+                out[at, place, (1 + slot) * rows : (2 + slot) * rows] = add_low(
+                    keep_ud[at, place, slot], got_ud[at, place, slot]
+                )
+
+
+def join_far_body(ids, base, part, back, out):
+    size = base.shape[1]
+    for at in range(2):
+        out[at, 0:size] = add_low(base[2 + at], part[2 + at])
+        out[at, size:] = back[at]
+
+
+def join_near_body(ids, base, part, back, got, out):
+    size = base.shape[1]
+    for at in range(2):
+        out[at, 0:size] = add_low(base[at], part[at], got[at, 0:size])
+        out[at, size:] = add_low(back[at], got[at, size:])
+
+
+def final_body(ids, g0, g1, g2, g3, gp, go, gu, gd):
     d, _, mine, _ = offsets(ids)
-    feat = go.shape[1]
+    rows, feat = go.shape
     for ref, how in zip((g0, g1, g2, g3), mine):
         block = flip(d, how)
 
         @pl.when(block < 3)
         def _():
             at = pl.multiple_of(lax.min(block, 2) * feat, 128)
-            gp[:, pl.ds(at, feat)] = ref[...].astype(F32)
+            gp[:, pl.ds(at, feat)] = ref[0:rows, :].astype(F32)
 
         @pl.when(block == 3)
         def _():
-            go[...] = ref[...].astype(F32)
-
-
-def final_ud_body(ids, g0, g1, g2, g3, gu, gd):
-    d, _, mine, _ = offsets(ids)
-    rows, feat = g0.shape[1:]
-    for ref, how in zip((g0, g1, g2, g3), mine):
-        block = flip(d, how)
-        gu[:, pl.ds(pl.multiple_of(block * feat, 128), feat)] = ref[0].astype(F32)
-        gd[pl.ds(pl.multiple_of(block * rows, 16), rows), :] = ref[1].astype(F32)
+            go[...] = ref[0:rows, :].astype(F32)
+
+        gu[:, pl.ds(pl.multiple_of(block * feat, 128), feat)] = ref[rows : 2 * rows, :].astype(F32)
+        gd[pl.ds(pl.multiple_of(block * rows, 16), rows), :] = ref[2 * rows : 3 * rows, :].astype(F32)
 
 
 def routes():
     core, first, second = [], [], []
-    levels = {1: [], 2: [], 3: []}
+    levels = {1: [], 2: []}
     for d in range(4):
         for f in range(8):
             i = d * 8 + f
@@ -463,49 +543,68 @@
     f = lax.axis_index("fsdp")
     ids = jnp.stack([d, f, counts[0]]).astype(jnp.int32)
 
-    q_po, q_ud, c_low = call(
-        pick_body, "pick", ids,
+    def after(x, *earlier):
+        return lax.optimization_barrier((x,) + earlier)[0]
+
+    (q_all,) = call(
+        pick_body, "pick", None,
         [projection_weight, output_weight, up_weight, down_weight, cond],
-        [((rows, feat), BF16), ((2, rows, feat), BF16), ((slots, feat), BF16)],
-    )
-
-    def gather(q):
-        own = jnp.stack([q] + [move(q, levels[m]) for m in (1, 2, 3)])
+        [((3 * rows + 16, feat), BF16)],
+        [pltpu.VMEM((slots, feat), BF16), pltpu.SemaphoreType.DMA((4,))],
+        far=(0, 1, 2, 3, 4), limit=60,
+    )
+
+    def over_dp(own):
         a = move(own, first)
         b = move(own, second)
-        ab = move(a, second)
-        mine = [own, a, b, ab]
-        return mine + [move(x, core) for x in mine]
-
-    c_pair = jnp.concatenate([c_low, move(c_low, core)], axis=0)
-    c_all = [c_pair] + [move(c_pair, levels[m]) for m in (1, 2, 3)]
-    w_po = gather(q_po)
-    *kept, sent = call(
-        mod_body, "modulation", ids,
-        c_all + [
-            modulation_weight, modulation_bias[None], query_value_bias[None],
-            output_bias[None], up_bias[None], down_bias[None],
-        ],
-        [((4, wide), F32)] * 4 + [((4, 4, wide), F32)],
-    )
-    arrived = move(sent, core)
-    paid = [kept[m] + arrived[m] for m in range(4)]
-    paid = [paid[0]] + [move(paid[m], levels[m]) for m in (1, 2, 3)]
-    w_ud = gather(q_ud)
+        return [own, a, b, move(a, second)]
+
+    whole = [projection_weight, output_weight, up_weight, down_weight]
+    w_whole = whole + [move(x, core) for x in whole]
+    biases = [modulation_bias, query_value_bias, output_bias, up_bias, down_bias]
+    wmod, placed = call(
+        prepare_body, "prepare", None, [modulation_weight] + biases,
+        [((rows, wide), BF16), ((3, wide), F32)],
+    )
+    q_far = move(q_all, levels[2])
+    ready = (placed, *w_whole[4:])
+    q_near = move(after(q_all, q_far, *ready), levels[1])
+    q_both = move(after(q_far, *ready), levels[1])
+    a_far, b_far = move(q_far, first), move(q_far, second)
+    c_own = [x[3 * rows : 3 * rows + slots] for x in (q_all, q_far, q_near, q_both)]
+    c_own = after(jnp.concatenate(c_own), a_far, b_far)
+    c_other = move(c_own, core)
+    near = jnp.stack([q_near[: 3 * rows], q_both[: 3 * rows]])
+    keep_lo, keep_hi, sent = call(
+        mod_body, "modulation", ids, [c_own, c_other, wmod, placed],
+        [((2, 4, wide), F32)] * 2 + [((4, 4, wide), F32)],
+    )
+    ab_far = move(a_far, second)
+    got = after(move(sent, core), ab_far)
+    paid_hi = keep_hi + got[2:]
+    paid_lo = keep_lo + got[:2]
+    paid_lo = paid_lo + move(paid_hi, levels[1])
+    paid_far = move(paid_lo[1], levels[2])
+    a_near, b_near = move(near, first), move(near, second)
+    ab_near = move(after(a_near, paid_far), second)
+    w_all = [q_far, a_far, b_far, ab_far, near, a_near, b_near, ab_near]
+    w_all = w_all + [move(x, core) for x in w_all]
 
     wpo, mod, n1, proj, att = call(
-        attend_body, "attention", ids, w_po + paid + [latents],
+        attend_body, "attention", ids,
+        w_all + [w_whole[k] for k in (0, 1, 4, 5)] + [paid_lo, paid_far, latents],
         [((4, feat, feat), BF16), ((4, wide), F32), ((tokens, feat), BF16),
          ((tokens, 3 * feat), BF16), ((tokens, feat), BF16)],
         flops=2 * tokens * feat * (3 * feat + 4 * length),
     )
     wout = wpo[3:4]
-    ud_shape = ((4, 2, rows, feat), BF16)
-    po_shape = ((4, rows, feat), BF16)
-    res, gmid, gbr, gatt, gsum, gmod, *ud = call(
-        mlp_body, "mlp", ids, w_ud + [wout, mod, latents, cotangent, att],
+    ud_shape = ((2, 4, 2, rows, feat), BF16)
+    po_shape = ((2, 4, rows, feat), BF16)
+    res, gmid, gbr, gatt, gsum, gmod, ud_odd, ud_even, ud_odd_out, ud_even_out = call(
+        mlp_body, "mlp", ids,
+        w_all + [w_whole[k] for k in (2, 3, 6, 7)] + [wout, mod, latents, cotangent, att],
         [((slots, length, feat), BF16), ((slots, length, feat), F32), ((tokens, feat), BF16),
-         ((tokens, feat), BF16), ((1, 6 * feat), F32), ((slots, 4 * feat), F32)] + [ud_shape] * 8,
+         ((tokens, feat), BF16), ((1, 6 * feat), F32), ((slots, 4 * feat), F32)] + [ud_shape] * 4,
         [
             pltpu.VMEM((4, feat, feat), BF16), pltpu.VMEM((hidden, feat), BF16),
             pltpu.VMEM((tokens, feat), BF16), pltpu.VMEM((tokens, hidden), BF16),
@@ -515,85 +614,92 @@
         ],
         flops=2 * tokens * feat * (6 * hidden + 2 * feat),
     )
-
-    def scatter(pieces):
-        keeps, sends = pieces[:4], pieces[4:]
-        from_core = {m: move(sends[m], core) for m in (1, 3, 0, 2)}
-        summed = {m: add_low(keeps[m], from_core[m]) for m in (1, 3, 0, 2)}
-        to_zero = move(summed[1], first)
-        to_two = move(summed[3], first)
-        summed_two = add_low(summed[2], to_two)
-        last = move(summed_two, second)
-        base = add_low(summed[0], to_zero)
-        total = [add_low(base[m], last[m]) for m in range(4)]
-        own = add_low(total[0], *[move(total[m], levels[m]) for m in (1, 2, 3)])
-        a = move(own, first)
-        b = move(own, second)
-        return [own, a, b, move(a, second)]
-
-    g_ud = scatter(ud)
-    gproj, bias, *po = call(
+    ud_odd_in = move(ud_odd_out, core)
+    ud_even_in = move(ud_even_out, core)
+    gproj, bias, po_odd, po_even, po_odd_out, po_even_out = call(
         functools.partial(attend_back_body, length=length), "attention_back", ids,
         [proj, gatt, att, gbr, n1, gsum],
-        [((tokens, 3 * feat), BF16), ((1, 8 * feat), F32)] + [po_shape] * 8,
+        [((tokens, 3 * feat), BF16), ((1, 8 * feat), F32)] + [po_shape] * 4,
         [pltpu.VMEM((tokens, 4 * feat), BF16), pltpu.VMEM((2, feat, tokens), BF16),
          pltpu.VMEM((feat, feat), BF16)],
         flops=2 * tokens * feat * (4 * feat + 10 * length),
     )
-    g_po = scatter(po)
+    po_odd_in = move(po_odd_out, core)
+    po_even_in = move(po_even_out, core)
+    all_shape = ((2, 4, 3 * rows, feat), BF16)
+    (odd,) = call(merge_body, "merge_odd", ids, [ud_odd, ud_odd_in, po_odd, po_odd_in], [all_shape])
+    got = move(odd, first)
+    (even,) = call(
+        merge_body, "merge_even", ids, [ud_even, ud_even_in, po_even, po_even_in], [all_shape]
+    )
     lgrad, gm = call(
-        input_back_body, "input_back", ids, [gproj, wpo, latents, gmid, mod, gmod],
-        [((slots, length, feat), BF16), ((slots, wide), F32)],
+        input_back_body, "input_back", ids, [after(gproj, even), wpo, latents, gmid, mod, gmod, bias],
+        [((slots, length, feat), BF16), ((slots, 10 * feat), BF16)],
+        [pltpu.VMEM((slots, 10 * feat), F32)],
         flops=2 * tokens * feat * 3 * feat,
     )
-    gm = gm.astype(BF16)
 
     gm_pair = jnp.concatenate([gm, move(gm, core)], axis=0)
-    gm_all = [gm_pair] + [move(gm_pair, levels[m]) for m in (1, 2, 3)]
-    back = call(
+    gm_far = move(gm_pair, levels[2])
+    turned = add_low(even[1], after(got[1], gm_far))
+    gm_all = [
+        gm_pair, gm_far,
+        move(after(gm_pair, turned), levels[1]), move(after(gm_far, turned), levels[1]),
+    ]
+    part = move(turned, second)
+    base = add_low(even[0], got[0])
+    every = jnp.concatenate(
+        [
+            jnp.concatenate(gm_all, axis=0),
+            jnp.concatenate(
+                [x[slots * n : slots * (n + 1)] for n in range(4) for x in (c_own, c_other)]
+            ),
+        ],
+        axis=1,
+    )
+    back_lo, back_hi = call(
         cond_back_body, "cond_back", ids, gm_all + [modulation_weight],
-        [((2 * slots, feat), F32)] * 4,
-    )
-    silu_pair = back[0]
-    for m in (1, 2, 3):
-        silu_pair = silu_pair + move(back[m], levels[m])
-    grad_silu = silu_pair[:slots] + move(silu_pair[slots:], core)
+        [((2, 16, feat), BF16)] * 2,
+    )
+
+    pair_shape = ((2, 3 * rows + 16, feat), BF16)
+    (turned,) = call(join_far_body, "join_far", ids, [base, part, back_hi], [pair_shape])
+    got = move(turned, levels[1])
+    every = after(every, turned)
+    e_first, e_second = move(every, first), move(every, second)
+    (base,) = call(join_near_body, "join_near", ids, [base, part, back_lo, got], [pair_shape])
+    e_both = move(after(e_first, base), second)
+    g_mod_weight, sums = call(
+        mod_weight_body, "mod_weight", ids, [every, e_first, e_second, e_both],
+        [((rows, wide), F32), ((1, wide + 8 * feat), F32)],
+    )
+    total = add_low(base[0], after(move(base[1], levels[2]), g_mod_weight))
+    a_total, b_total = move(total, first), move(total, second)
+    sums = after(sums[0], total)
+
+    def share(at, size):
+        size = size // 8
+        return lax.dynamic_slice_in_dim(sums, at + f * size, size)
+
+    g_biases = [
+        share(0, wide), share(wide, 2 * feat), share(wide + 2 * feat, feat),
+        share(wide + 3 * feat, hidden), share(wide + 7 * feat, feat),
+    ]
+    shares = [total, a_total, b_total, move(after(a_total, *g_biases), second)]
+    silu_pair = total[3 * rows : 3 * rows + 2 * slots].astype(F32)
+    silu_other = after(total, a_total, b_total)[3 * rows + slots : 3 * rows + 2 * slots]
+    grad_silu = silu_pair[:slots] + move(silu_other, core).astype(F32)
     cond_full = cond.astype(F32)
     sig = 1.0 / (1.0 + jnp.exp(-cond_full))
     cond_grad = (grad_silu * (sig * (1.0 + cond_full * (1.0 - sig)))).astype(BF16)
-
-    def over_dp(own):
-        a = move(own, first)
-        b = move(own, second)
-        return [own, a, b, move(a, second)]
-
-    c_every = over_dp(jnp.concatenate(c_all, axis=0))
-    gm_every = over_dp(jnp.concatenate(gm_all, axis=0))
-    g_mod_weight, g_mod_bias = call(
-        mod_weight_body, "mod_weight", ids, c_every + gm_every,
-        [((rows, wide), F32), ((1, wide), F32)],
-    )
-
-    bias = bias + move(bias, core)
-    bias = bias + move(bias, levels[1])
-    bias = bias + move(bias, levels[2])
-    bias = bias + move(bias, first)
-    bias = (bias + move(bias, second))[0]
-
-    def share(vector):
-        size = vector.shape[0] // 8
-        return lax.dynamic_slice_in_dim(vector, f * size, size)
-
-    g_proj, g_out = call(
-        final_po_body, "final_po", ids, g_po, [((rows, 3 * feat), F32), ((rows, feat), F32)]
-    )
-    g_up, g_down = call(
-        final_ud_body, "final_ud", ids, g_ud, [((rows, hidden), F32), ((4 * rows, feat), F32)]
+    g_proj, g_out, g_up, g_down = call(
+        final_body, "final", ids, shares,
+        [((rows, 3 * feat), F32), ((rows, feat), F32), ((rows, hidden), F32),
+         ((4 * rows, feat), F32)],
     )
     return (
-        res, lgrad, cond_grad, g_mod_weight, share(g_mod_bias[0]), g_proj, share(bias[: 2 * feat]),
-        g_out, share(bias[2 * feat : 3 * feat]), g_up, share(bias[3 * feat : 7 * feat]),
-        g_down, share(bias[7 * feat :]),
+        res, lgrad, cond_grad, g_mod_weight, g_biases[0], g_proj, g_biases[1],
+        g_out, g_biases[2], g_up, g_biases[3], g_down, g_biases[4],
     )
 
 

time: 169 us -> 123 us (0.73)
  starting transfers between devices: 68.9 us -> 39.9 us
  waiting for transfers between devices: 48.9 us -> 34.6 us
  local copies, waits for them, and re-layouts: 11.6 us -> 8.15 us
  Pallas kernels: 35.2 us -> 37.4 us
    ppermute x73 -> x44, starting transfers between devices: 68.9 us -> 39.9 us  [move(): return lax.ppermute(x, BOTH, route)]
    ppermute x73 -> x44, waiting for transfers between devices: 48.9 us -> 34.6 us  [move(): return lax.ppermute(x, BOTH, route)]
    unnamed x36, local copies, waits for them, and re-layouts: 7.57 us -> 4.65 us
    pallas_call x10 -> x14, Pallas kernels: 35.2 us -> 37.4 us  [call(): pl.pallas_call(body, out_shape=[jax.ShapeDtypeStruct(s, t) for s, t in ou...]
  transfers between devices with their start and end apart: 73 -> 44, of which waited for: 22 -> 24; matrix products, arithmetic and copies ran while one was open for 4% -> 4% of each run, Pallas kernels for 7% -> 15%
where the time goes in v2:
time: 123 us
  starting transfers between devices  39.9 us (32%)
  Pallas kernels  37.4 us (30%)
  waiting for transfers between devices  34.6 us (28%)
  local copies, waits for them, and re-layouts  8.15 us (7%)
  between operations  1.64 us (1%)
    ppermute x44, starting transfers between devices, move(): return lax.ppermute(x, BOTH, route)  39.9 us
    pallas_call x14, Pallas kernels, call(): pl.pallas_call(body, out_shape=[jax.ShapeDtypeStruct(s, t) for s, t in ou...  37.4 us
    ppermute x44, waiting for transfers between devices, move(): return lax.ppermute(x, BOTH, route)  34.6 us
    unnamed x36, local copies, waits for them, and re-layouts  4.65 us
    dynamic_slice x4, local copies, waits for them, and re-layouts, share(): return lax.dynamic_slice_in_dim(sums, at + f * size, size)  2.47 us
  transfers between devices with their start and end apart: 44, of which 24 were waited for; matrix products, arithmetic and copies ran while one was open for 4% of the time, Pallas kernels for 15%

profile of v2, /device:TPU:0, one launch (start us, length us, event | category | flops | bytes accessed | tf_op | source)
XLA Modules:
  0.0 122.8 jit_solution(1142195277065939985)
XLA Ops:
  1.3 1.5 %pick.1 = bf16[160,384]{1,0:T(8,128)(2,1)} custom-call(bf16[48,1152]{1,0:T(8,128)(2,1)} %refs_16_.2, bf16[48,384]{1,0:T(8,128)(2,1)} %refs_17_.2, bf16[48,1536]{1,0:T(8,128)(2,1)} %refs_16_.3, bf16[192,384]{1,0:T(8,128)(2,1)} %refs_17_.3, bf16[2,384]{1,0:T(2,128)(2,1)} %cond.1), custom_call_target="tpu_custom_call" | custom-call | bytes 566784 | tf_op jit(solution)/shard_map/pick/pallas_call | solution.py:43
  2.8 4.1 %collective-permute-start = (bf16[160,384]{1,0:T(8,128)(2,1)}, bf16[160,384]{1,0:T(8,128)(2,1)S(1)}, u32[]{:S(2)}, u32[]{:S(2)}) collective-permute-start(bf16[160,384]{1,0:T(8,128)(2,1)} %pick.1), channel_id=1, source_target_pairs={{0,4},{1,5},{2,6},{3,7},{4,0},{5,1},{6,2},{7,3},{8,12},{9,13},{10,... | collective-permute-start | bytes 368648 | tf_op jit(solution)/shard_map/ppermute | solution.py:535
  7.4 0.9 copy-done.1
  12.1 1.2 collective-permute-done.refs_0_
  13.3 1.5 %collective-permute-start.1 = (bf16[160,384]{1,0:T(8,128)(2,1)S(1)}, bf16[160,384]{1,0:T(8,128)(2,1)S(1)}, u32[]{:S(2)}, u32[]{:S(2)}) collective-permute-start(bf16[160,384]{1,0:T(8,128)(2,1)S(1)} %collective-permute-done.refs_0_), channel_id=1, source_target_pairs={{0,8},{1,17},{2,10},{3,19},{4,12},{5,21},{6,14},{7,23},{8,0},{9,25... | collective-permute-start | bytes 368648 | tf_op jit(solution)/shard_map/ppermute | solution.py:535
  15.7 1.2 %collective-permute-start.9 = (bf16[160,384]{1,0:T(8,128)(2,1)S(1)}, bf16[160,384]{1,0:T(8,128)(2,1)S(1)}, u32[]{:S(2)}, u32[]{:S(2)}) collective-permute-start(bf16[160,384]{1,0:T(8,128)(2,1)S(1)} %collective-permute-done.refs_0_), channel_id=1, source_target_pairs={{0,2},{1,3},{2,0},{3,1},{4,6},{5,7},{6,4},{7,5},{8,10},{9,11},{10,... | collective-permute-start | bytes 368648 | tf_op jit(solution)/shard_map/ppermute | solution.py:535
  17.6 1.6 %collective-permute-start.2 = (bf16[160,384]{1,0:T(8,128)(2,1)S(1)}, bf16[160,384]{1,0:T(8,128)(2,1)S(1)}, u32[]{:S(2)}, u32[]{:S(2)}) collective-permute-start(bf16[160,384]{1,0:T(8,128)(2,1)S(1)} %collective-permute-done.refs_0_), channel_id=1, source_target_pairs={{0,16},{1,9},{2,18},{3,11},{4,20},{5,13},{6,22},{7,15},{8,24},{9,1... | collective-permute-start | bytes 368648 | tf_op jit(solution)/shard_map/ppermute | solution.py:535
  20.7 1.3 %collective-permute-done.9 = bf16[160,384]{1,0:T(8,128)(2,1)S(1)} collective-permute-done((bf16[160,384]{1,0:T(8,128)(2,1)S(1)}, bf16[160,384]{1,0:T(8,128)(2,1)S(1)}, u32[]{:S(2)}, u32[]{:S(2)}) %collective-permute-start.9) | collective-permute-done | bytes 122912 | tf_op jit(solution)/shard_map/ppermute | solution.py:535
  22.6 1.1 collective-permute-done.12.c_other
  24.9 1.1 collective-permute-done.13
  26.0 1.2 collective-permute-start.14
  27.2 1.6 %collective-permute-start.10 = (bf16[2,144,384]{2,1,0:T(8,128)(2,1)S(1)}, bf16[2,144,384]{2,1,0:T(8,128)(2,1)S(1)}, u32[]{:S(2)}, u32[]{:S(2)}) collective-permute-start(bf16[2,144,384]{2,1,0:T(8,128)(2,1)S(1)} %pad_maximum_fusion.refs_4_), channel_id=1, source_target_pairs={{0,8},{1,17},{2,10},{3,19},{4,12},{5,21},{6,14},{7,23},{8,0},{9,25... | collective-permute-start | bytes 663560 | tf_op jit(solution)/shard_map/ppermute | solution.py:535
  28.8 1.7 %collective-permute-done.14 = f32[2,4,2304]{2,1,0:T(4,128)S(1)} collective-permute-done((f32[2,4,2304]{2,1,0:T(4,128)S(1)}, f32[2,4,2304]{2,1,0:T(4,128)S(1)}, u32[]{:S(2)}, u32[]{:S(2)}) %collective-permute-start.14) | collective-permute-done | bytes 73760 | tf_op jit(solution)/shard_map/ppermute | solution.py:535
  30.5 2.7 %collective-permute-start.15 = (f32[4,2304]{1,0:T(4,128)S(1)}, f32[4,2304]{1,0:T(4,128)S(1)}, u32[]{:S(2)}, u32[]{:S(2)}) collective-permute-start(f32[4,2304]{1,0:T(4,128)S(1)} %slice_bitcast_fusion.6), channel_id=1, source_target_pairs={{0,4},{1,5},{2,6},{3,7},{4,0},{5,1},{6,2},{7,3},{8,12},{9,13},{10,... | collective-permute-start | bytes 110600 | tf_op jit(solution)/shard_map/ppermute | solution.py:535
  33.2 1.2 collective-permute-start.11
  34.4 1.0 collective-permute-done.15.refs_21_
  35.4 1.5 %collective-permute-start.16 = (bf16[2,144,384]{2,1,0:T(8,128)(2,1)S(1)}, bf16[2,144,384]{2,1,0:T(8,128)(2,1)S(1)}, u32[]{:S(2)}, u32[]{:S(2)}) collective-permute-start(bf16[2,144,384]{2,1,0:T(8,128)(2,1)S(1)} %collective-permute-done.10.refs_5_), channel_id=1, source_target_pairs={{0,16},{1,9},{2,18},{3,11},{4,20},{5,13},{6,22},{7,15},{8,24},{9,1... | collective-permute-start | bytes 663560 | tf_op jit(solution)/shard_map/ppermute | solution.py:535
  39.2 2.4 %collective-permute-done.16.refs_7_ = bf16[2,144,384]{2,1,0:T(8,128)(2,1)S(1)} collective-permute-done((bf16[2,144,384]{2,1,0:T(8,128)(2,1)S(1)}, bf16[2,144,384]{2,1,0:T(8,128)(2,1)S(1)}, u32[]{:S(2)}, u32[]{:S(2)}) %collective-permute-start.16) | collective-permute-done | bytes 221216 | tf_op jit(solution)/shard_map/ppermute | solution.py:535
  42.0 1.1 collective-permute-done.20.refs_11_
  43.2 5.0 %attention.1 = (bf16[4,384,384]{2,1,0:T(8,128)(2,1)S(1)}, f32[4,2304]{1,0:T(4,128)S(1)}, bf16[512,384]{1,0:T(8,128)(2,1)S(1)}, bf16[512,1152]{1,0:T(8,128)(2,1)}, bf16[512,384]{1,0:T(8,128)(2,1)S(1)}) custom-call(s32[3]{0:T(128)S(1)} %pad_add_fusion.ids, bf16[160,384]{1,0:T(8,128)(2,1)S(1)} %collective-permute-done.refs_0_, ...), custom_call_target="tpu_custom_call" | custom-call | flops 855638016 | bytes 6733824 | tf_op jit(solution)/shard_map/attention/pallas_call | solution.py:43
  48.3 11.4 %mlp.1 = (bf16[2,256,384]{2,1,0:T(8,128)(2,1)}, f32[2,256,384]{2,1,0:T(8,128)}, bf16[512,384]{1,0:T(8,128)(2,1)S(1)}, bf16[512,384]{1,0:T(8,128)(2,1)S(1)}, f32[...) custom-call(s32[3]{0:T(128)S(1)} %pad_add_fusion.ids, ...), custom_call_target="tpu_custom_call" | custom-call | flops 3925868544 | bytes 9200640 | tf_op jit(solution)/shard_map/mlp/pallas_call | solution.py:43
  60.2 7.2 %attention_back.1 = (bf16[512,1152]{1,0:T(8,128)(2,1)S(1)}, f32[1,3072]{1,0:T(1,128)S(1)}, bf16[2,4,48,384]{3,2,1,0:T(8,128)(2,1)S(1)}, bf16[2,4,48,384]{3,2,1,0...) custom-call(s32[3]{0:T(128)S(1)} %pad_add_fusion.ids, ...), custom_call_target="tpu_custom_call" | custom-call | flops 1610612736 | bytes 5133312 | tf_op jit(solution)/shard_map/attention_back/pallas_call | solution.py:43
  68.0 1.1 collective-permute-done.28.got_po
  69.8 1.5 %collective-permute-start.29 = (bf16[2,4,144,384]{3,2,1,0:T(8,128)(2,1)S(1)}, bf16[2,4,144,384]{3,2,1,0:T(8,128)(2,1)S(1)}, u32[]{:S(2)}, u32[]{:S(2)}) collective-permute-start(bf16[2,4,144,384]{3,2,1,0:T(8,128)(2,1)S(1)} %merge_odd.1), channel_id=1, source_target_pairs={{0,8},{1,17},{2,10},{3,19},{4,12},{5,21},{6,14},{7,23},{8,0},{9,25... | collective-permute-start | bytes 2654216 | tf_op jit(solution)/shard_map/ppermute | solution.py:535
  72.5 2.9 %input_back.1 = (bf16[2,256,384]{2,1,0:T(8,128)(2,1)}, bf16[2,3840]{1,0:T(2,128)(2,1)S(1)}) custom-call(s32[3]{0:T(128)S(1)} %pad_add_fusion.ids, bf16[512,1152]{1,0:T(8,128)(2,1)S(1)} %get-tuple-element.88.gproj, bf16[4,384,384]{2,1,0:T(8,128)(2,1)S(1)} %get-tuple-element.74.wpo, bf16[2,256,384]{2,1,0:T(8,128)(2,1)S(1)} %copy-done, ...), custom_call_target="tpu_custom_call" | custom-call | flops 452984832 | bytes 4008960 | tf_op jit(solution)/shard_map/input_back/pallas_call | solution.py:43
  75.4 1.2 collective-permute-done.30
  76.7 2.6 %collective-permute-start.31 = (bf16[4,3840]{1,0:T(4,128)(2,1)S(1)}, bf16[4,3840]{1,0:T(4,128)(2,1)S(1)}, u32[]{:S(2)}, u32[]{:S(2)}) collective-permute-start(bf16[4,3840]{1,0:T(4,128)(2,1)S(1)} %pad_maximum_fusion.2.g0), channel_id=1, source_target_pairs={{0,4},{1,5},{2,6},{3,7},{4,0},{5,1},{6,2},{7,3},{8,12},{9,13},{10,... | collective-permute-start | bytes 92168 | tf_op jit(solution)/shard_map/ppermute | solution.py:535
  79.2 3.7 %collective-permute-done.29 = bf16[2,4,144,384]{3,2,1,0:T(8,128)(2,1)S(1)} collective-permute-done((bf16[2,4,144,384]{3,2,1,0:T(8,128)(2,1)S(1)}, bf16[2,4,144,384]{3,2,1,0:T(8,128)(2,1)S(1)}, u32[]{:S(2)}, u32[]{:S(2)}) %collective-permute-start.29) | collective-permute-done | bytes 884768 | tf_op jit(solution)/shard_map/ppermute | solution.py:535
  83.1 1.4 %collective-permute-start.32 = (bf16[4,144,384]{2,1,0:T(8,128)(2,1)S(1)}, bf16[4,144,384]{2,1,0:T(8,128)(2,1)S(1)}, u32[]{:S(2)}, u32[]{:S(2)}) collective-permute-start(bf16[4,144,384]{2,1,0:T(8,128)(2,1)S(1)} %fusion), channel_id=1, source_target_pairs={{0,16},{1,9},{2,18},{3,11},{4,20},{5,13},{6,22},{7,15},{8,24},{9,1... | collective-permute-start | bytes 1327112 | tf_op jit(solution)/shard_map/ppermute | solution.py:535
  84.6 1.6 %collective-permute-start.34 = (bf16[4,3840]{1,0:T(4,128)(2,1)S(1)}, bf16[4,3840]{1,0:T(4,128)(2,1)S(1)}, u32[]{:S(2)}, u32[]{:S(2)}) collective-permute-start(bf16[4,3840]{1,0:T(4,128)(2,1)S(1)} %collective-permute-done.31.g2), channel_id=1, source_target_pairs={{0,2},{1,3},{2,0},{3,1},{4,6},{5,7},{6,4},{7,5},{8,10},{9,11},{10,... | collective-permute-start | bytes 92168 | tf_op jit(solution)/shard_map/ppermute | solution.py:535
  86.8 1.8 %collective-permute-done.34.g3 = bf16[4,3840]{1,0:T(4,128)(2,1)S(1)} collective-permute-done((bf16[4,3840]{1,0:T(4,128)(2,1)S(1)}, bf16[4,3840]{1,0:T(4,128)(2,1)S(1)}, u32[]{:S(2)}, u32[]{:S(2)}) %collective-permute-start.34) | collective-permute-done | bytes 30752 | tf_op jit(solution)/shard_map/ppermute | solution.py:535
  88.6 1.5 %collective-permute-done.33.g1 = bf16[4,3840]{1,0:T(4,128)(2,1)S(1)} collective-permute-done((bf16[4,3840]{1,0:T(4,128)(2,1)S(1)}, bf16[4,3840]{1,0:T(4,128)(2,1)S(1)}, u32[]{:S(2)}, u32[]{:S(2)}) %collective-permute-start.33) | collective-permute-done | bytes 30752 | tf_op jit(solution)/shard_map/ppermute | solution.py:535
  90.3 1.6 %cond_back.1 = (bf16[2,16,384]{2,1,0:T(8,128)(2,1)S(1)}, bf16[2,16,384]{2,1,0:T(8,128)(2,1)S(1)}) custom-call(s32[3]{0:T(128)S(1)} %pad_add_fusion.ids, bf16[4,3840]{1,0:T(4,128)(2,1)S(1)} %pad_maximum_fusion.2.g0, bf16[4,3840]{1,0:T(4,128)(2,1)S(1)} %collective-permute-done.31.g2, bf16[4,3840]{1,0:T(4,128)(2,1)S(1)} %collective-permute-done.33.g1, ...), custom_call_target="tpu_custom_call" | custom-call | bytes 393216 | tf_op jit(solution)/shard_map/cond_back/pallas_call | solution.py:43
  92.5 1.4 %collective-permute-start.35 = (bf16[2,160,384]{2,1,0:T(8,128)(2,1)S(1)}, bf16[2,160,384]{2,1,0:T(8,128)(2,1)S(1)}, u32[]{:S(2)}, u32[]{:S(2)}) collective-permute-start(bf16[2,160,384]{2,1,0:T(8,128)(2,1)S(1)} %join_far.1), channel_id=1, source_target_pairs={{0,2},{1,3},{2,0},{3,1},{4,6},{5,7},{6,4},{7,5},{8,10},{9,11},{10,... | collective-permute-start | bytes 737288 | tf_op jit(solution)/shard_map/ppermute | solution.py:535
  93.9 1.5 %collective-permute-start.37 = (bf16[16,4224]{1,0:T(8,128)(2,1)S(1)}, bf16[16,4224]{1,0:T(8,128)(2,1)S(1)}, u32[]{:S(2)}, u32[]{:S(2)}) collective-permute-start(bf16[16,4224]{1,0:T(8,128)(2,1)S(1)} %pad_maximum_fusion.1.e0), channel_id=1, source_target_pairs={{0,8},{1,17},{2,10},{3,19},{4,12},{5,21},{6,14},{7,23},{8,0},{9,25... | collective-permute-start | bytes 405512 | tf_op jit(solution)/shard_map/ppermute | solution.py:535
  96.0 2.8 %collective-permute-done.35.got = bf16[2,160,384]{2,1,0:T(8,128)(2,1)S(1)} collective-permute-done((bf16[2,160,384]{2,1,0:T(8,128)(2,1)S(1)}, bf16[2,160,384]{2,1,0:T(8,128)(2,1)S(1)}, u32[]{:S(2)}, u32[]{:S(2)}) %collective-permute-start.35) | collective-permute-done | bytes 245792 | tf_op jit(solution)/shard_map/ppermute | solution.py:535
  99.4 1.2 collective-permute-start.39
  100.6 2.5 %collective-permute-start.36 = (bf16[160,384]{1,0:T(8,128)(2,1)S(1)}, bf16[160,384]{1,0:T(8,128)(2,1)S(1)}, u32[]{:S(2)}, u32[]{:S(2)}) collective-permute-start(bf16[160,384]{1,0:T(8,128)(2,1)S(1)} %slice_bitcast_fusion.2), channel_id=1, source_target_pairs={{0,4},{1,5},{2,6},{3,7},{4,0},{5,1},{6,2},{7,3},{8,12},{9,13},{10,... | collective-permute-start | bytes 368648 | tf_op jit(solution)/shard_map/ppermute | solution.py:535
  103.1 1.4 %collective-permute-done.39.e3 = bf16[16,4224]{1,0:T(8,128)(2,1)S(1)} collective-permute-done((bf16[16,4224]{1,0:T(8,128)(2,1)S(1)}, bf16[16,4224]{1,0:T(8,128)(2,1)S(1)}, u32[]{:S(2)}, u32[]{:S(2)}) %collective-permute-start.39) | collective-permute-done | bytes 135200 | tf_op jit(solution)/shard_map/ppermute | solution.py:535
  104.5 2.1 %mod_weight.1 = (f32[48,2304]{1,0:T(8,128)}, f32[1,5376]{1,0:T(1,128)S(1)}) custom-call(s32[3]{0:T(128)S(1)} %pad_add_fusion.ids, bf16[16,4224]{1,0:T(8,128)(2,1)S(1)} %pad_maximum_fusion.1.e0, bf16[16,4224]{1,0:T(8,128)(2,1)S(1)} %collective-permute-done.37.e1, bf16[16,4224]{1,0:T(8,128)(2,1)S(1)} %collective-permute-done.38.e2, ...), custom_call_target="tpu_custom_call" | custom-call | bytes 1004544 | tf_op jit(solution)/shard_map/mod_weight/pallas_call | solution.py:43
  106.6 1.1 collective-permute-done.36
  107.8 1.3 %collective-permute-start.40 = (bf16[160,384]{1,0:T(8,128)(2,1)S(1)}, bf16[160,384]{1,0:T(8,128)(2,1)S(1)}, u32[]{:S(2)}, u32[]{:S(2)}) collective-permute-start(bf16[160,384]{1,0:T(8,128)(2,1)S(1)} %fusion.2.g0), channel_id=1, source_target_pairs={{0,8},{1,17},{2,10},{3,19},{4,12},{5,21},{6,14},{7,23},{8,0},{9,25... | collective-permute-start | bytes 368648 | tf_op jit(solution)/shard_map/ppermute | solution.py:535
  109.0 1.0 collective-permute-start.41
  110.1 2.6 %collective-permute-done.40.g1 = bf16[160,384]{1,0:T(8,128)(2,1)S(1)} collective-permute-done((bf16[160,384]{1,0:T(8,128)(2,1)S(1)}, bf16[160,384]{1,0:T(8,128)(2,1)S(1)}, u32[]{:S(2)}, u32[]{:S(2)}) %collective-permute-start.40) | collective-permute-done | bytes 122912 | tf_op jit(solution)/shard_map/ppermute | solution.py:535
  112.7 1.2 collective-permute-done.41.g2
  116.4 1.0 collective-permute-start.43
  118.0 3.3 %collective-permute-done.43.g3 = bf16[160,384]{1,0:T(8,128)(2,1)S(1)} collective-permute-done((bf16[160,384]{1,0:T(8,128)(2,1)S(1)}, bf16[160,384]{1,0:T(8,128)(2,1)S(1)}, u32[]{:S(2)}, u32[]{:S(2)}) %collective-permute-start.43) | collective-permute-done | bytes 122912 | tf_op jit(solution)/shard_map/ppermute | solution.py:535
  121.3 1.5 %final.1 = (f32[48,1152]{1,0:T(8,128)}, f32[48,384]{1,0:T(8,128)}, f32[48,1536]{1,0:T(8,128)}, f32[192,384]{1,0:T(8,128)}) custom-call(s32[3]{0:T(128)S(1)} %pad_add_fusion.ids, bf16[160,384]{1,0:T(8,128)(2,1)S(1)} %fusion.2.g0, bf16[160,384]{1,0:T(8,128)(2,1)S(1)} %collective-permute-done.40.g1, bf16[160,384]{1,0:T(8,128)(2,1)S(1)} %collective-permute-done.41.g2, ...), custom_call_target="tpu_custom_call" | custom-call | bytes 1376256 | tf_op jit(solution)/shard_map/final/pallas_call | solution.py:43
  (121 shorter events, 20.8 us)
Async XLA Ops:
  0.6 42.6 %copy-start.6 = (bf16[48,1152]{1,0:T(8,128)(2,1)S(1)}, bf16[48,1152]{1,0:T(8,128)(2,1)}, u32[]{:S(2)}) copy-start(bf16[48,1152]{1,0:T(8,128)(2,1)} %refs_16_.2) | copy-start | bytes 331780
  0.7 42.6 %copy-start.7 = (bf16[48,384]{1,0:T(8,128)(2,1)S(1)}, bf16[48,384]{1,0:T(8,128)(2,1)}, u32[]{:S(2)}) copy-start(bf16[48,384]{1,0:T(8,128)(2,1)} %refs_17_.2) | copy-start | bytes 110596
  0.7 42.5 %copy-start = (bf16[2,256,384]{2,1,0:T(8,128)(2,1)S(1)}, bf16[2,256,384]{2,1,0:T(8,128)(2,1)}, u32[]{:S(2)}) copy-start(bf16[2,256,384]{2,1,0:T(8,128)(2,1)} %lat.1) | copy-start | bytes 1179652
  0.7 14.2 %collective-permute-start.6 = (bf16[48,1536]{1,0:T(8,128)(2,1)}, bf16[48,1536]{1,0:T(8,128)(2,1)S(1)}, u32[]{:S(2)}, u32[]{:S(2)}) collective-permute-start(bf16[48,1536]{1,0:T(8,128)(2,1)} %refs_16_.3), channel_id=1, source_target_pairs={{0,1},{1,0},{2,3},{3,2},{4,5},{5,4},{6,7},{7,6},{8,9},{9,8},{10,11... | collective-permute-start | bytes 442376 | tf_op jit(solution)/shard_map/ppermute | solution.py:535
  1.2 13.7 %collective-permute-start.7 = (bf16[192,384]{1,0:T(8,128)(2,1)}, bf16[192,384]{1,0:T(8,128)(2,1)S(1)}, u32[]{:S(2)}, u32[]{:S(2)}) collective-permute-start(bf16[192,384]{1,0:T(8,128)(2,1)} %refs_17_.3), channel_id=1, source_target_pairs={{0,1},{1,0},{2,3},{3,2},{4,5},{5,4},{6,7},{7,6},{8,9},{9,8},{10,11... | collective-permute-start | bytes 442376 | tf_op jit(solution)/shard_map/ppermute | solution.py:535
  2.8 10.5 %collective-permute-start = (bf16[160,384]{1,0:T(8,128)(2,1)}, bf16[160,384]{1,0:T(8,128)(2,1)S(1)}, u32[]{:S(2)}, u32[]{:S(2)}) collective-permute-start(bf16[160,384]{1,0:T(8,128)(2,1)} %pick.1), channel_id=1, source_target_pairs={{0,4},{1,5},{2,6},{3,7},{4,0},{5,1},{6,2},{7,3},{8,12},{9,13},{10,... | collective-permute-start | bytes 368648 | tf_op jit(solution)/shard_map/ppermute | solution.py:535
  6.9 8.0 %collective-permute-start.4 = (bf16[48,1152]{1,0:T(8,128)(2,1)}, bf16[48,1152]{1,0:T(8,128)(2,1)S(1)}, u32[]{:S(2)}, u32[]{:S(2)}) collective-permute-start(bf16[48,1152]{1,0:T(8,128)(2,1)} %refs_16_.2), channel_id=1, source_target_pairs={{0,1},{1,0},{2,3},{3,2},{4,5},{5,4},{6,7},{7,6},{8,9},{9,8},{10,11... | collective-permute-start | bytes 331784 | tf_op jit(solution)/shard_map/ppermute | solution.py:535
  6.9 8.0 %collective-permute-start.5 = (bf16[48,384]{1,0:T(8,128)(2,1)}, bf16[48,384]{1,0:T(8,128)(2,1)S(1)}, u32[]{:S(2)}, u32[]{:S(2)}) collective-permute-start(bf16[48,384]{1,0:T(8,128)(2,1)} %refs_17_.2), channel_id=1, source_target_pairs={{0,1},{1,0},{2,3},{3,2},{4,5},{5,4},{6,7},{7,6},{8,9},{9,8},{10,11... | collective-permute-start | bytes 110600 | tf_op jit(solution)/shard_map/ppermute | solution.py:535
  13.3 6.7 %collective-permute-start.1 = (bf16[160,384]{1,0:T(8,128)(2,1)S(1)}, bf16[160,384]{1,0:T(8,128)(2,1)S(1)}, u32[]{:S(2)}, u32[]{:S(2)}) collective-permute-start(bf16[160,384]{1,0:T(8,128)(2,1)S(1)} %collective-permute-done.refs_0_), channel_id=1, source_target_pairs={{0,8},{1,17},{2,10},{3,19},{4,12},{5,21},{6,14},{7,23},{8,0},{9,25... | collective-permute-start | bytes 368648 | tf_op jit(solution)/shard_map/ppermute | solution.py:535
  14.9 5.8 %collective-permute-start.8 = (bf16[160,384]{1,0:T(8,128)(2,1)}, bf16[160,384]{1,0:T(8,128)(2,1)S(1)}, u32[]{:S(2)}, u32[]{:S(2)}) collective-permute-start(bf16[160,384]{1,0:T(8,128)(2,1)} %pick.1), channel_id=1, source_target_pairs={{0,2},{1,3},{2,0},{3,1},{4,6},{5,7},{6,4},{7,5},{8,10},{9,11},{10,... | collective-permute-start | bytes 368648 | tf_op jit(solution)/shard_map/ppermute | solution.py:535
  15.7 6.3 %collective-permute-start.9 = (bf16[160,384]{1,0:T(8,128)(2,1)S(1)}, bf16[160,384]{1,0:T(8,128)(2,1)S(1)}, u32[]{:S(2)}, u32[]{:S(2)}) collective-permute-start(bf16[160,384]{1,0:T(8,128)(2,1)S(1)} %collective-permute-done.refs_0_), channel_id=1, source_target_pairs={{0,2},{1,3},{2,0},{3,1},{4,6},{5,7},{6,4},{7,5},{8,10},{9,11},{10,... | collective-permute-start | bytes 368648 | tf_op jit(solution)/shard_map/ppermute | solution.py:535
  17.6 4.9 %collective-permute-start.2 = (bf16[160,384]{1,0:T(8,128)(2,1)S(1)}, bf16[160,384]{1,0:T(8,128)(2,1)S(1)}, u32[]{:S(2)}, u32[]{:S(2)}) collective-permute-start(bf16[160,384]{1,0:T(8,128)(2,1)S(1)} %collective-permute-done.refs_0_), channel_id=1, source_target_pairs={{0,16},{1,9},{2,18},{3,11},{4,20},{5,13},{6,22},{7,15},{8,24},{9,1... | collective-permute-start | bytes 368648 | tf_op jit(solution)/shard_map/ppermute | solution.py:535
  20.0 4.9 %collective-permute-start.3 = (bf16[160,384]{1,0:T(8,128)(2,1)S(1)}, bf16[160,384]{1,0:T(8,128)(2,1)S(1)}, u32[]{:S(2)}, u32[]{:S(2)}) collective-permute-start(bf16[160,384]{1,0:T(8,128)(2,1)S(1)} %collective-permute-done.1.refs_1_), channel_id=1, source_target_pairs={{0,16},{1,9},{2,18},{3,11},{4,20},{5,13},{6,22},{7,15},{8,24},{9,1... | collective-permute-start | bytes 368648 | tf_op jit(solution)/shard_map/ppermute | solution.py:535
  22.6 1.2 collective-permute-start.12
  24.6 1.4 %collective-permute-start.13 = (f32[4,4,2304]{2,1,0:T(4,128)S(1)}, f32[4,4,2304]{2,1,0:T(4,128)S(1)}, u32[]{:S(2)}, u32[]{:S(2)}) collective-permute-start(f32[4,4,2304]{2,1,0:T(4,128)S(1)} %get-tuple-element.70), channel_id=1, source_target_pairs={{0,1},{1,0},{2,3},{3,2},{4,5},{5,4},{6,7},{7,6},{8,9},{9,8},{10,11... | collective-permute-start | bytes 442376 | tf_op jit(solution)/shard_map/ppermute | solution.py:535
  26.0 4.4 %collective-permute-start.14 = (f32[2,4,2304]{2,1,0:T(4,128)S(1)}, f32[2,4,2304]{2,1,0:T(4,128)S(1)}, u32[]{:S(2)}, u32[]{:S(2)}) collective-permute-start(f32[2,4,2304]{2,1,0:T(4,128)S(1)} %slice_add_fusion), channel_id=1, source_target_pairs={{0,2},{1,3},{2,0},{3,1},{4,6},{5,7},{6,4},{7,5},{8,10},{9,11},{10,... | collective-permute-start | bytes 221192 | tf_op jit(solution)/shard_map/ppermute | solution.py:535
  27.2 7.2 %collective-permute-start.10 = (bf16[2,144,384]{2,1,0:T(8,128)(2,1)S(1)}, bf16[2,144,384]{2,1,0:T(8,128)(2,1)S(1)}, u32[]{:S(2)}, u32[]{:S(2)}) collective-permute-start(bf16[2,144,384]{2,1,0:T(8,128)(2,1)S(1)} %pad_maximum_fusion.refs_4_), channel_id=1, source_target_pairs={{0,8},{1,17},{2,10},{3,19},{4,12},{5,21},{6,14},{7,23},{8,0},{9,25... | collective-permute-start | bytes 663560 | tf_op jit(solution)/shard_map/ppermute | solution.py:535
  30.5 4.9 %collective-permute-start.15 = (f32[4,2304]{1,0:T(4,128)S(1)}, f32[4,2304]{1,0:T(4,128)S(1)}, u32[]{:S(2)}, u32[]{:S(2)}) collective-permute-start(f32[4,2304]{1,0:T(4,128)S(1)} %slice_bitcast_fusion.6), channel_id=1, source_target_pairs={{0,4},{1,5},{2,6},{3,7},{4,0},{5,1},{6,2},{7,3},{8,12},{9,13},{10,... | collective-permute-start | bytes 110600 | tf_op jit(solution)/shard_map/ppermute | solution.py:535
  33.2 5.9 %collective-permute-start.11 = (bf16[2,144,384]{2,1,0:T(8,128)(2,1)S(1)}, bf16[2,144,384]{2,1,0:T(8,128)(2,1)S(1)}, u32[]{:S(2)}, u32[]{:S(2)}) collective-permute-start(bf16[2,144,384]{2,1,0:T(8,128)(2,1)S(1)} %pad_maximum_fusion.refs_4_), channel_id=1, source_target_pairs={{0,16},{1,9},{2,18},{3,11},{4,20},{5,13},{6,22},{7,15},{8,24},{9,1... | collective-permute-start | bytes 663560 | tf_op jit(solution)/shard_map/ppermute | solution.py:535
  35.4 6.1 %collective-permute-start.16 = (bf16[2,144,384]{2,1,0:T(8,128)(2,1)S(1)}, bf16[2,144,384]{2,1,0:T(8,128)(2,1)S(1)}, u32[]{:S(2)}, u32[]{:S(2)}) collective-permute-start(bf16[2,144,384]{2,1,0:T(8,128)(2,1)S(1)} %collective-permute-done.10.refs_5_), channel_id=1, source_target_pairs={{0,16},{1,9},{2,18},{3,11},{4,20},{5,13},{6,22},{7,15},{8,24},{9,1... | collective-permute-start | bytes 663560 | tf_op jit(solution)/shard_map/ppermute | solution.py:535
  37.0 1.3 %collective-permute-start.17 = (bf16[160,384]{1,0:T(8,128)(2,1)S(1)}, bf16[160,384]{1,0:T(8,128)(2,1)S(1)}, u32[]{:S(2)}, u32[]{:S(2)}) collective-permute-start(bf16[160,384]{1,0:T(8,128)(2,1)S(1)} %collective-permute-done.refs_0_), channel_id=1, source_target_pairs={{0,1},{1,0},{2,3},{3,2},{4,5},{5,4},{6,7},{7,6},{8,9},{9,8},{10,11... | collective-permute-start | bytes 368648 | tf_op jit(solution)/shard_map/ppermute | solution.py:535
  37.0 1.5 %collective-permute-start.18 = (bf16[160,384]{1,0:T(8,128)(2,1)S(1)}, bf16[160,384]{1,0:T(8,128)(2,1)S(1)}, u32[]{:S(2)}, u32[]{:S(2)}) collective-permute-start(bf16[160,384]{1,0:T(8,128)(2,1)S(1)} %collective-permute-done.1.refs_1_), channel_id=1, source_target_pairs={{0,1},{1,0},{2,3},{3,2},{4,5},{5,4},{6,7},{7,6},{8,9},{9,8},{10,11... | collective-permute-start | bytes 368648 | tf_op jit(solution)/shard_map/ppermute | solution.py:535
  37.5 4.1 %collective-permute-start.19 = (bf16[160,384]{1,0:T(8,128)(2,1)S(1)}, bf16[160,384]{1,0:T(8,128)(2,1)S(1)}, u32[]{:S(2)}, u32[]{:S(2)}) collective-permute-start(bf16[160,384]{1,0:T(8,128)(2,1)S(1)} %collective-permute-done.2.refs_2_), channel_id=1, source_target_pairs={{0,1},{1,0},{2,3},{3,2},{4,5},{5,4},{6,7},{7,6},{8,9},{9,8},{10,11... | collective-permute-start | bytes 368648 | tf_op jit(solution)/shard_map/ppermute | solution.py:535
  38.3 3.7 %collective-permute-start.21 = (bf16[2,144,384]{2,1,0:T(8,128)(2,1)S(1)}, bf16[2,144,384]{2,1,0:T(8,128)(2,1)S(1)}, u32[]{:S(2)}, u32[]{:S(2)}) collective-permute-start(bf16[2,144,384]{2,1,0:T(8,128)(2,1)S(1)} %pad_maximum_fusion.refs_4_), channel_id=1, source_target_pairs={{0,1},{1,0},{2,3},{3,2},{4,5},{5,4},{6,7},{7,6},{8,9},{9,8},{10,11... | collective-permute-start | bytes 663560 | tf_op jit(solution)/shard_map/ppermute | solution.py:535
  38.5 4.7 %collective-permute-start.22 = (bf16[2,144,384]{2,1,0:T(8,128)(2,1)S(1)}, bf16[2,144,384]{2,1,0:T(8,128)(2,1)S(1)}, u32[]{:S(2)}, u32[]{:S(2)}) collective-permute-start(bf16[2,144,384]{2,1,0:T(8,128)(2,1)S(1)} %collective-permute-done.10.refs_5_), channel_id=1, source_target_pairs={{0,1},{1,0},{2,3},{3,2},{4,5},{5,4},{6,7},{7,6},{8,9},{9,8},{10,11... | collective-permute-start | bytes 663560 | tf_op jit(solution)/shard_map/ppermute | solution.py:535
  39.2 4.0 %collective-permute-start.23 = (bf16[2,144,384]{2,1,0:T(8,128)(2,1)S(1)}, bf16[2,144,384]{2,1,0:T(8,128)(2,1)S(1)}, u32[]{:S(2)}, u32[]{:S(2)}) collective-permute-start(bf16[2,144,384]{2,1,0:T(8,128)(2,1)S(1)} %collective-permute-done.11.refs_6_), channel_id=1, source_target_pairs={{0,1},{1,0},{2,3},{3,2},{4,5},{5,4},{6,7},{7,6},{8,9},{9,8},{10,11... | collective-permute-start | bytes 663560 | tf_op jit(solution)/shard_map/ppermute | solution.py:535
  41.5 1.7 %collective-permute-start.24 = (bf16[2,144,384]{2,1,0:T(8,128)(2,1)S(1)}, bf16[2,144,384]{2,1,0:T(8,128)(2,1)S(1)}, u32[]{:S(2)}, u32[]{:S(2)}) collective-permute-start(bf16[2,144,384]{2,1,0:T(8,128)(2,1)S(1)} %collective-permute-done.16.refs_7_), channel_id=1, source_target_pairs={{0,1},{1,0},{2,3},{3,2},{4,5},{5,4},{6,7},{7,6},{8,9},{9,8},{10,11... | collective-permute-start | bytes 663560 | tf_op jit(solution)/shard_map/ppermute | solution.py:535
  41.5 1.6 %collective-permute-start.20 = (bf16[160,384]{1,0:T(8,128)(2,1)S(1)}, bf16[160,384]{1,0:T(8,128)(2,1)S(1)}, u32[]{:S(2)}, u32[]{:S(2)}) collective-permute-start(bf16[160,384]{1,0:T(8,128)(2,1)S(1)} %collective-permute-done.3.refs_3_), channel_id=1, source_target_pairs={{0,1},{1,0},{2,3},{3,2},{4,5},{5,4},{6,7},{7,6},{8,9},{9,8},{10,11... | collective-permute-start | bytes 368648 | tf_op jit(solution)/shard_map/ppermute | solution.py:535
  59.7 9.3 %collective-permute-start.27 = (bf16[2,4,2,48,384]{4,3,2,1,0:T(8,128)(2,1)}, bf16[2,4,2,48,384]{4,3,2,1,0:T(8,128)(2,1)S(1)}, u32[]{:S(2)}, u32[]{:S(2)}) collective-permute-start(bf16[2,4,2,48,384]{4,3,2,1,0:T(8,128)(2,1)} %get-tuple-element.94), channel_id=1, source_target_pairs={{0,1},{1,0},{2,3},{3,2},{4,5},{5,4},{6,7},{7,6},{8,9},{9,8},{10,11... | collective-permute-start | bytes 1769480 | tf_op jit(solution)/shard_map/ppermute | solution.py:535
  59.9 11.4 %collective-permute-start.25 = (bf16[2,4,2,48,384]{4,3,2,1,0:T(8,128)(2,1)}, bf16[2,4,2,48,384]{4,3,2,1,0:T(8,128)(2,1)S(1)}, u32[]{:S(2)}, u32[]{:S(2)}) collective-permute-start(bf16[2,4,2,48,384]{4,3,2,1,0:T(8,128)(2,1)} %get-tuple-element.85), channel_id=1, source_target_pairs={{0,1},{1,0},{2,3},{3,2},{4,5},{5,4},{6,7},{7,6},{8,9},{9,8},{10,11... | collective-permute-start | bytes 1769480 | tf_op jit(solution)/shard_map/ppermute | solution.py:535
  67.4 1.6 %collective-permute-start.28 = (bf16[2,4,48,384]{3,2,1,0:T(8,128)(2,1)S(1)}, bf16[2,4,48,384]{3,2,1,0:T(8,128)(2,1)S(1)}, u32[]{:S(2)}, u32[]{:S(2)}) collective-permute-start(bf16[2,4,48,384]{3,2,1,0:T(8,128)(2,1)S(1)} %get-tuple-element.96), channel_id=1, source_target_pairs={{0,1},{1,0},{2,3},{3,2},{4,5},{5,4},{6,7},{7,6},{8,9},{9,8},{10,11... | collective-permute-start | bytes 884744 | tf_op jit(solution)/shard_map/ppermute | solution.py:535
  67.6 3.7 %collective-permute-start.26 = (bf16[2,4,48,384]{3,2,1,0:T(8,128)(2,1)S(1)}, bf16[2,4,48,384]{3,2,1,0:T(8,128)(2,1)S(1)}, u32[]{:S(2)}, u32[]{:S(2)}) collective-permute-start(bf16[2,4,48,384]{3,2,1,0:T(8,128)(2,1)S(1)} %get-tuple-element.87), channel_id=1, source_target_pairs={{0,1},{1,0},{2,3},{3,2},{4,5},{5,4},{6,7},{7,6},{8,9},{9,8},{10,11... | collective-permute-start | bytes 884744 | tf_op jit(solution)/shard_map/ppermute | solution.py:535
  69.8 13.1 %collective-permute-start.29 = (bf16[2,4,144,384]{3,2,1,0:T(8,128)(2,1)S(1)}, bf16[2,4,144,384]{3,2,1,0:T(8,128)(2,1)S(1)}, u32[]{:S(2)}, u32[]{:S(2)}) collective-permute-start(bf16[2,4,144,384]{3,2,1,0:T(8,128)(2,1)S(1)} %merge_odd.1), channel_id=1, source_target_pairs={{0,8},{1,17},{2,10},{3,19},{4,12},{5,21},{6,14},{7,23},{8,0},{9,25... | collective-permute-start | bytes 2654216 | tf_op jit(solution)/shard_map/ppermute | solution.py:535
  75.4 1.2 collective-permute-start.30
  76.7 6.3 %collective-permute-start.31 = (bf16[4,3840]{1,0:T(4,128)(2,1)S(1)}, bf16[4,3840]{1,0:T(4,128)(2,1)S(1)}, u32[]{:S(2)}, u32[]{:S(2)}) collective-permute-start(bf16[4,3840]{1,0:T(4,128)(2,1)S(1)} %pad_maximum_fusion.2.g0), channel_id=1, source_target_pairs={{0,4},{1,5},{2,6},{3,7},{4,0},{5,1},{6,2},{7,3},{8,12},{9,13},{10,... | collective-permute-start | bytes 92168 | tf_op jit(solution)/shard_map/ppermute | solution.py:535
  83.1 8.7 %collective-permute-start.32 = (bf16[4,144,384]{2,1,0:T(8,128)(2,1)S(1)}, bf16[4,144,384]{2,1,0:T(8,128)(2,1)S(1)}, u32[]{:S(2)}, u32[]{:S(2)}) collective-permute-start(bf16[4,144,384]{2,1,0:T(8,128)(2,1)S(1)} %fusion), channel_id=1, source_target_pairs={{0,16},{1,9},{2,18},{3,11},{4,20},{5,13},{6,22},{7,15},{8,24},{9,1... | collective-permute-start | bytes 1327112 | tf_op jit(solution)/shard_map/ppermute | solution.py:535
  84.6 4.0 %collective-permute-start.34 = (bf16[4,3840]{1,0:T(4,128)(2,1)S(1)}, bf16[4,3840]{1,0:T(4,128)(2,1)S(1)}, u32[]{:S(2)}, u32[]{:S(2)}) collective-permute-start(bf16[4,3840]{1,0:T(4,128)(2,1)S(1)} %collective-permute-done.31.g2), channel_id=1, source_target_pairs={{0,2},{1,3},{2,0},{3,1},{4,6},{5,7},{6,4},{7,5},{8,10},{9,11},{10,... | collective-permute-start | bytes 92168 | tf_op jit(solution)/shard_map/ppermute | solution.py:535
  86.2 3.9 %collective-permute-start.33 = (bf16[4,3840]{1,0:T(4,128)(2,1)S(1)}, bf16[4,3840]{1,0:T(4,128)(2,1)S(1)}, u32[]{:S(2)}, u32[]{:S(2)}) collective-permute-start(bf16[4,3840]{1,0:T(4,128)(2,1)S(1)} %pad_maximum_fusion.2.g0), channel_id=1, source_target_pairs={{0,2},{1,3},{2,0},{3,1},{4,6},{5,7},{6,4},{7,5},{8,10},{9,11},{10,... | collective-permute-start | bytes 92168 | tf_op jit(solution)/shard_map/ppermute | solution.py:535
  92.5 6.3 %collective-permute-start.35 = (bf16[2,160,384]{2,1,0:T(8,128)(2,1)S(1)}, bf16[2,160,384]{2,1,0:T(8,128)(2,1)S(1)}, u32[]{:S(2)}, u32[]{:S(2)}) collective-permute-start(bf16[2,160,384]{2,1,0:T(8,128)(2,1)S(1)} %join_far.1), channel_id=1, source_target_pairs={{0,2},{1,3},{2,0},{3,1},{4,6},{5,7},{6,4},{7,5},{8,10},{9,11},{10,... | collective-permute-start | bytes 737288 | tf_op jit(solution)/shard_map/ppermute | solution.py:535
  93.9 5.5 %collective-permute-start.37 = (bf16[16,4224]{1,0:T(8,128)(2,1)S(1)}, bf16[16,4224]{1,0:T(8,128)(2,1)S(1)}, u32[]{:S(2)}, u32[]{:S(2)}) collective-permute-start(bf16[16,4224]{1,0:T(8,128)(2,1)S(1)} %pad_maximum_fusion.1.e0), channel_id=1, source_target_pairs={{0,8},{1,17},{2,10},{3,19},{4,12},{5,21},{6,14},{7,23},{8,0},{9,25... | collective-permute-start | bytes 405512 | tf_op jit(solution)/shard_map/ppermute | solution.py:535
  95.4 7.6 %collective-permute-start.38 = (bf16[16,4224]{1,0:T(8,128)(2,1)S(1)}, bf16[16,4224]{1,0:T(8,128)(2,1)S(1)}, u32[]{:S(2)}, u32[]{:S(2)}) collective-permute-start(bf16[16,4224]{1,0:T(8,128)(2,1)S(1)} %pad_maximum_fusion.1.e0), channel_id=1, source_target_pairs={{0,16},{1,9},{2,18},{3,11},{4,20},{5,13},{6,22},{7,15},{8,24},{9,1... | collective-permute-start | bytes 405512 | tf_op jit(solution)/shard_map/ppermute | solution.py:535
  98.7 18.7 %copy-start.17 = (bf16[2,384]{1,0:T(2,128)(2,1)S(1)}, bf16[2,384]{1,0:T(2,128)(2,1)}, u32[]{:S(2)}) copy-start(bf16[2,384]{1,0:T(2,128)(2,1)} %cond.1) | copy-start | bytes 4612
  99.4 5.1 %collective-permute-start.39 = (bf16[16,4224]{1,0:T(8,128)(2,1)S(1)}, bf16[16,4224]{1,0:T(8,128)(2,1)S(1)}, u32[]{:S(2)}, u32[]{:S(2)}) collective-permute-start(bf16[16,4224]{1,0:T(8,128)(2,1)S(1)} %collective-permute-done.37.e1), channel_id=1, source_target_pairs={{0,16},{1,9},{2,18},{3,11},{4,20},{5,13},{6,22},{7,15},{8,24},{9,1... | collective-permute-start | bytes 405512 | tf_op jit(solution)/shard_map/ppermute | solution.py:535
  100.6 7.2 %collective-permute-start.36 = (bf16[160,384]{1,0:T(8,128)(2,1)S(1)}, bf16[160,384]{1,0:T(8,128)(2,1)S(1)}, u32[]{:S(2)}, u32[]{:S(2)}) collective-permute-start(bf16[160,384]{1,0:T(8,128)(2,1)S(1)} %slice_bitcast_fusion.2), channel_id=1, source_target_pairs={{0,4},{1,5},{2,6},{3,7},{4,0},{5,1},{6,2},{7,3},{8,12},{9,13},{10,... | collective-permute-start | bytes 368648 | tf_op jit(solution)/shard_map/ppermute | solution.py:535
  107.8 4.9 %collective-permute-start.40 = (bf16[160,384]{1,0:T(8,128)(2,1)S(1)}, bf16[160,384]{1,0:T(8,128)(2,1)S(1)}, u32[]{:S(2)}, u32[]{:S(2)}) collective-permute-start(bf16[160,384]{1,0:T(8,128)(2,1)S(1)} %fusion.2.g0), channel_id=1, source_target_pairs={{0,8},{1,17},{2,10},{3,19},{4,12},{5,21},{6,14},{7,23},{8,0},{9,25... | collective-permute-start | bytes 368648 | tf_op jit(solution)/shard_map/ppermute | solution.py:535
  109.0 4.9 %collective-permute-start.41 = (bf16[160,384]{1,0:T(8,128)(2,1)S(1)}, bf16[160,384]{1,0:T(8,128)(2,1)S(1)}, u32[]{:S(2)}, u32[]{:S(2)}) collective-permute-start(bf16[160,384]{1,0:T(8,128)(2,1)S(1)} %fusion.2.g0), channel_id=1, source_target_pairs={{0,16},{1,9},{2,18},{3,11},{4,20},{5,13},{6,22},{7,15},{8,24},{9,1... | collective-permute-start | bytes 368648 | tf_op jit(solution)/shard_map/ppermute | solution.py:535
  113.9 3.5 %collective-permute-start.42 = (bf16[2,384]{1,0:T(2,128)(2,1)S(1)}, bf16[2,384]{1,0:T(2,128)(2,1)S(1)}, u32[]{:S(2)}, u32[]{:S(2)}) collective-permute-start(bf16[2,384]{1,0:T(2,128)(2,1)S(1)} %slice.109), channel_id=1, source_target_pairs={{0,1},{1,0},{2,3},{3,2},{4,5},{5,4},{6,7},{7,6},{8,9},{9,8},{10,11... | collective-permute-start | bytes 4616 | tf_op jit(solution)/shard_map/ppermute | solution.py:535
  116.4 4.9 %collective-permute-start.43 = (bf16[160,384]{1,0:T(8,128)(2,1)S(1)}, bf16[160,384]{1,0:T(8,128)(2,1)S(1)}, u32[]{:S(2)}, u32[]{:S(2)}) collective-permute-start(bf16[160,384]{1,0:T(8,128)(2,1)S(1)} %collective-permute-done.40.g1), channel_id=1, source_target_pairs={{0,16},{1,9},{2,18},{3,11},{4,20},{5,13},{6,22},{7,15},{8,24},{9,1... | collective-permute-start | bytes 368648 | tf_op jit(solution)/shard_map/ppermute | solution.py:535
  (14 other events, 89.0 us)

commit v3 on v2

--- a/solution.py
+++ b/solution.py
@@ -37,9 +37,6 @@
 
 def call(body, name, ids, ins, outs, scratch=(), flops=0, limit=48, far=()):
     fixed = [] if ids is None else [ids]
-    moved = sum(a.size * a.dtype.itemsize for a in ins) + sum(
-        jnp.dtype(t).itemsize * functools.reduce(lambda a, b: a * b, s, 1) for s, t in outs
-    )
     return pl.pallas_call(
         body,
         out_shape=[jax.ShapeDtypeStruct(s, t) for s, t in outs],
@@ -47,7 +44,7 @@
         out_specs=[vmem()] * len(outs),
         scratch_shapes=list(scratch),
         compiler_params=pltpu.CompilerParams(vmem_limit_bytes=limit * 1024 * 1024),
-        cost_estimate=pl.CostEstimate(flops=flops, bytes_accessed=moved, transcendentals=0),
+        cost_estimate=pl.CostEstimate(flops=1, bytes_accessed=1, transcendentals=0),
         name=name,
     )(*fixed, *ins)
 
@@ -108,9 +105,11 @@
     return jnp.where(c == r + shift, 1.0, 0.0).astype(BF16)
 
 
-def prepare_body(wmod_in, f0, f1, f2, f3, f4, wmod, placed):
+def prepare_body(wmod_own, wmod_other, f0, f1, f2, f3, f4, wmod, placed):
     f = lax.axis_index("fsdp")
-    wmod[...] = wmod_in[...]
+    shard = wmod_own.shape[0]
+    wmod[0:shard, :] = wmod_own[...]
+    wmod[shard:, :] = wmod_other[...]
     rows = []
     for ref in (f0, f1, f2, f3, f4):
         size = ref.shape[0]
@@ -122,23 +121,24 @@
     placed[2:3, :] = jnp.concatenate([b_out, b_down, jnp.zeros((1, 4 * feat), F32)], axis=1)
 
 
-def mod_body(ids, c_own, c_other, wmod, placed, keep_lo, keep_hi, send):
+def mod_body(ids, q0, q2, q1, q3, wmod, placed, placed_other, keep_lo, keep_hi, c_own):
     f = ids[1]
     rows, wide = wmod.shape
-    feat = c_own.shape[1]
-    slots = c_own.shape[0] // 4
+    slots, feat = c_own.shape[0] // 4, c_own.shape[1]
+    shard = rows // 2
+    at = q0.shape[0] - 16
     r = lax.broadcasted_iota(jnp.int32, (feat, rows), 0)
     c = lax.broadcasted_iota(jnp.int32, (feat, rows), 1)
-    select = jnp.where(r == c + f * rows, 1.0, 0.0).astype(BF16)
-    stacked = jnp.concatenate([c_own[...].astype(F32), c_other[...].astype(F32)], axis=0)
-    own = dot(stacked.astype(BF16), select).astype(BF16)
-    part = dot(own, wmod[...]) + placed[0:1, :]
+    start = jnp.where(c < shard, f * shard, flip(f, 1) * shard - shard)
+    select = jnp.where(r == c + start, 1.0, 0.0).astype(BF16)
+    stacked = jnp.concatenate([ref[at : at + slots, :] for ref in (q0, q2, q1, q3)], axis=0)
+    c_own[...] = stacked
+    bias = placed[...] + placed_other[...]
+    part = dot(dot(stacked, select).astype(BF16), wmod[...]) + bias[0:1]
     for n in range(4):
         keep = (keep_lo, keep_lo, keep_hi, keep_hi)[n]
         keep[n % 2, 0:slots, :] = part[slots * n : slots * (n + 1)]
-        send[n, 0:slots, :] = part[slots * (n + 4) : slots * (n + 5)]
-        keep[n % 2, 2:4, :] = placed[1:3, :]
-        send[n, 2:4, :] = placed[1:3, :]
+        keep[n % 2, 2:4, :] = bias[1:3]
 
 
 def norm_parts(x):
@@ -157,10 +157,10 @@
     ids, *refs,
 ):
     d, f, mine, theirs = offsets(ids)
-    pieces, (m_proj, m_out, o_proj, o_out, p0, p1, lat, wpo, mod, n1, proj, att) = refs[:16], refs[16:]
+    pieces, (m_proj, m_out, o_proj, o_out, p0, p1, lat, wpo, mod, n1, proj, att) = refs[:8], refs[8:]
     rows, feat = m_out.shape
     whole = ((m_proj, m_out), (o_proj, o_out))
-    split = (pieces[:8], mine, f), (pieces[8:], theirs, flip(f, 1))
+    split = (pieces[:4], mine, f), (pieces[4:], theirs, flip(f, 1))
     for (p_ref, o_ref), (found, flips, base) in zip(whole, split):
         at = pl.multiple_of(base * rows, 16)
         for block in range(3):
@@ -168,7 +168,8 @@
         wpo[3, pl.ds(at, rows), :] = o_ref[...]
         for n, how in enumerate(flips):
             block = flip(d, how)
-            for zm, get in ((2, found[n]), (1, found[4 + n].at[0]), (3, found[4 + n].at[1])):
+            for place, zm in enumerate(LEVELS[1:]):
+                get = found[n].at[place]
                 at = pl.multiple_of(flip(base, 2 * zm) * rows, 16)
                 wpo[block, pl.ds(at, rows), :] = get[0:rows, :]
     mod[...] = p0[0] + p1[...]
@@ -226,7 +227,7 @@
 def mlp_body(
     ids, *refs,
 ):
-    mlp_steps(ids, refs[:16], *refs[16:])
+    mlp_steps(ids, refs[:8], *refs[8:])
 
 
 def mlp_steps(
@@ -239,20 +240,22 @@
     rows, feat = m_up.shape[0], m_down.shape[1]
     hidden = wd.shape[0]
     blocks = hidden // feat
+    step = 512
     whole = ((m_up, m_down), (o_up, o_down))
-    split = (pieces[:8], mine, f), (pieces[8:], theirs, flip(f, 1))
+    split = (pieces[:4], mine, f), (pieces[4:], theirs, flip(f, 1))
     for (u_ref, d_ref), (found, flips, base) in zip(whole, split):
         at = pl.multiple_of(base * rows, 16)
-        for block in range(blocks):
-            wu[block, pl.ds(at, rows), :] = u_ref[:, block * feat : (block + 1) * feat]
+        wu[pl.ds(at, rows), :] = u_ref[...]
         wd[pl.ds(pl.multiple_of(base * 4 * rows, 16), 4 * rows), :] = d_ref[...]
         for n, how in enumerate(flips):
             block = flip(d, how)
-            for zm, get in ((2, found[n]), (1, found[4 + n].at[0]), (3, found[4 + n].at[1])):
+            for place, zm in enumerate(LEVELS[1:]):
+                get = found[n].at[place]
                 owner = flip(base, 2 * zm)
-                wu[block, pl.ds(pl.multiple_of(owner * rows, 16), rows), :] = get[
-                    rows : 2 * rows, :
-                ]
+                wu[
+                    pl.ds(pl.multiple_of(owner * rows, 16), rows),
+                    pl.ds(pl.multiple_of(block * feat, 128), feat),
+                ] = get[rows : 2 * rows, :]
                 at = pl.multiple_of((owner * 4 + block) * rows, 16)
                 wd[pl.ds(at, rows), :] = get[2 * rows : 3 * rows, :]
     length = lat.shape[1]
@@ -273,15 +276,14 @@
         n2 = (xhat * (1.0 + scale) + shift).astype(BF16)
         n2s[part, :] = n2
         mlp = jnp.zeros((length, feat), F32) + bdown
-        for j in range(blocks):
-            cols = slice(j * feat, (j + 1) * feat)
-            v = dot(n2, wu[j]) + bup[:, cols]
-            t = jnp.tanh(0.7978845608028654 * (v + 0.044715 * v * v * v))
-            half = 0.5 * (1.0 + t)
+        for j in range(0, hidden, step):
+            cols = slice(j, j + step)
+            v = dot(n2, wu[:, cols]) + bup[:, cols]
+            square = v * v
+            half = 0.5 + 0.5 * jnp.tanh(v * (0.7978845608028654 + 0.035677408136300125 * square))
             act = (v * half).astype(BF16)
-            dgs[:, cols] = half + 0.5 * v * (1.0 - t * t) * (
-                0.7978845608028654 * (1.0 + 0.134145 * v * v)
-            )
+            slope = v * (1.5957691216057308 + 0.21406444881780075 * square)
+            dgs[:, cols] = half * (1.0 + (1.0 - half) * slope)
             acts[part, cols] = act
             mlp = mlp + dot(act, wd[cols, :])
         res[i] = (alive * (middle + gate_two * mlp)).astype(BF16)
@@ -290,14 +292,12 @@
         gmlp = (gate_two * upstream).astype(BF16)
         gmlps[part, :] = gmlp
         gn = jnp.zeros((length, feat), F32)
-        for j in range(blocks):
-            cols = slice(j * feat, (j + 1) * feat)
+        for j in range(0, hidden, step):
+            cols = slice(j, j + step)
             gpre = (dot(gmlp, wd[cols, :], NT) * dgs[:, cols]).astype(BF16)
             gpres[part, cols] = gpre
-            gn = gn + dot(gpre, wu[j], NT)
-            gsum[:, feat + j * feat : 2 * feat + j * feat] += jnp.sum(
-                gpre.astype(F32), axis=0, keepdims=True
-            )
+            gn = gn + dot(gpre, wu[:, cols], NT)
+            gsum[:, feat + j : feat + j + step] += jnp.sum(gpre.astype(F32), axis=0, keepdims=True)
         g_shift = jnp.sum(gn, axis=0, keepdims=True)
         g_scale = jnp.sum(gn * xhat, axis=0, keepdims=True)
         gx = gn * (1.0 + scale)
@@ -318,30 +318,24 @@
 
     lax.fori_loop(0, lat.shape[0], one, 0)
     pieces = (k_odd, k_even, s_odd, s_even)
-    for j in range(blocks):
-        cols = slice(j * feat, (j + 1) * feat)
+    n2t[...] = n2s[...].T
+    for j in range(0, hidden, step):
+        cols = slice(j, j + step)
         tmpd[cols, :] = dot(acts[:, cols], gmlps[...], TN).astype(BF16)
-    n2t[...] = n2s[...].T
-    for dm in (1, 3, 0, 2):
+        tmp[:, cols] = dot(n2t[...], gpres[:, cols]).astype(BF16)
+    for dm in range(4):
         block = flip(d, mine[dm])
         spread(tmpd, lambda o: (o * 4 + block) * rows, dm, pieces, rows, f, 1)
-        tmp[...] = dot(
-            n2t[...], gpres[:, pl.ds(pl.multiple_of(block * feat, 128), feat)]
-        ).astype(BF16)
-        spread(tmp, lambda o: o * rows, dm, pieces, rows, f, 0)
-
-
-def attend_back_body(
-    ids, proj, gatt, att, gbr, n1, gsum, gproj, bias, k_odd, k_even, s_odd, s_even,
-    gall, xts, tmp, *, length,
-):
-    d, f, mine, _ = offsets(ids)
-    feat = att.shape[1]
-    rows = k_odd.shape[2]
+        cut = pl.ds(pl.multiple_of(block * feat, 128), feat)
+        spread(tmp.at[:, cut], lambda o: o * rows, dm, pieces, rows, f, 0)
+
+
+def attend_back_one(proj, gatt, gall, i, length):
+    feat = gatt.shape[1]
     low_half = lane_masks(length)
 
     def one(i, carry):
-        part = pl.ds(pl.multiple_of(i * length, 256), length)
+        part = slice(i * length, (i + 1) * length)
         for pair in range(HEADS // 2):
             lo = pair * 2 * HEAD_DIM
             hi = lo + 2 * HEAD_DIM
@@ -372,7 +366,23 @@
             gall[part, 2 * feat + lo : 2 * feat + hi] = gv.astype(BF16)
         return carry
 
-    lax.fori_loop(0, proj.shape[0] // length, one, 0)
+    one(i, 0)
+
+
+def attend_back_first_body(proj, gatt, gproj, *, length):
+    attend_back_one(proj, gatt, gproj, 0, length)
+
+
+def attend_back_body(
+    ids, proj, gatt, att, gbr, n1, gsum, g_first, gproj, bias, k_odd, k_even, s_odd, s_even,
+    gall, xts, tmp, *, length,
+):
+    d, f, mine, _ = offsets(ids)
+    feat = att.shape[1]
+    rows = k_odd.shape[2]
+    gall[0:length, : 3 * feat] = g_first[...]
+    for i in range(1, proj.shape[0] // length):
+        attend_back_one(proj, gatt, gall, i, length)
     gproj[...] = gall[:, : 3 * feat]
     gall[:, 3 * feat :] = gbr[...]
     xts[0] = n1[...].T
@@ -437,7 +447,7 @@
         out[at, 0 : part.shape[0], :] = dot(part, place).astype(BF16)
 
 
-def mod_weight_body(ids, e0, e1, e2, e3, wgrad, bgrad):
+def mod_weight_body(ids, e0, e1, e2, e3, wgrad, b_mod, b_qv, b_out, b_up, b_down):
     f = ids[1]
     rows, wide = wgrad.shape
     feat = wide // 6
@@ -454,34 +464,55 @@
     wgrad[...] = total
     low = sums[:, wide:]
     odd = lax.broadcasted_iota(jnp.int32, low.shape, 0) % 2 == 1
-    bgrad[:, :wide] = jnp.sum(sums[:, :wide], axis=0, keepdims=True)
-    bgrad[:, wide : wide + 4 * feat] = jnp.sum(jnp.where(odd, 0.0, low), axis=0, keepdims=True)
-    bgrad[:, wide + 4 * feat :] = jnp.sum(jnp.where(odd, low, 0.0), axis=0, keepdims=True)
-
-
-def merge_body(ids, keep_ud, got_ud, keep_po, got_po, out):
+    even_sum = jnp.sum(jnp.where(odd, 0.0, low), axis=0, keepdims=True)
+    odd_sum = jnp.sum(jnp.where(odd, low, 0.0), axis=0, keepdims=True)
+    whole = jnp.concatenate([jnp.sum(sums[:, :wide], axis=0, keepdims=True), even_sum, odd_sum], axis=1)
+    at = 0
+    for out in (b_mod, b_qv, b_out, b_up, b_down):
+        size = out.shape[0]
+        vector = jnp.broadcast_to(whole[:, at : at + 8 * size], (8, 8 * size))
+        out[...] = pltpu.roll(vector, lax.rem(8 - f, 8) * size, 1)[0, :size]
+        at += 8 * size
+
+
+def sum_body(keep, got, out):
+    out[...] = add_low(keep[...], got[...])
+
+
+def turn_body(keep_ud, in_ud, keep_po, in_po, got_ud, got_po, out, *, at):
     rows = keep_po.shape[2]
-    for at in range(out.shape[0]):
-        for place in range(out.shape[1]):
-            out[at, place, 0:rows] = add_low(keep_po[at, place], got_po[at, place])
-            for slot in range(2):
-                out[at, place, (1 + slot) * rows : (2 + slot) * rows] = add_low(
-                    keep_ud[at, place, slot], got_ud[at, place, slot]
-                )
-
-
-def join_far_body(ids, base, part, back, out):
+    for place in range(out.shape[0]):
+        out[place, 0:rows] = add_low(keep_po[at, place], in_po[at, place], got_po[at, place])
+        for slot in range(2):
+            out[place, (1 + slot) * rows : (2 + slot) * rows] = add_low(
+                keep_ud[at, place, slot], in_ud[at, place, slot], got_ud[at, place, slot]
+            )
+
+
+def pair_body(own, other, out):
+    out[0 : own.shape[0], :] = own[...]
+    out[own.shape[0] :, :] = other[...]
+
+
+def pack_body(g0, g2, g1, g3, c_own, c_other, out):
+    many, wide = g0.shape
+    half = many // 2
+    for n, ref in enumerate((g0, g2, g1, g3)):
+        out[many * n : many * (n + 1), 0:wide] = ref[...]
+        out[many * n : many * n + half, wide:] = c_own[half * n : half * (n + 1), :]
+        out[many * n + half : many * (n + 1), wide:] = c_other[half * n : half * (n + 1), :]
+
+
+def join_far_body(base, part, back, out):
     size = base.shape[1]
-    for at in range(2):
-        out[at, 0:size] = add_low(base[2 + at], part[2 + at])
-        out[at, size:] = back[at]
-
-
-def join_near_body(ids, base, part, back, got, out):
+    out[:, 0:size] = add_low(base[2:], part[2:])
+    out[:, size:] = back[...]
+
+
+def join_near_body(base, part, back, got, out):
     size = base.shape[1]
-    for at in range(2):
-        out[at, 0:size] = add_low(base[at], part[at], got[at, 0:size])
-        out[at, size:] = add_low(back[at], got[at, size:])
+    out[:, 0:size] = add_low(base[:2], part[:2], got[:, 0:size])
+    out[:, size:] = add_low(back[...], got[:, size:])
 
 
 def final_body(ids, g0, g1, g2, g3, gp, go, gu, gd):
@@ -504,7 +535,7 @@
 
 
 def routes():
-    core, first, second = [], [], []
+    core, first, second, across = [], [], [], []
     levels = {1: [], 2: []}
     for d in range(4):
         for f in range(8):
@@ -513,9 +544,10 @@
             a = 1 if f % 2 == 0 else 2
             first.append((i, (d ^ a) * 8 + f))
             second.append((i, (d ^ (3 - a)) * 8 + f))
+            across.append((i, (d ^ 3) * 8 + f))
             for m in levels:
                 levels[m].append((i, d * 8 + (f ^ (2 * m))))
-    return core, first, second, levels
+    return core, first, second, across, levels
 
 
 def add_low(*parts):
@@ -529,7 +561,7 @@
     latents, cond, counts, cotangent, modulation_weight, modulation_bias, projection_weight,
     query_value_bias, output_weight, output_bias, up_weight, up_bias, down_weight, down_bias,
 ):
-    core, first, second, levels = routes()
+    core, first, second, across, levels = routes()
 
     def move(x, route):
         return lax.ppermute(x, BOTH, route)
@@ -563,32 +595,26 @@
     w_whole = whole + [move(x, core) for x in whole]
     biases = [modulation_bias, query_value_bias, output_bias, up_bias, down_bias]
     wmod, placed = call(
-        prepare_body, "prepare", None, [modulation_weight] + biases,
-        [((rows, wide), BF16), ((3, wide), F32)],
+        prepare_body, "prepare", None, [modulation_weight, move(modulation_weight, core)] + biases,
+        [((2 * rows, wide), BF16), ((3, wide), F32)],
     )
     q_far = move(q_all, levels[2])
-    ready = (placed, *w_whole[4:])
-    q_near = move(after(q_all, q_far, *ready), levels[1])
-    q_both = move(after(q_far, *ready), levels[1])
-    a_far, b_far = move(q_far, first), move(q_far, second)
-    c_own = [x[3 * rows : 3 * rows + slots] for x in (q_all, q_far, q_near, q_both)]
-    c_own = after(jnp.concatenate(c_own), a_far, b_far)
-    c_other = move(c_own, core)
-    near = jnp.stack([q_near[: 3 * rows], q_both[: 3 * rows]])
-    keep_lo, keep_hi, sent = call(
-        mod_body, "modulation", ids, [c_own, c_other, wmod, placed],
-        [((2, 4, wide), F32)] * 2 + [((4, 4, wide), F32)],
-    )
-    ab_far = move(a_far, second)
-    got = after(move(sent, core), ab_far)
-    paid_hi = keep_hi + got[2:]
-    paid_lo = keep_lo + got[:2]
-    paid_lo = paid_lo + move(paid_hi, levels[1])
-    paid_far = move(paid_lo[1], levels[2])
-    a_near, b_near = move(near, first), move(near, second)
-    ab_near = move(after(a_near, paid_far), second)
-    w_all = [q_far, a_far, b_far, ab_far, near, a_near, b_near, ab_near]
-    w_all = w_all + [move(x, core) for x in w_all]
+    placed_other = move(placed, core)
+    ready = (placed_other, *w_whole[4:])
+    q_far = after(q_far, *ready)
+    q_near, q_both = move(after(q_all, q_far), levels[1]), move(q_far, levels[1])
+    own = jnp.stack([q_far, q_near, q_both])
+    keep_lo, keep_hi, c_own = call(
+        mod_body, "modulation", ids, [q_all, q_far, q_near, q_both, wmod, placed, placed_other],
+        [((2, 4, wide), F32)] * 2 + [((4 * slots, feat), BF16)],
+    )
+    a_own, b_own = move(own, first), move(own, second)
+    paid_lo = keep_lo + move(keep_hi, levels[1])
+    a_own = after(a_own, paid_lo)
+    paid_far = move(after(paid_lo[1], a_own), levels[2])
+    ab_own = move(a_own, second)
+    w_all = [own, a_own, b_own, ab_own]
+    w_all = w_all + [move(x, core) for x in w_all[:3]] + [move(after(ab_own, paid_far), core)]
 
     wpo, mod, n1, proj, att = call(
         attend_body, "attention", ids,
@@ -606,88 +632,77 @@
         [((slots, length, feat), BF16), ((slots, length, feat), F32), ((tokens, feat), BF16),
          ((tokens, feat), BF16), ((1, 6 * feat), F32), ((slots, 4 * feat), F32)] + [ud_shape] * 4,
         [
-            pltpu.VMEM((4, feat, feat), BF16), pltpu.VMEM((hidden, feat), BF16),
+            pltpu.VMEM((feat, hidden), BF16), pltpu.VMEM((hidden, feat), BF16),
             pltpu.VMEM((tokens, feat), BF16), pltpu.VMEM((tokens, hidden), BF16),
             pltpu.VMEM((length, hidden), F32), pltpu.VMEM((tokens, feat), BF16),
             pltpu.VMEM((tokens, hidden), BF16), pltpu.VMEM((feat, tokens), BF16),
-            pltpu.VMEM((feat, feat), BF16), pltpu.VMEM((hidden, feat), BF16),
+            pltpu.VMEM((feat, hidden), BF16), pltpu.VMEM((hidden, feat), BF16),
         ],
         flops=2 * tokens * feat * (6 * hidden + 2 * feat),
     )
     ud_odd_in = move(ud_odd_out, core)
     ud_even_in = move(ud_even_out, core)
+    (g_first,) = call(
+        functools.partial(attend_back_first_body, length=length), "attention_back_first", None,
+        [proj, gatt], [((length, 3 * feat), BF16)], flops=tokens * feat * 10 * length,
+    )
+    (odd_ud,) = call(sum_body, "sum_ud", None, [ud_odd, after(ud_odd_in, g_first)], [ud_shape])
+    got_ud = move(odd_ud, first)
     gproj, bias, po_odd, po_even, po_odd_out, po_even_out = call(
         functools.partial(attend_back_body, length=length), "attention_back", ids,
-        [proj, gatt, att, gbr, n1, gsum],
+        [proj, gatt, att, gbr, n1, gsum, after(g_first, odd_ud)],
         [((tokens, 3 * feat), BF16), ((1, 8 * feat), F32)] + [po_shape] * 4,
         [pltpu.VMEM((tokens, 4 * feat), BF16), pltpu.VMEM((2, feat, tokens), BF16),
          pltpu.VMEM((feat, feat), BF16)],
-        flops=2 * tokens * feat * (4 * feat + 10 * length),
+        flops=2 * tokens * feat * (4 * feat + 5 * length),
     )
     po_odd_in = move(po_odd_out, core)
     po_even_in = move(po_even_out, core)
-    all_shape = ((2, 4, 3 * rows, feat), BF16)
-    (odd,) = call(merge_body, "merge_odd", ids, [ud_odd, ud_odd_in, po_odd, po_odd_in], [all_shape])
-    got = move(odd, first)
-    (even,) = call(
-        merge_body, "merge_even", ids, [ud_even, ud_even_in, po_even, po_even_in], [all_shape]
-    )
     lgrad, gm = call(
-        input_back_body, "input_back", ids, [after(gproj, even), wpo, latents, gmid, mod, gmod, bias],
+        input_back_body, "input_back", ids,
+        [gproj, wpo, latents, gmid, mod, gmod, bias],
         [((slots, length, feat), BF16), ((slots, 10 * feat), BF16)],
         [pltpu.VMEM((slots, 10 * feat), F32)],
         flops=2 * tokens * feat * 3 * feat,
     )
-
-    gm_pair = jnp.concatenate([gm, move(gm, core)], axis=0)
+    (odd_po,) = call(sum_body, "sum_po", None, [po_odd, after(po_odd_in, gm, got_ud)], [po_shape])
+    got_po = move(odd_po, first)
+    c_other = move(c_own, core)
+
+    (gm_pair,) = call(pair_body, "pair", None, [after(gm, c_other), move(gm, core)], [((2 * slots, 10 * feat), BF16)])
     gm_far = move(gm_pair, levels[2])
-    turned = add_low(even[1], after(got[1], gm_far))
-    gm_all = [
-        gm_pair, gm_far,
-        move(after(gm_pair, turned), levels[1]), move(after(gm_far, turned), levels[1]),
-    ]
+
+    halves = [ud_even, ud_even_in, po_even, po_even_in, got_ud, after(got_po, gm_far)]
+    half_shape = ((4, 3 * rows, feat), BF16)
+    (turned,) = call(functools.partial(turn_body, at=1), "turn", None, halves, [half_shape])
     part = move(turned, second)
-    base = add_low(even[0], got[0])
-    every = jnp.concatenate(
-        [
-            jnp.concatenate(gm_all, axis=0),
-            jnp.concatenate(
-                [x[slots * n : slots * (n + 1)] for n in range(4) for x in (c_own, c_other)]
-            ),
-        ],
-        axis=1,
+    (base,) = call(
+        functools.partial(turn_body, at=0), "base", None, halves[:5] + [after(got_po, turned)], [half_shape]
+    )
+
+    gm_all = [gm_pair, gm_far, move(after(gm_pair, gm_far), levels[1]), move(gm_far, levels[1])]
+    (every,) = call(
+        pack_body, "pack", None, gm_all + [c_own, c_other], [((8 * slots, 11 * feat), BF16)]
     )
     back_lo, back_hi = call(
-        cond_back_body, "cond_back", ids, gm_all + [modulation_weight],
-        [((2, 16, feat), BF16)] * 2,
+        cond_back_body, "cond_back", ids, gm_all + [modulation_weight], [((2, 16, feat), BF16)] * 2
     )
 
     pair_shape = ((2, 3 * rows + 16, feat), BF16)
-    (turned,) = call(join_far_body, "join_far", ids, [base, part, back_hi], [pair_shape])
+    (turned,) = call(join_far_body, "join_far", None, [base, part, back_hi], [pair_shape])
     got = move(turned, levels[1])
     every = after(every, turned)
-    e_first, e_second = move(every, first), move(every, second)
-    (base,) = call(join_near_body, "join_near", ids, [base, part, back_lo, got], [pair_shape])
-    e_both = move(after(e_first, base), second)
-    g_mod_weight, sums = call(
+    e_first, e_second, e_both = move(every, first), move(every, second), move(every, across)
+    (base,) = call(join_near_body, "join_near", None, [base, part, back_lo, got], [pair_shape])
+    g_mod_weight, *g_biases = call(
         mod_weight_body, "mod_weight", ids, [every, e_first, e_second, e_both],
-        [((rows, wide), F32), ((1, wide + 8 * feat), F32)],
+        [((rows, wide), F32)] + [((size // 8,), F32) for size in (wide, 2 * feat, feat, hidden, feat)],
     )
     total = add_low(base[0], after(move(base[1], levels[2]), g_mod_weight))
     a_total, b_total = move(total, first), move(total, second)
-    sums = after(sums[0], total)
-
-    def share(at, size):
-        size = size // 8
-        return lax.dynamic_slice_in_dim(sums, at + f * size, size)
-
-    g_biases = [
-        share(0, wide), share(wide, 2 * feat), share(wide + 2 * feat, feat),
-        share(wide + 3 * feat, hidden), share(wide + 7 * feat, feat),
-    ]
-    shares = [total, a_total, b_total, move(after(a_total, *g_biases), second)]
+    shares = [total, a_total, b_total, move(a_total, second)]
     silu_pair = total[3 * rows : 3 * rows + 2 * slots].astype(F32)
-    silu_other = after(total, a_total, b_total)[3 * rows + slots : 3 * rows + 2 * slots]
+    silu_other = after(total, b_total)[3 * rows + slots : 3 * rows + 2 * slots]
     grad_silu = silu_pair[:slots] + move(silu_other, core).astype(F32)
     cond_full = cond.astype(F32)
     sig = 1.0 / (1.0 + jnp.exp(-cond_full))

time: 123 us -> 114 us (0.927)
  local copies, waits for them, and re-layouts: 8.15 us -> 4.35 us
  Pallas kernels: 37.4 us -> 34.4 us
  waiting for transfers between devices: 34.6 us -> 32.6 us
    pallas_call x14 -> x19, Pallas kernels: 37.4 us -> 34.4 us  [call(): pl.pallas_call(body, out_shape=[jax.ShapeDtypeStruct(s, t) for s, t in ou...]
    dynamic_slice x4 -> x0, local copies, waits for them, and re-layouts: 2.47 us -> none  [share(): return lax.dynamic_slice_in_dim(sums, at + f * size, size)]
    ppermute x44 -> x39, waiting for transfers between devices: 34.6 us -> 32.6 us  [move(): return lax.ppermute(x, BOTH, route)]
    unnamed x36 -> x40, local copies, waits for them, and re-layouts: 4.65 us -> 4.29 us
    ppermute x44 -> x39, starting transfers between devices: 39.9 us -> 39.7 us  [move(): return lax.ppermute(x, BOTH, route)]
  transfers between devices with their start and end apart: 44 -> 39, of which waited for: 24 -> 18; matrix products, arithmetic and copies ran while one was open for 4% -> 1% of each run, Pallas kernels for 15% -> 15%
where the time goes in v3:
time: 114 us; the launch traced here: 113 us
  starting transfers between devices  39.7 us (35%)
  Pallas kernels  34.4 us (30%)
  waiting for transfers between devices  32.6 us (29%)
  local copies, waits for them, and re-layouts  4.35 us (4%)
  between operations  1.58 us (1%)
    ppermute x39, starting transfers between devices, move(): return lax.ppermute(x, BOTH, route)  39.7 us
    pallas_call x19, Pallas kernels, call(): pl.pallas_call(body, out_shape=[jax.ShapeDtypeStruct(s, t) for s, t in ou...  34.4 us
    ppermute x39, waiting for transfers between devices, move(): return lax.ppermute(x, BOTH, route)  32.6 us
    unnamed x40, local copies, waits for them, and re-layouts  4.29 us
  transfers between devices with their start and end apart: 39, of which 18 were waited for; matrix products, arithmetic and copies ran while one was open for 1% of the time, Pallas kernels for 15%

profile of v3, /device:TPU:0, one launch (start us, length us, event | category | flops | bytes accessed | tf_op | source)
XLA Modules:
  0.0 113.5 jit_solution(14003940230179366230)
XLA Ops:
  1.7 1.6 %pick.1.q0 = bf16[160,384]{1,0:T(8,128)(2,1)} custom-call(bf16[48,1152]{1,0:T(8,128)(2,1)} %refs_8_.2, bf16[48,384]{1,0:T(8,128)(2,1)} %refs_9_.2, bf16[48,1536]{1,0:T(8,128)(2,1)} %refs_8_.3, bf16[192,384]{1,0:T(8,128)(2,1)} %refs_9_.3, bf16[2,384]{1,0:T(2,128)(2,1)} %cond.1), custom_call_target="tpu_custom_call" | custom-call | flops 1 | bytes 1 | tf_op jit(solution)/shard_map/pick/pallas_call | solution.py:40
  3.3 3.7 %collective-permute-start = (bf16[160,384]{1,0:T(8,128)(2,1)}, bf16[160,384]{1,0:T(8,128)(2,1)S(1)}, u32[]{:S(2)}, u32[]{:S(2)}) collective-permute-start(bf16[160,384]{1,0:T(8,128)(2,1)} %pick.1.q0), channel_id=1, source_target_pairs={{0,4},{1,5},{2,6},{3,7},{4,0},{5,1},{6,2},{7,3},{8,12},{9,13},{10,... | collective-permute-start | bytes 368648 | tf_op jit(solution)/shard_map/ppermute | solution.py:567
  7.5 0.9 copy-done.3
  8.4 0.7 copy-done.13
  12.5 1.3 %collective-permute-done.q2 = bf16[160,384]{1,0:T(8,128)(2,1)S(1)} collective-permute-done((bf16[160,384]{1,0:T(8,128)(2,1)}, bf16[160,384]{1,0:T(8,128)(2,1)S(1)}, u32[]{:S(2)}, u32[]{:S(2)}) %collective-permute-start) | collective-permute-done | bytes 122912 | tf_op jit(solution)/shard_map/ppermute | solution.py:567
  13.8 1.4 %collective-permute-start.7 = (bf16[160,384]{1,0:T(8,128)(2,1)}, bf16[160,384]{1,0:T(8,128)(2,1)S(1)}, u32[]{:S(2)}, u32[]{:S(2)}) collective-permute-start(bf16[160,384]{1,0:T(8,128)(2,1)} %pick.1.q0), channel_id=1, source_target_pairs={{0,2},{1,3},{2,0},{3,1},{4,6},{5,7},{6,4},{7,5},{8,10},{9,11},{10,... | collective-permute-start | bytes 368648 | tf_op jit(solution)/shard_map/ppermute | solution.py:567
  15.1 0.7 collective-permute-start.8
  15.9 4.4 %collective-permute-done.7.q1 = bf16[160,384]{1,0:T(8,128)(2,1)S(1)} collective-permute-done((bf16[160,384]{1,0:T(8,128)(2,1)}, bf16[160,384]{1,0:T(8,128)(2,1)S(1)}, u32[]{:S(2)}, u32[]{:S(2)}) %collective-permute-start.7) | collective-permute-done | bytes 122912 | tf_op jit(solution)/shard_map/ppermute | solution.py:567
  20.2 1.5 %collective-permute-done.8.q3 = bf16[160,384]{1,0:T(8,128)(2,1)S(1)} collective-permute-done((bf16[160,384]{1,0:T(8,128)(2,1)S(1)}, bf16[160,384]{1,0:T(8,128)(2,1)S(1)}, u32[]{:S(2)}, u32[]{:S(2)}) %collective-permute-start.8) | collective-permute-done | bytes 122912 | tf_op jit(solution)/shard_map/ppermute | solution.py:567
  21.8 1.6 %collective-permute-start.9 = (bf16[3,160,384]{2,1,0:T(8,128)(2,1)S(1)}, bf16[3,160,384]{2,1,0:T(8,128)(2,1)S(1)}, u32[]{:S(2)}, u32[]{:S(2)}) collective-permute-start(bf16[3,160,384]{2,1,0:T(8,128)(2,1)S(1)} %pad_maximum_fusion.refs_0_), channel_id=1, source_target_pairs={{0,8},{1,17},{2,10},{3,19},{4,12},{5,21},{6,14},{7,23},{8,0},{9,25... | collective-permute-start | bytes 1105928 | tf_op jit(solution)/shard_map/ppermute | solution.py:567
  24.1 0.9 modulation.1
  25.0 1.6 %collective-permute-start.10 = (f32[2,4,2304]{2,1,0:T(4,128)S(1)}, f32[2,4,2304]{2,1,0:T(4,128)S(1)}, u32[]{:S(2)}, u32[]{:S(2)}) collective-permute-start(f32[2,4,2304]{2,1,0:T(4,128)S(1)} %get-tuple-element.73), channel_id=1, source_target_pairs={{0,2},{1,3},{2,0},{3,1},{4,6},{5,7},{6,4},{7,5},{8,10},{9,11},{10,... | collective-permute-start | bytes 221192 | tf_op jit(solution)/shard_map/ppermute | solution.py:567
  26.6 1.5 %collective-permute-start.11 = (bf16[3,160,384]{2,1,0:T(8,128)(2,1)S(1)}, bf16[3,160,384]{2,1,0:T(8,128)(2,1)S(1)}, u32[]{:S(2)}, u32[]{:S(2)}) collective-permute-start(bf16[3,160,384]{2,1,0:T(8,128)(2,1)S(1)} %pad_maximum_fusion.refs_0_), channel_id=1, source_target_pairs={{0,16},{1,9},{2,18},{3,11},{4,20},{5,13},{6,22},{7,15},{8,24},{9,1... | collective-permute-start | bytes 1105928 | tf_op jit(solution)/shard_map/ppermute | solution.py:567
  28.1 1.3 %collective-permute-done.10 = f32[2,4,2304]{2,1,0:T(4,128)S(1)} collective-permute-done((f32[2,4,2304]{2,1,0:T(4,128)S(1)}, f32[2,4,2304]{2,1,0:T(4,128)S(1)}, u32[]{:S(2)}, u32[]{:S(2)}) %collective-permute-start.10) | collective-permute-done | bytes 73760 | tf_op jit(solution)/shard_map/ppermute | solution.py:567
  29.4 1.3 %collective-permute-done.9.refs_1_ = bf16[3,160,384]{2,1,0:T(8,128)(2,1)S(1)} collective-permute-done((bf16[3,160,384]{2,1,0:T(8,128)(2,1)S(1)}, bf16[3,160,384]{2,1,0:T(8,128)(2,1)S(1)}, u32[]{:S(2)}, u32[]{:S(2)}) %collective-permute-start.9) | collective-permute-done | bytes 368672 | tf_op jit(solution)/shard_map/ppermute | solution.py:567
  30.7 2.5 %collective-permute-start.12 = (bf16[3,160,384]{2,1,0:T(8,128)(2,1)S(1)}, bf16[3,160,384]{2,1,0:T(8,128)(2,1)S(1)}, u32[]{:S(2)}, u32[]{:S(2)}) collective-permute-start(bf16[3,160,384]{2,1,0:T(8,128)(2,1)S(1)} %collective-permute-done.9.refs_1_), channel_id=1, source_target_pairs={{0,16},{1,9},{2,18},{3,11},{4,20},{5,13},{6,22},{7,15},{8,24},{9,1... | collective-permute-start | bytes 1105928 | tf_op jit(solution)/shard_map/ppermute | solution.py:567
  33.3 2.6 %collective-permute-start.16 = (f32[4,2304]{1,0:T(4,128)S(1)}, f32[4,2304]{1,0:T(4,128)S(1)}, u32[]{:S(2)}, u32[]{:S(2)}) collective-permute-start(f32[4,2304]{1,0:T(4,128)S(1)} %slice_bitcast_fusion.2), channel_id=1, source_target_pairs={{0,4},{1,5},{2,6},{3,7},{4,0},{5,1},{6,2},{7,3},{8,12},{9,13},{10,... | collective-permute-start | bytes 110600 | tf_op jit(solution)/shard_map/ppermute | solution.py:567
  36.4 1.8 %collective-permute-done.16.refs_13_ = f32[4,2304]{1,0:T(4,128)S(1)} collective-permute-done((f32[4,2304]{1,0:T(4,128)S(1)}, f32[4,2304]{1,0:T(4,128)S(1)}, u32[]{:S(2)}, u32[]{:S(2)}) %collective-permute-start.16) | collective-permute-done | bytes 36896 | tf_op jit(solution)/shard_map/ppermute | solution.py:567
  38.8 1.7 %collective-permute-done.17.refs_7_ = bf16[3,160,384]{2,1,0:T(8,128)(2,1)S(1)} collective-permute-done((bf16[3,160,384]{2,1,0:T(8,128)(2,1)S(1)}, bf16[3,160,384]{2,1,0:T(8,128)(2,1)S(1)}, u32[]{:S(2)}, u32[]{:S(2)}) %collective-permute-start.17) | collective-permute-done | bytes 368672 | tf_op jit(solution)/shard_map/ppermute | solution.py:567
  40.5 5.0 %attention.1 = (bf16[4,384,384]{2,1,0:T(8,128)(2,1)S(1)}, f32[4,2304]{1,0:T(4,128)S(1)}, bf16[512,384]{1,0:T(8,128)(2,1)S(1)}, bf16[512,1152]{1,0:T(8,128)(2,1)}, bf16[512,384]{1,0:T(8,128)(2,1)S(1)}) custom-call(s32[3]{0:T(128)S(1)} %pad_add_fusion.ids, bf16[3,160,384]{2,1,0:T(8,128)(2,1)S(1)} %pad_maximum_fusion.refs_0_, ...), custom_call_target="tpu_custom_call" | custom-call | flops 1 | bytes 1 | tf_op jit(solution)/shard_map/attention/pallas_call | solution.py:40
  45.5 10.7 %mlp.1 = (bf16[2,256,384]{2,1,0:T(8,128)(2,1)}, f32[2,256,384]{2,1,0:T(8,128)}, bf16[512,384]{1,0:T(8,128)(2,1)S(1)}, bf16[512,384]{1,0:T(8,128)(2,1)S(1)}, f32[...) custom-call(s32[3]{0:T(128)S(1)} %pad_add_fusion.ids, ...), custom_call_target="tpu_custom_call" | custom-call | flops 1 | bytes 1 | tf_op jit(solution)/shard_map/mlp/pallas_call | solution.py:40
  56.3 2.6 %attention_back_first.1.g_first = bf16[256,1152]{1,0:T(8,128)(2,1)S(1)} custom-call(bf16[512,1152]{1,0:T(8,128)(2,1)S(1)} %copy-done, bf16[512,384]{1,0:T(8,128)(2,1)S(1)} %get-tuple-element.82.gatt), custom_call_target="tpu_custom_call" | custom-call | flops 1 | bytes 1 | tf_op jit(solution)/shard_map/attention_back_first/pallas_call | solution.py:40
  59.1 1.6 %collective-permute-start.21 = (bf16[2,4,2,48,384]{4,3,2,1,0:T(8,128)(2,1)S(1)}, bf16[2,4,2,48,384]{4,3,2,1,0:T(8,128)(2,1)S(1)}, u32[]{:S(2)}, u32[]{:S(2)}) collective-permute-start(bf16[2,4,2,48,384]{4,3,2,1,0:T(8,128)(2,1)S(1)} %sum_ud.1), channel_id=1, source_target_pairs={{0,8},{1,17},{2,10},{3,19},{4,12},{5,21},{6,14},{7,23},{8,0},{9,25... | collective-permute-start | bytes 1769480 | tf_op jit(solution)/shard_map/ppermute | solution.py:567
  60.6 4.4 %attention_back.1 = (bf16[512,1152]{1,0:T(8,128)(2,1)S(1)}, f32[1,3072]{1,0:T(1,128)S(1)}, bf16[2,4,48,384]{3,2,1,0:T(8,128)(2,1)S(1)}, bf16[2,4,48,384]{3,2,1,0...) custom-call(s32[3]{0:T(128)S(1)} %pad_add_fusion.ids, ...), custom_call_target="tpu_custom_call" | custom-call | flops 1 | bytes 1 | tf_op jit(solution)/shard_map/attention_back/pallas_call | solution.py:40
  65.0 0.7 collective-permute-start.22
  65.8 2.9 %input_back.1 = (bf16[2,256,384]{2,1,0:T(8,128)(2,1)}, bf16[2,3840]{1,0:T(2,128)(2,1)S(1)}) custom-call(s32[3]{0:T(128)S(1)} %pad_add_fusion.ids, bf16[512,1152]{1,0:T(8,128)(2,1)S(1)} %get-tuple-element.90.gproj, bf16[4,384,384]{2,1,0:T(8,128)(2,1)S(1)} %get-tuple-element.77.wpo, bf16[2,256,384]{2,1,0:T(8,128)(2,1)S(1)} %copy-done.1, ...), custom_call_target="tpu_custom_call" | custom-call | flops 1 | bytes 1 | tf_op jit(solution)/shard_map/input_back/pallas_call | solution.py:40
  69.1 1.6 %collective-permute-start.23 = (bf16[2,4,48,384]{3,2,1,0:T(8,128)(2,1)S(1)}, bf16[2,4,48,384]{3,2,1,0:T(8,128)(2,1)S(1)}, u32[]{:S(2)}, u32[]{:S(2)}) collective-permute-start(bf16[2,4,48,384]{3,2,1,0:T(8,128)(2,1)S(1)} %sum_po.1), channel_id=1, source_target_pairs={{0,8},{1,17},{2,10},{3,19},{4,12},{5,21},{6,14},{7,23},{8,0},{9,25... | collective-permute-start | bytes 884744 | tf_op jit(solution)/shard_map/ppermute | solution.py:567
  71.2 1.2 %collective-permute-done.24.c_other = bf16[8,384]{1,0:T(8,128)(2,1)S(1)} collective-permute-done((bf16[8,384]{1,0:T(8,128)(2,1)S(1)}, bf16[8,384]{1,0:T(8,128)(2,1)S(1)}, u32[]{:S(2)}, u32[]{:S(2)}) %collective-permute-start.24) | collective-permute-done | bytes 6176 | tf_op jit(solution)/shard_map/ppermute | solution.py:567
  72.3 2.6 %collective-permute-start.26 = (bf16[4,3840]{1,0:T(4,128)(2,1)S(1)}, bf16[4,3840]{1,0:T(4,128)(2,1)S(1)}, u32[]{:S(2)}, u32[]{:S(2)}) collective-permute-start(bf16[4,3840]{1,0:T(4,128)(2,1)S(1)} %pair.1.g0), channel_id=1, source_target_pairs={{0,4},{1,5},{2,6},{3,7},{4,0},{5,1},{6,2},{7,3},{8,12},{9,13},{10,... | collective-permute-start | bytes 92168 | tf_op jit(solution)/shard_map/ppermute | solution.py:567
  74.9 2.3 %collective-permute-done.26.g2 = bf16[4,3840]{1,0:T(4,128)(2,1)S(1)} collective-permute-done((bf16[4,3840]{1,0:T(4,128)(2,1)S(1)}, bf16[4,3840]{1,0:T(4,128)(2,1)S(1)}, u32[]{:S(2)}, u32[]{:S(2)}) %collective-permute-start.26) | collective-permute-done | bytes 30752 | tf_op jit(solution)/shard_map/ppermute | solution.py:567
  77.4 2.1 %collective-permute-start.27 = (bf16[4,144,384]{2,1,0:T(8,128)(2,1)S(1)}, bf16[4,144,384]{2,1,0:T(8,128)(2,1)S(1)}, u32[]{:S(2)}, u32[]{:S(2)}) collective-permute-start(bf16[4,144,384]{2,1,0:T(8,128)(2,1)S(1)} %turn.1), channel_id=1, source_target_pairs={{0,16},{1,9},{2,18},{3,11},{4,20},{5,13},{6,22},{7,15},{8,24},{9,1... | collective-permute-start | bytes 1327112 | tf_op jit(solution)/shard_map/ppermute | solution.py:567
  79.5 2.9 %collective-permute-start.28 = (bf16[4,3840]{1,0:T(4,128)(2,1)S(1)}, bf16[4,3840]{1,0:T(4,128)(2,1)S(1)}, u32[]{:S(2)}, u32[]{:S(2)}) collective-permute-start(bf16[4,3840]{1,0:T(4,128)(2,1)S(1)} %pair.1.g0), channel_id=1, source_target_pairs={{0,2},{1,3},{2,0},{3,1},{4,6},{5,7},{6,4},{7,5},{8,10},{9,11},{10,... | collective-permute-start | bytes 92168 | tf_op jit(solution)/shard_map/ppermute | solution.py:567
  82.4 1.8 %collective-permute-done.28.g1 = bf16[4,3840]{1,0:T(4,128)(2,1)S(1)} collective-permute-done((bf16[4,3840]{1,0:T(4,128)(2,1)S(1)}, bf16[4,3840]{1,0:T(4,128)(2,1)S(1)}, u32[]{:S(2)}, u32[]{:S(2)}) %collective-permute-start.28) | collective-permute-done | bytes 30752 | tf_op jit(solution)/shard_map/ppermute | solution.py:567
  84.2 2.0 %collective-permute-done.29.g3 = bf16[4,3840]{1,0:T(4,128)(2,1)S(1)} collective-permute-done((bf16[4,3840]{1,0:T(4,128)(2,1)S(1)}, bf16[4,3840]{1,0:T(4,128)(2,1)S(1)}, u32[]{:S(2)}, u32[]{:S(2)}) %collective-permute-start.29) | collective-permute-done | bytes 30752 | tf_op jit(solution)/shard_map/ppermute | solution.py:567
  86.3 1.6 %cond_back.1 = (bf16[2,16,384]{2,1,0:T(8,128)(2,1)S(1)}, bf16[2,16,384]{2,1,0:T(8,128)(2,1)S(1)}) custom-call(s32[3]{0:T(128)S(1)} %pad_add_fusion.ids, bf16[4,3840]{1,0:T(4,128)(2,1)S(1)} %pair.1.g0, bf16[4,3840]{1,0:T(4,128)(2,1)S(1)} %collective-permute-done.26.g2, bf16[4,3840]{1,0:T(4,128)(2,1)S(1)} %collective-permute-done.28.g1, ...), custom_call_target="tpu_custom_call" | custom-call | flops 1 | bytes 1 | tf_op jit(solution)/shard_map/cond_back/pallas_call | solution.py:40
  88.1 0.7 collective-permute-start.30
  88.8 1.0 collective-permute-start.32
  89.8 1.6 %collective-permute-start.33 = (bf16[16,4224]{1,0:T(8,128)(2,1)S(1)}, bf16[16,4224]{1,0:T(8,128)(2,1)S(1)}, u32[]{:S(2)}, u32[]{:S(2)}) collective-permute-start(bf16[16,4224]{1,0:T(8,128)(2,1)S(1)} %pack.1.e0), channel_id=1, source_target_pairs={{0,16},{1,9},{2,18},{3,11},{4,20},{5,13},{6,22},{7,15},{8,24},{9,1... | collective-permute-start | bytes 405512 | tf_op jit(solution)/shard_map/ppermute | solution.py:567
  91.4 0.9 collective-permute-start.34
  92.4 3.3 %collective-permute-done.30.got = bf16[2,160,384]{2,1,0:T(8,128)(2,1)S(1)} collective-permute-done((bf16[2,160,384]{2,1,0:T(8,128)(2,1)S(1)}, bf16[2,160,384]{2,1,0:T(8,128)(2,1)S(1)}, u32[]{:S(2)}, u32[]{:S(2)}) %collective-permute-start.30) | collective-permute-done | bytes 245792 | tf_op jit(solution)/shard_map/ppermute | solution.py:567
  95.8 2.7 %collective-permute-start.31 = (bf16[160,384]{1,0:T(8,128)(2,1)S(1)}, bf16[160,384]{1,0:T(8,128)(2,1)S(1)}, u32[]{:S(2)}, u32[]{:S(2)}) collective-permute-start(bf16[160,384]{1,0:T(8,128)(2,1)S(1)} %slice_bitcast_fusion), channel_id=1, source_target_pairs={{0,4},{1,5},{2,6},{3,7},{4,0},{5,1},{6,2},{7,3},{8,12},{9,13},{10,... | collective-permute-start | bytes 368648 | tf_op jit(solution)/shard_map/ppermute | solution.py:567
  98.5 2.1 %mod_weight.1 = (f32[48,2304]{1,0:T(8,128)}, f32[288]{0:T(512)}, f32[96]{0:T(128)}, f32[48]{0:T(128)}, f32[192]{0:T(256)}, /*index=5*/f32[48]{0:T(128)}) custom-call(s32[3]{0:T(128)S(1)} %pad_add_fusion.ids, bf16[16,4224]{1,0:T(8,128)(2,1)S(1)} %pack.1.e0, bf16[16,4224]{1,0:T(8,128)(2,1)S(1)} %collective-permute-done.32.e1, ...), custom_call_target="tpu_custom_call" | custom-call | flops 1 | bytes 1 | tf_op jit(solution)/shard_map/mod_weight/pallas_call | solution.py:40
  100.6 1.3 %collective-permute-done.31 = bf16[160,384]{1,0:T(8,128)(2,1)S(1)} collective-permute-done((bf16[160,384]{1,0:T(8,128)(2,1)S(1)}, bf16[160,384]{1,0:T(8,128)(2,1)S(1)}, u32[]{:S(2)}, u32[]{:S(2)}) %collective-permute-start.31) | collective-permute-done | bytes 122912 | tf_op jit(solution)/shard_map/ppermute | solution.py:567
  102.1 0.7 collective-permute-start.37
  102.8 4.1 %collective-permute-done.35.g2 = bf16[160,384]{1,0:T(8,128)(2,1)S(1)} collective-permute-done((bf16[160,384]{1,0:T(8,128)(2,1)S(1)}, bf16[160,384]{1,0:T(8,128)(2,1)S(1)}, u32[]{:S(2)}, u32[]{:S(2)}) %collective-permute-start.35) | collective-permute-done | bytes 122912 | tf_op jit(solution)/shard_map/ppermute | solution.py:567
  107.0 1.9 %collective-permute-start.38 = (bf16[160,384]{1,0:T(8,128)(2,1)S(1)}, bf16[160,384]{1,0:T(8,128)(2,1)S(1)}, u32[]{:S(2)}, u32[]{:S(2)}) collective-permute-start(bf16[160,384]{1,0:T(8,128)(2,1)S(1)} %collective-permute-done.37.g1), channel_id=1, source_target_pairs={{0,16},{1,9},{2,18},{3,11},{4,20},{5,13},{6,22},{7,15},{8,24},{9,1... | collective-permute-start | bytes 368648 | tf_op jit(solution)/shard_map/ppermute | solution.py:567
  109.6 2.3 %collective-permute-done.38.g3 = bf16[160,384]{1,0:T(8,128)(2,1)S(1)} collective-permute-done((bf16[160,384]{1,0:T(8,128)(2,1)S(1)}, bf16[160,384]{1,0:T(8,128)(2,1)S(1)}, u32[]{:S(2)}, u32[]{:S(2)}) %collective-permute-start.38) | collective-permute-done | bytes 122912 | tf_op jit(solution)/shard_map/ppermute | solution.py:567
  111.9 1.5 %final.1 = (f32[48,1152]{1,0:T(8,128)}, f32[48,384]{1,0:T(8,128)}, f32[48,1536]{1,0:T(8,128)}, f32[192,384]{1,0:T(8,128)}) custom-call(s32[3]{0:T(128)S(1)} %pad_add_fusion.ids, bf16[160,384]{1,0:T(8,128)(2,1)S(1)} %fusion.g0, bf16[160,384]{1,0:T(8,128)(2,1)S(1)} %collective-permute-done.37.g1, bf16[160,384]{1,0:T(8,128)(2,1)S(1)} %collective-permute-done.35.g2, ...), custom_call_target="tpu_custom_call" | custom-call | flops 1 | bytes 1 | tf_op jit(solution)/shard_map/final/pallas_call | solution.py:40
  (98 shorter events, 8.8 us)
Async XLA Ops:
  0.6 6.5 %collective-permute-start.1 = (bf16[48,2304]{1,0:T(8,128)(2,1)}, bf16[48,2304]{1,0:T(8,128)(2,1)S(1)}, u32[]{:S(2)}, u32[]{:S(2)}) collective-permute-start(bf16[48,2304]{1,0:T(8,128)(2,1)} %wmod.1), channel_id=1, source_target_pairs={{0,1},{1,0},{2,3},{3,2},{4,5},{5,4},{6,7},{7,6},{8,9},{9,8},{10,11... | collective-permute-start | bytes 663560 | tf_op jit(solution)/shard_map/ppermute | solution.py:567
  1.2 12.6 %collective-permute-start.5 = (bf16[48,1536]{1,0:T(8,128)(2,1)}, bf16[48,1536]{1,0:T(8,128)(2,1)S(1)}, u32[]{:S(2)}, u32[]{:S(2)}) collective-permute-start(bf16[48,1536]{1,0:T(8,128)(2,1)} %refs_8_.3), channel_id=1, source_target_pairs={{0,1},{1,0},{2,3},{3,2},{4,5},{5,4},{6,7},{7,6},{8,9},{9,8},{10,11... | collective-permute-start | bytes 442376 | tf_op jit(solution)/shard_map/ppermute | solution.py:567
  1.2 12.5 %collective-permute-start.6 = (bf16[192,384]{1,0:T(8,128)(2,1)}, bf16[192,384]{1,0:T(8,128)(2,1)S(1)}, u32[]{:S(2)}, u32[]{:S(2)}) collective-permute-start(bf16[192,384]{1,0:T(8,128)(2,1)} %refs_9_.3), channel_id=1, source_target_pairs={{0,1},{1,0},{2,3},{3,2},{4,5},{5,4},{6,7},{7,6},{8,9},{9,8},{10,11... | collective-permute-start | bytes 442376 | tf_op jit(solution)/shard_map/ppermute | solution.py:567
  1.7 38.8 %copy-start.10 = (bf16[48,1152]{1,0:T(8,128)(2,1)S(1)}, bf16[48,1152]{1,0:T(8,128)(2,1)}, u32[]{:S(2)}) copy-start(bf16[48,1152]{1,0:T(8,128)(2,1)} %refs_8_.2) | copy-start | bytes 331780
  1.7 38.8 %copy-start.12 = (bf16[48,384]{1,0:T(8,128)(2,1)S(1)}, bf16[48,384]{1,0:T(8,128)(2,1)}, u32[]{:S(2)}) copy-start(bf16[48,384]{1,0:T(8,128)(2,1)} %refs_9_.2) | copy-start | bytes 110596
  3.2 37.2 %copy-start.1 = (bf16[2,256,384]{2,1,0:T(8,128)(2,1)S(1)}, bf16[2,256,384]{2,1,0:T(8,128)(2,1)}, u32[]{:S(2)}) copy-start(bf16[2,256,384]{2,1,0:T(8,128)(2,1)} %lat.1) | copy-start | bytes 1179652
  3.3 10.5 %collective-permute-start = (bf16[160,384]{1,0:T(8,128)(2,1)}, bf16[160,384]{1,0:T(8,128)(2,1)S(1)}, u32[]{:S(2)}, u32[]{:S(2)}) collective-permute-start(bf16[160,384]{1,0:T(8,128)(2,1)} %pick.1.q0), channel_id=1, source_target_pairs={{0,4},{1,5},{2,6},{3,7},{4,0},{5,1},{6,2},{7,3},{8,12},{9,13},{10,... | collective-permute-start | bytes 368648 | tf_op jit(solution)/shard_map/ppermute | solution.py:567
  7.0 5.5 %collective-permute-start.3 = (bf16[48,1152]{1,0:T(8,128)(2,1)}, bf16[48,1152]{1,0:T(8,128)(2,1)S(1)}, u32[]{:S(2)}, u32[]{:S(2)}) collective-permute-start(bf16[48,1152]{1,0:T(8,128)(2,1)} %refs_8_.2), channel_id=1, source_target_pairs={{0,1},{1,0},{2,3},{3,2},{4,5},{5,4},{6,7},{7,6},{8,9},{9,8},{10,11... | collective-permute-start | bytes 331784 | tf_op jit(solution)/shard_map/ppermute | solution.py:567
  7.2 5.1 %collective-permute-start.4 = (bf16[48,384]{1,0:T(8,128)(2,1)}, bf16[48,384]{1,0:T(8,128)(2,1)S(1)}, u32[]{:S(2)}, u32[]{:S(2)}) collective-permute-start(bf16[48,384]{1,0:T(8,128)(2,1)} %refs_9_.2), channel_id=1, source_target_pairs={{0,1},{1,0},{2,3},{3,2},{4,5},{5,4},{6,7},{7,6},{8,9},{9,8},{10,11... | collective-permute-start | bytes 110600 | tf_op jit(solution)/shard_map/ppermute | solution.py:567
  11.7 12.4 %copy-start.9 = (bf16[160,384]{1,0:T(8,128)(2,1)S(1)}, bf16[160,384]{1,0:T(8,128)(2,1)}, u32[]{:S(2)}) copy-start(bf16[160,384]{1,0:T(8,128)(2,1)} %pick.1.q0) | copy-start | bytes 368644
  12.3 1.5 %collective-permute-start.2 = (f32[3,2304]{1,0:T(4,128)S(1)}, f32[3,2304]{1,0:T(4,128)S(1)}, u32[]{:S(2)}, u32[]{:S(2)}) collective-permute-start(f32[3,2304]{1,0:T(4,128)S(1)} %get-tuple-element.68.placed), channel_id=1, source_target_pairs={{0,1},{1,0},{2,3},{3,2},{4,5},{5,4},{6,7},{7,6},{8,9},{9,8},{10,11... | collective-permute-start | bytes 82952 | tf_op jit(solution)/shard_map/ppermute | solution.py:567
  13.8 6.5 %collective-permute-start.7 = (bf16[160,384]{1,0:T(8,128)(2,1)}, bf16[160,384]{1,0:T(8,128)(2,1)S(1)}, u32[]{:S(2)}, u32[]{:S(2)}) collective-permute-start(bf16[160,384]{1,0:T(8,128)(2,1)} %pick.1.q0), channel_id=1, source_target_pairs={{0,2},{1,3},{2,0},{3,1},{4,6},{5,7},{6,4},{7,5},{8,10},{9,11},{10,... | collective-permute-start | bytes 368648 | tf_op jit(solution)/shard_map/ppermute | solution.py:567
  15.1 6.7 %collective-permute-start.8 = (bf16[160,384]{1,0:T(8,128)(2,1)S(1)}, bf16[160,384]{1,0:T(8,128)(2,1)S(1)}, u32[]{:S(2)}, u32[]{:S(2)}) collective-permute-start(bf16[160,384]{1,0:T(8,128)(2,1)S(1)} %collective-permute-done.q2), channel_id=1, source_target_pairs={{0,2},{1,3},{2,0},{3,1},{4,6},{5,7},{6,4},{7,5},{8,10},{9,11},{10,... | collective-permute-start | bytes 368648 | tf_op jit(solution)/shard_map/ppermute | solution.py:567
  21.8 8.9 %collective-permute-start.9 = (bf16[3,160,384]{2,1,0:T(8,128)(2,1)S(1)}, bf16[3,160,384]{2,1,0:T(8,128)(2,1)S(1)}, u32[]{:S(2)}, u32[]{:S(2)}) collective-permute-start(bf16[3,160,384]{2,1,0:T(8,128)(2,1)S(1)} %pad_maximum_fusion.refs_0_), channel_id=1, source_target_pairs={{0,8},{1,17},{2,10},{3,19},{4,12},{5,21},{6,14},{7,23},{8,0},{9,25... | collective-permute-start | bytes 1105928 | tf_op jit(solution)/shard_map/ppermute | solution.py:567
  25.0 4.4 %collective-permute-start.10 = (f32[2,4,2304]{2,1,0:T(4,128)S(1)}, f32[2,4,2304]{2,1,0:T(4,128)S(1)}, u32[]{:S(2)}, u32[]{:S(2)}) collective-permute-start(f32[2,4,2304]{2,1,0:T(4,128)S(1)} %get-tuple-element.73), channel_id=1, source_target_pairs={{0,2},{1,3},{2,0},{3,1},{4,6},{5,7},{6,4},{7,5},{8,10},{9,11},{10,... | collective-permute-start | bytes 221192 | tf_op jit(solution)/shard_map/ppermute | solution.py:567
  26.6 9.8 %collective-permute-start.11 = (bf16[3,160,384]{2,1,0:T(8,128)(2,1)S(1)}, bf16[3,160,384]{2,1,0:T(8,128)(2,1)S(1)}, u32[]{:S(2)}, u32[]{:S(2)}) collective-permute-start(bf16[3,160,384]{2,1,0:T(8,128)(2,1)S(1)} %pad_maximum_fusion.refs_0_), channel_id=1, source_target_pairs={{0,16},{1,9},{2,18},{3,11},{4,20},{5,13},{6,22},{7,15},{8,24},{9,1... | collective-permute-start | bytes 1105928 | tf_op jit(solution)/shard_map/ppermute | solution.py:567
  30.7 8.0 %collective-permute-start.12 = (bf16[3,160,384]{2,1,0:T(8,128)(2,1)S(1)}, bf16[3,160,384]{2,1,0:T(8,128)(2,1)S(1)}, u32[]{:S(2)}, u32[]{:S(2)}) collective-permute-start(bf16[3,160,384]{2,1,0:T(8,128)(2,1)S(1)} %collective-permute-done.9.refs_1_), channel_id=1, source_target_pairs={{0,16},{1,9},{2,18},{3,11},{4,20},{5,13},{6,22},{7,15},{8,24},{9,1... | collective-permute-start | bytes 1105928 | tf_op jit(solution)/shard_map/ppermute | solution.py:567
  33.3 12.2 %copy-start.6 = (bf16[48,1536]{1,0:T(8,128)(2,1)S(1)}, bf16[48,1536]{1,0:T(8,128)(2,1)}, u32[]{:S(2)}) copy-start(bf16[48,1536]{1,0:T(8,128)(2,1)} %refs_8_.3) | copy-start | bytes 442372
  33.3 12.2 %copy-start.7 = (bf16[192,384]{1,0:T(8,128)(2,1)S(1)}, bf16[192,384]{1,0:T(8,128)(2,1)}, u32[]{:S(2)}) copy-start(bf16[192,384]{1,0:T(8,128)(2,1)} %refs_9_.3) | copy-start | bytes 442372
  33.3 12.2 %copy-start.11 = (bf16[2,256,384]{2,1,0:T(8,128)(2,1)S(1)}, bf16[2,256,384]{2,1,0:T(8,128)(2,1)}, u32[]{:S(2)}) copy-start(bf16[2,256,384]{2,1,0:T(8,128)(2,1)} %refs_15_.1) | copy-start | bytes 1179652
  33.3 4.9 %collective-permute-start.16 = (f32[4,2304]{1,0:T(4,128)S(1)}, f32[4,2304]{1,0:T(4,128)S(1)}, u32[]{:S(2)}, u32[]{:S(2)}) collective-permute-start(f32[4,2304]{1,0:T(4,128)S(1)} %slice_bitcast_fusion.2), channel_id=1, source_target_pairs={{0,4},{1,5},{2,6},{3,7},{4,0},{5,1},{6,2},{7,3},{8,12},{9,13},{10,... | collective-permute-start | bytes 110600 | tf_op jit(solution)/shard_map/ppermute | solution.py:567
  35.9 2.9 %collective-permute-start.13 = (bf16[3,160,384]{2,1,0:T(8,128)(2,1)S(1)}, bf16[3,160,384]{2,1,0:T(8,128)(2,1)S(1)}, u32[]{:S(2)}, u32[]{:S(2)}) collective-permute-start(bf16[3,160,384]{2,1,0:T(8,128)(2,1)S(1)} %pad_maximum_fusion.refs_0_), channel_id=1, source_target_pairs={{0,1},{1,0},{2,3},{3,2},{4,5},{5,4},{6,7},{7,6},{8,9},{9,8},{10,11... | collective-permute-start | bytes 1105928 | tf_op jit(solution)/shard_map/ppermute | solution.py:567
  35.9 2.9 %collective-permute-start.14 = (bf16[3,160,384]{2,1,0:T(8,128)(2,1)S(1)}, bf16[3,160,384]{2,1,0:T(8,128)(2,1)S(1)}, u32[]{:S(2)}, u32[]{:S(2)}) collective-permute-start(bf16[3,160,384]{2,1,0:T(8,128)(2,1)S(1)} %collective-permute-done.9.refs_1_), channel_id=1, source_target_pairs={{0,1},{1,0},{2,3},{3,2},{4,5},{5,4},{6,7},{7,6},{8,9},{9,8},{10,11... | collective-permute-start | bytes 1105928 | tf_op jit(solution)/shard_map/ppermute | solution.py:567
  36.4 2.4 %collective-permute-start.15 = (bf16[3,160,384]{2,1,0:T(8,128)(2,1)S(1)}, bf16[3,160,384]{2,1,0:T(8,128)(2,1)S(1)}, u32[]{:S(2)}, u32[]{:S(2)}) collective-permute-start(bf16[3,160,384]{2,1,0:T(8,128)(2,1)S(1)} %collective-permute-done.11.refs_2_), channel_id=1, source_target_pairs={{0,1},{1,0},{2,3},{3,2},{4,5},{5,4},{6,7},{7,6},{8,9},{9,8},{10,11... | collective-permute-start | bytes 1105928 | tf_op jit(solution)/shard_map/ppermute | solution.py:567
  38.8 1.7 %collective-permute-start.17 = (bf16[3,160,384]{2,1,0:T(8,128)(2,1)S(1)}, bf16[3,160,384]{2,1,0:T(8,128)(2,1)S(1)}, u32[]{:S(2)}, u32[]{:S(2)}) collective-permute-start(bf16[3,160,384]{2,1,0:T(8,128)(2,1)S(1)} %collective-permute-done.12.refs_3_), channel_id=1, source_target_pairs={{0,1},{1,0},{2,3},{3,2},{4,5},{5,4},{6,7},{7,6},{8,9},{9,8},{10,11... | collective-permute-start | bytes 1105928 | tf_op jit(solution)/shard_map/ppermute | solution.py:567
  45.5 10.8 %copy-start = (bf16[512,1152]{1,0:T(8,128)(2,1)S(1)}, bf16[512,1152]{1,0:T(8,128)(2,1)}, u32[]{:S(2)}) copy-start(bf16[512,1152]{1,0:T(8,128)(2,1)} %get-tuple-element.81.proj) | copy-start | bytes 3538948
  56.2 2.7 %collective-permute-start.18 = (bf16[2,4,2,48,384]{4,3,2,1,0:T(8,128)(2,1)}, bf16[2,4,2,48,384]{4,3,2,1,0:T(8,128)(2,1)S(1)}, u32[]{:S(2)}, u32[]{:S(2)}) collective-permute-start(bf16[2,4,2,48,384]{4,3,2,1,0:T(8,128)(2,1)} %get-tuple-element.87), channel_id=1, source_target_pairs={{0,1},{1,0},{2,3},{3,2},{4,5},{5,4},{6,7},{7,6},{8,9},{9,8},{10,11... | collective-permute-start | bytes 1769480 | tf_op jit(solution)/shard_map/ppermute | solution.py:567
  59.1 9.9 %collective-permute-start.21 = (bf16[2,4,2,48,384]{4,3,2,1,0:T(8,128)(2,1)S(1)}, bf16[2,4,2,48,384]{4,3,2,1,0:T(8,128)(2,1)S(1)}, u32[]{:S(2)}, u32[]{:S(2)}) collective-permute-start(bf16[2,4,2,48,384]{4,3,2,1,0:T(8,128)(2,1)S(1)} %sum_ud.1), channel_id=1, source_target_pairs={{0,8},{1,17},{2,10},{3,19},{4,12},{5,21},{6,14},{7,23},{8,0},{9,25... | collective-permute-start | bytes 1769480 | tf_op jit(solution)/shard_map/ppermute | solution.py:567
  65.0 3.7 %collective-permute-start.22 = (bf16[2,4,48,384]{3,2,1,0:T(8,128)(2,1)S(1)}, bf16[2,4,48,384]{3,2,1,0:T(8,128)(2,1)S(1)}, u32[]{:S(2)}, u32[]{:S(2)}) collective-permute-start(bf16[2,4,48,384]{3,2,1,0:T(8,128)(2,1)S(1)} %get-tuple-element.100), channel_id=1, source_target_pairs={{0,1},{1,0},{2,3},{3,2},{4,5},{5,4},{6,7},{7,6},{8,9},{9,8},{10,11... | collective-permute-start | bytes 884744 | tf_op jit(solution)/shard_map/ppermute | solution.py:567
  65.7 11.5 %collective-permute-start.19 = (bf16[2,4,2,48,384]{4,3,2,1,0:T(8,128)(2,1)S(1)}, bf16[2,4,2,48,384]{4,3,2,1,0:T(8,128)(2,1)S(1)}, u32[]{:S(2)}, u32[]{:S(2)}) collective-permute-start(bf16[2,4,2,48,384]{4,3,2,1,0:T(8,128)(2,1)S(1)} %copy-done.19), channel_id=1, source_target_pairs={{0,1},{1,0},{2,3},{3,2},{4,5},{5,4},{6,7},{7,6},{8,9},{9,8},{10,11... | collective-permute-start | bytes 1769480 | tf_op jit(solution)/shard_map/ppermute | solution.py:567
  69.1 8.1 %collective-permute-start.23 = (bf16[2,4,48,384]{3,2,1,0:T(8,128)(2,1)S(1)}, bf16[2,4,48,384]{3,2,1,0:T(8,128)(2,1)S(1)}, u32[]{:S(2)}, u32[]{:S(2)}) collective-permute-start(bf16[2,4,48,384]{3,2,1,0:T(8,128)(2,1)S(1)} %sum_po.1), channel_id=1, source_target_pairs={{0,8},{1,17},{2,10},{3,19},{4,12},{5,21},{6,14},{7,23},{8,0},{9,25... | collective-permute-start | bytes 884744 | tf_op jit(solution)/shard_map/ppermute | solution.py:567
  70.6 6.6 %collective-permute-start.20 = (bf16[2,4,48,384]{3,2,1,0:T(8,128)(2,1)S(1)}, bf16[2,4,48,384]{3,2,1,0:T(8,128)(2,1)S(1)}, u32[]{:S(2)}, u32[]{:S(2)}) collective-permute-start(bf16[2,4,48,384]{3,2,1,0:T(8,128)(2,1)S(1)} %get-tuple-element.98), channel_id=1, source_target_pairs={{0,1},{1,0},{2,3},{3,2},{4,5},{5,4},{6,7},{7,6},{8,9},{9,8},{10,11... | collective-permute-start | bytes 884744 | tf_op jit(solution)/shard_map/ppermute | solution.py:567
  70.6 1.7 %collective-permute-start.25 = (bf16[2,3840]{1,0:T(2,128)(2,1)S(1)}, bf16[2,3840]{1,0:T(2,128)(2,1)S(1)}, u32[]{:S(2)}, u32[]{:S(2)}) collective-permute-start(bf16[2,3840]{1,0:T(2,128)(2,1)S(1)} %get-tuple-element.104.own), channel_id=1, source_target_pairs={{0,1},{1,0},{2,3},{3,2},{4,5},{5,4},{6,7},{7,6},{8,9},{9,8},{10,11... | collective-permute-start | bytes 46088 | tf_op jit(solution)/shard_map/ppermute | solution.py:567
  71.2 1.2 %collective-permute-start.24 = (bf16[8,384]{1,0:T(8,128)(2,1)S(1)}, bf16[8,384]{1,0:T(8,128)(2,1)S(1)}, u32[]{:S(2)}, u32[]{:S(2)}) collective-permute-start(bf16[8,384]{1,0:T(8,128)(2,1)S(1)} %get-tuple-element.103.c_own), channel_id=1, source_target_pairs={{0,1},{1,0},{2,3},{3,2},{4,5},{5,4},{6,7},{7,6},{8,9},{9,8},{10,11... | collective-permute-start | bytes 18440 | tf_op jit(solution)/shard_map/ppermute | solution.py:567
  72.3 4.9 %collective-permute-start.26 = (bf16[4,3840]{1,0:T(4,128)(2,1)S(1)}, bf16[4,3840]{1,0:T(4,128)(2,1)S(1)}, u32[]{:S(2)}, u32[]{:S(2)}) collective-permute-start(bf16[4,3840]{1,0:T(4,128)(2,1)S(1)} %pair.1.g0), channel_id=1, source_target_pairs={{0,4},{1,5},{2,6},{3,7},{4,0},{5,1},{6,2},{7,3},{8,12},{9,13},{10,... | collective-permute-start | bytes 92168 | tf_op jit(solution)/shard_map/ppermute | solution.py:567
  77.4 10.6 %collective-permute-start.27 = (bf16[4,144,384]{2,1,0:T(8,128)(2,1)S(1)}, bf16[4,144,384]{2,1,0:T(8,128)(2,1)S(1)}, u32[]{:S(2)}, u32[]{:S(2)}) collective-permute-start(bf16[4,144,384]{2,1,0:T(8,128)(2,1)S(1)} %turn.1), channel_id=1, source_target_pairs={{0,16},{1,9},{2,18},{3,11},{4,20},{5,13},{6,22},{7,15},{8,24},{9,1... | collective-permute-start | bytes 1327112 | tf_op jit(solution)/shard_map/ppermute | solution.py:567
  79.5 4.7 %collective-permute-start.28 = (bf16[4,3840]{1,0:T(4,128)(2,1)S(1)}, bf16[4,3840]{1,0:T(4,128)(2,1)S(1)}, u32[]{:S(2)}, u32[]{:S(2)}) collective-permute-start(bf16[4,3840]{1,0:T(4,128)(2,1)S(1)} %pair.1.g0), channel_id=1, source_target_pairs={{0,2},{1,3},{2,0},{3,1},{4,6},{5,7},{6,4},{7,5},{8,10},{9,11},{10,... | collective-permute-start | bytes 92168 | tf_op jit(solution)/shard_map/ppermute | solution.py:567
  82.4 3.9 %collective-permute-start.29 = (bf16[4,3840]{1,0:T(4,128)(2,1)S(1)}, bf16[4,3840]{1,0:T(4,128)(2,1)S(1)}, u32[]{:S(2)}, u32[]{:S(2)}) collective-permute-start(bf16[4,3840]{1,0:T(4,128)(2,1)S(1)} %collective-permute-done.26.g2), channel_id=1, source_target_pairs={{0,2},{1,3},{2,0},{3,1},{4,6},{5,7},{6,4},{7,5},{8,10},{9,11},{10,... | collective-permute-start | bytes 92168 | tf_op jit(solution)/shard_map/ppermute | solution.py:567
  88.1 7.6 %collective-permute-start.30 = (bf16[2,160,384]{2,1,0:T(8,128)(2,1)S(1)}, bf16[2,160,384]{2,1,0:T(8,128)(2,1)S(1)}, u32[]{:S(2)}, u32[]{:S(2)}) collective-permute-start(bf16[2,160,384]{2,1,0:T(8,128)(2,1)S(1)} %join_far.1), channel_id=1, source_target_pairs={{0,2},{1,3},{2,0},{3,1},{4,6},{5,7},{6,4},{7,5},{8,10},{9,11},{10,... | collective-permute-start | bytes 737288 | tf_op jit(solution)/shard_map/ppermute | solution.py:567
  88.8 9.7 %collective-permute-start.32 = (bf16[16,4224]{1,0:T(8,128)(2,1)S(1)}, bf16[16,4224]{1,0:T(8,128)(2,1)S(1)}, u32[]{:S(2)}, u32[]{:S(2)}) collective-permute-start(bf16[16,4224]{1,0:T(8,128)(2,1)S(1)} %pack.1.e0), channel_id=1, source_target_pairs={{0,8},{1,17},{2,10},{3,19},{4,12},{5,21},{6,14},{7,23},{8,0},{9,25... | collective-permute-start | bytes 405512 | tf_op jit(solution)/shard_map/ppermute | solution.py:567
  89.8 8.7 %collective-permute-start.33 = (bf16[16,4224]{1,0:T(8,128)(2,1)S(1)}, bf16[16,4224]{1,0:T(8,128)(2,1)S(1)}, u32[]{:S(2)}, u32[]{:S(2)}) collective-permute-start(bf16[16,4224]{1,0:T(8,128)(2,1)S(1)} %pack.1.e0), channel_id=1, source_target_pairs={{0,16},{1,9},{2,18},{3,11},{4,20},{5,13},{6,22},{7,15},{8,24},{9,1... | collective-permute-start | bytes 405512 | tf_op jit(solution)/shard_map/ppermute | solution.py:567
  91.4 7.1 %collective-permute-start.34 = (bf16[16,4224]{1,0:T(8,128)(2,1)S(1)}, bf16[16,4224]{1,0:T(8,128)(2,1)S(1)}, u32[]{:S(2)}, u32[]{:S(2)}) collective-permute-start(bf16[16,4224]{1,0:T(8,128)(2,1)S(1)} %pack.1.e0), channel_id=1, source_target_pairs={{0,24},{1,25},{2,26},{3,27},{4,28},{5,29},{6,30},{7,31},{8,16},{9,... | collective-permute-start | bytes 405512 | tf_op jit(solution)/shard_map/ppermute | solution.py:567
  95.7 13.3 %copy-start.18 = (bf16[2,384]{1,0:T(2,128)(2,1)S(1)}, bf16[2,384]{1,0:T(2,128)(2,1)}, u32[]{:S(2)}) copy-start(bf16[2,384]{1,0:T(2,128)(2,1)} %cond.1) | copy-start | bytes 4612
  95.8 6.2 %collective-permute-start.31 = (bf16[160,384]{1,0:T(8,128)(2,1)S(1)}, bf16[160,384]{1,0:T(8,128)(2,1)S(1)}, u32[]{:S(2)}, u32[]{:S(2)}) collective-permute-start(bf16[160,384]{1,0:T(8,128)(2,1)S(1)} %slice_bitcast_fusion), channel_id=1, source_target_pairs={{0,4},{1,5},{2,6},{3,7},{4,0},{5,1},{6,2},{7,3},{8,12},{9,13},{10,... | collective-permute-start | bytes 368648 | tf_op jit(solution)/shard_map/ppermute | solution.py:567
  102.0 4.9 %collective-permute-start.35 = (bf16[160,384]{1,0:T(8,128)(2,1)S(1)}, bf16[160,384]{1,0:T(8,128)(2,1)S(1)}, u32[]{:S(2)}, u32[]{:S(2)}) collective-permute-start(bf16[160,384]{1,0:T(8,128)(2,1)S(1)} %fusion.g0), channel_id=1, source_target_pairs={{0,16},{1,9},{2,18},{3,11},{4,20},{5,13},{6,22},{7,15},{8,24},{9,1... | collective-permute-start | bytes 368648 | tf_op jit(solution)/shard_map/ppermute | solution.py:567
  102.1 4.9 %collective-permute-start.37 = (bf16[160,384]{1,0:T(8,128)(2,1)S(1)}, bf16[160,384]{1,0:T(8,128)(2,1)S(1)}, u32[]{:S(2)}, u32[]{:S(2)}) collective-permute-start(bf16[160,384]{1,0:T(8,128)(2,1)S(1)} %fusion.g0), channel_id=1, source_target_pairs={{0,8},{1,17},{2,10},{3,19},{4,12},{5,21},{6,14},{7,23},{8,0},{9,25... | collective-permute-start | bytes 368648 | tf_op jit(solution)/shard_map/ppermute | solution.py:567
  107.0 2.0 %collective-permute-start.36 = (bf16[2,384]{1,0:T(2,128)(2,1)S(1)}, bf16[2,384]{1,0:T(2,128)(2,1)S(1)}, u32[]{:S(2)}, u32[]{:S(2)}) collective-permute-start(bf16[2,384]{1,0:T(2,128)(2,1)S(1)} %slice.29), channel_id=1, source_target_pairs={{0,1},{1,0},{2,3},{3,2},{4,5},{5,4},{6,7},{7,6},{8,9},{9,8},{10,11... | collective-permute-start | bytes 4616 | tf_op jit(solution)/shard_map/ppermute | solution.py:567
  107.0 4.9 %collective-permute-start.38 = (bf16[160,384]{1,0:T(8,128)(2,1)S(1)}, bf16[160,384]{1,0:T(8,128)(2,1)S(1)}, u32[]{:S(2)}, u32[]{:S(2)}) collective-permute-start(bf16[160,384]{1,0:T(8,128)(2,1)S(1)} %collective-permute-done.37.g1), channel_id=1, source_target_pairs={{0,16},{1,9},{2,18},{3,11},{4,20},{5,13},{6,22},{7,15},{8,24},{9,1... | collective-permute-start | bytes 368648 | tf_op jit(solution)/shard_map/ppermute | solution.py:567
  (11 other events, 34.8 us)

commit v4 on v3

--- a/solution.py
+++ b/solution.py
@@ -177,16 +177,18 @@
     low_half = lane_masks(length)
     qv = mod[2:3, 4 * feat :]
 
+    for i in range(lat.shape[0]):
+        xhat, rstd = norm_parts(lat[i].astype(F32))
+        row = mod[i : i + 1, :]
+        n1[i * length : (i + 1) * length, :] = (
+            xhat * (1.0 + row[:, feat : 2 * feat]) + row[:, :feat]
+        ).astype(BF16)
+    proj[:, 0:feat] = (dot(n1[...], wpo[0]) + qv[:, :feat]).astype(BF16)
+    proj[:, feat : 2 * feat] = dot(n1[...], wpo[1]).astype(BF16)
+    proj[:, 2 * feat :] = (dot(n1[...], wpo[2]) + qv[:, feat:]).astype(BF16)
+
     def one(i, carry):
-        at = pl.multiple_of(i * length, 256)
-        x = lat[i].astype(F32)
-        xhat, rstd = norm_parts(x)
-        row = mod[pl.ds(i, 1), :]
-        n = (xhat * (1.0 + row[:, feat : 2 * feat]) + row[:, :feat]).astype(BF16)
-        n1[pl.ds(at, length), :] = n
-        proj[pl.ds(at, length), 0:feat] = (dot(n, wpo[0]) + qv[:, :feat]).astype(BF16)
-        proj[pl.ds(at, length), feat : 2 * feat] = dot(n, wpo[1]).astype(BF16)
-        proj[pl.ds(at, length), 2 * feat :] = (dot(n, wpo[2]) + qv[:, feat:]).astype(BF16)
+        at = i * length
         for pair in range(HEADS // 2):
             lo = pair * 2 * HEAD_DIM
             hi = lo + 2 * HEAD_DIM
@@ -204,7 +206,8 @@
             att[pl.ds(at, length), lo:hi] = jnp.where(low_half, outs[0], outs[1]).astype(BF16)
         return carry
 
-    lax.fori_loop(0, lat.shape[0], one, 0)
+    for i in range(lat.shape[0]):
+        one(i, 0)
 
 
 def spread(tmp, at_row, dm, pieces, rows, f, slot=None):
@@ -233,7 +236,7 @@
 def mlp_steps(
     ids, pieces, m_up, m_down, o_up, o_down, wout, mod, lat, cot, att,
     res, gmid, gbr, gatt, gsum, gmod, k_odd, k_even, s_odd, s_even,
-    wu, wd, n2s, acts, dgs, gmlps, gpres, n2t, tmp, tmpd,
+    wu, wd, n2s, acts, dgs, gmlps, gpres, n2t, tmp, tmpd, brs, xhats, rstds, mlps,
 ):
     d, f, mine, theirs = offsets(ids)
     count = ids[2]
@@ -262,61 +265,74 @@
     bup = mod[2:3, : 4 * feat]
     bout = mod[3:4, :feat]
     bdown = mod[3:4, feat : 2 * feat]
-    gsum[...] = jnp.zeros_like(gsum)
-
-    def one(i, carry):
-        at = pl.multiple_of(i * length, 256)
-        part = pl.ds(at, length)
-        row = mod[pl.ds(i, 1), :]
-        gate_one, shift, scale, gate_two = (row[:, j * feat : (j + 1) * feat] for j in (2, 3, 4, 5))
+    members = lat.shape[0]
+
+    def rows_of(i):
+        row = mod[i : i + 1, :]
+        return (row[:, j * feat : (j + 1) * feat] for j in (2, 3, 4, 5))
+
+    brs[...] = dot(att[...], wout[0]) + bout
+    for i in range(members):
+        part = slice(i * length, (i + 1) * length)
+        gate_one, shift, scale, _ = rows_of(i)
+        middle = lat[i].astype(F32) + gate_one * brs[part, :]
+        xhat, rstd = norm_parts(middle)
+        gmid[i] = middle
+        xhats[part, :] = xhat
+        rstds[part, :] = jnp.broadcast_to(rstd, (length, 128))
+        n2s[part, :] = (xhat * (1.0 + scale) + shift).astype(BF16)
+    mlp = None
+    for j in range(0, hidden, step):
+        cols = slice(j, j + step)
+        v = dot(n2s[...], wu[:, cols]) + bup[:, cols]
+        square = v * v
+        half = 0.5 + 0.5 * jnp.tanh(v * (0.7978845608028654 + 0.035677408136300125 * square))
+        act = (v * half).astype(BF16)
+        slope = v * (1.5957691216057308 + 0.21406444881780075 * square)
+        dgs[:, cols] = half * (1.0 + (1.0 - half) * slope)
+        acts[:, cols] = act
+        term = dot(act, wd[cols, :])
+        mlp = term if mlp is None else mlp + term
+    mlps[...] = mlp + bdown
+    g_gate_two = []
+    for i in range(members):
+        part = slice(i * length, (i + 1) * length)
+        gate_two = list(rows_of(i))[3]
         alive = jnp.where(i < count, 1.0, 0.0).astype(F32)
-        branch = dot(att[part, :], wout[0]) + bout
-        middle = lat[i].astype(F32) + gate_one * branch
-        xhat, rstd = norm_parts(middle)
-        n2 = (xhat * (1.0 + scale) + shift).astype(BF16)
-        n2s[part, :] = n2
-        mlp = jnp.zeros((length, feat), F32) + bdown
-        for j in range(0, hidden, step):
-            cols = slice(j, j + step)
-            v = dot(n2, wu[:, cols]) + bup[:, cols]
-            square = v * v
-            half = 0.5 + 0.5 * jnp.tanh(v * (0.7978845608028654 + 0.035677408136300125 * square))
-            act = (v * half).astype(BF16)
-            slope = v * (1.5957691216057308 + 0.21406444881780075 * square)
-            dgs[:, cols] = half * (1.0 + (1.0 - half) * slope)
-            acts[part, cols] = act
-            mlp = mlp + dot(act, wd[cols, :])
-        res[i] = (alive * (middle + gate_two * mlp)).astype(BF16)
+        mlp = mlps[part, :]
+        res[i] = (alive * (gmid[i] + gate_two * mlp)).astype(BF16)
         upstream = alive * cot[i].astype(F32)
-        g_gate_two = jnp.sum(upstream * mlp, axis=0, keepdims=True)
-        gmlp = (gate_two * upstream).astype(BF16)
-        gmlps[part, :] = gmlp
-        gn = jnp.zeros((length, feat), F32)
-        for j in range(0, hidden, step):
-            cols = slice(j, j + step)
-            gpre = (dot(gmlp, wd[cols, :], NT) * dgs[:, cols]).astype(BF16)
-            gpres[part, cols] = gpre
-            gn = gn + dot(gpre, wu[:, cols], NT)
-            gsum[:, feat + j : feat + j + step] += jnp.sum(gpre.astype(F32), axis=0, keepdims=True)
+        g_gate_two.append(jnp.sum(upstream * mlp, axis=0, keepdims=True))
+        gmlps[part, :] = (gate_two * upstream).astype(BF16)
+    gn = None
+    for j in range(0, hidden, step):
+        cols = slice(j, j + step)
+        gpre = (dot(gmlps[...], wd[cols, :], NT) * dgs[:, cols]).astype(BF16)
+        gpres[:, cols] = gpre
+        term = dot(gpre, wu[:, cols], NT)
+        gn = term if gn is None else gn + term
+        gsum[:, feat + j : feat + j + step] = jnp.sum(gpre.astype(F32), axis=0, keepdims=True)
+    mlps[...] = gn
+    for i in range(members):
+        part = slice(i * length, (i + 1) * length)
+        gate_one, _, scale, _ = rows_of(i)
+        alive = jnp.where(i < count, 1.0, 0.0).astype(F32)
+        gn, xhat = mlps[part, :], xhats[part, :]
         g_shift = jnp.sum(gn, axis=0, keepdims=True)
         g_scale = jnp.sum(gn * xhat, axis=0, keepdims=True)
         gx = gn * (1.0 + scale)
-        gmiddle = upstream + rstd * (
+        gmiddle = alive * cot[i].astype(F32) + rstds[part, 0:1] * (
             gx
             - jnp.mean(gx, axis=-1, keepdims=True)
             - xhat * jnp.mean(gx * xhat, axis=-1, keepdims=True)
         )
         gmid[i] = gmiddle
-        g_gate_one = jnp.sum(gmiddle * branch, axis=0, keepdims=True)
-        gbranch = (gate_one * gmiddle).astype(BF16)
-        gbr[part, :] = gbranch
-        gatt[part, :] = dot(gbranch, wout[0], NT).astype(BF16)
-        gsum[:, 0:feat] += jnp.sum(gbranch.astype(F32), axis=0, keepdims=True)
-        gsum[:, 5 * feat : 6 * feat] += jnp.sum(gmlp.astype(F32), axis=0, keepdims=True)
-        gmod[pl.ds(i, 1), :] = jnp.concatenate([g_gate_one, g_shift, g_scale, g_gate_two], axis=1)
-        return carry
-
-    lax.fori_loop(0, lat.shape[0], one, 0)
+        g_gate_one = jnp.sum(gmiddle * brs[part, :], axis=0, keepdims=True)
+        gbr[part, :] = (gate_one * gmiddle).astype(BF16)
+        gmod[i : i + 1, :] = jnp.concatenate([g_gate_one, g_shift, g_scale, g_gate_two[i]], axis=1)
+    gatt[...] = dot(gbr[...], wout[0], NT).astype(BF16)
+    gsum[:, 0:feat] = jnp.sum(gbr[...].astype(F32), axis=0, keepdims=True)
+    gsum[:, 5 * feat : 6 * feat] = jnp.sum(gmlps[...].astype(F32), axis=0, keepdims=True)
     pieces = (k_odd, k_even, s_odd, s_even)
     n2t[...] = n2s[...].T
     for j in range(0, hidden, step):
@@ -407,7 +423,7 @@
     feat = lat.shape[2]
 
     def one(i, carry):
-        part = pl.ds(pl.multiple_of(i * length, 256), length)
+        part = pl.ds(i * length, length)
         row = mod[pl.ds(i, 1), :]
         xhat, rstd = norm_parts(lat[i].astype(F32))
         gn = dot(gproj[part, 0:feat], wpo[0], NT)
@@ -430,7 +446,8 @@
         )
         return carry
 
-    lax.fori_loop(0, lat.shape[0], one, 0)
+    for i in range(lat.shape[0]):
+        one(i, 0)
     full[0:1, 6 * feat :] = bias[:, : 4 * feat]
     full[1:2, 6 * feat :] = bias[:, 4 * feat :]
     gm[...] = full[...].astype(BF16)
@@ -439,12 +456,13 @@
 def cond_back_body(ids, g0, g2, g1, g3, wmod, lo, hi):
     f = ids[1]
     rows, wide = wmod.shape
+    many = g0.shape[0]
     place = one_hot((rows, lo.shape[2]), f * rows)
-    lo[...] = jnp.zeros_like(lo)
-    hi[...] = jnp.zeros_like(hi)
-    for ref, out, at in ((g0, lo, 0), (g2, lo, 1), (g1, hi, 0), (g3, hi, 1)):
-        part = dot(ref[:, :wide], wmod[...], NT).astype(BF16)
-        out[at, 0 : part.shape[0], :] = dot(part, place).astype(BF16)
+    grads = jnp.concatenate([ref[:, :wide] for ref in (g0, g2, g1, g3)], axis=0)
+    whole = dot(dot(grads, wmod[...], NT).astype(BF16), place).astype(BF16)
+    for n, (out, at) in enumerate(((lo, 0), (lo, 1), (hi, 0), (hi, 1))):
+        out[at] = jnp.zeros(out.shape[1:], BF16)
+        out[at, 0:many, :] = whole[many * n : many * (n + 1)]
 
 
 def mod_weight_body(ids, e0, e1, e2, e3, wgrad, b_mod, b_qv, b_out, b_up, b_down):
@@ -489,6 +507,11 @@
             )
 
 
+def stack_body(q2, q1, q3, out):
+    for n, ref in enumerate((q2, q1, q3)):
+        out[n] = ref[0 : out.shape[1], :]
+
+
 def pair_body(own, other, out):
     out[0 : own.shape[0], :] = own[...]
     out[own.shape[0] :, :] = other[...]
@@ -509,10 +532,17 @@
     out[:, size:] = back[...]
 
 
-def join_near_body(base, part, back, got, out):
+def join_near_body(base, part, back, got, out, far):
     size = base.shape[1]
-    out[:, 0:size] = add_low(base[:2], part[:2], got[:, 0:size])
-    out[:, size:] = add_low(back[...], got[:, size:])
+    for at, ref in enumerate((out, far)):
+        ref[0:size, :] = add_low(base[at], part[at], got[at, 0:size])
+        ref[size:, :] = add_low(back[at], got[at, size:])
+
+
+def total_body(base, got, out, back):
+    size = out.shape[0]
+    out[...] = add_low(base[0:size, :], got[0:size, :])
+    back[...] = base[size:, :].astype(F32) + got[size:, :].astype(F32)
 
 
 def final_body(ids, g0, g1, g2, g3, gp, go, gu, gd):
@@ -592,10 +622,10 @@
         return [own, a, b, move(a, second)]
 
     whole = [projection_weight, output_weight, up_weight, down_weight]
-    w_whole = whole + [move(x, core) for x in whole]
+    w_whole = whole + [move(after(x, q_all), core) for x in whole]
     biases = [modulation_bias, query_value_bias, output_bias, up_bias, down_bias]
     wmod, placed = call(
-        prepare_body, "prepare", None, [modulation_weight, move(modulation_weight, core)] + biases,
+        prepare_body, "prepare", None, [modulation_weight, move(after(modulation_weight, q_all), core)] + biases,
         [((2 * rows, wide), BF16), ((3, wide), F32)],
     )
     q_far = move(q_all, levels[2])
@@ -603,7 +633,7 @@
     ready = (placed_other, *w_whole[4:])
     q_far = after(q_far, *ready)
     q_near, q_both = move(after(q_all, q_far), levels[1]), move(q_far, levels[1])
-    own = jnp.stack([q_far, q_near, q_both])
+    (own,) = call(stack_body, "stack", None, [q_far, q_near, q_both], [((3, 3 * rows, feat), BF16)])
     keep_lo, keep_hi, c_own = call(
         mod_body, "modulation", ids, [q_all, q_far, q_near, q_both, wmod, placed, placed_other],
         [((2, 4, wide), F32)] * 2 + [((4 * slots, feat), BF16)],
@@ -634,9 +664,11 @@
         [
             pltpu.VMEM((feat, hidden), BF16), pltpu.VMEM((hidden, feat), BF16),
             pltpu.VMEM((tokens, feat), BF16), pltpu.VMEM((tokens, hidden), BF16),
-            pltpu.VMEM((length, hidden), F32), pltpu.VMEM((tokens, feat), BF16),
+            pltpu.VMEM((tokens, hidden), F32), pltpu.VMEM((tokens, feat), BF16),
             pltpu.VMEM((tokens, hidden), BF16), pltpu.VMEM((feat, tokens), BF16),
             pltpu.VMEM((feat, hidden), BF16), pltpu.VMEM((hidden, feat), BF16),
+            pltpu.VMEM((tokens, feat), F32), pltpu.VMEM((tokens, feat), F32),
+            pltpu.VMEM((tokens, 128), F32), pltpu.VMEM((tokens, feat), F32),
         ],
         flops=2 * tokens * feat * (6 * hidden + 2 * feat),
     )
@@ -693,17 +725,20 @@
     got = move(turned, levels[1])
     every = after(every, turned)
     e_first, e_second, e_both = move(every, first), move(every, second), move(every, across)
-    (base,) = call(join_near_body, "join_near", None, [base, part, back_lo, got], [pair_shape])
+    base, far = call(
+        join_near_body, "join_near", None, [base, part, back_lo, got], [((3 * rows + 16, feat), BF16)] * 2
+    )
     g_mod_weight, *g_biases = call(
         mod_weight_body, "mod_weight", ids, [every, e_first, e_second, e_both],
         [((rows, wide), F32)] + [((size // 8,), F32) for size in (wide, 2 * feat, feat, hidden, feat)],
     )
-    total = add_low(base[0], after(move(base[1], levels[2]), g_mod_weight))
+    total, back = call(
+        total_body, "total", None, [base, after(move(far, levels[2]), g_mod_weight)],
+        [((3 * rows, feat), BF16), ((16, feat), F32)],
+    )
     a_total, b_total = move(total, first), move(total, second)
-    shares = [total, a_total, b_total, move(a_total, second)]
-    silu_pair = total[3 * rows : 3 * rows + 2 * slots].astype(F32)
-    silu_other = after(total, b_total)[3 * rows + slots : 3 * rows + 2 * slots]
-    grad_silu = silu_pair[:slots] + move(silu_other, core).astype(F32)
+    shares = [total, a_total, b_total, move(total, across)]
+    grad_silu = back[:slots] + move(back[slots : 2 * slots], core)
     cond_full = cond.astype(F32)
     sig = 1.0 / (1.0 + jnp.exp(-cond_full))
     cond_grad = (grad_silu * (sig * (1.0 + cond_full * (1.0 - sig)))).astype(BF16)

time: 114 us -> 107 us (0.939)
  waiting for transfers between devices: 32.6 us -> 27.3 us
  Pallas kernels: 34.4 us -> 30.6 us
  starting transfers between devices: 39.7 us -> 41.8 us
    ppermute x39, waiting for transfers between devices: 32.6 us -> 27.3 us  [move(): return lax.ppermute(x, BOTH, route)]
    pallas_call x19 -> x21, Pallas kernels: 34.4 us -> 30.6 us  [call(): pl.pallas_call(body, out_shape=[jax.ShapeDtypeStruct(s, t) for s, t in ou...]
    ppermute x39, starting transfers between devices: 39.7 us -> 41.8 us  [move(): return lax.ppermute(x, BOTH, route)]
    unnamed x40 -> x38, local copies, waits for them, and re-layouts: 4.29 us -> 4.3 us
  transfers between devices with their start and end apart: 39 -> 39, of which waited for: 18 -> 19; matrix products, arithmetic and copies ran while one was open for 1% -> 1% of each run, Pallas kernels for 15% -> 13%
where the time goes in v4:
time: 107 us; the launch traced here: 106 us
  starting transfers between devices  41.8 us (39%)
  Pallas kernels  30.6 us (29%)
  waiting for transfers between devices  27.3 us (26%)
  local copies, waits for them, and re-layouts  4.34 us (4%)
  between operations  1.59 us (1%)
    ppermute x39, starting transfers between devices, move(): return lax.ppermute(x, BOTH, route)  41.8 us
    pallas_call x21, Pallas kernels, call(): pl.pallas_call(body, out_shape=[jax.ShapeDtypeStruct(s, t) for s, t in ou...  30.6 us
    ppermute x39, waiting for transfers between devices, move(): return lax.ppermute(x, BOTH, route)  27.3 us
    unnamed x38, local copies, waits for them, and re-layouts  4.3 us
  transfers between devices with their start and end apart: 39, of which 19 were waited for; matrix products, arithmetic and copies ran while one was open for 1% of the time, Pallas kernels for 13%

profile of v4, /device:TPU:0, one launch (start us, length us, event | category | flops | bytes accessed | tf_op | source)
XLA Modules:
  0.0 106.4 jit_solution(12791725227502294472)
XLA Ops:
  0.7 1.6 %pick.1.q0 = bf16[160,384]{1,0:T(8,128)(2,1)} custom-call(bf16[48,1152]{1,0:T(8,128)(2,1)} %refs_8_.2, bf16[48,384]{1,0:T(8,128)(2,1)} %refs_9_.2, bf16[48,1536]{1,0:T(8,128)(2,1)} %refs_8_.3, bf16[192,384]{1,0:T(8,128)(2,1)} %refs_9_.3, bf16[2,384]{1,0:T(2,128)(2,1)} %cond.1), custom_call_target="tpu_custom_call" | custom-call | flops 1 | bytes 1 | tf_op jit(solution)/shard_map/pick/pallas_call | solution.py:40
  3.3 3.7 %collective-permute-start = (bf16[160,384]{1,0:T(8,128)(2,1)}, bf16[160,384]{1,0:T(8,128)(2,1)S(1)}, u32[]{:S(2)}, u32[]{:S(2)}) collective-permute-start(bf16[160,384]{1,0:T(8,128)(2,1)} %pick.1.q0), channel_id=1, source_target_pairs={{0,4},{1,5},{2,6},{3,7},{4,0},{5,1},{6,2},{7,3},{8,12},{9,13},{10,... | collective-permute-start | bytes 368648 | tf_op jit(solution)/shard_map/ppermute | solution.py:597
  7.5 0.9 copy-done.3
  8.4 0.7 copy-done.12
  9.1 0.7 copy-done.13
  12.5 1.3 %collective-permute-done.q2 = bf16[160,384]{1,0:T(8,128)(2,1)S(1)} collective-permute-done((bf16[160,384]{1,0:T(8,128)(2,1)}, bf16[160,384]{1,0:T(8,128)(2,1)S(1)}, u32[]{:S(2)}, u32[]{:S(2)}) %collective-permute-start) | collective-permute-done | bytes 122912 | tf_op jit(solution)/shard_map/ppermute | solution.py:597
  13.7 1.4 %collective-permute-start.7 = (bf16[160,384]{1,0:T(8,128)(2,1)}, bf16[160,384]{1,0:T(8,128)(2,1)S(1)}, u32[]{:S(2)}, u32[]{:S(2)}) collective-permute-start(bf16[160,384]{1,0:T(8,128)(2,1)} %pick.1.q0), channel_id=1, source_target_pairs={{0,2},{1,3},{2,0},{3,1},{4,6},{5,7},{6,4},{7,5},{8,10},{9,11},{10,... | collective-permute-start | bytes 368648 | tf_op jit(solution)/shard_map/ppermute | solution.py:597
  15.1 0.7 collective-permute-start.8
  15.8 4.4 %collective-permute-done.7.q1 = bf16[160,384]{1,0:T(8,128)(2,1)S(1)} collective-permute-done((bf16[160,384]{1,0:T(8,128)(2,1)}, bf16[160,384]{1,0:T(8,128)(2,1)S(1)}, u32[]{:S(2)}, u32[]{:S(2)}) %collective-permute-start.7) | collective-permute-done | bytes 122912 | tf_op jit(solution)/shard_map/ppermute | solution.py:597
  20.2 1.5 %collective-permute-done.8.q3 = bf16[160,384]{1,0:T(8,128)(2,1)S(1)} collective-permute-done((bf16[160,384]{1,0:T(8,128)(2,1)S(1)}, bf16[160,384]{1,0:T(8,128)(2,1)S(1)}, u32[]{:S(2)}, u32[]{:S(2)}) %collective-permute-start.8) | collective-permute-done | bytes 122912 | tf_op jit(solution)/shard_map/ppermute | solution.py:597
  21.8 1.6 %collective-permute-start.9 = (bf16[3,144,384]{2,1,0:T(8,128)(2,1)S(1)}, bf16[3,144,384]{2,1,0:T(8,128)(2,1)S(1)}, u32[]{:S(2)}, u32[]{:S(2)}) collective-permute-start(bf16[3,144,384]{2,1,0:T(8,128)(2,1)S(1)} %stack.13.refs_0_), channel_id=1, source_target_pairs={{0,8},{1,17},{2,10},{3,19},{4,12},{5,21},{6,14},{7,23},{8,0},{9,25... | collective-permute-start | bytes 995336 | tf_op jit(solution)/shard_map/ppermute | solution.py:597
  24.1 0.9 modulation.1
  24.9 1.6 %collective-permute-start.10 = (f32[2,4,2304]{2,1,0:T(4,128)S(1)}, f32[2,4,2304]{2,1,0:T(4,128)S(1)}, u32[]{:S(2)}, u32[]{:S(2)}) collective-permute-start(f32[2,4,2304]{2,1,0:T(4,128)S(1)} %get-tuple-element.86), channel_id=1, source_target_pairs={{0,2},{1,3},{2,0},{3,1},{4,6},{5,7},{6,4},{7,5},{8,10},{9,11},{10,... | collective-permute-start | bytes 221192 | tf_op jit(solution)/shard_map/ppermute | solution.py:597
  26.6 1.5 %collective-permute-start.11 = (bf16[3,144,384]{2,1,0:T(8,128)(2,1)S(1)}, bf16[3,144,384]{2,1,0:T(8,128)(2,1)S(1)}, u32[]{:S(2)}, u32[]{:S(2)}) collective-permute-start(bf16[3,144,384]{2,1,0:T(8,128)(2,1)S(1)} %stack.13.refs_0_), channel_id=1, source_target_pairs={{0,16},{1,9},{2,18},{3,11},{4,20},{5,13},{6,22},{7,15},{8,24},{9,1... | collective-permute-start | bytes 995336 | tf_op jit(solution)/shard_map/ppermute | solution.py:597
  28.1 1.3 %collective-permute-done.10 = f32[2,4,2304]{2,1,0:T(4,128)S(1)} collective-permute-done((f32[2,4,2304]{2,1,0:T(4,128)S(1)}, f32[2,4,2304]{2,1,0:T(4,128)S(1)}, u32[]{:S(2)}, u32[]{:S(2)}) %collective-permute-start.10) | collective-permute-done | bytes 73760 | tf_op jit(solution)/shard_map/ppermute | solution.py:597
  29.9 2.5 %collective-permute-start.12 = (bf16[3,144,384]{2,1,0:T(8,128)(2,1)S(1)}, bf16[3,144,384]{2,1,0:T(8,128)(2,1)S(1)}, u32[]{:S(2)}, u32[]{:S(2)}) collective-permute-start(bf16[3,144,384]{2,1,0:T(8,128)(2,1)S(1)} %collective-permute-done.9.refs_1_), channel_id=1, source_target_pairs={{0,16},{1,9},{2,18},{3,11},{4,20},{5,13},{6,22},{7,15},{8,24},{9,1... | collective-permute-start | bytes 995336 | tf_op jit(solution)/shard_map/ppermute | solution.py:597
  32.5 2.6 %collective-permute-start.16 = (f32[4,2304]{1,0:T(4,128)S(1)}, f32[4,2304]{1,0:T(4,128)S(1)}, u32[]{:S(2)}, u32[]{:S(2)}) collective-permute-start(f32[4,2304]{1,0:T(4,128)S(1)} %slice_bitcast_fusion), channel_id=1, source_target_pairs={{0,4},{1,5},{2,6},{3,7},{4,0},{5,1},{6,2},{7,3},{8,12},{9,13},{10,... | collective-permute-start | bytes 110600 | tf_op jit(solution)/shard_map/ppermute | solution.py:597
  35.5 1.8 %collective-permute-done.16.refs_13_ = f32[4,2304]{1,0:T(4,128)S(1)} collective-permute-done((f32[4,2304]{1,0:T(4,128)S(1)}, f32[4,2304]{1,0:T(4,128)S(1)}, u32[]{:S(2)}, u32[]{:S(2)}) %collective-permute-start.16) | collective-permute-done | bytes 36896 | tf_op jit(solution)/shard_map/ppermute | solution.py:597
  37.6 1.5 %collective-permute-done.17.refs_7_ = bf16[3,144,384]{2,1,0:T(8,128)(2,1)S(1)} collective-permute-done((bf16[3,144,384]{2,1,0:T(8,128)(2,1)S(1)}, bf16[3,144,384]{2,1,0:T(8,128)(2,1)S(1)}, u32[]{:S(2)}, u32[]{:S(2)}) %collective-permute-start.17) | collective-permute-done | bytes 331808 | tf_op jit(solution)/shard_map/ppermute | solution.py:597
  39.2 3.5 %attention.1 = (bf16[4,384,384]{2,1,0:T(8,128)(2,1)S(1)}, f32[4,2304]{1,0:T(4,128)S(1)}, bf16[512,384]{1,0:T(8,128)(2,1)S(1)}, bf16[512,1152]{1,0:T(8,128)(2,1)}, bf16[512,384]{1,0:T(8,128)(2,1)S(1)}) custom-call(s32[3]{0:T(128)S(1)} %pad_add_fusion.ids, bf16[3,144,384]{2,1,0:T(8,128)(2,1)S(1)} %stack.13.refs_0_, ...), custom_call_target="tpu_custom_call" | custom-call | flops 1 | bytes 1 | tf_op jit(solution)/shard_map/attention/pallas_call | solution.py:40
  42.8 9.2 %mlp.1 = (bf16[2,256,384]{2,1,0:T(8,128)(2,1)}, f32[2,256,384]{2,1,0:T(8,128)}, bf16[512,384]{1,0:T(8,128)(2,1)S(1)}, bf16[512,384]{1,0:T(8,128)(2,1)S(1)}, f32[...) custom-call(s32[3]{0:T(128)S(1)} %pad_add_fusion.ids, ...), custom_call_target="tpu_custom_call" | custom-call | flops 1 | bytes 1 | tf_op jit(solution)/shard_map/mlp/pallas_call | solution.py:40
  52.1 2.8 %attention_back_first.1.g_first = bf16[256,1152]{1,0:T(8,128)(2,1)S(1)} custom-call(bf16[512,1152]{1,0:T(8,128)(2,1)S(1)} %copy-done, bf16[512,384]{1,0:T(8,128)(2,1)S(1)} %get-tuple-element.95.gatt), custom_call_target="tpu_custom_call" | custom-call | flops 1 | bytes 1 | tf_op jit(solution)/shard_map/attention_back_first/pallas_call | solution.py:40
  55.1 1.6 %collective-permute-start.21 = (bf16[2,4,2,48,384]{4,3,2,1,0:T(8,128)(2,1)S(1)}, bf16[2,4,2,48,384]{4,3,2,1,0:T(8,128)(2,1)S(1)}, u32[]{:S(2)}, u32[]{:S(2)}) collective-permute-start(bf16[2,4,2,48,384]{4,3,2,1,0:T(8,128)(2,1)S(1)} %sum_ud.1), channel_id=1, source_target_pairs={{0,8},{1,17},{2,10},{3,19},{4,12},{5,21},{6,14},{7,23},{8,0},{9,25... | collective-permute-start | bytes 1769480 | tf_op jit(solution)/shard_map/ppermute | solution.py:597
  56.6 4.4 %attention_back.1 = (bf16[512,1152]{1,0:T(8,128)(2,1)S(1)}, f32[1,3072]{1,0:T(1,128)S(1)}, bf16[2,4,48,384]{3,2,1,0:T(8,128)(2,1)S(1)}, bf16[2,4,48,384]{3,2,1,0...) custom-call(s32[3]{0:T(128)S(1)} %pad_add_fusion.ids, ...), custom_call_target="tpu_custom_call" | custom-call | flops 1 | bytes 1 | tf_op jit(solution)/shard_map/attention_back/pallas_call | solution.py:40
  61.1 0.7 collective-permute-start.22
  61.8 2.5 %input_back.1 = (bf16[2,256,384]{2,1,0:T(8,128)(2,1)}, bf16[2,3840]{1,0:T(2,128)(2,1)S(1)}) custom-call(s32[3]{0:T(128)S(1)} %pad_add_fusion.ids, bf16[512,1152]{1,0:T(8,128)(2,1)S(1)} %get-tuple-element.103.gproj, bf16[4,384,384]{2,1,0:T(8,128)(2,1)S(1)} %get-tuple-element.90.wpo, bf16[2,256,384]{2,1,0:T(8,128)(2,1)S(1)} %copy-done.1, ...), custom_call_target="tpu_custom_call" | custom-call | flops 1 | bytes 1 | tf_op jit(solution)/shard_map/input_back/pallas_call | solution.py:40
  64.3 0.7 collective-permute-done.21.got_ud
  65.1 1.6 %collective-permute-start.23 = (bf16[2,4,48,384]{3,2,1,0:T(8,128)(2,1)S(1)}, bf16[2,4,48,384]{3,2,1,0:T(8,128)(2,1)S(1)}, u32[]{:S(2)}, u32[]{:S(2)}) collective-permute-start(bf16[2,4,48,384]{3,2,1,0:T(8,128)(2,1)S(1)} %sum_po.1), channel_id=1, source_target_pairs={{0,8},{1,17},{2,10},{3,19},{4,12},{5,21},{6,14},{7,23},{8,0},{9,25... | collective-permute-start | bytes 884744 | tf_op jit(solution)/shard_map/ppermute | solution.py:597
  67.2 1.2 %collective-permute-done.24.c_other = bf16[8,384]{1,0:T(8,128)(2,1)S(1)} collective-permute-done((bf16[8,384]{1,0:T(8,128)(2,1)S(1)}, bf16[8,384]{1,0:T(8,128)(2,1)S(1)}, u32[]{:S(2)}, u32[]{:S(2)}) %collective-permute-start.24) | collective-permute-done | bytes 6176 | tf_op jit(solution)/shard_map/ppermute | solution.py:597
  68.4 2.6 %collective-permute-start.26 = (bf16[4,3840]{1,0:T(4,128)(2,1)S(1)}, bf16[4,3840]{1,0:T(4,128)(2,1)S(1)}, u32[]{:S(2)}, u32[]{:S(2)}) collective-permute-start(bf16[4,3840]{1,0:T(4,128)(2,1)S(1)} %pair.1.g0), channel_id=1, source_target_pairs={{0,4},{1,5},{2,6},{3,7},{4,0},{5,1},{6,2},{7,3},{8,12},{9,13},{10,... | collective-permute-start | bytes 92168 | tf_op jit(solution)/shard_map/ppermute | solution.py:597
  71.0 2.3 %collective-permute-done.26.g2 = bf16[4,3840]{1,0:T(4,128)(2,1)S(1)} collective-permute-done((bf16[4,3840]{1,0:T(4,128)(2,1)S(1)}, bf16[4,3840]{1,0:T(4,128)(2,1)S(1)}, u32[]{:S(2)}, u32[]{:S(2)}) %collective-permute-start.26) | collective-permute-done | bytes 30752 | tf_op jit(solution)/shard_map/ppermute | solution.py:597
  73.4 2.1 %collective-permute-start.27 = (bf16[4,144,384]{2,1,0:T(8,128)(2,1)S(1)}, bf16[4,144,384]{2,1,0:T(8,128)(2,1)S(1)}, u32[]{:S(2)}, u32[]{:S(2)}) collective-permute-start(bf16[4,144,384]{2,1,0:T(8,128)(2,1)S(1)} %turn.1), channel_id=1, source_target_pairs={{0,16},{1,9},{2,18},{3,11},{4,20},{5,13},{6,22},{7,15},{8,24},{9,1... | collective-permute-start | bytes 1327112 | tf_op jit(solution)/shard_map/ppermute | solution.py:597
  75.5 2.9 %collective-permute-start.28 = (bf16[4,3840]{1,0:T(4,128)(2,1)S(1)}, bf16[4,3840]{1,0:T(4,128)(2,1)S(1)}, u32[]{:S(2)}, u32[]{:S(2)}) collective-permute-start(bf16[4,3840]{1,0:T(4,128)(2,1)S(1)} %pair.1.g0), channel_id=1, source_target_pairs={{0,2},{1,3},{2,0},{3,1},{4,6},{5,7},{6,4},{7,5},{8,10},{9,11},{10,... | collective-permute-start | bytes 92168 | tf_op jit(solution)/shard_map/ppermute | solution.py:597
  78.4 1.8 %collective-permute-done.28.g1 = bf16[4,3840]{1,0:T(4,128)(2,1)S(1)} collective-permute-done((bf16[4,3840]{1,0:T(4,128)(2,1)S(1)}, bf16[4,3840]{1,0:T(4,128)(2,1)S(1)}, u32[]{:S(2)}, u32[]{:S(2)}) %collective-permute-start.28) | collective-permute-done | bytes 30752 | tf_op jit(solution)/shard_map/ppermute | solution.py:597
  80.2 2.0 %collective-permute-done.29.g3 = bf16[4,3840]{1,0:T(4,128)(2,1)S(1)} collective-permute-done((bf16[4,3840]{1,0:T(4,128)(2,1)S(1)}, bf16[4,3840]{1,0:T(4,128)(2,1)S(1)}, u32[]{:S(2)}, u32[]{:S(2)}) %collective-permute-start.29) | collective-permute-done | bytes 30752 | tf_op jit(solution)/shard_map/ppermute | solution.py:597
  82.3 0.8 cond_back.1
  83.4 1.4 %collective-permute-start.30 = (bf16[2,160,384]{2,1,0:T(8,128)(2,1)S(1)}, bf16[2,160,384]{2,1,0:T(8,128)(2,1)S(1)}, u32[]{:S(2)}, u32[]{:S(2)}) collective-permute-start(bf16[2,160,384]{2,1,0:T(8,128)(2,1)S(1)} %join_far.1), channel_id=1, source_target_pairs={{0,2},{1,3},{2,0},{3,1},{4,6},{5,7},{6,4},{7,5},{8,10},{9,11},{10,... | collective-permute-start | bytes 737288 | tf_op jit(solution)/shard_map/ppermute | solution.py:597
  84.8 1.0 collective-permute-start.32
  85.8 1.6 %collective-permute-start.33 = (bf16[16,4224]{1,0:T(8,128)(2,1)S(1)}, bf16[16,4224]{1,0:T(8,128)(2,1)S(1)}, u32[]{:S(2)}, u32[]{:S(2)}) collective-permute-start(bf16[16,4224]{1,0:T(8,128)(2,1)S(1)} %pack.1.e0), channel_id=1, source_target_pairs={{0,16},{1,9},{2,18},{3,11},{4,20},{5,13},{6,22},{7,15},{8,24},{9,1... | collective-permute-start | bytes 405512 | tf_op jit(solution)/shard_map/ppermute | solution.py:597
  87.5 0.9 collective-permute-start.34
  88.4 1.3 %collective-permute-done.30.got = bf16[2,160,384]{2,1,0:T(8,128)(2,1)S(1)} collective-permute-done((bf16[2,160,384]{2,1,0:T(8,128)(2,1)S(1)}, bf16[2,160,384]{2,1,0:T(8,128)(2,1)S(1)}, u32[]{:S(2)}, u32[]{:S(2)}) %collective-permute-start.30) | collective-permute-done | bytes 245792 | tf_op jit(solution)/shard_map/ppermute | solution.py:597
  89.7 3.3 %collective-permute-start.31 = (bf16[160,384]{1,0:T(8,128)(2,1)S(1)}, bf16[160,384]{1,0:T(8,128)(2,1)S(1)}, u32[]{:S(2)}, u32[]{:S(2)}) collective-permute-start(bf16[160,384]{1,0:T(8,128)(2,1)S(1)} %get-tuple-element.124), channel_id=1, source_target_pairs={{0,4},{1,5},{2,6},{3,7},{4,0},{5,1},{6,2},{7,3},{8,12},{9,13},{10,... | collective-permute-start | bytes 368648 | tf_op jit(solution)/shard_map/ppermute | solution.py:597
  93.4 2.1 %mod_weight.1 = (f32[48,2304]{1,0:T(8,128)}, f32[288]{0:T(512)}, f32[96]{0:T(128)}, f32[48]{0:T(128)}, f32[192]{0:T(256)}, /*index=5*/f32[48]{0:T(128)}) custom-call(s32[3]{0:T(128)S(1)} %pad_add_fusion.ids, bf16[16,4224]{1,0:T(8,128)(2,1)S(1)} %pack.1.e0, bf16[16,4224]{1,0:T(8,128)(2,1)S(1)} %collective-permute-done.32.e1, ...), custom_call_target="tpu_custom_call" | custom-call | flops 1 | bytes 1 | tf_op jit(solution)/shard_map/mod_weight/pallas_call | solution.py:40
  95.5 1.8 %collective-permute-done.31.got = bf16[160,384]{1,0:T(8,128)(2,1)S(1)} collective-permute-done((bf16[160,384]{1,0:T(8,128)(2,1)S(1)}, bf16[160,384]{1,0:T(8,128)(2,1)S(1)}, u32[]{:S(2)}, u32[]{:S(2)}) %collective-permute-start.31) | collective-permute-done | bytes 122912 | tf_op jit(solution)/shard_map/ppermute | solution.py:597
  98.0 2.9 %collective-permute-start.38 = (bf16[144,384]{1,0:T(8,128)(2,1)S(1)}, bf16[144,384]{1,0:T(8,128)(2,1)S(1)}, u32[]{:S(2)}, u32[]{:S(2)}) collective-permute-start(bf16[144,384]{1,0:T(8,128)(2,1)S(1)} %get-tuple-element.130.g0), channel_id=1, source_target_pairs={{0,24},{1,25},{2,26},{3,27},{4,28},{5,29},{6,30},{7,31},{8,16},{9,... | collective-permute-start | bytes 331784 | tf_op jit(solution)/shard_map/ppermute | solution.py:597
  101.5 1.8 %collective-permute-done.36.g1 = bf16[144,384]{1,0:T(8,128)(2,1)S(1)} collective-permute-done((bf16[144,384]{1,0:T(8,128)(2,1)S(1)}, bf16[144,384]{1,0:T(8,128)(2,1)S(1)}, u32[]{:S(2)}, u32[]{:S(2)}) %collective-permute-start.36) | collective-permute-done | bytes 110624 | tf_op jit(solution)/shard_map/ppermute | solution.py:597
  103.3 1.6 %collective-permute-done.38.g3 = bf16[144,384]{1,0:T(8,128)(2,1)S(1)} collective-permute-done((bf16[144,384]{1,0:T(8,128)(2,1)S(1)}, bf16[144,384]{1,0:T(8,128)(2,1)S(1)}, u32[]{:S(2)}, u32[]{:S(2)}) %collective-permute-start.38) | collective-permute-done | bytes 110624 | tf_op jit(solution)/shard_map/ppermute | solution.py:597
  104.8 1.5 %final.1 = (f32[48,1152]{1,0:T(8,128)}, f32[48,384]{1,0:T(8,128)}, f32[48,1536]{1,0:T(8,128)}, f32[192,384]{1,0:T(8,128)}) custom-call(s32[3]{0:T(128)S(1)} %pad_add_fusion.ids, bf16[144,384]{1,0:T(8,128)(2,1)S(1)} %get-tuple-element.130.g0, bf16[144,384]{1,0:T(8,128)(2,1)S(1)} %collective-permute-done.36.g1, ...), custom_call_target="tpu_custom_call" | custom-call | flops 1 | bytes 1 | tf_op jit(solution)/shard_map/final/pallas_call | solution.py:40
  (95 shorter events, 9.0 us)
Async XLA Ops:
  0.6 38.5 %copy-start.9 = (bf16[48,1152]{1,0:T(8,128)(2,1)S(1)}, bf16[48,1152]{1,0:T(8,128)(2,1)}, u32[]{:S(2)}) copy-start(bf16[48,1152]{1,0:T(8,128)(2,1)} %refs_8_.2) | copy-start | bytes 331780
  0.7 38.5 %copy-start.11 = (bf16[48,384]{1,0:T(8,128)(2,1)S(1)}, bf16[48,384]{1,0:T(8,128)(2,1)}, u32[]{:S(2)}) copy-start(bf16[48,384]{1,0:T(8,128)(2,1)} %refs_9_.2) | copy-start | bytes 110596
  2.2 36.9 %copy-start.1 = (bf16[2,256,384]{2,1,0:T(8,128)(2,1)S(1)}, bf16[2,256,384]{2,1,0:T(8,128)(2,1)}, u32[]{:S(2)}) copy-start(bf16[2,256,384]{2,1,0:T(8,128)(2,1)} %lat.1) | copy-start | bytes 1179652
  2.3 4.9 %collective-permute-start.1 = (bf16[48,2304]{1,0:T(8,128)(2,1)}, bf16[48,2304]{1,0:T(8,128)(2,1)S(1)}, u32[]{:S(2)}, u32[]{:S(2)}) collective-permute-start(bf16[48,2304]{1,0:T(8,128)(2,1)} %wmod.1), channel_id=1, source_target_pairs={{0,1},{1,0},{2,3},{3,2},{4,5},{5,4},{6,7},{7,6},{8,9},{9,8},{10,11... | collective-permute-start | bytes 663560 | tf_op jit(solution)/shard_map/ppermute | solution.py:597
  2.8 10.9 %collective-permute-start.5 = (bf16[48,1536]{1,0:T(8,128)(2,1)}, bf16[48,1536]{1,0:T(8,128)(2,1)S(1)}, u32[]{:S(2)}, u32[]{:S(2)}) collective-permute-start(bf16[48,1536]{1,0:T(8,128)(2,1)} %refs_8_.3), channel_id=1, source_target_pairs={{0,1},{1,0},{2,3},{3,2},{4,5},{5,4},{6,7},{7,6},{8,9},{9,8},{10,11... | collective-permute-start | bytes 442376 | tf_op jit(solution)/shard_map/ppermute | solution.py:597
  2.9 10.9 %collective-permute-start.6 = (bf16[192,384]{1,0:T(8,128)(2,1)}, bf16[192,384]{1,0:T(8,128)(2,1)S(1)}, u32[]{:S(2)}, u32[]{:S(2)}) collective-permute-start(bf16[192,384]{1,0:T(8,128)(2,1)} %refs_9_.3), channel_id=1, source_target_pairs={{0,1},{1,0},{2,3},{3,2},{4,5},{5,4},{6,7},{7,6},{8,9},{9,8},{10,11... | collective-permute-start | bytes 442376 | tf_op jit(solution)/shard_map/ppermute | solution.py:597
  3.3 10.4 %collective-permute-start = (bf16[160,384]{1,0:T(8,128)(2,1)}, bf16[160,384]{1,0:T(8,128)(2,1)S(1)}, u32[]{:S(2)}, u32[]{:S(2)}) collective-permute-start(bf16[160,384]{1,0:T(8,128)(2,1)} %pick.1.q0), channel_id=1, source_target_pairs={{0,4},{1,5},{2,6},{3,7},{4,0},{5,1},{6,2},{7,3},{8,12},{9,13},{10,... | collective-permute-start | bytes 368648 | tf_op jit(solution)/shard_map/ppermute | solution.py:597
  7.0 5.5 %collective-permute-start.3 = (bf16[48,1152]{1,0:T(8,128)(2,1)}, bf16[48,1152]{1,0:T(8,128)(2,1)S(1)}, u32[]{:S(2)}, u32[]{:S(2)}) collective-permute-start(bf16[48,1152]{1,0:T(8,128)(2,1)} %refs_8_.2), channel_id=1, source_target_pairs={{0,1},{1,0},{2,3},{3,2},{4,5},{5,4},{6,7},{7,6},{8,9},{9,8},{10,11... | collective-permute-start | bytes 331784 | tf_op jit(solution)/shard_map/ppermute | solution.py:597
  7.1 5.1 %collective-permute-start.4 = (bf16[48,384]{1,0:T(8,128)(2,1)}, bf16[48,384]{1,0:T(8,128)(2,1)S(1)}, u32[]{:S(2)}, u32[]{:S(2)}) collective-permute-start(bf16[48,384]{1,0:T(8,128)(2,1)} %refs_9_.2), channel_id=1, source_target_pairs={{0,1},{1,0},{2,3},{3,2},{4,5},{5,4},{6,7},{7,6},{8,9},{9,8},{10,11... | collective-permute-start | bytes 110600 | tf_op jit(solution)/shard_map/ppermute | solution.py:597
  11.7 12.4 %copy-start.8 = (bf16[160,384]{1,0:T(8,128)(2,1)S(1)}, bf16[160,384]{1,0:T(8,128)(2,1)}, u32[]{:S(2)}) copy-start(bf16[160,384]{1,0:T(8,128)(2,1)} %pick.1.q0) | copy-start | bytes 368644
  12.2 1.5 %collective-permute-start.2 = (f32[3,2304]{1,0:T(4,128)S(1)}, f32[3,2304]{1,0:T(4,128)S(1)}, u32[]{:S(2)}, u32[]{:S(2)}) collective-permute-start(f32[3,2304]{1,0:T(4,128)S(1)} %get-tuple-element.77.placed), channel_id=1, source_target_pairs={{0,1},{1,0},{2,3},{3,2},{4,5},{5,4},{6,7},{7,6},{8,9},{9,8},{10,11... | collective-permute-start | bytes 82952 | tf_op jit(solution)/shard_map/ppermute | solution.py:597
  13.7 6.5 %collective-permute-start.7 = (bf16[160,384]{1,0:T(8,128)(2,1)}, bf16[160,384]{1,0:T(8,128)(2,1)S(1)}, u32[]{:S(2)}, u32[]{:S(2)}) collective-permute-start(bf16[160,384]{1,0:T(8,128)(2,1)} %pick.1.q0), channel_id=1, source_target_pairs={{0,2},{1,3},{2,0},{3,1},{4,6},{5,7},{6,4},{7,5},{8,10},{9,11},{10,... | collective-permute-start | bytes 368648 | tf_op jit(solution)/shard_map/ppermute | solution.py:597
  15.1 6.7 %collective-permute-start.8 = (bf16[160,384]{1,0:T(8,128)(2,1)S(1)}, bf16[160,384]{1,0:T(8,128)(2,1)S(1)}, u32[]{:S(2)}, u32[]{:S(2)}) collective-permute-start(bf16[160,384]{1,0:T(8,128)(2,1)S(1)} %collective-permute-done.q2), channel_id=1, source_target_pairs={{0,2},{1,3},{2,0},{3,1},{4,6},{5,7},{6,4},{7,5},{8,10},{9,11},{10,... | collective-permute-start | bytes 368648 | tf_op jit(solution)/shard_map/ppermute | solution.py:597
  21.8 8.1 %collective-permute-start.9 = (bf16[3,144,384]{2,1,0:T(8,128)(2,1)S(1)}, bf16[3,144,384]{2,1,0:T(8,128)(2,1)S(1)}, u32[]{:S(2)}, u32[]{:S(2)}) collective-permute-start(bf16[3,144,384]{2,1,0:T(8,128)(2,1)S(1)} %stack.13.refs_0_), channel_id=1, source_target_pairs={{0,8},{1,17},{2,10},{3,19},{4,12},{5,21},{6,14},{7,23},{8,0},{9,25... | collective-permute-start | bytes 995336 | tf_op jit(solution)/shard_map/ppermute | solution.py:597
  24.9 4.4 %collective-permute-start.10 = (f32[2,4,2304]{2,1,0:T(4,128)S(1)}, f32[2,4,2304]{2,1,0:T(4,128)S(1)}, u32[]{:S(2)}, u32[]{:S(2)}) collective-permute-start(f32[2,4,2304]{2,1,0:T(4,128)S(1)} %get-tuple-element.86), channel_id=1, source_target_pairs={{0,2},{1,3},{2,0},{3,1},{4,6},{5,7},{6,4},{7,5},{8,10},{9,11},{10,... | collective-permute-start | bytes 221192 | tf_op jit(solution)/shard_map/ppermute | solution.py:597
  26.6 9.0 %collective-permute-start.11 = (bf16[3,144,384]{2,1,0:T(8,128)(2,1)S(1)}, bf16[3,144,384]{2,1,0:T(8,128)(2,1)S(1)}, u32[]{:S(2)}, u32[]{:S(2)}) collective-permute-start(bf16[3,144,384]{2,1,0:T(8,128)(2,1)S(1)} %stack.13.refs_0_), channel_id=1, source_target_pairs={{0,16},{1,9},{2,18},{3,11},{4,20},{5,13},{6,22},{7,15},{8,24},{9,1... | collective-permute-start | bytes 995336 | tf_op jit(solution)/shard_map/ppermute | solution.py:597
  29.9 7.6 %collective-permute-start.12 = (bf16[3,144,384]{2,1,0:T(8,128)(2,1)S(1)}, bf16[3,144,384]{2,1,0:T(8,128)(2,1)S(1)}, u32[]{:S(2)}, u32[]{:S(2)}) collective-permute-start(bf16[3,144,384]{2,1,0:T(8,128)(2,1)S(1)} %collective-permute-done.9.refs_1_), channel_id=1, source_target_pairs={{0,16},{1,9},{2,18},{3,11},{4,20},{5,13},{6,22},{7,15},{8,24},{9,1... | collective-permute-start | bytes 995336 | tf_op jit(solution)/shard_map/ppermute | solution.py:597
  32.4 10.3 %copy-start.6 = (bf16[48,1536]{1,0:T(8,128)(2,1)S(1)}, bf16[48,1536]{1,0:T(8,128)(2,1)}, u32[]{:S(2)}) copy-start(bf16[48,1536]{1,0:T(8,128)(2,1)} %refs_8_.3) | copy-start | bytes 442372
  32.4 10.3 %copy-start.7 = (bf16[192,384]{1,0:T(8,128)(2,1)S(1)}, bf16[192,384]{1,0:T(8,128)(2,1)}, u32[]{:S(2)}) copy-start(bf16[192,384]{1,0:T(8,128)(2,1)} %refs_9_.3) | copy-start | bytes 442372
  32.4 10.3 %copy-start.10 = (bf16[2,256,384]{2,1,0:T(8,128)(2,1)S(1)}, bf16[2,256,384]{2,1,0:T(8,128)(2,1)}, u32[]{:S(2)}) copy-start(bf16[2,256,384]{2,1,0:T(8,128)(2,1)} %refs_15_.1) | copy-start | bytes 1179652
  32.5 4.9 %collective-permute-start.16 = (f32[4,2304]{1,0:T(4,128)S(1)}, f32[4,2304]{1,0:T(4,128)S(1)}, u32[]{:S(2)}, u32[]{:S(2)}) collective-permute-start(f32[4,2304]{1,0:T(4,128)S(1)} %slice_bitcast_fusion), channel_id=1, source_target_pairs={{0,4},{1,5},{2,6},{3,7},{4,0},{5,1},{6,2},{7,3},{8,12},{9,13},{10,... | collective-permute-start | bytes 110600 | tf_op jit(solution)/shard_map/ppermute | solution.py:597
  35.0 2.5 %collective-permute-start.13 = (bf16[3,144,384]{2,1,0:T(8,128)(2,1)S(1)}, bf16[3,144,384]{2,1,0:T(8,128)(2,1)S(1)}, u32[]{:S(2)}, u32[]{:S(2)}) collective-permute-start(bf16[3,144,384]{2,1,0:T(8,128)(2,1)S(1)} %stack.13.refs_0_), channel_id=1, source_target_pairs={{0,1},{1,0},{2,3},{3,2},{4,5},{5,4},{6,7},{7,6},{8,9},{9,8},{10,11... | collective-permute-start | bytes 995336 | tf_op jit(solution)/shard_map/ppermute | solution.py:597
  35.0 2.5 %collective-permute-start.14 = (bf16[3,144,384]{2,1,0:T(8,128)(2,1)S(1)}, bf16[3,144,384]{2,1,0:T(8,128)(2,1)S(1)}, u32[]{:S(2)}, u32[]{:S(2)}) collective-permute-start(bf16[3,144,384]{2,1,0:T(8,128)(2,1)S(1)} %collective-permute-done.9.refs_1_), channel_id=1, source_target_pairs={{0,1},{1,0},{2,3},{3,2},{4,5},{5,4},{6,7},{7,6},{8,9},{9,8},{10,11... | collective-permute-start | bytes 995336 | tf_op jit(solution)/shard_map/ppermute | solution.py:597
  35.5 2.1 %collective-permute-start.15 = (bf16[3,144,384]{2,1,0:T(8,128)(2,1)S(1)}, bf16[3,144,384]{2,1,0:T(8,128)(2,1)S(1)}, u32[]{:S(2)}, u32[]{:S(2)}) collective-permute-start(bf16[3,144,384]{2,1,0:T(8,128)(2,1)S(1)} %collective-permute-done.11.refs_2_), channel_id=1, source_target_pairs={{0,1},{1,0},{2,3},{3,2},{4,5},{5,4},{6,7},{7,6},{8,9},{9,8},{10,11... | collective-permute-start | bytes 995336 | tf_op jit(solution)/shard_map/ppermute | solution.py:597
  37.5 1.6 %collective-permute-start.17 = (bf16[3,144,384]{2,1,0:T(8,128)(2,1)S(1)}, bf16[3,144,384]{2,1,0:T(8,128)(2,1)S(1)}, u32[]{:S(2)}, u32[]{:S(2)}) collective-permute-start(bf16[3,144,384]{2,1,0:T(8,128)(2,1)S(1)} %collective-permute-done.12.refs_3_), channel_id=1, source_target_pairs={{0,1},{1,0},{2,3},{3,2},{4,5},{5,4},{6,7},{7,6},{8,9},{9,8},{10,11... | collective-permute-start | bytes 995336 | tf_op jit(solution)/shard_map/ppermute | solution.py:597
  42.8 9.3 %copy-start = (bf16[512,1152]{1,0:T(8,128)(2,1)S(1)}, bf16[512,1152]{1,0:T(8,128)(2,1)}, u32[]{:S(2)}) copy-start(bf16[512,1152]{1,0:T(8,128)(2,1)} %get-tuple-element.94.proj) | copy-start | bytes 3538948
  52.0 2.9 %collective-permute-start.18 = (bf16[2,4,2,48,384]{4,3,2,1,0:T(8,128)(2,1)}, bf16[2,4,2,48,384]{4,3,2,1,0:T(8,128)(2,1)S(1)}, u32[]{:S(2)}, u32[]{:S(2)}) collective-permute-start(bf16[2,4,2,48,384]{4,3,2,1,0:T(8,128)(2,1)} %get-tuple-element.100), channel_id=1, source_target_pairs={{0,1},{1,0},{2,3},{3,2},{4,5},{5,4},{6,7},{7,6},{8,9},{9,8},{10,11... | collective-permute-start | bytes 1769480 | tf_op jit(solution)/shard_map/ppermute | solution.py:597
  55.1 9.9 %collective-permute-start.21 = (bf16[2,4,2,48,384]{4,3,2,1,0:T(8,128)(2,1)S(1)}, bf16[2,4,2,48,384]{4,3,2,1,0:T(8,128)(2,1)S(1)}, u32[]{:S(2)}, u32[]{:S(2)}) collective-permute-start(bf16[2,4,2,48,384]{4,3,2,1,0:T(8,128)(2,1)S(1)} %sum_ud.1), channel_id=1, source_target_pairs={{0,8},{1,17},{2,10},{3,19},{4,12},{5,21},{6,14},{7,23},{8,0},{9,25... | collective-permute-start | bytes 1769480 | tf_op jit(solution)/shard_map/ppermute | solution.py:597
  61.1 3.3 %collective-permute-start.22 = (bf16[2,4,48,384]{3,2,1,0:T(8,128)(2,1)S(1)}, bf16[2,4,48,384]{3,2,1,0:T(8,128)(2,1)S(1)}, u32[]{:S(2)}, u32[]{:S(2)}) collective-permute-start(bf16[2,4,48,384]{3,2,1,0:T(8,128)(2,1)S(1)} %get-tuple-element.113), channel_id=1, source_target_pairs={{0,1},{1,0},{2,3},{3,2},{4,5},{5,4},{6,7},{7,6},{8,9},{9,8},{10,11... | collective-permute-start | bytes 884744 | tf_op jit(solution)/shard_map/ppermute | solution.py:597
  61.8 11.5 %collective-permute-start.19 = (bf16[2,4,2,48,384]{4,3,2,1,0:T(8,128)(2,1)S(1)}, bf16[2,4,2,48,384]{4,3,2,1,0:T(8,128)(2,1)S(1)}, u32[]{:S(2)}, u32[]{:S(2)}) collective-permute-start(bf16[2,4,2,48,384]{4,3,2,1,0:T(8,128)(2,1)S(1)} %copy-done.18), channel_id=1, source_target_pairs={{0,1},{1,0},{2,3},{3,2},{4,5},{5,4},{6,7},{7,6},{8,9},{9,8},{10,11... | collective-permute-start | bytes 1769480 | tf_op jit(solution)/shard_map/ppermute | solution.py:597
  65.1 8.1 %collective-permute-start.23 = (bf16[2,4,48,384]{3,2,1,0:T(8,128)(2,1)S(1)}, bf16[2,4,48,384]{3,2,1,0:T(8,128)(2,1)S(1)}, u32[]{:S(2)}, u32[]{:S(2)}) collective-permute-start(bf16[2,4,48,384]{3,2,1,0:T(8,128)(2,1)S(1)} %sum_po.1), channel_id=1, source_target_pairs={{0,8},{1,17},{2,10},{3,19},{4,12},{5,21},{6,14},{7,23},{8,0},{9,25... | collective-permute-start | bytes 884744 | tf_op jit(solution)/shard_map/ppermute | solution.py:597
  66.7 6.6 %collective-permute-start.20 = (bf16[2,4,48,384]{3,2,1,0:T(8,128)(2,1)S(1)}, bf16[2,4,48,384]{3,2,1,0:T(8,128)(2,1)S(1)}, u32[]{:S(2)}, u32[]{:S(2)}) collective-permute-start(bf16[2,4,48,384]{3,2,1,0:T(8,128)(2,1)S(1)} %get-tuple-element.111), channel_id=1, source_target_pairs={{0,1},{1,0},{2,3},{3,2},{4,5},{5,4},{6,7},{7,6},{8,9},{9,8},{10,11... | collective-permute-start | bytes 884744 | tf_op jit(solution)/shard_map/ppermute | solution.py:597
  66.7 1.7 %collective-permute-start.25 = (bf16[2,3840]{1,0:T(2,128)(2,1)S(1)}, bf16[2,3840]{1,0:T(2,128)(2,1)S(1)}, u32[]{:S(2)}, u32[]{:S(2)}) collective-permute-start(bf16[2,3840]{1,0:T(2,128)(2,1)S(1)} %get-tuple-element.117.own), channel_id=1, source_target_pairs={{0,1},{1,0},{2,3},{3,2},{4,5},{5,4},{6,7},{7,6},{8,9},{9,8},{10,11... | collective-permute-start | bytes 46088 | tf_op jit(solution)/shard_map/ppermute | solution.py:597
  67.2 1.2 %collective-permute-start.24 = (bf16[8,384]{1,0:T(8,128)(2,1)S(1)}, bf16[8,384]{1,0:T(8,128)(2,1)S(1)}, u32[]{:S(2)}, u32[]{:S(2)}) collective-permute-start(bf16[8,384]{1,0:T(8,128)(2,1)S(1)} %get-tuple-element.116.c_own), channel_id=1, source_target_pairs={{0,1},{1,0},{2,3},{3,2},{4,5},{5,4},{6,7},{7,6},{8,9},{9,8},{10,11... | collective-permute-start | bytes 18440 | tf_op jit(solution)/shard_map/ppermute | solution.py:597
  68.4 4.9 %collective-permute-start.26 = (bf16[4,3840]{1,0:T(4,128)(2,1)S(1)}, bf16[4,3840]{1,0:T(4,128)(2,1)S(1)}, u32[]{:S(2)}, u32[]{:S(2)}) collective-permute-start(bf16[4,3840]{1,0:T(4,128)(2,1)S(1)} %pair.1.g0), channel_id=1, source_target_pairs={{0,4},{1,5},{2,6},{3,7},{4,0},{5,1},{6,2},{7,3},{8,12},{9,13},{10,... | collective-permute-start | bytes 92168 | tf_op jit(solution)/shard_map/ppermute | solution.py:597
  73.4 9.9 %collective-permute-start.27 = (bf16[4,144,384]{2,1,0:T(8,128)(2,1)S(1)}, bf16[4,144,384]{2,1,0:T(8,128)(2,1)S(1)}, u32[]{:S(2)}, u32[]{:S(2)}) collective-permute-start(bf16[4,144,384]{2,1,0:T(8,128)(2,1)S(1)} %turn.1), channel_id=1, source_target_pairs={{0,16},{1,9},{2,18},{3,11},{4,20},{5,13},{6,22},{7,15},{8,24},{9,1... | collective-permute-start | bytes 1327112 | tf_op jit(solution)/shard_map/ppermute | solution.py:597
  75.5 4.7 %collective-permute-start.28 = (bf16[4,3840]{1,0:T(4,128)(2,1)S(1)}, bf16[4,3840]{1,0:T(4,128)(2,1)S(1)}, u32[]{:S(2)}, u32[]{:S(2)}) collective-permute-start(bf16[4,3840]{1,0:T(4,128)(2,1)S(1)} %pair.1.g0), channel_id=1, source_target_pairs={{0,2},{1,3},{2,0},{3,1},{4,6},{5,7},{6,4},{7,5},{8,10},{9,11},{10,... | collective-permute-start | bytes 92168 | tf_op jit(solution)/shard_map/ppermute | solution.py:597
  78.4 3.9 %collective-permute-start.29 = (bf16[4,3840]{1,0:T(4,128)(2,1)S(1)}, bf16[4,3840]{1,0:T(4,128)(2,1)S(1)}, u32[]{:S(2)}, u32[]{:S(2)}) collective-permute-start(bf16[4,3840]{1,0:T(4,128)(2,1)S(1)} %collective-permute-done.26.g2), channel_id=1, source_target_pairs={{0,2},{1,3},{2,0},{3,1},{4,6},{5,7},{6,4},{7,5},{8,10},{9,11},{10,... | collective-permute-start | bytes 92168 | tf_op jit(solution)/shard_map/ppermute | solution.py:597
  83.4 17.5 %copy-start.17 = (bf16[2,384]{1,0:T(2,128)(2,1)S(1)}, bf16[2,384]{1,0:T(2,128)(2,1)}, u32[]{:S(2)}) copy-start(bf16[2,384]{1,0:T(2,128)(2,1)} %cond.1) | copy-start | bytes 4612
  83.4 6.3 %collective-permute-start.30 = (bf16[2,160,384]{2,1,0:T(8,128)(2,1)S(1)}, bf16[2,160,384]{2,1,0:T(8,128)(2,1)S(1)}, u32[]{:S(2)}, u32[]{:S(2)}) collective-permute-start(bf16[2,160,384]{2,1,0:T(8,128)(2,1)S(1)} %join_far.1), channel_id=1, source_target_pairs={{0,2},{1,3},{2,0},{3,1},{4,6},{5,7},{6,4},{7,5},{8,10},{9,11},{10,... | collective-permute-start | bytes 737288 | tf_op jit(solution)/shard_map/ppermute | solution.py:597
  84.8 8.2 %collective-permute-start.32 = (bf16[16,4224]{1,0:T(8,128)(2,1)S(1)}, bf16[16,4224]{1,0:T(8,128)(2,1)S(1)}, u32[]{:S(2)}, u32[]{:S(2)}) collective-permute-start(bf16[16,4224]{1,0:T(8,128)(2,1)S(1)} %pack.1.e0), channel_id=1, source_target_pairs={{0,8},{1,17},{2,10},{3,19},{4,12},{5,21},{6,14},{7,23},{8,0},{9,25... | collective-permute-start | bytes 405512 | tf_op jit(solution)/shard_map/ppermute | solution.py:597
  85.8 7.2 %collective-permute-start.33 = (bf16[16,4224]{1,0:T(8,128)(2,1)S(1)}, bf16[16,4224]{1,0:T(8,128)(2,1)S(1)}, u32[]{:S(2)}, u32[]{:S(2)}) collective-permute-start(bf16[16,4224]{1,0:T(8,128)(2,1)S(1)} %pack.1.e0), channel_id=1, source_target_pairs={{0,16},{1,9},{2,18},{3,11},{4,20},{5,13},{6,22},{7,15},{8,24},{9,1... | collective-permute-start | bytes 405512 | tf_op jit(solution)/shard_map/ppermute | solution.py:597
  87.5 5.9 %collective-permute-start.34 = (bf16[16,4224]{1,0:T(8,128)(2,1)S(1)}, bf16[16,4224]{1,0:T(8,128)(2,1)S(1)}, u32[]{:S(2)}, u32[]{:S(2)}) collective-permute-start(bf16[16,4224]{1,0:T(8,128)(2,1)S(1)} %pack.1.e0), channel_id=1, source_target_pairs={{0,24},{1,25},{2,26},{3,27},{4,28},{5,29},{6,30},{7,31},{8,16},{9,... | collective-permute-start | bytes 405512 | tf_op jit(solution)/shard_map/ppermute | solution.py:597
  89.7 7.5 %collective-permute-start.31 = (bf16[160,384]{1,0:T(8,128)(2,1)S(1)}, bf16[160,384]{1,0:T(8,128)(2,1)S(1)}, u32[]{:S(2)}, u32[]{:S(2)}) collective-permute-start(bf16[160,384]{1,0:T(8,128)(2,1)S(1)} %get-tuple-element.124), channel_id=1, source_target_pairs={{0,4},{1,5},{2,6},{3,7},{4,0},{5,1},{6,2},{7,3},{8,12},{9,13},{10,... | collective-permute-start | bytes 368648 | tf_op jit(solution)/shard_map/ppermute | solution.py:597
  97.3 3.6 %collective-permute-start.35 = (f32[2,384]{1,0:T(2,128)S(1)}, f32[2,384]{1,0:T(2,128)S(1)}, u32[]{:S(2)}, u32[]{:S(2)}) collective-permute-start(f32[2,384]{1,0:T(2,128)S(1)} %slice.15), channel_id=1, source_target_pairs={{0,1},{1,0},{2,3},{3,2},{4,5},{5,4},{6,7},{7,6},{8,9},{9,8},{10,11... | collective-permute-start | bytes 9224 | tf_op jit(solution)/shard_map/ppermute | solution.py:597
  97.3 5.9 %collective-permute-start.36 = (bf16[144,384]{1,0:T(8,128)(2,1)S(1)}, bf16[144,384]{1,0:T(8,128)(2,1)S(1)}, u32[]{:S(2)}, u32[]{:S(2)}) collective-permute-start(bf16[144,384]{1,0:T(8,128)(2,1)S(1)} %get-tuple-element.130.g0), channel_id=1, source_target_pairs={{0,8},{1,17},{2,10},{3,19},{4,12},{5,21},{6,14},{7,23},{8,0},{9,25... | collective-permute-start | bytes 331784 | tf_op jit(solution)/shard_map/ppermute | solution.py:597
  97.7 5.6 %collective-permute-start.37 = (bf16[144,384]{1,0:T(8,128)(2,1)S(1)}, bf16[144,384]{1,0:T(8,128)(2,1)S(1)}, u32[]{:S(2)}, u32[]{:S(2)}) collective-permute-start(bf16[144,384]{1,0:T(8,128)(2,1)S(1)} %get-tuple-element.130.g0), channel_id=1, source_target_pairs={{0,16},{1,9},{2,18},{3,11},{4,20},{5,13},{6,22},{7,15},{8,24},{9,1... | collective-permute-start | bytes 331784 | tf_op jit(solution)/shard_map/ppermute | solution.py:597
  98.0 6.8 %collective-permute-start.38 = (bf16[144,384]{1,0:T(8,128)(2,1)S(1)}, bf16[144,384]{1,0:T(8,128)(2,1)S(1)}, u32[]{:S(2)}, u32[]{:S(2)}) collective-permute-start(bf16[144,384]{1,0:T(8,128)(2,1)S(1)} %get-tuple-element.130.g0), channel_id=1, source_target_pairs={{0,24},{1,25},{2,26},{3,27},{4,28},{5,29},{6,30},{7,31},{8,16},{9,... | collective-permute-start | bytes 331784 | tf_op jit(solution)/shard_map/ppermute | solution.py:597
  (10 other events, 32.5 us)

commit v5 on v4

--- a/solution.py
+++ b/solution.py
@@ -623,16 +623,17 @@
 
     whole = [projection_weight, output_weight, up_weight, down_weight]
     w_whole = whole + [move(after(x, q_all), core) for x in whole]
+    wmod_other = move(after(modulation_weight, q_all), core)
     biases = [modulation_bias, query_value_bias, output_bias, up_bias, down_bias]
     wmod, placed = call(
-        prepare_body, "prepare", None, [modulation_weight, move(after(modulation_weight, q_all), core)] + biases,
+        prepare_body, "prepare", None, [modulation_weight, wmod_other] + biases,
         [((2 * rows, wide), BF16), ((3, wide), F32)],
     )
     q_far = move(q_all, levels[2])
     placed_other = move(placed, core)
     ready = (placed_other, *w_whole[4:])
     q_far = after(q_far, *ready)
-    q_near, q_both = move(after(q_all, q_far), levels[1]), move(q_far, levels[1])
+    q_near, q_both = move(after(q_all, wmod_other), levels[1]), move(q_far, levels[1])
     (own,) = call(stack_body, "stack", None, [q_far, q_near, q_both], [((3, 3 * rows, feat), BF16)])
     keep_lo, keep_hi, c_own = call(
         mod_body, "modulation", ids, [q_all, q_far, q_near, q_both, wmod, placed, placed_other],
@@ -712,7 +713,7 @@
         functools.partial(turn_body, at=0), "base", None, halves[:5] + [after(got_po, turned)], [half_shape]
     )
 
-    gm_all = [gm_pair, gm_far, move(after(gm_pair, gm_far), levels[1]), move(gm_far, levels[1])]
+    gm_all = [gm_pair, gm_far, move(gm_pair, levels[1]), move(gm_far, levels[1])]
     (every,) = call(
         pack_body, "pack", None, gm_all + [c_own, c_other], [((8 * slots, 11 * feat), BF16)]
     )

time: 107 us -> 105 us (0.981)
  starting transfers between devices: 41.8 us -> 36.7 us
  waiting for transfers between devices: 27.3 us -> 31.3 us
    ppermute x39, starting transfers between devices: 41.8 us -> 36.7 us  [move(): return lax.ppermute(x, BOTH, route)]
    ppermute x39, waiting for transfers between devices: 27.3 us -> 31.3 us  [move(): return lax.ppermute(x, BOTH, route)]
  transfers between devices with their start and end apart: 39 -> 39, of which waited for: 19 -> 20; matrix products, arithmetic and copies ran while one was open for 1% -> 1% of each run, Pallas kernels for 13% -> 14%
where the time goes in v5:
time: 105 us
  starting transfers between devices  36.7 us (35%)
  waiting for transfers between devices  31.3 us (30%)
  Pallas kernels  30.6 us (29%)
  local copies, waits for them, and re-layouts  4.34 us (4%)
  between operations  1.6 us (2%)
    ppermute x39, starting transfers between devices, move(): return lax.ppermute(x, BOTH, route)  36.7 us
    ppermute x39, waiting for transfers between devices, move(): return lax.ppermute(x, BOTH, route)  31.3 us
    pallas_call x21, Pallas kernels, call(): pl.pallas_call(body, out_shape=[jax.ShapeDtypeStruct(s, t) for s, t in ou...  30.6 us
    unnamed x38, local copies, waits for them, and re-layouts  4.3 us
  transfers between devices with their start and end apart: 39, of which 20 were waited for; matrix products, arithmetic and copies ran while one was open for 1% of the time, Pallas kernels for 14%

profile of v5, /device:TPU:0, one launch (start us, length us, event | category | flops | bytes accessed | tf_op | source)
XLA Modules:
  0.0 105.2 jit_solution(17851625626670198168)
XLA Ops:
  0.7 1.6 %pick.1.q0 = bf16[160,384]{1,0:T(8,128)(2,1)} custom-call(bf16[48,1152]{1,0:T(8,128)(2,1)} %refs_8_.2, bf16[48,384]{1,0:T(8,128)(2,1)} %refs_9_.2, bf16[48,1536]{1,0:T(8,128)(2,1)} %refs_8_.3, bf16[192,384]{1,0:T(8,128)(2,1)} %refs_9_.3, bf16[2,384]{1,0:T(2,128)(2,1)} %cond.1), custom_call_target="tpu_custom_call" | custom-call | flops 1 | bytes 1 | tf_op jit(solution)/shard_map/pick/pallas_call | solution.py:40
  3.3 3.7 %collective-permute-start = (bf16[160,384]{1,0:T(8,128)(2,1)}, bf16[160,384]{1,0:T(8,128)(2,1)S(1)}, u32[]{:S(2)}, u32[]{:S(2)}) collective-permute-start(bf16[160,384]{1,0:T(8,128)(2,1)} %pick.1.q0), channel_id=1, source_target_pairs={{0,4},{1,5},{2,6},{3,7},{4,0},{5,1},{6,2},{7,3},{8,12},{9,13},{10,... | collective-permute-start | bytes 368648 | tf_op jit(solution)/shard_map/ppermute | solution.py:597
  7.5 0.9 copy-done.3
  12.5 1.6 %collective-permute-start.7 = (bf16[160,384]{1,0:T(8,128)(2,1)}, bf16[160,384]{1,0:T(8,128)(2,1)S(1)}, u32[]{:S(2)}, u32[]{:S(2)}) collective-permute-start(bf16[160,384]{1,0:T(8,128)(2,1)} %pick.1.q0), channel_id=1, source_target_pairs={{0,2},{1,3},{2,0},{3,1},{4,6},{5,7},{6,4},{7,5},{8,10},{9,11},{10,... | collective-permute-start | bytes 368648 | tf_op jit(solution)/shard_map/ppermute | solution.py:597
  14.1 1.0 collective-permute-start.8
  15.1 3.7 %collective-permute-done.7.q1 = bf16[160,384]{1,0:T(8,128)(2,1)S(1)} collective-permute-done((bf16[160,384]{1,0:T(8,128)(2,1)}, bf16[160,384]{1,0:T(8,128)(2,1)S(1)}, u32[]{:S(2)}, u32[]{:S(2)}) %collective-permute-start.7) | collective-permute-done | bytes 122912 | tf_op jit(solution)/shard_map/ppermute | solution.py:597
  18.8 2.1 %collective-permute-done.8.q3 = bf16[160,384]{1,0:T(8,128)(2,1)S(1)} collective-permute-done((bf16[160,384]{1,0:T(8,128)(2,1)S(1)}, bf16[160,384]{1,0:T(8,128)(2,1)S(1)}, u32[]{:S(2)}, u32[]{:S(2)}) %collective-permute-start.8) | collective-permute-done | bytes 122912 | tf_op jit(solution)/shard_map/ppermute | solution.py:597
  20.9 1.6 %collective-permute-start.9 = (bf16[3,144,384]{2,1,0:T(8,128)(2,1)S(1)}, bf16[3,144,384]{2,1,0:T(8,128)(2,1)S(1)}, u32[]{:S(2)}, u32[]{:S(2)}) collective-permute-start(bf16[3,144,384]{2,1,0:T(8,128)(2,1)S(1)} %stack.13.refs_0_), channel_id=1, source_target_pairs={{0,8},{1,17},{2,10},{3,19},{4,12},{5,21},{6,14},{7,23},{8,0},{9,25... | collective-permute-start | bytes 995336 | tf_op jit(solution)/shard_map/ppermute | solution.py:597
  23.2 0.9 modulation.1
  24.0 1.6 %collective-permute-start.10 = (f32[2,4,2304]{2,1,0:T(4,128)S(1)}, f32[2,4,2304]{2,1,0:T(4,128)S(1)}, u32[]{:S(2)}, u32[]{:S(2)}) collective-permute-start(f32[2,4,2304]{2,1,0:T(4,128)S(1)} %get-tuple-element.85), channel_id=1, source_target_pairs={{0,2},{1,3},{2,0},{3,1},{4,6},{5,7},{6,4},{7,5},{8,10},{9,11},{10,... | collective-permute-start | bytes 221192 | tf_op jit(solution)/shard_map/ppermute | solution.py:597
  25.7 1.5 %collective-permute-start.11 = (bf16[3,144,384]{2,1,0:T(8,128)(2,1)S(1)}, bf16[3,144,384]{2,1,0:T(8,128)(2,1)S(1)}, u32[]{:S(2)}, u32[]{:S(2)}) collective-permute-start(bf16[3,144,384]{2,1,0:T(8,128)(2,1)S(1)} %stack.13.refs_0_), channel_id=1, source_target_pairs={{0,16},{1,9},{2,18},{3,11},{4,20},{5,13},{6,22},{7,15},{8,24},{9,1... | collective-permute-start | bytes 995336 | tf_op jit(solution)/shard_map/ppermute | solution.py:597
  27.2 1.3 %collective-permute-done.10 = f32[2,4,2304]{2,1,0:T(4,128)S(1)} collective-permute-done((f32[2,4,2304]{2,1,0:T(4,128)S(1)}, f32[2,4,2304]{2,1,0:T(4,128)S(1)}, u32[]{:S(2)}, u32[]{:S(2)}) %collective-permute-start.10) | collective-permute-done | bytes 73760 | tf_op jit(solution)/shard_map/ppermute | solution.py:597
  28.8 2.5 %collective-permute-start.12 = (bf16[3,144,384]{2,1,0:T(8,128)(2,1)S(1)}, bf16[3,144,384]{2,1,0:T(8,128)(2,1)S(1)}, u32[]{:S(2)}, u32[]{:S(2)}) collective-permute-start(bf16[3,144,384]{2,1,0:T(8,128)(2,1)S(1)} %collective-permute-done.9.refs_1_), channel_id=1, source_target_pairs={{0,16},{1,9},{2,18},{3,11},{4,20},{5,13},{6,22},{7,15},{8,24},{9,1... | collective-permute-start | bytes 995336 | tf_op jit(solution)/shard_map/ppermute | solution.py:597
  31.4 1.1 %collective-permute-start.16 = (f32[4,2304]{1,0:T(4,128)S(1)}, f32[4,2304]{1,0:T(4,128)S(1)}, u32[]{:S(2)}, u32[]{:S(2)}) collective-permute-start(f32[4,2304]{1,0:T(4,128)S(1)} %slice_bitcast_fusion), channel_id=1, source_target_pairs={{0,4},{1,5},{2,6},{3,7},{4,0},{5,1},{6,2},{7,3},{8,12},{9,13},{10,... | collective-permute-start | bytes 110600 | tf_op jit(solution)/shard_map/ppermute | solution.py:597
  33.0 3.3 %collective-permute-done.16.refs_13_ = f32[4,2304]{1,0:T(4,128)S(1)} collective-permute-done((f32[4,2304]{1,0:T(4,128)S(1)}, f32[4,2304]{1,0:T(4,128)S(1)}, u32[]{:S(2)}, u32[]{:S(2)}) %collective-permute-start.16) | collective-permute-done | bytes 36896 | tf_op jit(solution)/shard_map/ppermute | solution.py:597
  36.5 1.6 %collective-permute-done.17.refs_7_ = bf16[3,144,384]{2,1,0:T(8,128)(2,1)S(1)} collective-permute-done((bf16[3,144,384]{2,1,0:T(8,128)(2,1)S(1)}, bf16[3,144,384]{2,1,0:T(8,128)(2,1)S(1)}, u32[]{:S(2)}, u32[]{:S(2)}) %collective-permute-start.17) | collective-permute-done | bytes 331808 | tf_op jit(solution)/shard_map/ppermute | solution.py:597
  38.1 3.6 %attention.1 = (bf16[4,384,384]{2,1,0:T(8,128)(2,1)S(1)}, f32[4,2304]{1,0:T(4,128)S(1)}, bf16[512,384]{1,0:T(8,128)(2,1)S(1)}, bf16[512,1152]{1,0:T(8,128)(2,1)}, bf16[512,384]{1,0:T(8,128)(2,1)S(1)}) custom-call(s32[3]{0:T(128)S(1)} %pad_add_fusion.ids, bf16[3,144,384]{2,1,0:T(8,128)(2,1)S(1)} %stack.13.refs_0_, ...), custom_call_target="tpu_custom_call" | custom-call | flops 1 | bytes 1 | tf_op jit(solution)/shard_map/attention/pallas_call | solution.py:40
  41.7 9.2 %mlp.1 = (bf16[2,256,384]{2,1,0:T(8,128)(2,1)}, f32[2,256,384]{2,1,0:T(8,128)}, bf16[512,384]{1,0:T(8,128)(2,1)S(1)}, bf16[512,384]{1,0:T(8,128)(2,1)S(1)}, f32[...) custom-call(s32[3]{0:T(128)S(1)} %pad_add_fusion.ids, ...), custom_call_target="tpu_custom_call" | custom-call | flops 1 | bytes 1 | tf_op jit(solution)/shard_map/mlp/pallas_call | solution.py:40
  51.1 2.8 %attention_back_first.1.g_first = bf16[256,1152]{1,0:T(8,128)(2,1)S(1)} custom-call(bf16[512,1152]{1,0:T(8,128)(2,1)S(1)} %copy-done, bf16[512,384]{1,0:T(8,128)(2,1)S(1)} %get-tuple-element.94.gatt), custom_call_target="tpu_custom_call" | custom-call | flops 1 | bytes 1 | tf_op jit(solution)/shard_map/attention_back_first/pallas_call | solution.py:40
  54.0 1.5 %collective-permute-start.21 = (bf16[2,4,2,48,384]{4,3,2,1,0:T(8,128)(2,1)S(1)}, bf16[2,4,2,48,384]{4,3,2,1,0:T(8,128)(2,1)S(1)}, u32[]{:S(2)}, u32[]{:S(2)}) collective-permute-start(bf16[2,4,2,48,384]{4,3,2,1,0:T(8,128)(2,1)S(1)} %sum_ud.1), channel_id=1, source_target_pairs={{0,8},{1,17},{2,10},{3,19},{4,12},{5,21},{6,14},{7,23},{8,0},{9,25... | collective-permute-start | bytes 1769480 | tf_op jit(solution)/shard_map/ppermute | solution.py:597
  55.6 4.4 %attention_back.1 = (bf16[512,1152]{1,0:T(8,128)(2,1)S(1)}, f32[1,3072]{1,0:T(1,128)S(1)}, bf16[2,4,48,384]{3,2,1,0:T(8,128)(2,1)S(1)}, bf16[2,4,48,384]{3,2,1,0...) custom-call(s32[3]{0:T(128)S(1)} %pad_add_fusion.ids, ...), custom_call_target="tpu_custom_call" | custom-call | flops 1 | bytes 1 | tf_op jit(solution)/shard_map/attention_back/pallas_call | solution.py:40
  60.8 2.5 %input_back.1 = (bf16[2,256,384]{2,1,0:T(8,128)(2,1)}, bf16[2,3840]{1,0:T(2,128)(2,1)S(1)}) custom-call(s32[3]{0:T(128)S(1)} %pad_add_fusion.ids, bf16[512,1152]{1,0:T(8,128)(2,1)S(1)} %get-tuple-element.102.gproj, bf16[4,384,384]{2,1,0:T(8,128)(2,1)S(1)} %get-tuple-element.89.wpo, bf16[2,256,384]{2,1,0:T(8,128)(2,1)S(1)} %copy-done.1, ...), custom_call_target="tpu_custom_call" | custom-call | flops 1 | bytes 1 | tf_op jit(solution)/shard_map/input_back/pallas_call | solution.py:40
  63.2 0.7 collective-permute-done.21.got_ud
  64.0 1.5 %collective-permute-start.23 = (bf16[2,4,48,384]{3,2,1,0:T(8,128)(2,1)S(1)}, bf16[2,4,48,384]{3,2,1,0:T(8,128)(2,1)S(1)}, u32[]{:S(2)}, u32[]{:S(2)}) collective-permute-start(bf16[2,4,48,384]{3,2,1,0:T(8,128)(2,1)S(1)} %sum_po.1), channel_id=1, source_target_pairs={{0,8},{1,17},{2,10},{3,19},{4,12},{5,21},{6,14},{7,23},{8,0},{9,25... | collective-permute-start | bytes 884744 | tf_op jit(solution)/shard_map/ppermute | solution.py:597
  66.1 1.2 %collective-permute-done.24.c_other = bf16[8,384]{1,0:T(8,128)(2,1)S(1)} collective-permute-done((bf16[8,384]{1,0:T(8,128)(2,1)S(1)}, bf16[8,384]{1,0:T(8,128)(2,1)S(1)}, u32[]{:S(2)}, u32[]{:S(2)}) %collective-permute-start.24) | collective-permute-done | bytes 6176 | tf_op jit(solution)/shard_map/ppermute | solution.py:597
  67.3 1.1 %collective-permute-start.26 = (bf16[4,3840]{1,0:T(4,128)(2,1)S(1)}, bf16[4,3840]{1,0:T(4,128)(2,1)S(1)}, u32[]{:S(2)}, u32[]{:S(2)}) collective-permute-start(bf16[4,3840]{1,0:T(4,128)(2,1)S(1)} %pair.1.g0), channel_id=1, source_target_pairs={{0,4},{1,5},{2,6},{3,7},{4,0},{5,1},{6,2},{7,3},{8,12},{9,13},{10,... | collective-permute-start | bytes 92168 | tf_op jit(solution)/shard_map/ppermute | solution.py:597
  68.4 3.8 %collective-permute-done.26.g2 = bf16[4,3840]{1,0:T(4,128)(2,1)S(1)} collective-permute-done((bf16[4,3840]{1,0:T(4,128)(2,1)S(1)}, bf16[4,3840]{1,0:T(4,128)(2,1)S(1)}, u32[]{:S(2)}, u32[]{:S(2)}) %collective-permute-start.26) | collective-permute-done | bytes 30752 | tf_op jit(solution)/shard_map/ppermute | solution.py:597
  72.4 2.1 %collective-permute-start.27 = (bf16[4,144,384]{2,1,0:T(8,128)(2,1)S(1)}, bf16[4,144,384]{2,1,0:T(8,128)(2,1)S(1)}, u32[]{:S(2)}, u32[]{:S(2)}) collective-permute-start(bf16[4,144,384]{2,1,0:T(8,128)(2,1)S(1)} %turn.1), channel_id=1, source_target_pairs={{0,16},{1,9},{2,18},{3,11},{4,20},{5,13},{6,22},{7,15},{8,24},{9,1... | collective-permute-start | bytes 1327112 | tf_op jit(solution)/shard_map/ppermute | solution.py:597
  74.4 2.8 %collective-permute-start.28 = (bf16[4,3840]{1,0:T(4,128)(2,1)S(1)}, bf16[4,3840]{1,0:T(4,128)(2,1)S(1)}, u32[]{:S(2)}, u32[]{:S(2)}) collective-permute-start(bf16[4,3840]{1,0:T(4,128)(2,1)S(1)} %pair.1.g0), channel_id=1, source_target_pairs={{0,2},{1,3},{2,0},{3,1},{4,6},{5,7},{6,4},{7,5},{8,10},{9,11},{10,... | collective-permute-start | bytes 92168 | tf_op jit(solution)/shard_map/ppermute | solution.py:597
  77.3 1.8 %collective-permute-done.28.g1 = bf16[4,3840]{1,0:T(4,128)(2,1)S(1)} collective-permute-done((bf16[4,3840]{1,0:T(4,128)(2,1)S(1)}, bf16[4,3840]{1,0:T(4,128)(2,1)S(1)}, u32[]{:S(2)}, u32[]{:S(2)}) %collective-permute-start.28) | collective-permute-done | bytes 30752 | tf_op jit(solution)/shard_map/ppermute | solution.py:597
  79.1 2.0 %collective-permute-done.29.g3 = bf16[4,3840]{1,0:T(4,128)(2,1)S(1)} collective-permute-done((bf16[4,3840]{1,0:T(4,128)(2,1)S(1)}, bf16[4,3840]{1,0:T(4,128)(2,1)S(1)}, u32[]{:S(2)}, u32[]{:S(2)}) %collective-permute-start.29) | collective-permute-done | bytes 30752 | tf_op jit(solution)/shard_map/ppermute | solution.py:597
  81.2 0.8 cond_back.1
  82.3 1.4 %collective-permute-start.30 = (bf16[2,160,384]{2,1,0:T(8,128)(2,1)S(1)}, bf16[2,160,384]{2,1,0:T(8,128)(2,1)S(1)}, u32[]{:S(2)}, u32[]{:S(2)}) collective-permute-start(bf16[2,160,384]{2,1,0:T(8,128)(2,1)S(1)} %join_far.1), channel_id=1, source_target_pairs={{0,2},{1,3},{2,0},{3,1},{4,6},{5,7},{6,4},{7,5},{8,10},{9,11},{10,... | collective-permute-start | bytes 737288 | tf_op jit(solution)/shard_map/ppermute | solution.py:597
  83.7 1.0 collective-permute-start.32
  84.7 1.6 %collective-permute-start.33 = (bf16[16,4224]{1,0:T(8,128)(2,1)S(1)}, bf16[16,4224]{1,0:T(8,128)(2,1)S(1)}, u32[]{:S(2)}, u32[]{:S(2)}) collective-permute-start(bf16[16,4224]{1,0:T(8,128)(2,1)S(1)} %pack.1.e0), channel_id=1, source_target_pairs={{0,16},{1,9},{2,18},{3,11},{4,20},{5,13},{6,22},{7,15},{8,24},{9,1... | collective-permute-start | bytes 405512 | tf_op jit(solution)/shard_map/ppermute | solution.py:597
  86.3 0.9 collective-permute-start.34
  87.3 1.3 %collective-permute-done.30.got = bf16[2,160,384]{2,1,0:T(8,128)(2,1)S(1)} collective-permute-done((bf16[2,160,384]{2,1,0:T(8,128)(2,1)S(1)}, bf16[2,160,384]{2,1,0:T(8,128)(2,1)S(1)}, u32[]{:S(2)}, u32[]{:S(2)}) %collective-permute-start.30) | collective-permute-done | bytes 245792 | tf_op jit(solution)/shard_map/ppermute | solution.py:597
  89.3 1.0 collective-permute-done.32.e1
  90.3 1.0 collective-permute-done.33.e2
  91.3 0.9 collective-permute-done.34.e3
  92.3 2.1 %mod_weight.1 = (f32[48,2304]{1,0:T(8,128)}, f32[288]{0:T(512)}, f32[96]{0:T(128)}, f32[48]{0:T(128)}, f32[192]{0:T(256)}, /*index=5*/f32[48]{0:T(128)}) custom-call(s32[3]{0:T(128)S(1)} %pad_add_fusion.ids, bf16[16,4224]{1,0:T(8,128)(2,1)S(1)} %pack.1.e0, bf16[16,4224]{1,0:T(8,128)(2,1)S(1)} %collective-permute-done.32.e1, ...), custom_call_target="tpu_custom_call" | custom-call | flops 1 | bytes 1 | tf_op jit(solution)/shard_map/mod_weight/pallas_call | solution.py:40
  94.6 1.4 %collective-permute-start.36 = (bf16[144,384]{1,0:T(8,128)(2,1)S(1)}, bf16[144,384]{1,0:T(8,128)(2,1)S(1)}, u32[]{:S(2)}, u32[]{:S(2)}) collective-permute-start(bf16[144,384]{1,0:T(8,128)(2,1)S(1)} %get-tuple-element.128.g0), channel_id=1, source_target_pairs={{0,8},{1,17},{2,10},{3,19},{4,12},{5,21},{6,14},{7,23},{8,0},{9,25... | collective-permute-start | bytes 331784 | tf_op jit(solution)/shard_map/ppermute | solution.py:597
  96.1 0.8 collective-permute-start.37
  96.9 1.3 %collective-permute-start.38 = (bf16[144,384]{1,0:T(8,128)(2,1)S(1)}, bf16[144,384]{1,0:T(8,128)(2,1)S(1)}, u32[]{:S(2)}, u32[]{:S(2)}) collective-permute-start(bf16[144,384]{1,0:T(8,128)(2,1)S(1)} %get-tuple-element.128.g0), channel_id=1, source_target_pairs={{0,24},{1,25},{2,26},{3,27},{4,28},{5,29},{6,30},{7,31},{8,16},{9,... | collective-permute-start | bytes 331784 | tf_op jit(solution)/shard_map/ppermute | solution.py:597
  98.8 1.2 %collective-permute-done.36.g1 = bf16[144,384]{1,0:T(8,128)(2,1)S(1)} collective-permute-done((bf16[144,384]{1,0:T(8,128)(2,1)S(1)}, bf16[144,384]{1,0:T(8,128)(2,1)S(1)}, u32[]{:S(2)}, u32[]{:S(2)}) %collective-permute-start.36) | collective-permute-done | bytes 110624 | tf_op jit(solution)/shard_map/ppermute | solution.py:597
  100.0 0.8 collective-permute-done.37.g2
  100.8 2.8 %collective-permute-done.38.g3 = bf16[144,384]{1,0:T(8,128)(2,1)S(1)} collective-permute-done((bf16[144,384]{1,0:T(8,128)(2,1)S(1)}, bf16[144,384]{1,0:T(8,128)(2,1)S(1)}, u32[]{:S(2)}, u32[]{:S(2)}) %collective-permute-start.38) | collective-permute-done | bytes 110624 | tf_op jit(solution)/shard_map/ppermute | solution.py:597
  103.7 1.5 %final.1 = (f32[48,1152]{1,0:T(8,128)}, f32[48,384]{1,0:T(8,128)}, f32[48,1536]{1,0:T(8,128)}, f32[192,384]{1,0:T(8,128)}) custom-call(s32[3]{0:T(128)S(1)} %pad_add_fusion.ids, bf16[144,384]{1,0:T(8,128)(2,1)S(1)} %get-tuple-element.128.g0, bf16[144,384]{1,0:T(8,128)(2,1)S(1)} %collective-permute-done.36.g1, ...), custom_call_target="tpu_custom_call" | custom-call | flops 1 | bytes 1 | tf_op jit(solution)/shard_map/final/pallas_call | solution.py:40
  (95 shorter events, 10.6 us)
Async XLA Ops:
  0.6 37.5 %copy-start.9 = (bf16[48,1152]{1,0:T(8,128)(2,1)S(1)}, bf16[48,1152]{1,0:T(8,128)(2,1)}, u32[]{:S(2)}) copy-start(bf16[48,1152]{1,0:T(8,128)(2,1)} %refs_8_.2) | copy-start | bytes 331780
  0.7 37.4 %copy-start.11 = (bf16[48,384]{1,0:T(8,128)(2,1)S(1)}, bf16[48,384]{1,0:T(8,128)(2,1)}, u32[]{:S(2)}) copy-start(bf16[48,384]{1,0:T(8,128)(2,1)} %refs_9_.2) | copy-start | bytes 110596
  2.2 35.8 %copy-start.1 = (bf16[2,256,384]{2,1,0:T(8,128)(2,1)S(1)}, bf16[2,256,384]{2,1,0:T(8,128)(2,1)}, u32[]{:S(2)}) copy-start(bf16[2,256,384]{2,1,0:T(8,128)(2,1)} %lat.1) | copy-start | bytes 1179652
  2.3 4.9 %collective-permute-start.1 = (bf16[48,2304]{1,0:T(8,128)(2,1)}, bf16[48,2304]{1,0:T(8,128)(2,1)S(1)}, u32[]{:S(2)}, u32[]{:S(2)}) collective-permute-start(bf16[48,2304]{1,0:T(8,128)(2,1)} %wmod.1), channel_id=1, source_target_pairs={{0,1},{1,0},{2,3},{3,2},{4,5},{5,4},{6,7},{7,6},{8,9},{9,8},{10,11... | collective-permute-start | bytes 663560 | tf_op jit(solution)/shard_map/ppermute | solution.py:597
  2.8 11.3 %collective-permute-start.5 = (bf16[48,1536]{1,0:T(8,128)(2,1)}, bf16[48,1536]{1,0:T(8,128)(2,1)S(1)}, u32[]{:S(2)}, u32[]{:S(2)}) collective-permute-start(bf16[48,1536]{1,0:T(8,128)(2,1)} %refs_8_.3), channel_id=1, source_target_pairs={{0,1},{1,0},{2,3},{3,2},{4,5},{5,4},{6,7},{7,6},{8,9},{9,8},{10,11... | collective-permute-start | bytes 442376 | tf_op jit(solution)/shard_map/ppermute | solution.py:597
  2.9 11.2 %collective-permute-start.6 = (bf16[192,384]{1,0:T(8,128)(2,1)}, bf16[192,384]{1,0:T(8,128)(2,1)S(1)}, u32[]{:S(2)}, u32[]{:S(2)}) collective-permute-start(bf16[192,384]{1,0:T(8,128)(2,1)} %refs_9_.3), channel_id=1, source_target_pairs={{0,1},{1,0},{2,3},{3,2},{4,5},{5,4},{6,7},{7,6},{8,9},{9,8},{10,11... | collective-permute-start | bytes 442376 | tf_op jit(solution)/shard_map/ppermute | solution.py:597
  3.3 10.7 %collective-permute-start = (bf16[160,384]{1,0:T(8,128)(2,1)}, bf16[160,384]{1,0:T(8,128)(2,1)S(1)}, u32[]{:S(2)}, u32[]{:S(2)}) collective-permute-start(bf16[160,384]{1,0:T(8,128)(2,1)} %pick.1.q0), channel_id=1, source_target_pairs={{0,4},{1,5},{2,6},{3,7},{4,0},{5,1},{6,2},{7,3},{8,12},{9,13},{10,... | collective-permute-start | bytes 368648 | tf_op jit(solution)/shard_map/ppermute | solution.py:597
  7.0 5.5 %collective-permute-start.3 = (bf16[48,1152]{1,0:T(8,128)(2,1)}, bf16[48,1152]{1,0:T(8,128)(2,1)S(1)}, u32[]{:S(2)}, u32[]{:S(2)}) collective-permute-start(bf16[48,1152]{1,0:T(8,128)(2,1)} %refs_8_.2), channel_id=1, source_target_pairs={{0,1},{1,0},{2,3},{3,2},{4,5},{5,4},{6,7},{7,6},{8,9},{9,8},{10,11... | collective-permute-start | bytes 331784 | tf_op jit(solution)/shard_map/ppermute | solution.py:597
  7.1 5.1 %collective-permute-start.4 = (bf16[48,384]{1,0:T(8,128)(2,1)}, bf16[48,384]{1,0:T(8,128)(2,1)S(1)}, u32[]{:S(2)}, u32[]{:S(2)}) collective-permute-start(bf16[48,384]{1,0:T(8,128)(2,1)} %refs_9_.2), channel_id=1, source_target_pairs={{0,1},{1,0},{2,3},{3,2},{4,5},{5,4},{6,7},{7,6},{8,9},{9,8},{10,11... | collective-permute-start | bytes 110600 | tf_op jit(solution)/shard_map/ppermute | solution.py:597
  11.7 11.5 %copy-start.8 = (bf16[160,384]{1,0:T(8,128)(2,1)S(1)}, bf16[160,384]{1,0:T(8,128)(2,1)}, u32[]{:S(2)}) copy-start(bf16[160,384]{1,0:T(8,128)(2,1)} %pick.1.q0) | copy-start | bytes 368644
  12.2 1.8 %collective-permute-start.2 = (f32[3,2304]{1,0:T(4,128)S(1)}, f32[3,2304]{1,0:T(4,128)S(1)}, u32[]{:S(2)}, u32[]{:S(2)}) collective-permute-start(f32[3,2304]{1,0:T(4,128)S(1)} %get-tuple-element.76.placed), channel_id=1, source_target_pairs={{0,1},{1,0},{2,3},{3,2},{4,5},{5,4},{6,7},{7,6},{8,9},{9,8},{10,11... | collective-permute-start | bytes 82952 | tf_op jit(solution)/shard_map/ppermute | solution.py:597
  12.5 6.3 %collective-permute-start.7 = (bf16[160,384]{1,0:T(8,128)(2,1)}, bf16[160,384]{1,0:T(8,128)(2,1)S(1)}, u32[]{:S(2)}, u32[]{:S(2)}) collective-permute-start(bf16[160,384]{1,0:T(8,128)(2,1)} %pick.1.q0), channel_id=1, source_target_pairs={{0,2},{1,3},{2,0},{3,1},{4,6},{5,7},{6,4},{7,5},{8,10},{9,11},{10,... | collective-permute-start | bytes 368648 | tf_op jit(solution)/shard_map/ppermute | solution.py:597
  14.1 6.8 %collective-permute-start.8 = (bf16[160,384]{1,0:T(8,128)(2,1)S(1)}, bf16[160,384]{1,0:T(8,128)(2,1)S(1)}, u32[]{:S(2)}, u32[]{:S(2)}) collective-permute-start(bf16[160,384]{1,0:T(8,128)(2,1)S(1)} %collective-permute-done.q2), channel_id=1, source_target_pairs={{0,2},{1,3},{2,0},{3,1},{4,6},{5,7},{6,4},{7,5},{8,10},{9,11},{10,... | collective-permute-start | bytes 368648 | tf_op jit(solution)/shard_map/ppermute | solution.py:597
  20.9 7.9 %collective-permute-start.9 = (bf16[3,144,384]{2,1,0:T(8,128)(2,1)S(1)}, bf16[3,144,384]{2,1,0:T(8,128)(2,1)S(1)}, u32[]{:S(2)}, u32[]{:S(2)}) collective-permute-start(bf16[3,144,384]{2,1,0:T(8,128)(2,1)S(1)} %stack.13.refs_0_), channel_id=1, source_target_pairs={{0,8},{1,17},{2,10},{3,19},{4,12},{5,21},{6,14},{7,23},{8,0},{9,25... | collective-permute-start | bytes 995336 | tf_op jit(solution)/shard_map/ppermute | solution.py:597
  24.0 4.4 %collective-permute-start.10 = (f32[2,4,2304]{2,1,0:T(4,128)S(1)}, f32[2,4,2304]{2,1,0:T(4,128)S(1)}, u32[]{:S(2)}, u32[]{:S(2)}) collective-permute-start(f32[2,4,2304]{2,1,0:T(4,128)S(1)} %get-tuple-element.85), channel_id=1, source_target_pairs={{0,2},{1,3},{2,0},{3,1},{4,6},{5,7},{6,4},{7,5},{8,10},{9,11},{10,... | collective-permute-start | bytes 221192 | tf_op jit(solution)/shard_map/ppermute | solution.py:597
  25.7 7.3 %collective-permute-start.11 = (bf16[3,144,384]{2,1,0:T(8,128)(2,1)S(1)}, bf16[3,144,384]{2,1,0:T(8,128)(2,1)S(1)}, u32[]{:S(2)}, u32[]{:S(2)}) collective-permute-start(bf16[3,144,384]{2,1,0:T(8,128)(2,1)S(1)} %stack.13.refs_0_), channel_id=1, source_target_pairs={{0,16},{1,9},{2,18},{3,11},{4,20},{5,13},{6,22},{7,15},{8,24},{9,1... | collective-permute-start | bytes 995336 | tf_op jit(solution)/shard_map/ppermute | solution.py:597
  28.8 7.6 %collective-permute-start.12 = (bf16[3,144,384]{2,1,0:T(8,128)(2,1)S(1)}, bf16[3,144,384]{2,1,0:T(8,128)(2,1)S(1)}, u32[]{:S(2)}, u32[]{:S(2)}) collective-permute-start(bf16[3,144,384]{2,1,0:T(8,128)(2,1)S(1)} %collective-permute-done.9.refs_1_), channel_id=1, source_target_pairs={{0,16},{1,9},{2,18},{3,11},{4,20},{5,13},{6,22},{7,15},{8,24},{9,1... | collective-permute-start | bytes 995336 | tf_op jit(solution)/shard_map/ppermute | solution.py:597
  31.4 10.3 %copy-start.6 = (bf16[48,1536]{1,0:T(8,128)(2,1)S(1)}, bf16[48,1536]{1,0:T(8,128)(2,1)}, u32[]{:S(2)}) copy-start(bf16[48,1536]{1,0:T(8,128)(2,1)} %refs_8_.3) | copy-start | bytes 442372
  31.4 10.3 %copy-start.7 = (bf16[192,384]{1,0:T(8,128)(2,1)S(1)}, bf16[192,384]{1,0:T(8,128)(2,1)}, u32[]{:S(2)}) copy-start(bf16[192,384]{1,0:T(8,128)(2,1)} %refs_9_.3) | copy-start | bytes 442372
  31.4 10.4 %copy-start.10 = (bf16[2,256,384]{2,1,0:T(8,128)(2,1)S(1)}, bf16[2,256,384]{2,1,0:T(8,128)(2,1)}, u32[]{:S(2)}) copy-start(bf16[2,256,384]{2,1,0:T(8,128)(2,1)} %refs_15_.1) | copy-start | bytes 1179652
  31.4 4.9 %collective-permute-start.16 = (f32[4,2304]{1,0:T(4,128)S(1)}, f32[4,2304]{1,0:T(4,128)S(1)}, u32[]{:S(2)}, u32[]{:S(2)}) collective-permute-start(f32[4,2304]{1,0:T(4,128)S(1)} %slice_bitcast_fusion), channel_id=1, source_target_pairs={{0,4},{1,5},{2,6},{3,7},{4,0},{5,1},{6,2},{7,3},{8,12},{9,13},{10,... | collective-permute-start | bytes 110600 | tf_op jit(solution)/shard_map/ppermute | solution.py:597
  32.5 4.0 %collective-permute-start.13 = (bf16[3,144,384]{2,1,0:T(8,128)(2,1)S(1)}, bf16[3,144,384]{2,1,0:T(8,128)(2,1)S(1)}, u32[]{:S(2)}, u32[]{:S(2)}) collective-permute-start(bf16[3,144,384]{2,1,0:T(8,128)(2,1)S(1)} %stack.13.refs_0_), channel_id=1, source_target_pairs={{0,1},{1,0},{2,3},{3,2},{4,5},{5,4},{6,7},{7,6},{8,9},{9,8},{10,11... | collective-permute-start | bytes 995336 | tf_op jit(solution)/shard_map/ppermute | solution.py:597
  32.5 4.0 %collective-permute-start.14 = (bf16[3,144,384]{2,1,0:T(8,128)(2,1)S(1)}, bf16[3,144,384]{2,1,0:T(8,128)(2,1)S(1)}, u32[]{:S(2)}, u32[]{:S(2)}) collective-permute-start(bf16[3,144,384]{2,1,0:T(8,128)(2,1)S(1)} %collective-permute-done.9.refs_1_), channel_id=1, source_target_pairs={{0,1},{1,0},{2,3},{3,2},{4,5},{5,4},{6,7},{7,6},{8,9},{9,8},{10,11... | collective-permute-start | bytes 995336 | tf_op jit(solution)/shard_map/ppermute | solution.py:597
  33.0 3.5 %collective-permute-start.15 = (bf16[3,144,384]{2,1,0:T(8,128)(2,1)S(1)}, bf16[3,144,384]{2,1,0:T(8,128)(2,1)S(1)}, u32[]{:S(2)}, u32[]{:S(2)}) collective-permute-start(bf16[3,144,384]{2,1,0:T(8,128)(2,1)S(1)} %collective-permute-done.11.refs_2_), channel_id=1, source_target_pairs={{0,1},{1,0},{2,3},{3,2},{4,5},{5,4},{6,7},{7,6},{8,9},{9,8},{10,11... | collective-permute-start | bytes 995336 | tf_op jit(solution)/shard_map/ppermute | solution.py:597
  36.5 1.6 %collective-permute-start.17 = (bf16[3,144,384]{2,1,0:T(8,128)(2,1)S(1)}, bf16[3,144,384]{2,1,0:T(8,128)(2,1)S(1)}, u32[]{:S(2)}, u32[]{:S(2)}) collective-permute-start(bf16[3,144,384]{2,1,0:T(8,128)(2,1)S(1)} %collective-permute-done.12.refs_3_), channel_id=1, source_target_pairs={{0,1},{1,0},{2,3},{3,2},{4,5},{5,4},{6,7},{7,6},{8,9},{9,8},{10,11... | collective-permute-start | bytes 995336 | tf_op jit(solution)/shard_map/ppermute | solution.py:597
  41.7 9.3 %copy-start = (bf16[512,1152]{1,0:T(8,128)(2,1)S(1)}, bf16[512,1152]{1,0:T(8,128)(2,1)}, u32[]{:S(2)}) copy-start(bf16[512,1152]{1,0:T(8,128)(2,1)} %get-tuple-element.93.proj) | copy-start | bytes 3538948
  50.9 2.9 %collective-permute-start.18 = (bf16[2,4,2,48,384]{4,3,2,1,0:T(8,128)(2,1)}, bf16[2,4,2,48,384]{4,3,2,1,0:T(8,128)(2,1)S(1)}, u32[]{:S(2)}, u32[]{:S(2)}) collective-permute-start(bf16[2,4,2,48,384]{4,3,2,1,0:T(8,128)(2,1)} %get-tuple-element.99), channel_id=1, source_target_pairs={{0,1},{1,0},{2,3},{3,2},{4,5},{5,4},{6,7},{7,6},{8,9},{9,8},{10,11... | collective-permute-start | bytes 1769480 | tf_op jit(solution)/shard_map/ppermute | solution.py:597
  54.0 9.9 %collective-permute-start.21 = (bf16[2,4,2,48,384]{4,3,2,1,0:T(8,128)(2,1)S(1)}, bf16[2,4,2,48,384]{4,3,2,1,0:T(8,128)(2,1)S(1)}, u32[]{:S(2)}, u32[]{:S(2)}) collective-permute-start(bf16[2,4,2,48,384]{4,3,2,1,0:T(8,128)(2,1)S(1)} %sum_ud.1), channel_id=1, source_target_pairs={{0,8},{1,17},{2,10},{3,19},{4,12},{5,21},{6,14},{7,23},{8,0},{9,25... | collective-permute-start | bytes 1769480 | tf_op jit(solution)/shard_map/ppermute | solution.py:597
  60.0 3.3 %collective-permute-start.22 = (bf16[2,4,48,384]{3,2,1,0:T(8,128)(2,1)S(1)}, bf16[2,4,48,384]{3,2,1,0:T(8,128)(2,1)S(1)}, u32[]{:S(2)}, u32[]{:S(2)}) collective-permute-start(bf16[2,4,48,384]{3,2,1,0:T(8,128)(2,1)S(1)} %get-tuple-element.112), channel_id=1, source_target_pairs={{0,1},{1,0},{2,3},{3,2},{4,5},{5,4},{6,7},{7,6},{8,9},{9,8},{10,11... | collective-permute-start | bytes 884744 | tf_op jit(solution)/shard_map/ppermute | solution.py:597
  60.7 11.5 %collective-permute-start.19 = (bf16[2,4,2,48,384]{4,3,2,1,0:T(8,128)(2,1)S(1)}, bf16[2,4,2,48,384]{4,3,2,1,0:T(8,128)(2,1)S(1)}, u32[]{:S(2)}, u32[]{:S(2)}) collective-permute-start(bf16[2,4,2,48,384]{4,3,2,1,0:T(8,128)(2,1)S(1)} %copy-done.18), channel_id=1, source_target_pairs={{0,1},{1,0},{2,3},{3,2},{4,5},{5,4},{6,7},{7,6},{8,9},{9,8},{10,11... | collective-permute-start | bytes 1769480 | tf_op jit(solution)/shard_map/ppermute | solution.py:597
  64.0 8.1 %collective-permute-start.23 = (bf16[2,4,48,384]{3,2,1,0:T(8,128)(2,1)S(1)}, bf16[2,4,48,384]{3,2,1,0:T(8,128)(2,1)S(1)}, u32[]{:S(2)}, u32[]{:S(2)}) collective-permute-start(bf16[2,4,48,384]{3,2,1,0:T(8,128)(2,1)S(1)} %sum_po.1), channel_id=1, source_target_pairs={{0,8},{1,17},{2,10},{3,19},{4,12},{5,21},{6,14},{7,23},{8,0},{9,25... | collective-permute-start | bytes 884744 | tf_op jit(solution)/shard_map/ppermute | solution.py:597
  65.6 6.6 %collective-permute-start.20 = (bf16[2,4,48,384]{3,2,1,0:T(8,128)(2,1)S(1)}, bf16[2,4,48,384]{3,2,1,0:T(8,128)(2,1)S(1)}, u32[]{:S(2)}, u32[]{:S(2)}) collective-permute-start(bf16[2,4,48,384]{3,2,1,0:T(8,128)(2,1)S(1)} %get-tuple-element.110), channel_id=1, source_target_pairs={{0,1},{1,0},{2,3},{3,2},{4,5},{5,4},{6,7},{7,6},{8,9},{9,8},{10,11... | collective-permute-start | bytes 884744 | tf_op jit(solution)/shard_map/ppermute | solution.py:597
  65.6 1.7 %collective-permute-start.25 = (bf16[2,3840]{1,0:T(2,128)(2,1)S(1)}, bf16[2,3840]{1,0:T(2,128)(2,1)S(1)}, u32[]{:S(2)}, u32[]{:S(2)}) collective-permute-start(bf16[2,3840]{1,0:T(2,128)(2,1)S(1)} %get-tuple-element.116.own), channel_id=1, source_target_pairs={{0,1},{1,0},{2,3},{3,2},{4,5},{5,4},{6,7},{7,6},{8,9},{9,8},{10,11... | collective-permute-start | bytes 46088 | tf_op jit(solution)/shard_map/ppermute | solution.py:597
  66.1 1.2 %collective-permute-start.24 = (bf16[8,384]{1,0:T(8,128)(2,1)S(1)}, bf16[8,384]{1,0:T(8,128)(2,1)S(1)}, u32[]{:S(2)}, u32[]{:S(2)}) collective-permute-start(bf16[8,384]{1,0:T(8,128)(2,1)S(1)} %get-tuple-element.115.c_own), channel_id=1, source_target_pairs={{0,1},{1,0},{2,3},{3,2},{4,5},{5,4},{6,7},{7,6},{8,9},{9,8},{10,11... | collective-permute-start | bytes 18440 | tf_op jit(solution)/shard_map/ppermute | solution.py:597
  67.3 4.9 %collective-permute-start.26 = (bf16[4,3840]{1,0:T(4,128)(2,1)S(1)}, bf16[4,3840]{1,0:T(4,128)(2,1)S(1)}, u32[]{:S(2)}, u32[]{:S(2)}) collective-permute-start(bf16[4,3840]{1,0:T(4,128)(2,1)S(1)} %pair.1.g0), channel_id=1, source_target_pairs={{0,4},{1,5},{2,6},{3,7},{4,0},{5,1},{6,2},{7,3},{8,12},{9,13},{10,... | collective-permute-start | bytes 92168 | tf_op jit(solution)/shard_map/ppermute | solution.py:597
  72.4 9.8 %collective-permute-start.27 = (bf16[4,144,384]{2,1,0:T(8,128)(2,1)S(1)}, bf16[4,144,384]{2,1,0:T(8,128)(2,1)S(1)}, u32[]{:S(2)}, u32[]{:S(2)}) collective-permute-start(bf16[4,144,384]{2,1,0:T(8,128)(2,1)S(1)} %turn.1), channel_id=1, source_target_pairs={{0,16},{1,9},{2,18},{3,11},{4,20},{5,13},{6,22},{7,15},{8,24},{9,1... | collective-permute-start | bytes 1327112 | tf_op jit(solution)/shard_map/ppermute | solution.py:597
  74.4 4.7 %collective-permute-start.28 = (bf16[4,3840]{1,0:T(4,128)(2,1)S(1)}, bf16[4,3840]{1,0:T(4,128)(2,1)S(1)}, u32[]{:S(2)}, u32[]{:S(2)}) collective-permute-start(bf16[4,3840]{1,0:T(4,128)(2,1)S(1)} %pair.1.g0), channel_id=1, source_target_pairs={{0,2},{1,3},{2,0},{3,1},{4,6},{5,7},{6,4},{7,5},{8,10},{9,11},{10,... | collective-permute-start | bytes 92168 | tf_op jit(solution)/shard_map/ppermute | solution.py:597
  77.3 3.9 %collective-permute-start.29 = (bf16[4,3840]{1,0:T(4,128)(2,1)S(1)}, bf16[4,3840]{1,0:T(4,128)(2,1)S(1)}, u32[]{:S(2)}, u32[]{:S(2)}) collective-permute-start(bf16[4,3840]{1,0:T(4,128)(2,1)S(1)} %collective-permute-done.26.g2), channel_id=1, source_target_pairs={{0,2},{1,3},{2,0},{3,1},{4,6},{5,7},{6,4},{7,5},{8,10},{9,11},{10,... | collective-permute-start | bytes 92168 | tf_op jit(solution)/shard_map/ppermute | solution.py:597
  82.3 15.9 %copy-start.17 = (bf16[2,384]{1,0:T(2,128)(2,1)S(1)}, bf16[2,384]{1,0:T(2,128)(2,1)}, u32[]{:S(2)}) copy-start(bf16[2,384]{1,0:T(2,128)(2,1)} %cond.1) | copy-start | bytes 4612
  82.3 6.3 %collective-permute-start.30 = (bf16[2,160,384]{2,1,0:T(8,128)(2,1)S(1)}, bf16[2,160,384]{2,1,0:T(8,128)(2,1)S(1)}, u32[]{:S(2)}, u32[]{:S(2)}) collective-permute-start(bf16[2,160,384]{2,1,0:T(8,128)(2,1)S(1)} %join_far.1), channel_id=1, source_target_pairs={{0,2},{1,3},{2,0},{3,1},{4,6},{5,7},{6,4},{7,5},{8,10},{9,11},{10,... | collective-permute-start | bytes 737288 | tf_op jit(solution)/shard_map/ppermute | solution.py:597
  83.7 6.6 %collective-permute-start.32 = (bf16[16,4224]{1,0:T(8,128)(2,1)S(1)}, bf16[16,4224]{1,0:T(8,128)(2,1)S(1)}, u32[]{:S(2)}, u32[]{:S(2)}) collective-permute-start(bf16[16,4224]{1,0:T(8,128)(2,1)S(1)} %pack.1.e0), channel_id=1, source_target_pairs={{0,8},{1,17},{2,10},{3,19},{4,12},{5,21},{6,14},{7,23},{8,0},{9,25... | collective-permute-start | bytes 405512 | tf_op jit(solution)/shard_map/ppermute | solution.py:597
  84.7 6.6 %collective-permute-start.33 = (bf16[16,4224]{1,0:T(8,128)(2,1)S(1)}, bf16[16,4224]{1,0:T(8,128)(2,1)S(1)}, u32[]{:S(2)}, u32[]{:S(2)}) collective-permute-start(bf16[16,4224]{1,0:T(8,128)(2,1)S(1)} %pack.1.e0), channel_id=1, source_target_pairs={{0,16},{1,9},{2,18},{3,11},{4,20},{5,13},{6,22},{7,15},{8,24},{9,1... | collective-permute-start | bytes 405512 | tf_op jit(solution)/shard_map/ppermute | solution.py:597
  86.3 5.9 %collective-permute-start.34 = (bf16[16,4224]{1,0:T(8,128)(2,1)S(1)}, bf16[16,4224]{1,0:T(8,128)(2,1)S(1)}, u32[]{:S(2)}, u32[]{:S(2)}) collective-permute-start(bf16[16,4224]{1,0:T(8,128)(2,1)S(1)} %pack.1.e0), channel_id=1, source_target_pairs={{0,24},{1,25},{2,26},{3,27},{4,28},{5,29},{6,30},{7,31},{8,16},{9,... | collective-permute-start | bytes 405512 | tf_op jit(solution)/shard_map/ppermute | solution.py:597
  88.7 5.8 %collective-permute-start.31 = (bf16[160,384]{1,0:T(8,128)(2,1)S(1)}, bf16[160,384]{1,0:T(8,128)(2,1)S(1)}, u32[]{:S(2)}, u32[]{:S(2)}) collective-permute-start(bf16[160,384]{1,0:T(8,128)(2,1)S(1)} %get-tuple-element.122), channel_id=1, source_target_pairs={{0,4},{1,5},{2,6},{3,7},{4,0},{5,1},{6,2},{7,3},{8,12},{9,13},{10,... | collective-permute-start | bytes 368648 | tf_op jit(solution)/shard_map/ppermute | solution.py:597
  94.6 3.6 %collective-permute-start.35 = (f32[2,384]{1,0:T(2,128)S(1)}, f32[2,384]{1,0:T(2,128)S(1)}, u32[]{:S(2)}, u32[]{:S(2)}) collective-permute-start(f32[2,384]{1,0:T(2,128)S(1)} %slice.15), channel_id=1, source_target_pairs={{0,1},{1,0},{2,3},{3,2},{4,5},{5,4},{6,7},{7,6},{8,9},{9,8},{10,11... | collective-permute-start | bytes 9224 | tf_op jit(solution)/shard_map/ppermute | solution.py:597
  94.6 5.3 %collective-permute-start.36 = (bf16[144,384]{1,0:T(8,128)(2,1)S(1)}, bf16[144,384]{1,0:T(8,128)(2,1)S(1)}, u32[]{:S(2)}, u32[]{:S(2)}) collective-permute-start(bf16[144,384]{1,0:T(8,128)(2,1)S(1)} %get-tuple-element.128.g0), channel_id=1, source_target_pairs={{0,8},{1,17},{2,10},{3,19},{4,12},{5,21},{6,14},{7,23},{8,0},{9,25... | collective-permute-start | bytes 331784 | tf_op jit(solution)/shard_map/ppermute | solution.py:597
  96.1 4.7 %collective-permute-start.37 = (bf16[144,384]{1,0:T(8,128)(2,1)S(1)}, bf16[144,384]{1,0:T(8,128)(2,1)S(1)}, u32[]{:S(2)}, u32[]{:S(2)}) collective-permute-start(bf16[144,384]{1,0:T(8,128)(2,1)S(1)} %get-tuple-element.128.g0), channel_id=1, source_target_pairs={{0,16},{1,9},{2,18},{3,11},{4,20},{5,13},{6,22},{7,15},{8,24},{9,1... | collective-permute-start | bytes 331784 | tf_op jit(solution)/shard_map/ppermute | solution.py:597
  96.9 6.8 %collective-permute-start.38 = (bf16[144,384]{1,0:T(8,128)(2,1)S(1)}, bf16[144,384]{1,0:T(8,128)(2,1)S(1)}, u32[]{:S(2)}, u32[]{:S(2)}) collective-permute-start(bf16[144,384]{1,0:T(8,128)(2,1)S(1)} %get-tuple-element.128.g0), channel_id=1, source_target_pairs={{0,24},{1,25},{2,26},{3,27},{4,28},{5,29},{6,30},{7,31},{8,16},{9,... | collective-permute-start | bytes 331784 | tf_op jit(solution)/shard_map/ppermute | solution.py:597
  (10 other events, 32.5 us)

commit v6 on v5

--- a/solution.py
+++ b/solution.py
@@ -192,14 +192,14 @@
         for pair in range(HEADS // 2):
             lo = pair * 2 * HEAD_DIM
             hi = lo + 2 * HEAD_DIM
-            q = proj[pl.ds(at, length), lo:hi]
+            q = proj[pl.ds(at, length), lo:hi] * jnp.asarray(HEAD_DIM ** (-0.5), BF16)
             k = proj[pl.ds(at, length), feat + lo : feat + hi]
             v = proj[pl.ds(at, length), 2 * feat + lo : 2 * feat + hi]
             zero = jnp.zeros_like(q)
             outs = []
             for side in range(2):
                 q_one = jnp.where(low_half, q, zero) if side == 0 else jnp.where(low_half, zero, q)
-                s = dot(q_one, k, NT) * HEAD_DIM ** (-0.5)
+                s = dot(q_one, k, NT)
                 e = jnp.exp(s - jnp.max(s, axis=-1, keepdims=True))
                 inv = 1.0 / jnp.sum(e, axis=-1, keepdims=True)
                 outs.append(dot((e * inv).astype(BF16), v))
@@ -355,7 +355,7 @@
         for pair in range(HEADS // 2):
             lo = pair * 2 * HEAD_DIM
             hi = lo + 2 * HEAD_DIM
-            q = proj[part, lo:hi]
+            q = proj[part, lo:hi] * jnp.asarray(HEAD_DIM ** (-0.5), BF16)
             k = proj[part, feat + lo : feat + hi]
             v = proj[part, 2 * feat + lo : 2 * feat + hi]
             ga = gatt[part, lo:hi]
@@ -368,7 +368,7 @@
                     jnp.where(low_half, a, zero) if side == 0 else jnp.where(low_half, zero, a)
                 )
                 q_one, ga_one = own(q), own(ga)
-                s = dot(k, q_one, NT) * HEAD_DIM ** (-0.5)
+                s = dot(k, q_one, NT)
                 e = jnp.exp(s - jnp.max(s, axis=0, keepdims=True))
                 prob = e * (1.0 / jnp.sum(e, axis=0, keepdims=True))
                 gv = gv + dot(prob.astype(BF16), ga_one)
@@ -378,7 +378,7 @@
                 gk = gk + dot(gs, q_one)
                 gq = gq + dot(gs, own(k), TN)
             gall[part, lo:hi] = (gq * HEAD_DIM ** (-0.5)).astype(BF16)
-            gall[part, feat + lo : feat + hi] = (gk * HEAD_DIM ** (-0.5)).astype(BF16)
+            gall[part, feat + lo : feat + hi] = gk.astype(BF16)
             gall[part, 2 * feat + lo : 2 * feat + hi] = gv.astype(BF16)
         return carry
 

time: 105 us -> 105 us (level)
  no operation moved by 1% of the time
where the time goes in v6:
time: 105 us
  starting transfers between devices  36.7 us (35%)
  waiting for transfers between devices  31.2 us (30%)
  Pallas kernels  30.5 us (29%)
  local copies, waits for them, and re-layouts  4.34 us (4%)
  between operations  1.6 us (2%)
    ppermute x39, starting transfers between devices, move(): return lax.ppermute(x, BOTH, route)  36.7 us
    ppermute x39, waiting for transfers between devices, move(): return lax.ppermute(x, BOTH, route)  31.2 us
    pallas_call x21, Pallas kernels, call(): pl.pallas_call(body, out_shape=[jax.ShapeDtypeStruct(s, t) for s, t in ou...  30.5 us
    unnamed x38, local copies, waits for them, and re-layouts  4.3 us
  transfers between devices with their start and end apart: 39, of which 20 were waited for; matrix products, arithmetic and copies ran while one was open for 1% of the time, Pallas kernels for 14%

profile of v6, /device:TPU:0, one launch (start us, length us, event | category | flops | bytes accessed | tf_op | source)
XLA Modules:
  0.0 105.1 jit_solution(593481588029282039)
XLA Ops:
  0.7 1.6 %pick.1.q0 = bf16[160,384]{1,0:T(8,128)(2,1)} custom-call(bf16[48,1152]{1,0:T(8,128)(2,1)} %refs_8_.2, bf16[48,384]{1,0:T(8,128)(2,1)} %refs_9_.2, bf16[48,1536]{1,0:T(8,128)(2,1)} %refs_8_.3, bf16[192,384]{1,0:T(8,128)(2,1)} %refs_9_.3, bf16[2,384]{1,0:T(2,128)(2,1)} %cond.1), custom_call_target="tpu_custom_call" | custom-call | flops 1 | bytes 1 | tf_op jit(solution)/shard_map/pick/pallas_call | solution.py:40
  3.3 3.7 %collective-permute-start = (bf16[160,384]{1,0:T(8,128)(2,1)}, bf16[160,384]{1,0:T(8,128)(2,1)S(1)}, u32[]{:S(2)}, u32[]{:S(2)}) collective-permute-start(bf16[160,384]{1,0:T(8,128)(2,1)} %pick.1.q0), channel_id=1, source_target_pairs={{0,4},{1,5},{2,6},{3,7},{4,0},{5,1},{6,2},{7,3},{8,12},{9,13},{10,... | collective-permute-start | bytes 368648 | tf_op jit(solution)/shard_map/ppermute | solution.py:597
  7.5 0.9 copy-done.3
  12.5 1.6 %collective-permute-start.7 = (bf16[160,384]{1,0:T(8,128)(2,1)}, bf16[160,384]{1,0:T(8,128)(2,1)S(1)}, u32[]{:S(2)}, u32[]{:S(2)}) collective-permute-start(bf16[160,384]{1,0:T(8,128)(2,1)} %pick.1.q0), channel_id=1, source_target_pairs={{0,2},{1,3},{2,0},{3,1},{4,6},{5,7},{6,4},{7,5},{8,10},{9,11},{10,... | collective-permute-start | bytes 368648 | tf_op jit(solution)/shard_map/ppermute | solution.py:597
  14.1 1.0 collective-permute-start.8
  15.1 3.7 %collective-permute-done.7.q1 = bf16[160,384]{1,0:T(8,128)(2,1)S(1)} collective-permute-done((bf16[160,384]{1,0:T(8,128)(2,1)}, bf16[160,384]{1,0:T(8,128)(2,1)S(1)}, u32[]{:S(2)}, u32[]{:S(2)}) %collective-permute-start.7) | collective-permute-done | bytes 122912 | tf_op jit(solution)/shard_map/ppermute | solution.py:597
  18.8 2.1 %collective-permute-done.8.q3 = bf16[160,384]{1,0:T(8,128)(2,1)S(1)} collective-permute-done((bf16[160,384]{1,0:T(8,128)(2,1)S(1)}, bf16[160,384]{1,0:T(8,128)(2,1)S(1)}, u32[]{:S(2)}, u32[]{:S(2)}) %collective-permute-start.8) | collective-permute-done | bytes 122912 | tf_op jit(solution)/shard_map/ppermute | solution.py:597
  20.9 1.6 %collective-permute-start.9 = (bf16[3,144,384]{2,1,0:T(8,128)(2,1)S(1)}, bf16[3,144,384]{2,1,0:T(8,128)(2,1)S(1)}, u32[]{:S(2)}, u32[]{:S(2)}) collective-permute-start(bf16[3,144,384]{2,1,0:T(8,128)(2,1)S(1)} %stack.13.refs_0_), channel_id=1, source_target_pairs={{0,8},{1,17},{2,10},{3,19},{4,12},{5,21},{6,14},{7,23},{8,0},{9,25... | collective-permute-start | bytes 995336 | tf_op jit(solution)/shard_map/ppermute | solution.py:597
  23.2 0.9 modulation.1
  24.0 1.6 %collective-permute-start.10 = (f32[2,4,2304]{2,1,0:T(4,128)S(1)}, f32[2,4,2304]{2,1,0:T(4,128)S(1)}, u32[]{:S(2)}, u32[]{:S(2)}) collective-permute-start(f32[2,4,2304]{2,1,0:T(4,128)S(1)} %get-tuple-element.85), channel_id=1, source_target_pairs={{0,2},{1,3},{2,0},{3,1},{4,6},{5,7},{6,4},{7,5},{8,10},{9,11},{10,... | collective-permute-start | bytes 221192 | tf_op jit(solution)/shard_map/ppermute | solution.py:597
  25.7 1.5 %collective-permute-start.11 = (bf16[3,144,384]{2,1,0:T(8,128)(2,1)S(1)}, bf16[3,144,384]{2,1,0:T(8,128)(2,1)S(1)}, u32[]{:S(2)}, u32[]{:S(2)}) collective-permute-start(bf16[3,144,384]{2,1,0:T(8,128)(2,1)S(1)} %stack.13.refs_0_), channel_id=1, source_target_pairs={{0,16},{1,9},{2,18},{3,11},{4,20},{5,13},{6,22},{7,15},{8,24},{9,1... | collective-permute-start | bytes 995336 | tf_op jit(solution)/shard_map/ppermute | solution.py:597
  27.2 1.3 %collective-permute-done.10 = f32[2,4,2304]{2,1,0:T(4,128)S(1)} collective-permute-done((f32[2,4,2304]{2,1,0:T(4,128)S(1)}, f32[2,4,2304]{2,1,0:T(4,128)S(1)}, u32[]{:S(2)}, u32[]{:S(2)}) %collective-permute-start.10) | collective-permute-done | bytes 73760 | tf_op jit(solution)/shard_map/ppermute | solution.py:597
  28.8 2.5 %collective-permute-start.12 = (bf16[3,144,384]{2,1,0:T(8,128)(2,1)S(1)}, bf16[3,144,384]{2,1,0:T(8,128)(2,1)S(1)}, u32[]{:S(2)}, u32[]{:S(2)}) collective-permute-start(bf16[3,144,384]{2,1,0:T(8,128)(2,1)S(1)} %collective-permute-done.9.refs_1_), channel_id=1, source_target_pairs={{0,16},{1,9},{2,18},{3,11},{4,20},{5,13},{6,22},{7,15},{8,24},{9,1... | collective-permute-start | bytes 995336 | tf_op jit(solution)/shard_map/ppermute | solution.py:597
  31.4 1.1 %collective-permute-start.16 = (f32[4,2304]{1,0:T(4,128)S(1)}, f32[4,2304]{1,0:T(4,128)S(1)}, u32[]{:S(2)}, u32[]{:S(2)}) collective-permute-start(f32[4,2304]{1,0:T(4,128)S(1)} %slice_bitcast_fusion), channel_id=1, source_target_pairs={{0,4},{1,5},{2,6},{3,7},{4,0},{5,1},{6,2},{7,3},{8,12},{9,13},{10,... | collective-permute-start | bytes 110600 | tf_op jit(solution)/shard_map/ppermute | solution.py:597
  33.0 3.3 %collective-permute-done.16.refs_13_ = f32[4,2304]{1,0:T(4,128)S(1)} collective-permute-done((f32[4,2304]{1,0:T(4,128)S(1)}, f32[4,2304]{1,0:T(4,128)S(1)}, u32[]{:S(2)}, u32[]{:S(2)}) %collective-permute-start.16) | collective-permute-done | bytes 36896 | tf_op jit(solution)/shard_map/ppermute | solution.py:597
  36.5 1.6 %collective-permute-done.17.refs_7_ = bf16[3,144,384]{2,1,0:T(8,128)(2,1)S(1)} collective-permute-done((bf16[3,144,384]{2,1,0:T(8,128)(2,1)S(1)}, bf16[3,144,384]{2,1,0:T(8,128)(2,1)S(1)}, u32[]{:S(2)}, u32[]{:S(2)}) %collective-permute-start.17) | collective-permute-done | bytes 331808 | tf_op jit(solution)/shard_map/ppermute | solution.py:597
  38.1 3.5 %attention.1 = (bf16[4,384,384]{2,1,0:T(8,128)(2,1)S(1)}, f32[4,2304]{1,0:T(4,128)S(1)}, bf16[512,384]{1,0:T(8,128)(2,1)S(1)}, bf16[512,1152]{1,0:T(8,128)(2,1)}, bf16[512,384]{1,0:T(8,128)(2,1)S(1)}) custom-call(s32[3]{0:T(128)S(1)} %pad_add_fusion.ids, bf16[3,144,384]{2,1,0:T(8,128)(2,1)S(1)} %stack.13.refs_0_, ...), custom_call_target="tpu_custom_call" | custom-call | flops 1 | bytes 1 | tf_op jit(solution)/shard_map/attention/pallas_call | solution.py:40
  41.7 9.2 %mlp.1 = (bf16[2,256,384]{2,1,0:T(8,128)(2,1)}, f32[2,256,384]{2,1,0:T(8,128)}, bf16[512,384]{1,0:T(8,128)(2,1)S(1)}, bf16[512,384]{1,0:T(8,128)(2,1)S(1)}, f32[...) custom-call(s32[3]{0:T(128)S(1)} %pad_add_fusion.ids, ...), custom_call_target="tpu_custom_call" | custom-call | flops 1 | bytes 1 | tf_op jit(solution)/shard_map/mlp/pallas_call | solution.py:40
  51.0 2.7 %attention_back_first.1.g_first = bf16[256,1152]{1,0:T(8,128)(2,1)S(1)} custom-call(bf16[512,1152]{1,0:T(8,128)(2,1)S(1)} %copy-done, bf16[512,384]{1,0:T(8,128)(2,1)S(1)} %get-tuple-element.94.gatt), custom_call_target="tpu_custom_call" | custom-call | flops 1 | bytes 1 | tf_op jit(solution)/shard_map/attention_back_first/pallas_call | solution.py:40
  54.0 1.6 %collective-permute-start.21 = (bf16[2,4,2,48,384]{4,3,2,1,0:T(8,128)(2,1)S(1)}, bf16[2,4,2,48,384]{4,3,2,1,0:T(8,128)(2,1)S(1)}, u32[]{:S(2)}, u32[]{:S(2)}) collective-permute-start(bf16[2,4,2,48,384]{4,3,2,1,0:T(8,128)(2,1)S(1)} %sum_ud.1), channel_id=1, source_target_pairs={{0,8},{1,17},{2,10},{3,19},{4,12},{5,21},{6,14},{7,23},{8,0},{9,25... | collective-permute-start | bytes 1769480 | tf_op jit(solution)/shard_map/ppermute | solution.py:597
  55.5 4.4 %attention_back.1 = (bf16[512,1152]{1,0:T(8,128)(2,1)S(1)}, f32[1,3072]{1,0:T(1,128)S(1)}, bf16[2,4,48,384]{3,2,1,0:T(8,128)(2,1)S(1)}, bf16[2,4,48,384]{3,2,1,0...) custom-call(s32[3]{0:T(128)S(1)} %pad_add_fusion.ids, ...), custom_call_target="tpu_custom_call" | custom-call | flops 1 | bytes 1 | tf_op jit(solution)/shard_map/attention_back/pallas_call | solution.py:40
  60.7 2.5 %input_back.1 = (bf16[2,256,384]{2,1,0:T(8,128)(2,1)}, bf16[2,3840]{1,0:T(2,128)(2,1)S(1)}) custom-call(s32[3]{0:T(128)S(1)} %pad_add_fusion.ids, bf16[512,1152]{1,0:T(8,128)(2,1)S(1)} %get-tuple-element.102.gproj, bf16[4,384,384]{2,1,0:T(8,128)(2,1)S(1)} %get-tuple-element.89.wpo, bf16[2,256,384]{2,1,0:T(8,128)(2,1)S(1)} %copy-done.1, ...), custom_call_target="tpu_custom_call" | custom-call | flops 1 | bytes 1 | tf_op jit(solution)/shard_map/input_back/pallas_call | solution.py:40
  63.2 0.7 collective-permute-done.21.got_ud
  64.0 1.6 %collective-permute-start.23 = (bf16[2,4,48,384]{3,2,1,0:T(8,128)(2,1)S(1)}, bf16[2,4,48,384]{3,2,1,0:T(8,128)(2,1)S(1)}, u32[]{:S(2)}, u32[]{:S(2)}) collective-permute-start(bf16[2,4,48,384]{3,2,1,0:T(8,128)(2,1)S(1)} %sum_po.1), channel_id=1, source_target_pairs={{0,8},{1,17},{2,10},{3,19},{4,12},{5,21},{6,14},{7,23},{8,0},{9,25... | collective-permute-start | bytes 884744 | tf_op jit(solution)/shard_map/ppermute | solution.py:597
  66.1 1.2 %collective-permute-done.24.c_other = bf16[8,384]{1,0:T(8,128)(2,1)S(1)} collective-permute-done((bf16[8,384]{1,0:T(8,128)(2,1)S(1)}, bf16[8,384]{1,0:T(8,128)(2,1)S(1)}, u32[]{:S(2)}, u32[]{:S(2)}) %collective-permute-start.24) | collective-permute-done | bytes 6176 | tf_op jit(solution)/shard_map/ppermute | solution.py:597
  67.2 1.1 %collective-permute-start.26 = (bf16[4,3840]{1,0:T(4,128)(2,1)S(1)}, bf16[4,3840]{1,0:T(4,128)(2,1)S(1)}, u32[]{:S(2)}, u32[]{:S(2)}) collective-permute-start(bf16[4,3840]{1,0:T(4,128)(2,1)S(1)} %pair.1.g0), channel_id=1, source_target_pairs={{0,4},{1,5},{2,6},{3,7},{4,0},{5,1},{6,2},{7,3},{8,12},{9,13},{10,... | collective-permute-start | bytes 92168 | tf_op jit(solution)/shard_map/ppermute | solution.py:597
  68.3 3.8 %collective-permute-done.26.g2 = bf16[4,3840]{1,0:T(4,128)(2,1)S(1)} collective-permute-done((bf16[4,3840]{1,0:T(4,128)(2,1)S(1)}, bf16[4,3840]{1,0:T(4,128)(2,1)S(1)}, u32[]{:S(2)}, u32[]{:S(2)}) %collective-permute-start.26) | collective-permute-done | bytes 30752 | tf_op jit(solution)/shard_map/ppermute | solution.py:597
  72.3 2.1 %collective-permute-start.27 = (bf16[4,144,384]{2,1,0:T(8,128)(2,1)S(1)}, bf16[4,144,384]{2,1,0:T(8,128)(2,1)S(1)}, u32[]{:S(2)}, u32[]{:S(2)}) collective-permute-start(bf16[4,144,384]{2,1,0:T(8,128)(2,1)S(1)} %turn.1), channel_id=1, source_target_pairs={{0,16},{1,9},{2,18},{3,11},{4,20},{5,13},{6,22},{7,15},{8,24},{9,1... | collective-permute-start | bytes 1327112 | tf_op jit(solution)/shard_map/ppermute | solution.py:597
  74.4 2.8 %collective-permute-start.28 = (bf16[4,3840]{1,0:T(4,128)(2,1)S(1)}, bf16[4,3840]{1,0:T(4,128)(2,1)S(1)}, u32[]{:S(2)}, u32[]{:S(2)}) collective-permute-start(bf16[4,3840]{1,0:T(4,128)(2,1)S(1)} %pair.1.g0), channel_id=1, source_target_pairs={{0,2},{1,3},{2,0},{3,1},{4,6},{5,7},{6,4},{7,5},{8,10},{9,11},{10,... | collective-permute-start | bytes 92168 | tf_op jit(solution)/shard_map/ppermute | solution.py:597
  77.2 1.8 %collective-permute-done.28.g1 = bf16[4,3840]{1,0:T(4,128)(2,1)S(1)} collective-permute-done((bf16[4,3840]{1,0:T(4,128)(2,1)S(1)}, bf16[4,3840]{1,0:T(4,128)(2,1)S(1)}, u32[]{:S(2)}, u32[]{:S(2)}) %collective-permute-start.28) | collective-permute-done | bytes 30752 | tf_op jit(solution)/shard_map/ppermute | solution.py:597
  79.1 2.0 %collective-permute-done.29.g3 = bf16[4,3840]{1,0:T(4,128)(2,1)S(1)} collective-permute-done((bf16[4,3840]{1,0:T(4,128)(2,1)S(1)}, bf16[4,3840]{1,0:T(4,128)(2,1)S(1)}, u32[]{:S(2)}, u32[]{:S(2)}) %collective-permute-start.29) | collective-permute-done | bytes 30752 | tf_op jit(solution)/shard_map/ppermute | solution.py:597
  81.1 0.8 cond_back.1
  82.2 1.4 %collective-permute-start.30 = (bf16[2,160,384]{2,1,0:T(8,128)(2,1)S(1)}, bf16[2,160,384]{2,1,0:T(8,128)(2,1)S(1)}, u32[]{:S(2)}, u32[]{:S(2)}) collective-permute-start(bf16[2,160,384]{2,1,0:T(8,128)(2,1)S(1)} %join_far.1), channel_id=1, source_target_pairs={{0,2},{1,3},{2,0},{3,1},{4,6},{5,7},{6,4},{7,5},{8,10},{9,11},{10,... | collective-permute-start | bytes 737288 | tf_op jit(solution)/shard_map/ppermute | solution.py:597
  83.7 1.0 collective-permute-start.32
  84.7 1.6 %collective-permute-start.33 = (bf16[16,4224]{1,0:T(8,128)(2,1)S(1)}, bf16[16,4224]{1,0:T(8,128)(2,1)S(1)}, u32[]{:S(2)}, u32[]{:S(2)}) collective-permute-start(bf16[16,4224]{1,0:T(8,128)(2,1)S(1)} %pack.1.e0), channel_id=1, source_target_pairs={{0,16},{1,9},{2,18},{3,11},{4,20},{5,13},{6,22},{7,15},{8,24},{9,1... | collective-permute-start | bytes 405512 | tf_op jit(solution)/shard_map/ppermute | solution.py:597
  86.3 0.9 collective-permute-start.34
  87.2 1.3 %collective-permute-done.30.got = bf16[2,160,384]{2,1,0:T(8,128)(2,1)S(1)} collective-permute-done((bf16[2,160,384]{2,1,0:T(8,128)(2,1)S(1)}, bf16[2,160,384]{2,1,0:T(8,128)(2,1)S(1)}, u32[]{:S(2)}, u32[]{:S(2)}) %collective-permute-start.30) | collective-permute-done | bytes 245792 | tf_op jit(solution)/shard_map/ppermute | solution.py:597
  89.3 1.0 collective-permute-done.32.e1
  90.3 1.0 collective-permute-done.33.e2
  91.3 0.9 collective-permute-done.34.e3
  92.2 2.1 %mod_weight.1 = (f32[48,2304]{1,0:T(8,128)}, f32[288]{0:T(512)}, f32[96]{0:T(128)}, f32[48]{0:T(128)}, f32[192]{0:T(256)}, /*index=5*/f32[48]{0:T(128)}) custom-call(s32[3]{0:T(128)S(1)} %pad_add_fusion.ids, bf16[16,4224]{1,0:T(8,128)(2,1)S(1)} %pack.1.e0, bf16[16,4224]{1,0:T(8,128)(2,1)S(1)} %collective-permute-done.32.e1, ...), custom_call_target="tpu_custom_call" | custom-call | flops 1 | bytes 1 | tf_op jit(solution)/shard_map/mod_weight/pallas_call | solution.py:40
  94.6 1.4 %collective-permute-start.36 = (bf16[144,384]{1,0:T(8,128)(2,1)S(1)}, bf16[144,384]{1,0:T(8,128)(2,1)S(1)}, u32[]{:S(2)}, u32[]{:S(2)}) collective-permute-start(bf16[144,384]{1,0:T(8,128)(2,1)S(1)} %get-tuple-element.128.g0), channel_id=1, source_target_pairs={{0,8},{1,17},{2,10},{3,19},{4,12},{5,21},{6,14},{7,23},{8,0},{9,25... | collective-permute-start | bytes 331784 | tf_op jit(solution)/shard_map/ppermute | solution.py:597
  96.0 0.9 collective-permute-start.37
  96.9 1.3 %collective-permute-start.38 = (bf16[144,384]{1,0:T(8,128)(2,1)S(1)}, bf16[144,384]{1,0:T(8,128)(2,1)S(1)}, u32[]{:S(2)}, u32[]{:S(2)}) collective-permute-start(bf16[144,384]{1,0:T(8,128)(2,1)S(1)} %get-tuple-element.128.g0), channel_id=1, source_target_pairs={{0,24},{1,25},{2,26},{3,27},{4,28},{5,29},{6,30},{7,31},{8,16},{9,... | collective-permute-start | bytes 331784 | tf_op jit(solution)/shard_map/ppermute | solution.py:597
  98.7 1.2 %collective-permute-done.36.g1 = bf16[144,384]{1,0:T(8,128)(2,1)S(1)} collective-permute-done((bf16[144,384]{1,0:T(8,128)(2,1)S(1)}, bf16[144,384]{1,0:T(8,128)(2,1)S(1)}, u32[]{:S(2)}, u32[]{:S(2)}) %collective-permute-start.36) | collective-permute-done | bytes 110624 | tf_op jit(solution)/shard_map/ppermute | solution.py:597
  99.9 0.8 collective-permute-done.37.g2
  100.7 2.8 %collective-permute-done.38.g3 = bf16[144,384]{1,0:T(8,128)(2,1)S(1)} collective-permute-done((bf16[144,384]{1,0:T(8,128)(2,1)S(1)}, bf16[144,384]{1,0:T(8,128)(2,1)S(1)}, u32[]{:S(2)}, u32[]{:S(2)}) %collective-permute-start.38) | collective-permute-done | bytes 110624 | tf_op jit(solution)/shard_map/ppermute | solution.py:597
  103.6 1.5 %final.1 = (f32[48,1152]{1,0:T(8,128)}, f32[48,384]{1,0:T(8,128)}, f32[48,1536]{1,0:T(8,128)}, f32[192,384]{1,0:T(8,128)}) custom-call(s32[3]{0:T(128)S(1)} %pad_add_fusion.ids, bf16[144,384]{1,0:T(8,128)(2,1)S(1)} %get-tuple-element.128.g0, bf16[144,384]{1,0:T(8,128)(2,1)S(1)} %collective-permute-done.36.g1, ...), custom_call_target="tpu_custom_call" | custom-call | flops 1 | bytes 1 | tf_op jit(solution)/shard_map/final/pallas_call | solution.py:40
  (95 shorter events, 10.6 us)
Async XLA Ops:
  0.6 37.5 %copy-start.9 = (bf16[48,1152]{1,0:T(8,128)(2,1)S(1)}, bf16[48,1152]{1,0:T(8,128)(2,1)}, u32[]{:S(2)}) copy-start(bf16[48,1152]{1,0:T(8,128)(2,1)} %refs_8_.2) | copy-start | bytes 331780
  0.7 37.4 %copy-start.11 = (bf16[48,384]{1,0:T(8,128)(2,1)S(1)}, bf16[48,384]{1,0:T(8,128)(2,1)}, u32[]{:S(2)}) copy-start(bf16[48,384]{1,0:T(8,128)(2,1)} %refs_9_.2) | copy-start | bytes 110596
  2.2 35.8 %copy-start.1 = (bf16[2,256,384]{2,1,0:T(8,128)(2,1)S(1)}, bf16[2,256,384]{2,1,0:T(8,128)(2,1)}, u32[]{:S(2)}) copy-start(bf16[2,256,384]{2,1,0:T(8,128)(2,1)} %lat.1) | copy-start | bytes 1179652
  2.3 4.9 %collective-permute-start.1 = (bf16[48,2304]{1,0:T(8,128)(2,1)}, bf16[48,2304]{1,0:T(8,128)(2,1)S(1)}, u32[]{:S(2)}, u32[]{:S(2)}) collective-permute-start(bf16[48,2304]{1,0:T(8,128)(2,1)} %wmod.1), channel_id=1, source_target_pairs={{0,1},{1,0},{2,3},{3,2},{4,5},{5,4},{6,7},{7,6},{8,9},{9,8},{10,11... | collective-permute-start | bytes 663560 | tf_op jit(solution)/shard_map/ppermute | solution.py:597
  2.8 11.3 %collective-permute-start.5 = (bf16[48,1536]{1,0:T(8,128)(2,1)}, bf16[48,1536]{1,0:T(8,128)(2,1)S(1)}, u32[]{:S(2)}, u32[]{:S(2)}) collective-permute-start(bf16[48,1536]{1,0:T(8,128)(2,1)} %refs_8_.3), channel_id=1, source_target_pairs={{0,1},{1,0},{2,3},{3,2},{4,5},{5,4},{6,7},{7,6},{8,9},{9,8},{10,11... | collective-permute-start | bytes 442376 | tf_op jit(solution)/shard_map/ppermute | solution.py:597
  2.9 11.2 %collective-permute-start.6 = (bf16[192,384]{1,0:T(8,128)(2,1)}, bf16[192,384]{1,0:T(8,128)(2,1)S(1)}, u32[]{:S(2)}, u32[]{:S(2)}) collective-permute-start(bf16[192,384]{1,0:T(8,128)(2,1)} %refs_9_.3), channel_id=1, source_target_pairs={{0,1},{1,0},{2,3},{3,2},{4,5},{5,4},{6,7},{7,6},{8,9},{9,8},{10,11... | collective-permute-start | bytes 442376 | tf_op jit(solution)/shard_map/ppermute | solution.py:597
  3.3 10.7 %collective-permute-start = (bf16[160,384]{1,0:T(8,128)(2,1)}, bf16[160,384]{1,0:T(8,128)(2,1)S(1)}, u32[]{:S(2)}, u32[]{:S(2)}) collective-permute-start(bf16[160,384]{1,0:T(8,128)(2,1)} %pick.1.q0), channel_id=1, source_target_pairs={{0,4},{1,5},{2,6},{3,7},{4,0},{5,1},{6,2},{7,3},{8,12},{9,13},{10,... | collective-permute-start | bytes 368648 | tf_op jit(solution)/shard_map/ppermute | solution.py:597
  7.0 5.5 %collective-permute-start.3 = (bf16[48,1152]{1,0:T(8,128)(2,1)}, bf16[48,1152]{1,0:T(8,128)(2,1)S(1)}, u32[]{:S(2)}, u32[]{:S(2)}) collective-permute-start(bf16[48,1152]{1,0:T(8,128)(2,1)} %refs_8_.2), channel_id=1, source_target_pairs={{0,1},{1,0},{2,3},{3,2},{4,5},{5,4},{6,7},{7,6},{8,9},{9,8},{10,11... | collective-permute-start | bytes 331784 | tf_op jit(solution)/shard_map/ppermute | solution.py:597
  7.1 5.1 %collective-permute-start.4 = (bf16[48,384]{1,0:T(8,128)(2,1)}, bf16[48,384]{1,0:T(8,128)(2,1)S(1)}, u32[]{:S(2)}, u32[]{:S(2)}) collective-permute-start(bf16[48,384]{1,0:T(8,128)(2,1)} %refs_9_.2), channel_id=1, source_target_pairs={{0,1},{1,0},{2,3},{3,2},{4,5},{5,4},{6,7},{7,6},{8,9},{9,8},{10,11... | collective-permute-start | bytes 110600 | tf_op jit(solution)/shard_map/ppermute | solution.py:597
  11.7 11.5 %copy-start.8 = (bf16[160,384]{1,0:T(8,128)(2,1)S(1)}, bf16[160,384]{1,0:T(8,128)(2,1)}, u32[]{:S(2)}) copy-start(bf16[160,384]{1,0:T(8,128)(2,1)} %pick.1.q0) | copy-start | bytes 368644
  12.2 1.8 %collective-permute-start.2 = (f32[3,2304]{1,0:T(4,128)S(1)}, f32[3,2304]{1,0:T(4,128)S(1)}, u32[]{:S(2)}, u32[]{:S(2)}) collective-permute-start(f32[3,2304]{1,0:T(4,128)S(1)} %get-tuple-element.76.placed), channel_id=1, source_target_pairs={{0,1},{1,0},{2,3},{3,2},{4,5},{5,4},{6,7},{7,6},{8,9},{9,8},{10,11... | collective-permute-start | bytes 82952 | tf_op jit(solution)/shard_map/ppermute | solution.py:597
  12.5 6.3 %collective-permute-start.7 = (bf16[160,384]{1,0:T(8,128)(2,1)}, bf16[160,384]{1,0:T(8,128)(2,1)S(1)}, u32[]{:S(2)}, u32[]{:S(2)}) collective-permute-start(bf16[160,384]{1,0:T(8,128)(2,1)} %pick.1.q0), channel_id=1, source_target_pairs={{0,2},{1,3},{2,0},{3,1},{4,6},{5,7},{6,4},{7,5},{8,10},{9,11},{10,... | collective-permute-start | bytes 368648 | tf_op jit(solution)/shard_map/ppermute | solution.py:597
  14.1 6.8 %collective-permute-start.8 = (bf16[160,384]{1,0:T(8,128)(2,1)S(1)}, bf16[160,384]{1,0:T(8,128)(2,1)S(1)}, u32[]{:S(2)}, u32[]{:S(2)}) collective-permute-start(bf16[160,384]{1,0:T(8,128)(2,1)S(1)} %collective-permute-done.q2), channel_id=1, source_target_pairs={{0,2},{1,3},{2,0},{3,1},{4,6},{5,7},{6,4},{7,5},{8,10},{9,11},{10,... | collective-permute-start | bytes 368648 | tf_op jit(solution)/shard_map/ppermute | solution.py:597
  20.9 7.9 %collective-permute-start.9 = (bf16[3,144,384]{2,1,0:T(8,128)(2,1)S(1)}, bf16[3,144,384]{2,1,0:T(8,128)(2,1)S(1)}, u32[]{:S(2)}, u32[]{:S(2)}) collective-permute-start(bf16[3,144,384]{2,1,0:T(8,128)(2,1)S(1)} %stack.13.refs_0_), channel_id=1, source_target_pairs={{0,8},{1,17},{2,10},{3,19},{4,12},{5,21},{6,14},{7,23},{8,0},{9,25... | collective-permute-start | bytes 995336 | tf_op jit(solution)/shard_map/ppermute | solution.py:597
  24.0 4.4 %collective-permute-start.10 = (f32[2,4,2304]{2,1,0:T(4,128)S(1)}, f32[2,4,2304]{2,1,0:T(4,128)S(1)}, u32[]{:S(2)}, u32[]{:S(2)}) collective-permute-start(f32[2,4,2304]{2,1,0:T(4,128)S(1)} %get-tuple-element.85), channel_id=1, source_target_pairs={{0,2},{1,3},{2,0},{3,1},{4,6},{5,7},{6,4},{7,5},{8,10},{9,11},{10,... | collective-permute-start | bytes 221192 | tf_op jit(solution)/shard_map/ppermute | solution.py:597
  25.7 7.3 %collective-permute-start.11 = (bf16[3,144,384]{2,1,0:T(8,128)(2,1)S(1)}, bf16[3,144,384]{2,1,0:T(8,128)(2,1)S(1)}, u32[]{:S(2)}, u32[]{:S(2)}) collective-permute-start(bf16[3,144,384]{2,1,0:T(8,128)(2,1)S(1)} %stack.13.refs_0_), channel_id=1, source_target_pairs={{0,16},{1,9},{2,18},{3,11},{4,20},{5,13},{6,22},{7,15},{8,24},{9,1... | collective-permute-start | bytes 995336 | tf_op jit(solution)/shard_map/ppermute | solution.py:597
  28.8 7.6 %collective-permute-start.12 = (bf16[3,144,384]{2,1,0:T(8,128)(2,1)S(1)}, bf16[3,144,384]{2,1,0:T(8,128)(2,1)S(1)}, u32[]{:S(2)}, u32[]{:S(2)}) collective-permute-start(bf16[3,144,384]{2,1,0:T(8,128)(2,1)S(1)} %collective-permute-done.9.refs_1_), channel_id=1, source_target_pairs={{0,16},{1,9},{2,18},{3,11},{4,20},{5,13},{6,22},{7,15},{8,24},{9,1... | collective-permute-start | bytes 995336 | tf_op jit(solution)/shard_map/ppermute | solution.py:597
  31.4 10.3 %copy-start.6 = (bf16[48,1536]{1,0:T(8,128)(2,1)S(1)}, bf16[48,1536]{1,0:T(8,128)(2,1)}, u32[]{:S(2)}) copy-start(bf16[48,1536]{1,0:T(8,128)(2,1)} %refs_8_.3) | copy-start | bytes 442372
  31.4 10.3 %copy-start.7 = (bf16[192,384]{1,0:T(8,128)(2,1)S(1)}, bf16[192,384]{1,0:T(8,128)(2,1)}, u32[]{:S(2)}) copy-start(bf16[192,384]{1,0:T(8,128)(2,1)} %refs_9_.3) | copy-start | bytes 442372
  31.4 10.3 %copy-start.10 = (bf16[2,256,384]{2,1,0:T(8,128)(2,1)S(1)}, bf16[2,256,384]{2,1,0:T(8,128)(2,1)}, u32[]{:S(2)}) copy-start(bf16[2,256,384]{2,1,0:T(8,128)(2,1)} %refs_15_.1) | copy-start | bytes 1179652
  31.4 4.9 %collective-permute-start.16 = (f32[4,2304]{1,0:T(4,128)S(1)}, f32[4,2304]{1,0:T(4,128)S(1)}, u32[]{:S(2)}, u32[]{:S(2)}) collective-permute-start(f32[4,2304]{1,0:T(4,128)S(1)} %slice_bitcast_fusion), channel_id=1, source_target_pairs={{0,4},{1,5},{2,6},{3,7},{4,0},{5,1},{6,2},{7,3},{8,12},{9,13},{10,... | collective-permute-start | bytes 110600 | tf_op jit(solution)/shard_map/ppermute | solution.py:597
  32.5 4.0 %collective-permute-start.13 = (bf16[3,144,384]{2,1,0:T(8,128)(2,1)S(1)}, bf16[3,144,384]{2,1,0:T(8,128)(2,1)S(1)}, u32[]{:S(2)}, u32[]{:S(2)}) collective-permute-start(bf16[3,144,384]{2,1,0:T(8,128)(2,1)S(1)} %stack.13.refs_0_), channel_id=1, source_target_pairs={{0,1},{1,0},{2,3},{3,2},{4,5},{5,4},{6,7},{7,6},{8,9},{9,8},{10,11... | collective-permute-start | bytes 995336 | tf_op jit(solution)/shard_map/ppermute | solution.py:597
  32.5 4.0 %collective-permute-start.14 = (bf16[3,144,384]{2,1,0:T(8,128)(2,1)S(1)}, bf16[3,144,384]{2,1,0:T(8,128)(2,1)S(1)}, u32[]{:S(2)}, u32[]{:S(2)}) collective-permute-start(bf16[3,144,384]{2,1,0:T(8,128)(2,1)S(1)} %collective-permute-done.9.refs_1_), channel_id=1, source_target_pairs={{0,1},{1,0},{2,3},{3,2},{4,5},{5,4},{6,7},{7,6},{8,9},{9,8},{10,11... | collective-permute-start | bytes 995336 | tf_op jit(solution)/shard_map/ppermute | solution.py:597
  33.0 3.5 %collective-permute-start.15 = (bf16[3,144,384]{2,1,0:T(8,128)(2,1)S(1)}, bf16[3,144,384]{2,1,0:T(8,128)(2,1)S(1)}, u32[]{:S(2)}, u32[]{:S(2)}) collective-permute-start(bf16[3,144,384]{2,1,0:T(8,128)(2,1)S(1)} %collective-permute-done.11.refs_2_), channel_id=1, source_target_pairs={{0,1},{1,0},{2,3},{3,2},{4,5},{5,4},{6,7},{7,6},{8,9},{9,8},{10,11... | collective-permute-start | bytes 995336 | tf_op jit(solution)/shard_map/ppermute | solution.py:597
  36.5 1.6 %collective-permute-start.17 = (bf16[3,144,384]{2,1,0:T(8,128)(2,1)S(1)}, bf16[3,144,384]{2,1,0:T(8,128)(2,1)S(1)}, u32[]{:S(2)}, u32[]{:S(2)}) collective-permute-start(bf16[3,144,384]{2,1,0:T(8,128)(2,1)S(1)} %collective-permute-done.12.refs_3_), channel_id=1, source_target_pairs={{0,1},{1,0},{2,3},{3,2},{4,5},{5,4},{6,7},{7,6},{8,9},{9,8},{10,11... | collective-permute-start | bytes 995336 | tf_op jit(solution)/shard_map/ppermute | solution.py:597
  41.7 9.3 %copy-start = (bf16[512,1152]{1,0:T(8,128)(2,1)S(1)}, bf16[512,1152]{1,0:T(8,128)(2,1)}, u32[]{:S(2)}) copy-start(bf16[512,1152]{1,0:T(8,128)(2,1)} %get-tuple-element.93.proj) | copy-start | bytes 3538948
  50.9 2.9 %collective-permute-start.18 = (bf16[2,4,2,48,384]{4,3,2,1,0:T(8,128)(2,1)}, bf16[2,4,2,48,384]{4,3,2,1,0:T(8,128)(2,1)S(1)}, u32[]{:S(2)}, u32[]{:S(2)}) collective-permute-start(bf16[2,4,2,48,384]{4,3,2,1,0:T(8,128)(2,1)} %get-tuple-element.99), channel_id=1, source_target_pairs={{0,1},{1,0},{2,3},{3,2},{4,5},{5,4},{6,7},{7,6},{8,9},{9,8},{10,11... | collective-permute-start | bytes 1769480 | tf_op jit(solution)/shard_map/ppermute | solution.py:597
  54.0 9.9 %collective-permute-start.21 = (bf16[2,4,2,48,384]{4,3,2,1,0:T(8,128)(2,1)S(1)}, bf16[2,4,2,48,384]{4,3,2,1,0:T(8,128)(2,1)S(1)}, u32[]{:S(2)}, u32[]{:S(2)}) collective-permute-start(bf16[2,4,2,48,384]{4,3,2,1,0:T(8,128)(2,1)S(1)} %sum_ud.1), channel_id=1, source_target_pairs={{0,8},{1,17},{2,10},{3,19},{4,12},{5,21},{6,14},{7,23},{8,0},{9,25... | collective-permute-start | bytes 1769480 | tf_op jit(solution)/shard_map/ppermute | solution.py:597
  59.9 3.3 %collective-permute-start.22 = (bf16[2,4,48,384]{3,2,1,0:T(8,128)(2,1)S(1)}, bf16[2,4,48,384]{3,2,1,0:T(8,128)(2,1)S(1)}, u32[]{:S(2)}, u32[]{:S(2)}) collective-permute-start(bf16[2,4,48,384]{3,2,1,0:T(8,128)(2,1)S(1)} %get-tuple-element.112), channel_id=1, source_target_pairs={{0,1},{1,0},{2,3},{3,2},{4,5},{5,4},{6,7},{7,6},{8,9},{9,8},{10,11... | collective-permute-start | bytes 884744 | tf_op jit(solution)/shard_map/ppermute | solution.py:597
  60.6 11.5 %collective-permute-start.19 = (bf16[2,4,2,48,384]{4,3,2,1,0:T(8,128)(2,1)S(1)}, bf16[2,4,2,48,384]{4,3,2,1,0:T(8,128)(2,1)S(1)}, u32[]{:S(2)}, u32[]{:S(2)}) collective-permute-start(bf16[2,4,2,48,384]{4,3,2,1,0:T(8,128)(2,1)S(1)} %copy-done.18), channel_id=1, source_target_pairs={{0,1},{1,0},{2,3},{3,2},{4,5},{5,4},{6,7},{7,6},{8,9},{9,8},{10,11... | collective-permute-start | bytes 1769480 | tf_op jit(solution)/shard_map/ppermute | solution.py:597
  64.0 8.1 %collective-permute-start.23 = (bf16[2,4,48,384]{3,2,1,0:T(8,128)(2,1)S(1)}, bf16[2,4,48,384]{3,2,1,0:T(8,128)(2,1)S(1)}, u32[]{:S(2)}, u32[]{:S(2)}) collective-permute-start(bf16[2,4,48,384]{3,2,1,0:T(8,128)(2,1)S(1)} %sum_po.1), channel_id=1, source_target_pairs={{0,8},{1,17},{2,10},{3,19},{4,12},{5,21},{6,14},{7,23},{8,0},{9,25... | collective-permute-start | bytes 884744 | tf_op jit(solution)/shard_map/ppermute | solution.py:597
  65.5 6.6 %collective-permute-start.20 = (bf16[2,4,48,384]{3,2,1,0:T(8,128)(2,1)S(1)}, bf16[2,4,48,384]{3,2,1,0:T(8,128)(2,1)S(1)}, u32[]{:S(2)}, u32[]{:S(2)}) collective-permute-start(bf16[2,4,48,384]{3,2,1,0:T(8,128)(2,1)S(1)} %get-tuple-element.110), channel_id=1, source_target_pairs={{0,1},{1,0},{2,3},{3,2},{4,5},{5,4},{6,7},{7,6},{8,9},{9,8},{10,11... | collective-permute-start | bytes 884744 | tf_op jit(solution)/shard_map/ppermute | solution.py:597
  65.5 1.7 %collective-permute-start.25 = (bf16[2,3840]{1,0:T(2,128)(2,1)S(1)}, bf16[2,3840]{1,0:T(2,128)(2,1)S(1)}, u32[]{:S(2)}, u32[]{:S(2)}) collective-permute-start(bf16[2,3840]{1,0:T(2,128)(2,1)S(1)} %get-tuple-element.116.own), channel_id=1, source_target_pairs={{0,1},{1,0},{2,3},{3,2},{4,5},{5,4},{6,7},{7,6},{8,9},{9,8},{10,11... | collective-permute-start | bytes 46088 | tf_op jit(solution)/shard_map/ppermute | solution.py:597
  66.1 1.2 %collective-permute-start.24 = (bf16[8,384]{1,0:T(8,128)(2,1)S(1)}, bf16[8,384]{1,0:T(8,128)(2,1)S(1)}, u32[]{:S(2)}, u32[]{:S(2)}) collective-permute-start(bf16[8,384]{1,0:T(8,128)(2,1)S(1)} %get-tuple-element.115.c_own), channel_id=1, source_target_pairs={{0,1},{1,0},{2,3},{3,2},{4,5},{5,4},{6,7},{7,6},{8,9},{9,8},{10,11... | collective-permute-start | bytes 18440 | tf_op jit(solution)/shard_map/ppermute | solution.py:597
  67.2 4.9 %collective-permute-start.26 = (bf16[4,3840]{1,0:T(4,128)(2,1)S(1)}, bf16[4,3840]{1,0:T(4,128)(2,1)S(1)}, u32[]{:S(2)}, u32[]{:S(2)}) collective-permute-start(bf16[4,3840]{1,0:T(4,128)(2,1)S(1)} %pair.1.g0), channel_id=1, source_target_pairs={{0,4},{1,5},{2,6},{3,7},{4,0},{5,1},{6,2},{7,3},{8,12},{9,13},{10,... | collective-permute-start | bytes 92168 | tf_op jit(solution)/shard_map/ppermute | solution.py:597
  72.3 9.8 %collective-permute-start.27 = (bf16[4,144,384]{2,1,0:T(8,128)(2,1)S(1)}, bf16[4,144,384]{2,1,0:T(8,128)(2,1)S(1)}, u32[]{:S(2)}, u32[]{:S(2)}) collective-permute-start(bf16[4,144,384]{2,1,0:T(8,128)(2,1)S(1)} %turn.1), channel_id=1, source_target_pairs={{0,16},{1,9},{2,18},{3,11},{4,20},{5,13},{6,22},{7,15},{8,24},{9,1... | collective-permute-start | bytes 1327112 | tf_op jit(solution)/shard_map/ppermute | solution.py:597
  74.4 4.7 %collective-permute-start.28 = (bf16[4,3840]{1,0:T(4,128)(2,1)S(1)}, bf16[4,3840]{1,0:T(4,128)(2,1)S(1)}, u32[]{:S(2)}, u32[]{:S(2)}) collective-permute-start(bf16[4,3840]{1,0:T(4,128)(2,1)S(1)} %pair.1.g0), channel_id=1, source_target_pairs={{0,2},{1,3},{2,0},{3,1},{4,6},{5,7},{6,4},{7,5},{8,10},{9,11},{10,... | collective-permute-start | bytes 92168 | tf_op jit(solution)/shard_map/ppermute | solution.py:597
  77.2 3.9 %collective-permute-start.29 = (bf16[4,3840]{1,0:T(4,128)(2,1)S(1)}, bf16[4,3840]{1,0:T(4,128)(2,1)S(1)}, u32[]{:S(2)}, u32[]{:S(2)}) collective-permute-start(bf16[4,3840]{1,0:T(4,128)(2,1)S(1)} %collective-permute-done.26.g2), channel_id=1, source_target_pairs={{0,2},{1,3},{2,0},{3,1},{4,6},{5,7},{6,4},{7,5},{8,10},{9,11},{10,... | collective-permute-start | bytes 92168 | tf_op jit(solution)/shard_map/ppermute | solution.py:597
  82.2 15.9 %copy-start.17 = (bf16[2,384]{1,0:T(2,128)(2,1)S(1)}, bf16[2,384]{1,0:T(2,128)(2,1)}, u32[]{:S(2)}) copy-start(bf16[2,384]{1,0:T(2,128)(2,1)} %cond.1) | copy-start | bytes 4612
  82.2 6.3 %collective-permute-start.30 = (bf16[2,160,384]{2,1,0:T(8,128)(2,1)S(1)}, bf16[2,160,384]{2,1,0:T(8,128)(2,1)S(1)}, u32[]{:S(2)}, u32[]{:S(2)}) collective-permute-start(bf16[2,160,384]{2,1,0:T(8,128)(2,1)S(1)} %join_far.1), channel_id=1, source_target_pairs={{0,2},{1,3},{2,0},{3,1},{4,6},{5,7},{6,4},{7,5},{8,10},{9,11},{10,... | collective-permute-start | bytes 737288 | tf_op jit(solution)/shard_map/ppermute | solution.py:597
  83.7 6.6 %collective-permute-start.32 = (bf16[16,4224]{1,0:T(8,128)(2,1)S(1)}, bf16[16,4224]{1,0:T(8,128)(2,1)S(1)}, u32[]{:S(2)}, u32[]{:S(2)}) collective-permute-start(bf16[16,4224]{1,0:T(8,128)(2,1)S(1)} %pack.1.e0), channel_id=1, source_target_pairs={{0,8},{1,17},{2,10},{3,19},{4,12},{5,21},{6,14},{7,23},{8,0},{9,25... | collective-permute-start | bytes 405512 | tf_op jit(solution)/shard_map/ppermute | solution.py:597
  84.7 6.6 %collective-permute-start.33 = (bf16[16,4224]{1,0:T(8,128)(2,1)S(1)}, bf16[16,4224]{1,0:T(8,128)(2,1)S(1)}, u32[]{:S(2)}, u32[]{:S(2)}) collective-permute-start(bf16[16,4224]{1,0:T(8,128)(2,1)S(1)} %pack.1.e0), channel_id=1, source_target_pairs={{0,16},{1,9},{2,18},{3,11},{4,20},{5,13},{6,22},{7,15},{8,24},{9,1... | collective-permute-start | bytes 405512 | tf_op jit(solution)/shard_map/ppermute | solution.py:597
  86.3 5.9 %collective-permute-start.34 = (bf16[16,4224]{1,0:T(8,128)(2,1)S(1)}, bf16[16,4224]{1,0:T(8,128)(2,1)S(1)}, u32[]{:S(2)}, u32[]{:S(2)}) collective-permute-start(bf16[16,4224]{1,0:T(8,128)(2,1)S(1)} %pack.1.e0), channel_id=1, source_target_pairs={{0,24},{1,25},{2,26},{3,27},{4,28},{5,29},{6,30},{7,31},{8,16},{9,... | collective-permute-start | bytes 405512 | tf_op jit(solution)/shard_map/ppermute | solution.py:597
  88.6 5.8 %collective-permute-start.31 = (bf16[160,384]{1,0:T(8,128)(2,1)S(1)}, bf16[160,384]{1,0:T(8,128)(2,1)S(1)}, u32[]{:S(2)}, u32[]{:S(2)}) collective-permute-start(bf16[160,384]{1,0:T(8,128)(2,1)S(1)} %get-tuple-element.122), channel_id=1, source_target_pairs={{0,4},{1,5},{2,6},{3,7},{4,0},{5,1},{6,2},{7,3},{8,12},{9,13},{10,... | collective-permute-start | bytes 368648 | tf_op jit(solution)/shard_map/ppermute | solution.py:597
  94.5 3.6 %collective-permute-start.35 = (f32[2,384]{1,0:T(2,128)S(1)}, f32[2,384]{1,0:T(2,128)S(1)}, u32[]{:S(2)}, u32[]{:S(2)}) collective-permute-start(f32[2,384]{1,0:T(2,128)S(1)} %slice.15), channel_id=1, source_target_pairs={{0,1},{1,0},{2,3},{3,2},{4,5},{5,4},{6,7},{7,6},{8,9},{9,8},{10,11... | collective-permute-start | bytes 9224 | tf_op jit(solution)/shard_map/ppermute | solution.py:597
  94.6 5.4 %collective-permute-start.36 = (bf16[144,384]{1,0:T(8,128)(2,1)S(1)}, bf16[144,384]{1,0:T(8,128)(2,1)S(1)}, u32[]{:S(2)}, u32[]{:S(2)}) collective-permute-start(bf16[144,384]{1,0:T(8,128)(2,1)S(1)} %get-tuple-element.128.g0), channel_id=1, source_target_pairs={{0,8},{1,17},{2,10},{3,19},{4,12},{5,21},{6,14},{7,23},{8,0},{9,25... | collective-permute-start | bytes 331784 | tf_op jit(solution)/shard_map/ppermute | solution.py:597
  96.0 4.7 %collective-permute-start.37 = (bf16[144,384]{1,0:T(8,128)(2,1)S(1)}, bf16[144,384]{1,0:T(8,128)(2,1)S(1)}, u32[]{:S(2)}, u32[]{:S(2)}) collective-permute-start(bf16[144,384]{1,0:T(8,128)(2,1)S(1)} %get-tuple-element.128.g0), channel_id=1, source_target_pairs={{0,16},{1,9},{2,18},{3,11},{4,20},{5,13},{6,22},{7,15},{8,24},{9,1... | collective-permute-start | bytes 331784 | tf_op jit(solution)/shard_map/ppermute | solution.py:597
  96.9 6.7 %collective-permute-start.38 = (bf16[144,384]{1,0:T(8,128)(2,1)S(1)}, bf16[144,384]{1,0:T(8,128)(2,1)S(1)}, u32[]{:S(2)}, u32[]{:S(2)}) collective-permute-start(bf16[144,384]{1,0:T(8,128)(2,1)S(1)} %get-tuple-element.128.g0), channel_id=1, source_target_pairs={{0,24},{1,25},{2,26},{3,27},{4,28},{5,29},{6,30},{7,31},{8,16},{9,... | collective-permute-start | bytes 331784 | tf_op jit(solution)/shard_map/ppermute | solution.py:597
  (10 other events, 32.5 us)
